TPU v7x, 32 devices: a whole 2x2x4 slice. The times are simulated.
32 devices in a mesh: fsdp: 8 (over y, x, core), ctx: 4 (over z).
Axes of the slice: x: 2, y: 2, z: 4, core: 2. Of those that a mesh axis runs over, the one named last changes fastest.
Arguments:
- byte_ids: int32 [8, 4096], P('fsdp', 'ctx'), may hold values from 0 to 255
- byte_table: bfloat16 [256, 768], replicated, may hold values from -6 to 6
- w_conv: bfloat16 [3072, 1024], P('fsdp'), may hold values from -0.109375 to 0.109375
- w_qkv: bfloat16 [1024, 1536], P('fsdp'), may hold values from -4 to 4
- w_out: bfloat16 [1024, 1024], P('fsdp'), may hold values from -0.1875 to 0.1875
- norm_gain: bfloat16 [1024], replicated, may hold values from 0.5 to 1.5
- teacher: bfloat16 [8, 1024, 1024], P('fsdp', 'ctx'), may hold values from -6 to 6
- align: int32 [8, 1024], P('fsdp', 'ctx'), may hold values from 0 to 1023, as said below
Outputs:
- hidden_out: bfloat16 [8, 1024, 1024], P('fsdp', 'ctx')
- token_loss: float32 [8, 1024], P('fsdp', 'ctx')
Inputs may be any that keep to these rules, and one draw needn't show every extreme that they name: Teacher token j of a sequence points at a latent of its own aligned block of 256 rows (align // 256 == j // 256); the first and the last token of each block point at that block's first and last latent.
All inputs are finite; a program needn't handle non-finite values.
Results may differ from a plain program's by a relative error of at most 0.039.
Values may be sent and summed in bfloat16 or wider, within the bound.
No kernel may reach another device: no remote copies, remote signals or barrier semaphores. Data moves between devices by JAX's collectives and lax.ppermute only.
A program may use at most 64 MiB of HBM per device.

v0:
```python
import math

import jax
import jax.numpy as jnp
from jax import lax
from jax.sharding import PartitionSpec as P

KW = 4
HQ = 16
HK = 4
HD = 64


theta_base = 500000.0
norm_eps = 1e-05
masked_score = -1e30


def rotate(values, positions):
    half_dim = values.shape[-1] // 2
    frequency = theta_base ** (-jnp.arange(half_dim, dtype=jnp.float32) * 2.0 / values.shape[-1])
    angles = positions.astype(jnp.float32)[:, None] * frequency[None, :]
    angles = jnp.concatenate([angles, angles], axis=-1)[:, None, :]
    turned = jnp.concatenate([-values[..., half_dim:], values[..., :half_dim]], axis=-1)
    return values * jnp.cos(angles) + turned * jnp.sin(angles)


def project(inputs, weight):
    return jnp.dot(
        inputs,
        lax.all_gather(weight, "fsdp", axis=0, tiled=True),
        preferred_element_type=jnp.float32,
    )


def body(byte_ids, byte_table, w_conv, w_qkv, w_out, norm_gain, teacher, align):
    score_scale = 1.0 / math.sqrt(HD)
    seq_bytes = byte_ids.shape[1]
    lat_rows = seq_bytes // KW
    query_width = HQ * HD
    key_width = HK * HD
    one_hot = (
        byte_ids[0][:, None] == jnp.arange(byte_table.shape[0], dtype=jnp.int32)[None, :]
    ).astype(jnp.bfloat16)
    embedded = jnp.dot(one_hot, byte_table, preferred_element_type=jnp.float32).astype(jnp.bfloat16)
    stacked = embedded.reshape(lat_rows, KW * byte_table.shape[1])
    latent = project(stacked, w_conv).astype(jnp.bfloat16)
    latent_wide = latent.astype(jnp.float32)
    scale_rows = lax.rsqrt(jnp.mean(latent_wide * latent_wide, axis=1, keepdims=True) + norm_eps)
    normed = (latent_wide * scale_rows * norm_gain.astype(jnp.float32)[None, :]).astype(
        jnp.bfloat16
    )
    projected = project(normed, w_qkv)
    ctx_index = lax.axis_index("ctx")
    positions = ctx_index * lat_rows + jnp.arange(lat_rows, dtype=jnp.int32)
    queries = rotate(projected[:, :query_width].reshape(lat_rows, HQ, HD), positions).astype(
        jnp.bfloat16
    )
    key_rows = rotate(
        projected[:, query_width : query_width + key_width].reshape(lat_rows, HK, HD), positions
    )
    key_rows = key_rows.astype(jnp.bfloat16).reshape(lat_rows, key_width)
    value_rows = projected[:, query_width + key_width :].astype(jnp.bfloat16)
    grouped = queries.reshape(lat_rows, HK, HQ // HK, HD)
    start_state = (
        jnp.full((HK, HQ // HK, lat_rows), masked_score, jnp.float32),
        jnp.zeros((HK, HQ // HK, lat_rows), jnp.float32),
        jnp.zeros((HK, HQ // HK, lat_rows, HD), jnp.float32),
    )
    key_all = lax.all_gather(key_rows, "ctx", axis=0, tiled=True)
    value_all = lax.all_gather(value_rows, "ctx", axis=0, tiled=True)
    blocks = key_all.shape[0] // lat_rows
    key_blocks = key_all.reshape(blocks, lat_rows, HK, HD)
    value_blocks = value_all.reshape(blocks, lat_rows, HK, HD)
    block_starts = lat_rows * jnp.arange(blocks, dtype=jnp.int32)

    def one_block(partial_value, block_data):
        key_block, value_block, key_start = block_data
        row_top, row_mass, weighted = partial_value
        scores = (
            jnp.einsum("qkgd,skd->kgqs", grouped, key_block, preferred_element_type=jnp.float32)
            * score_scale
        )
        key_pos = key_start + jnp.arange(lat_rows, dtype=jnp.int32)
        allowed = key_pos[None, :] <= positions[:, None]
        scores = jnp.where(allowed[None, None], scores, masked_score)
        new_top = jnp.maximum(row_top, jnp.max(scores, axis=-1))
        weights = jnp.exp(scores - new_top[..., None])
        shrink = jnp.exp(row_top - new_top)
        row_mass = row_mass * shrink + jnp.sum(weights, axis=-1)
        weighted = weighted * shrink[..., None] + jnp.einsum(
            "kgqs,skd->kgqd",
            weights.astype(jnp.bfloat16),
            value_block,
            preferred_element_type=jnp.float32,
        )
        return ((new_top, row_mass, weighted), None)

    result, unused = lax.scan(one_block, start_state, (key_blocks, value_blocks, block_starts))
    final_top, final_mass, final_sum = result
    attended = final_sum / final_mass[..., None]
    attended = jnp.transpose(attended, (2, 0, 1, 3)).reshape(lat_rows, HQ * HD).astype(jnp.bfloat16)
    branch = project(attended, w_out)
    hidden_out = (latent_wide + branch).astype(jnp.bfloat16)
    local_rows = align[0] - ctx_index * lat_rows
    picked = jnp.take(hidden_out, local_rows, axis=0)
    difference = picked.astype(jnp.float32) - teacher[0].astype(jnp.float32)
    token_loss = jnp.mean(difference * difference, axis=1)
    return (hidden_out[None], token_loss[None])


def solution(mesh):
    in_specs = (
        P("fsdp", "ctx"),
        P(),
        P("fsdp", None),
        P("fsdp", None),
        P("fsdp", None),
        P(),
        P("fsdp", "ctx", None),
        P("fsdp", "ctx"),
    )
    out_specs = (P("fsdp", "ctx", None), P("fsdp", "ctx"))
    return jax.shard_map(body, mesh=mesh, in_specs=in_specs, out_specs=out_specs, check_vma=False)
```

profile of v0, /device:TPU:24, one launch (start us, length us, event | category | flops | bytes accessed | tf_op | source)
XLA Modules:
  0.0 192.7 jit_solution(6115952278736330827)
XLA Ops:
  7.2 0.7 all-gather.4.cloned.1.call-update
  8.0 0.7 all-gather.6.cloned.1.call-update
  8.7 0.7 all-gather.8.cloned.1.call-update
  9.5 0.5 iota_multiply_fusion
  9.9 1.3 convolution_convert_fusion
  11.3 1.9 reshape.178
  13.2 0.7 fusion.35
  14.0 0.6 copy-done.8
  14.6 0.1 copy.19
  14.7 0.7 compare_select_fusion
  15.4 0.6 pad_clamp_fusion
  16.0 0.5 compare_and_fusion
  16.6 39.9 %all-gather.4.cloned.1.call-done = bf16[3072,1024]{1,0:T(8,128)(2,1)} async-done(((bf16[384,1024]{1,0:T(8,128)(2,1)}), bf16[3072,1024]{1,0:T(8,128)(2,1)}) %all-gather.4.cloned.1.call-update) | async-done | bytes 6291472 | tf_op jit(solution)/shard_map/all_gather | solution.py:31
  56.4 5.1 %fusion.22 = (f32[256]{0:T(256)S(1)}, bf16[256,1024]{1,0:T(8,128)(2,1)S(1)}) fusion(bf16[256,3072]{1,0:T(8,128)(2,1)} %reshape.178, bf16[3072,1024]{1,0:T(8,128)(2,1)} %all-gather.4.cloned.1.call-done), kind=kOutput, calls=%fused_computation.33 | convolution fusion | flops 1611661056 | bytes 8389632 | tf_op jit(solution)/shard_map/dot_general | solution.py:29
  61.6 29.1 %all-gather.6.cloned.1.call-done = bf16[1024,1536]{1,0:T(8,128)(2,1)} async-done(((bf16[128,1536]{1,0:T(8,128)(2,1)}), bf16[1024,1536]{1,0:T(8,128)(2,1)}) %all-gather.6.cloned.1.call-update) | async-done | bytes 3145744 | tf_op jit(solution)/shard_map/all_gather | solution.py:31
  90.7 2.9 %fusion.29 = f32[256,1536]{1,0:T(8,128)S(1)} fusion(bf16[1024,1536]{1,0:T(8,128)(2,1)} %all-gather.6.cloned.1.call-done, bf16[256,1024]{1,0:T(8,128)(2,1)S(1)} %get-tuple-element.136, f32[1024]{0:T(1024)S(1)} %convert_element_type.60, f32[256]{0:T(256)S(1)} %add_rsqrt_fusion), kind=kOutput, calls=%fused_computation.44 | convolution fusion | flops 806354944 | bytes 5248000 | tf_op jit(solution)/shard_map/dot_general | solution.py:29
  93.6 1.2 slice.34
  94.8 0.3 copy-done.3
  95.1 0.7 slice.42
  95.8 1.6 copy.23
  97.4 1.0 slice_negate_fusion
  98.5 0.1 copy.20
  98.7 0.1 copy.21
  98.8 1.0 add_convert_fusion
  99.8 16.3 %all_gather.17 = bf16[1024,256]{1,0:T(8,128)(2,1)S(1)} all-gather(bf16[256,256]{1,0:T(8,128)(2,1)S(1)} %add_convert_fusion), channel_id=1, replica_groups=mesh['fsdp'=8,'ctx'=4] {'ctx'}, dimensions={0}, use_global_device_ids=true | all-gather | bytes 655360 | tf_op jit(solution)/shard_map/all_gather | solution.py:70
  116.1 1.4 reshape.195
  117.5 1.5 copy.26
  119.0 15.5 %all_gather.18 = bf16[1024,256]{1,0:T(8,128)(2,1)S(1)} all-gather(bf16[256,256]{1,0:T(8,128)(2,1)} %slice.42), channel_id=1, replica_groups=mesh['fsdp'=8,'ctx'=4] {'ctx'}, dimensions={0}, use_global_device_ids=true | all-gather | bytes 655360 | tf_op jit(solution)/shard_map/all_gather | solution.py:71
  134.5 1.4 reshape.196
  135.9 2.2 %copy.27 = bf16[4,256,4,64]{1,3,2,0:T(8,128)(2,1)} copy(bf16[4,256,4,64]{3,2,1,0:T(4,128)(2,1)} %reshape.196) | data formatting | bytes 1048576
  138.1 1.4 fusion.26
  139.5 41.2 %while.15 = (s32[]{:T(128)}, f32[4,4,256]{2,1,0:T(4,128)S(1)}, f32[4,4,256]{2,1,0:T(4,128)}, f32[4,4,256,64]{2,3,1,0:T(8,128)S(1)}, s32[4]{0:T(128)}, /*index=5*...) while((s32[]{:T(128)}, f32[4,4,256]{2,1,0:T(4,128)S(1)}, ...), condition=%wide.region_4.5_spmd.clone, body=%wide.region_1.4_spmd.clone.sunk | while | flops 280842752 | bytes 32903908 | solution.py:99
  139.5 1.2 dynamic_slice.29
  140.7 0.6 iota_add_fusion.3
  141.4 0.1 broadcast_compare_fusion.2
  141.5 2.7 %fusion.53 = (f32[4,4,256]{2,1,0:T(4,128)S(1)}, f32[4,256,256,4]{2,1,3,0:T(8,128)}) fusion(pred[256,256]{0,1:T(8,128)(4,1)S(1)} %broadcast_compare_fusion.2, bf16[256,4,4,64]{0,3,2,1:T(8,128)(2,1)S(1)} %get-tuple-element.232, bf16[4,256,4,64]{1,3,2,0:T(8,128)(2,1)S(1)} %get-tuple-element.231, s32[]{:T(128)} %get-tuple-element.215), kind=kOutput, calls=%fused_computation.6.clone.1 | convolution fusion | flops 137359360 | bytes 4931588 | tf_op jit(solution)/shard_map/while/body/eval_jaxpr/qkgd,skd->kgqs/dot_general | solution.py:81
  144.2 3.2 %fusion.54 = f32[4,4,256]{2,1,0:T(4,128)S(1)} fusion(f32[4,256,256,4]{2,1,3,0:T(8,128)} %get-tuple-element.201, f32[4,4,256]{2,1,0:T(4,128)S(1)} %select_maximum_fusion.2, pred[256,256]{0,1:T(8,128)(4,1)S(1)} %broadcast_compare_fusion.2), kind=kLoop, calls=%fused_computation.5.clone.1 | loop fusion | flops 4190208 | bytes 4292608 | tf_op jit(solution)/shard_map/while/body/eval_jaxpr/reduce_sum | solution.py:90
  147.5 0.2 copy-done.1
  147.7 2.1 %fusion.56 = f32[4,4,256,64]{2,3,1,0:T(8,128)S(1)} fusion(f32[4,256,256,4]{2,1,3,0:T(8,128)S(1)} %copy-done.1, f32[4,4,256]{2,1,0:T(4,128)S(1)} %select_maximum_fusion.2, pred[256,256]{0,1:T(8,128)(4,1)S(1)} %broadcast_compare_fusion.2, f32[4,4,256,64]{2,3,1,0:T(8,128)S(1)} %get-tuple-element.218, f32[4,4,256]{2,1,0:T(4,128)S(1)} %get-tuple-element.203, ...), kind=kOutput, calls=%fused_computation.9.clone.1 | convolution fusion | flops 139198464 | bytes 6521345 | tf_op jit(solution)/shard_map/while/body/eval_jaxpr/kgqs,skd->kgqd/dot_general | solution.py:91
  149.8 1.2 dynamic_slice.29
  151.0 0.6 iota_add_fusion.3
  151.6 0.1 broadcast_compare_fusion.2
  151.8 2.7 %fusion.53 = (f32[4,4,256]{2,1,0:T(4,128)S(1)}, f32[4,256,256,4]{2,1,3,0:T(8,128)}) fusion(pred[256,256]{0,1:T(8,128)(4,1)S(1)} %broadcast_compare_fusion.2, bf16[256,4,4,64]{0,3,2,1:T(8,128)(2,1)S(1)} %get-tuple-element.232, bf16[4,256,4,64]{1,3,2,0:T(8,128)(2,1)S(1)} %get-tuple-element.231, s32[]{:T(128)} %get-tuple-element.215), kind=kOutput, calls=%fused_computation.6.clone.1 | convolution fusion | flops 137359360 | bytes 4931588 | tf_op jit(solution)/shard_map/while/body/eval_jaxpr/qkgd,skd->kgqs/dot_general | solution.py:81
  154.5 3.2 %fusion.54 = f32[4,4,256]{2,1,0:T(4,128)S(1)} fusion(f32[4,256,256,4]{2,1,3,0:T(8,128)} %get-tuple-element.201, f32[4,4,256]{2,1,0:T(4,128)S(1)} %select_maximum_fusion.2, pred[256,256]{0,1:T(8,128)(4,1)S(1)} %broadcast_compare_fusion.2), kind=kLoop, calls=%fused_computation.5.clone.1 | loop fusion | flops 4190208 | bytes 4292608 | tf_op jit(solution)/shard_map/while/body/eval_jaxpr/reduce_sum | solution.py:90
  157.8 0.2 copy-done.1
  157.9 2.1 %fusion.56 = f32[4,4,256,64]{2,3,1,0:T(8,128)S(1)} fusion(f32[4,256,256,4]{2,1,3,0:T(8,128)S(1)} %copy-done.1, f32[4,4,256]{2,1,0:T(4,128)S(1)} %select_maximum_fusion.2, pred[256,256]{0,1:T(8,128)(4,1)S(1)} %broadcast_compare_fusion.2, f32[4,4,256,64]{2,3,1,0:T(8,128)S(1)} %get-tuple-element.218, f32[4,4,256]{2,1,0:T(4,128)S(1)} %get-tuple-element.203, ...), kind=kOutput, calls=%fused_computation.9.clone.1 | convolution fusion | flops 139198464 | bytes 6521345 | tf_op jit(solution)/shard_map/while/body/eval_jaxpr/kgqs,skd->kgqd/dot_general | solution.py:91
  160.1 1.2 dynamic_slice.29
  161.3 0.6 iota_add_fusion.3
  161.9 0.1 broadcast_compare_fusion.2
  162.0 2.7 %fusion.53 = (f32[4,4,256]{2,1,0:T(4,128)S(1)}, f32[4,256,256,4]{2,1,3,0:T(8,128)}) fusion(pred[256,256]{0,1:T(8,128)(4,1)S(1)} %broadcast_compare_fusion.2, bf16[256,4,4,64]{0,3,2,1:T(8,128)(2,1)S(1)} %get-tuple-element.232, bf16[4,256,4,64]{1,3,2,0:T(8,128)(2,1)S(1)} %get-tuple-element.231, s32[]{:T(128)} %get-tuple-element.215), kind=kOutput, calls=%fused_computation.6.clone.1 | convolution fusion | flops 137359360 | bytes 4931588 | tf_op jit(solution)/shard_map/while/body/eval_jaxpr/qkgd,skd->kgqs/dot_general | solution.py:81
  164.8 3.2 %fusion.54 = f32[4,4,256]{2,1,0:T(4,128)S(1)} fusion(f32[4,256,256,4]{2,1,3,0:T(8,128)} %get-tuple-element.201, f32[4,4,256]{2,1,0:T(4,128)S(1)} %select_maximum_fusion.2, pred[256,256]{0,1:T(8,128)(4,1)S(1)} %broadcast_compare_fusion.2), kind=kLoop, calls=%fused_computation.5.clone.1 | loop fusion | flops 4190208 | bytes 4292608 | tf_op jit(solution)/shard_map/while/body/eval_jaxpr/reduce_sum | solution.py:90
  168.0 0.2 copy-done.1
  168.2 2.1 %fusion.56 = f32[4,4,256,64]{2,3,1,0:T(8,128)S(1)} fusion(f32[4,256,256,4]{2,1,3,0:T(8,128)S(1)} %copy-done.1, f32[4,4,256]{2,1,0:T(4,128)S(1)} %select_maximum_fusion.2, pred[256,256]{0,1:T(8,128)(4,1)S(1)} %broadcast_compare_fusion.2, f32[4,4,256,64]{2,3,1,0:T(8,128)S(1)} %get-tuple-element.218, f32[4,4,256]{2,1,0:T(4,128)S(1)} %get-tuple-element.203, ...), kind=kOutput, calls=%fused_computation.9.clone.1 | convolution fusion | flops 139198464 | bytes 6521345 | tf_op jit(solution)/shard_map/while/body/eval_jaxpr/kgqs,skd->kgqd/dot_general | solution.py:91
  170.4 1.2 dynamic_slice.29
  171.5 0.6 iota_add_fusion.3
  172.3 2.7 %fusion.53 = (f32[4,4,256]{2,1,0:T(4,128)S(1)}, f32[4,256,256,4]{2,1,3,0:T(8,128)}) fusion(pred[256,256]{0,1:T(8,128)(4,1)S(1)} %broadcast_compare_fusion.2, bf16[256,4,4,64]{0,3,2,1:T(8,128)(2,1)S(1)} %get-tuple-element.232, bf16[4,256,4,64]{1,3,2,0:T(8,128)(2,1)S(1)} %get-tuple-element.231, s32[]{:T(128)} %get-tuple-element.215), kind=kOutput, calls=%fused_computation.6.clone.1 | convolution fusion | flops 137359360 | bytes 4931588 | tf_op jit(solution)/shard_map/while/body/eval_jaxpr/qkgd,skd->kgqs/dot_general | solution.py:81
  175.1 3.2 %fusion.54 = f32[4,4,256]{2,1,0:T(4,128)S(1)} fusion(f32[4,256,256,4]{2,1,3,0:T(8,128)} %get-tuple-element.201, f32[4,4,256]{2,1,0:T(4,128)S(1)} %select_maximum_fusion.2, pred[256,256]{0,1:T(8,128)(4,1)S(1)} %broadcast_compare_fusion.2), kind=kLoop, calls=%fused_computation.5.clone.1 | loop fusion | flops 4190208 | bytes 4292608 | tf_op jit(solution)/shard_map/while/body/eval_jaxpr/reduce_sum | solution.py:90
  178.3 0.2 copy-done.1
  178.5 2.1 %fusion.56 = f32[4,4,256,64]{2,3,1,0:T(8,128)S(1)} fusion(f32[4,256,256,4]{2,1,3,0:T(8,128)S(1)} %copy-done.1, f32[4,4,256]{2,1,0:T(4,128)S(1)} %select_maximum_fusion.2, pred[256,256]{0,1:T(8,128)(4,1)S(1)} %broadcast_compare_fusion.2, f32[4,4,256,64]{2,3,1,0:T(8,128)S(1)} %get-tuple-element.218, f32[4,4,256]{2,1,0:T(4,128)S(1)} %get-tuple-element.203, ...), kind=kOutput, calls=%fused_computation.9.clone.1 | convolution fusion | flops 139198464 | bytes 6521345 | tf_op jit(solution)/shard_map/while/body/eval_jaxpr/kgqs,skd->kgqd/dot_general | solution.py:91
  180.7 0.8 divide_convert_fusion
  181.5 2.4 %fusion.21 = bf16[256,1024]{1,0:T(8,128)(2,1)S(1)} fusion(bf16[256,1024]{0,1:T(8,128)(2,1)S(1)} %bitcast.70, bf16[1024,1024]{1,0:T(8,128)(2,1)} %all-gather.8.cloned.1.call-done, bf16[256,1024]{1,0:T(8,128)(2,1)S(1)} %copy-done.5), kind=kOutput, calls=%fused_computation.31 | convolution fusion | flops 537657344 | bytes 3670016 | tf_op jit(solution)/shard_map/dot_general | solution.py:29
  183.9 1.3 gather_fusion
  185.3 0.4 fusion.28
  185.6 0.6 broadcast_multiply_fusion.1
  (68 shorter events, 0.6 us)
Async XLA Ops:
  7.2 2.8 %copy-start = (bf16[256,768]{1,0:T(8,128)(2,1)S(1)}, bf16[256,768]{1,0:T(8,128)(2,1)}, u32[]{:S(2)}) copy-start(bf16[256,768]{1,0:T(8,128)(2,1)} %param.11) | copy-start | bytes 1179652
  7.2 6.0 %copy-start.11 = (bf16[1024]{0:T(1024)(128)(2,1)S(1)}, bf16[1024]{0:T(1024)(128)(2,1)}, u32[]{:S(2)}) copy-start(bf16[1024]{0:T(1024)(128)(2,1)} %param.15) | copy-start | bytes 6148
  7.2 49.3 %all-gather.4.cloned.1.call-start = ((), (), s32[]{:S(2)}) async-start(), calls=%async_computation | async-start | bytes 7077888 | tf_op jit(solution)/shard_map/all_gather | solution.py:31
  7.9 82.8 %all-gather.6.cloned.1.call-start = ((), (), s32[]{:S(2)}) async-start(), calls=%async_computation.1 | async-start | bytes 3538944 | tf_op jit(solution)/shard_map/all_gather | solution.py:31
  8.7 172.8 %all-gather.8.cloned.1.call-start = ((), (), s32[]{:S(2)}) async-start(), calls=%async_computation.2 | async-start | bytes 2359296 | tf_op jit(solution)/shard_map/all_gather | solution.py:31
  14.0 0.6 copy-start.8
  61.6 33.2 %copy-start.4 = (bf16[256,1024]{1,0:T(8,128)(2,1)}, bf16[256,1024]{1,0:T(8,128)(2,1)S(1)}, u32[]{:S(2)}) copy-start(bf16[256,1024]{1,0:T(8,128)(2,1)S(1)} %get-tuple-element.136) | copy-start | bytes 1572868
  93.6 1.5 copy-start.3
  93.6 5.0 %copy-start.9 = (f32[256,64]{0,1:T(8,128)S(1)}, f32[256,64]{0,1:T(8,128)}, u32[]{:S(2)}) copy-start(f32[256,64]{0,1:T(8,128)} %get-tuple-element.134) | copy-start | bytes 196612
  95.8 2.7 %slice-start = ((f32[256,1536]{1,0:T(8,128)}), f32[256,256]{1,0:T(8,128)S(1)}, s32[]{:S(2)}) async-start(f32[256,1536]{1,0:T(8,128)} %copy-done.3), calls=%async_computation.3 | async-start | bytes 524288 | tf_op jit(solution)/shard_map/slice | solution.py:60
  139.5 42.0 %copy-start.5 = (bf16[256,1024]{1,0:T(8,128)(2,1)S(1)}, bf16[256,1024]{1,0:T(8,128)(2,1)}, u32[]{:S(2)}) copy-start(bf16[256,1024]{1,0:T(8,128)(2,1)} %copy-done.4) | copy-start | bytes 1572868
  141.5 6.0 %copy-start.6 = (f32[4,4,256]{2,1,0:T(4,128)S(1)}, f32[4,4,256]{2,1,0:T(4,128)}, u32[]{:S(2)}) copy-start(f32[4,4,256]{2,1,0:T(4,128)} %get-tuple-element.217) | copy-start | bytes 49156 | tf_op jit(solution)/shard_map/while
  144.2 3.4 %copy-start.1 = (f32[4,256,256,4]{2,1,3,0:T(8,128)S(1)}, f32[4,256,256,4]{2,1,3,0:T(8,128)}, u32[]{:S(2)}) copy-start(f32[4,256,256,4]{2,1,3,0:T(8,128)} %get-tuple-element.201) | copy-start | bytes 12582916 | tf_op jit(solution)/shard_map/while
  147.5 2.3 %copy-start.7 = (f32[4,4,256]{2,1,0:T(4,128)}, f32[4,4,256]{2,1,0:T(4,128)S(1)}, u32[]{:S(2)}) copy-start(f32[4,4,256]{2,1,0:T(4,128)S(1)} %get-tuple-element.228) | copy-start | bytes 49156 | tf_op jit(solution)/shard_map/while
  151.8 6.0 %copy-start.6 = (f32[4,4,256]{2,1,0:T(4,128)S(1)}, f32[4,4,256]{2,1,0:T(4,128)}, u32[]{:S(2)}) copy-start(f32[4,4,256]{2,1,0:T(4,128)} %get-tuple-element.217) | copy-start | bytes 49156 | tf_op jit(solution)/shard_map/while
  154.5 3.4 %copy-start.1 = (f32[4,256,256,4]{2,1,3,0:T(8,128)S(1)}, f32[4,256,256,4]{2,1,3,0:T(8,128)}, u32[]{:S(2)}) copy-start(f32[4,256,256,4]{2,1,3,0:T(8,128)} %get-tuple-element.201) | copy-start | bytes 12582916 | tf_op jit(solution)/shard_map/while
  157.8 2.3 %copy-start.7 = (f32[4,4,256]{2,1,0:T(4,128)}, f32[4,4,256]{2,1,0:T(4,128)S(1)}, u32[]{:S(2)}) copy-start(f32[4,4,256]{2,1,0:T(4,128)S(1)} %get-tuple-element.228) | copy-start | bytes 49156 | tf_op jit(solution)/shard_map/while
  162.0 6.0 %copy-start.6 = (f32[4,4,256]{2,1,0:T(4,128)S(1)}, f32[4,4,256]{2,1,0:T(4,128)}, u32[]{:S(2)}) copy-start(f32[4,4,256]{2,1,0:T(4,128)} %get-tuple-element.217) | copy-start | bytes 49156 | tf_op jit(solution)/shard_map/while
  164.8 3.4 %copy-start.1 = (f32[4,256,256,4]{2,1,3,0:T(8,128)S(1)}, f32[4,256,256,4]{2,1,3,0:T(8,128)}, u32[]{:S(2)}) copy-start(f32[4,256,256,4]{2,1,3,0:T(8,128)} %get-tuple-element.201) | copy-start | bytes 12582916 | tf_op jit(solution)/shard_map/while
  168.0 2.3 %copy-start.7 = (f32[4,4,256]{2,1,0:T(4,128)}, f32[4,4,256]{2,1,0:T(4,128)S(1)}, u32[]{:S(2)}) copy-start(f32[4,4,256]{2,1,0:T(4,128)S(1)} %get-tuple-element.228) | copy-start | bytes 49156 | tf_op jit(solution)/shard_map/while
  172.3 6.0 %copy-start.6 = (f32[4,4,256]{2,1,0:T(4,128)S(1)}, f32[4,4,256]{2,1,0:T(4,128)}, u32[]{:S(2)}) copy-start(f32[4,4,256]{2,1,0:T(4,128)} %get-tuple-element.217) | copy-start | bytes 49156 | tf_op jit(solution)/shard_map/while
  175.0 3.4 %copy-start.1 = (f32[4,256,256,4]{2,1,3,0:T(8,128)S(1)}, f32[4,256,256,4]{2,1,3,0:T(8,128)}, u32[]{:S(2)}) copy-start(f32[4,256,256,4]{2,1,3,0:T(8,128)} %get-tuple-element.201) | copy-start | bytes 12582916 | tf_op jit(solution)/shard_map/while
  178.3 2.3 %copy-start.7 = (f32[4,4,256]{2,1,0:T(4,128)}, f32[4,4,256]{2,1,0:T(4,128)S(1)}, u32[]{:S(2)}) copy-start(f32[4,4,256]{2,1,0:T(4,128)S(1)} %get-tuple-element.228) | copy-start | bytes 49156 | tf_op jit(solution)/shard_map/while
  181.5 3.7 %copy-start.10 = (bf16[1,256,1024]{2,1,0:T(8,128)(2,1)S(1)}, bf16[1,256,1024]{2,1,0:T(8,128)(2,1)}, u32[]{:S(2)}) copy-start(bf16[1,256,1024]{2,1,0:T(8,128)(2,1)} %param.16) | copy-start | bytes 1572868
  181.5 3.7 %copy-start.12 = (pred[256]{0:T(512)(128)(4,1)S(1)}, pred[256]{0:T(512)(128)(4,1)}, u32[]{:S(2)}) copy-start(pred[256]{0:T(512)(128)(4,1)} %compare_and_fusion) | copy-start | bytes 772
  183.9 2.3 %copy-start.2 = (bf16[256,1024]{1,0:T(8,128)(2,1)}, bf16[256,1024]{1,0:T(8,128)(2,1)S(1)}, u32[]{:S(2)}) copy-start(bf16[256,1024]{1,0:T(8,128)(2,1)S(1)} %fusion.21) | copy-start | bytes 1572868
Sparse Core Ops, SparseCore 0:
  9.9 46.4 all-gather.3
  58.3 32.3 all-gather.5
  92.6 27.8 all-gather.7
where the time goes:
time: 195 us; the launch traced here: 193 us
  waiting for transfers between devices  71 us (36%)
  blocking collectives  31.8 us (16%)
  matrix products  31.1 us (16%)
  other arithmetic  24.4 us (13%)
  local copies, waits for them, and re-layouts  19.9 us (10%)
  between operations  14 us (7%)
    all_gather x3, waiting for transfers between devices, project(): lax.all_gather(weight, 'fsdp', axis=0, tiled=True)  69 us
    all_gather x1, blocking collectives, body(): key_all = lax.all_gather(key_rows, 'ctx', axis=0, tiled=True)  16.3 us
    all_gather x1, blocking collectives, body(): value_all = lax.all_gather(value_rows, 'ctx', axis=0, tiled=True)  15.5 us
    reduce_sum x4, other arithmetic, one_block(): row_mass = row_mass * shrink + jnp.sum(weights, axis=-1)  12.9 us
    dot_general x4, matrix products, one_block(): jnp.einsum('qkgd,skd->kgqs', grouped, key_block, preferred_element_type=j...  10.9 us
    dot_general x3, matrix products, project(): jnp.dot(inputs, lax.all_gather(weight, 'fsdp', axis=0, tiled=True), prefe...  10.4 us
    dot_general x4, matrix products, one_block(): jnp.einsum('kgqs,skd->kgqd', weights.astype(jnp.bfloat16), value_block, p...  8.52 us
    dynamic_slice x4, local copies, waits for them, and re-layouts, body(): lax.scan(one_block, start_state, (key_blocks, value_blocks, block_starts))  4.7 us
  transfers between devices with their start and end apart: 3, of which 2 were waited for; matrix products, arithmetic and copies ran while one was open for 36% of the time, Pallas kernels for 0%

commit v1 on v0

--- a/solution.py
+++ b/solution.py
@@ -1,19 +1,25 @@
+import functools
 import math
 
 import jax
 import jax.numpy as jnp
+import numpy as np
 from jax import lax
+from jax.experimental import pallas as pl
+from jax.experimental.pallas import tpu as pltpu
 from jax.sharding import PartitionSpec as P
 
 KW = 4
 HQ = 16
 HK = 4
 HD = 64
-
+GROUP = HQ // HK
+VOCAB = 256
 
 theta_base = 500000.0
 norm_eps = 1e-05
 masked_score = -1e30
+score_scale = 1.0 / math.sqrt(HD)
 
 
 def rotate(values, positions):
@@ -33,8 +39,7 @@
     )
 
 
-def body(byte_ids, byte_table, w_conv, w_qkv, w_out, norm_gain, teacher, align):
-    score_scale = 1.0 / math.sqrt(HD)
+def general_body(byte_ids, byte_table, w_conv, w_qkv, w_out, norm_gain, teacher, align):
     seq_bytes = byte_ids.shape[1]
     lat_rows = seq_bytes // KW
     query_width = HQ * HD
@@ -109,6 +114,251 @@
     return (hidden_out[None], token_loss[None])
 
 
+def rope_tables(length):
+    half = HD // 2
+    frequency = np.float32(theta_base) ** (-np.arange(half, dtype=np.float32) * np.float32(2.0 / HD))
+    angles = np.arange(length, dtype=np.float32)[:, None] * frequency[None, :]
+    angles = angles.astype(np.float64)
+    cos, sin = np.cos(angles).astype(np.float32), np.sin(angles).astype(np.float32)
+    return np.concatenate([cos] * 4, axis=1), np.concatenate([-sin, sin] * 2, axis=1)
+
+
+def turn(x, cos, sin):
+    half = HD // 2
+    lane = lax.broadcasted_iota(jnp.int32, x.shape, 1)
+    low = (lane & half) == 0
+    swapped = jnp.where(low, pltpu.roll(x, 128 - half, axis=1), pltpu.roll(x, half, axis=1))
+    return x * cos + swapped * sin
+
+
+def own_kernel(where_ref, bytes_ref, conv_ref, qkv_ref, total_ref, part_ref):
+    core, ctx = where_ref[1], where_ref[2]
+    taps_in = conv_ref.shape[0]
+    half = total_ref.shape[0]
+    rows = pl.ds(pl.multiple_of(core * half, half), half)
+    mine = bytes_ref[rows, pl.ds(pl.multiple_of(core * taps_in, taps_in), taps_in)]
+    total_ref[...] = jnp.dot(mine, conv_ref[...], preferred_element_type=jnp.float32)
+    q_width = GROUP * HD
+    part_ref[:, :q_width] = qkv_ref[:, pl.ds(pl.multiple_of(ctx * q_width, q_width), q_width)]
+    heads = []
+    for start in (HQ * HD, HQ * HD + HK * HD):
+        pair = qkv_ref[:, pl.ds(pl.multiple_of(start + ctx // 2 * 128, 128), 128)].astype(jnp.float32)
+        heads.append(jnp.where(ctx % 2 == 1, pltpu.roll(pair, HD, axis=1), pair)[:, :HD])
+    part_ref[:, q_width:] = jnp.concatenate(heads, axis=1).astype(jnp.bfloat16)
+
+
+def mate_kernel(where_ref, bytes_ref, conv_ref, total_ref, part_ref, out_ref):
+    core = where_ref[1]
+    taps_in = conv_ref.shape[0]
+    half, width = total_ref.shape
+    rows = pl.ds(pl.multiple_of(core * half, half), half)
+    mates = bytes_ref[rows, pl.ds(pl.multiple_of((1 - core) * taps_in, taps_in), taps_in)]
+    total = total_ref[...] + jnp.dot(mates, conv_ref[...], preferred_element_type=jnp.float32)
+    out_ref[:, :width] = total.astype(jnp.bfloat16)
+    out_ref[:, width:] = part_ref[...]
+
+
+def ordered(chip, core, pieces):
+    own, near, mate_own, mate_near = pieces
+    depth = own.shape[0]
+    for j, (mine, mates) in enumerate(zip((own,) + near, (mate_own,) + mate_near)):
+        base = (chip ^ j) * 2
+        for which, piece in ((core, mine), (1 - core, mates)):
+            yield pl.ds(pl.multiple_of((base + which) * depth, depth), depth), piece
+
+
+def attend_kernel(
+    where_ref, ids_refs, own, near, mate_own, mate_near, gain_ref, cos_ref, sin_ref, att_ref, lat_ref,
+    table_s, weight_s, ids_s, lat_s, q_s, k_s, v_s,
+):
+    chip, core, ctx = where_ref[0], where_ref[1], where_ref[2]
+    blocks, rows = len(ids_refs), ids_refs[0].shape[1]
+    features = lat_ref.shape[1]
+    for span, piece in ordered(chip, core, (own, near, mate_own, mate_near)):
+        table_s[span, :] = piece[:, :features]
+        weight_s[span, :] = piece[:, features:]
+    for d, ids in enumerate(ids_refs):
+        ids_s[(ctx - d) & (blocks - 1)] = ids[...]
+    gain = gain_ref[...].astype(jnp.float32)
+    q_width = GROUP * HD
+    v_s[:, HD:, :] = jnp.ones((blocks, v_s.shape[1] - HD, rows), jnp.bfloat16)
+
+    def lift(i):
+        span = slice(i * rows, (i + 1) * rows)
+        ids = jnp.transpose(ids_s[i])
+        byte = lax.broadcasted_iota(jnp.int32, (rows, VOCAB), 1)
+        one_hot = jnp.concatenate(
+            [(ids[:, k : k + 1] == byte).astype(jnp.float32).astype(jnp.bfloat16) for k in range(KW)], axis=1
+        )
+        latent = jnp.dot(one_hot, table_s[...], preferred_element_type=jnp.float32).astype(jnp.bfloat16)
+        lat_s[i] = latent
+        wide = latent.astype(jnp.float32)
+        scale = lax.rsqrt(jnp.mean(wide * wide, axis=1, keepdims=True) + norm_eps)
+        normed = (wide * scale * gain).astype(jnp.bfloat16)
+        projected = jnp.dot(normed, weight_s[...], preferred_element_type=jnp.float32)
+        cos, sin = cos_ref[span, :], sin_ref[span, :]
+        for pair in range(GROUP // 2):
+            turned = turn(projected[:, pair * 128 : (pair + 1) * 128], cos, sin)
+            turned = (turned * score_scale).astype(jnp.bfloat16)
+            q_s[i, 2 * pair] = turned[:, :HD]
+            q_s[i, 2 * pair + 1] = turned[:, HD:]
+        last = projected[:, q_width:]
+        k_s[span, :] = turn(last, cos, sin)[:, :HD].astype(jnp.bfloat16)
+        v_s[i, :HD, :] = jnp.transpose(last)[HD:].astype(jnp.bfloat16)
+
+    allowed = lax.broadcasted_iota(jnp.int32, (rows, rows), 0) <= lax.broadcasted_iota(
+        jnp.int32, (rows, rows), 1
+    )
+
+    def one_head(i, h):
+        query = q_s[i, h]
+        scores = [
+            lax.dot_general(
+                k_s[j * rows : (j + 1) * rows, :], query, (((1,), (1,)), ((), ())),
+                preferred_element_type=jnp.float32,
+            )
+            for j in range(i + 1)
+        ]
+        scores[i] = jnp.where(allowed, scores[i], masked_score)
+        top = functools.reduce(jnp.maximum, [jnp.max(s, axis=0, keepdims=True) for s in scores])
+        total = None
+        for j, s in enumerate(scores):
+            probs = jnp.exp(s - top).astype(jnp.bfloat16)
+            term = jnp.dot(v_s[j], probs, preferred_element_type=jnp.float32)
+            total = term if total is None else total + term
+        return total[:HD] / total[HD : HD + 1]
+
+    for i in range(blocks):
+        lift(i)
+    lat_ref[...] = lat_s[ctx]
+    for i in range(blocks):
+        slot = (i - ctx) & (blocks - 1)
+        for pair in range(GROUP // 2):
+            result = jnp.concatenate([one_head(i, 2 * pair), one_head(i, 2 * pair + 1)], axis=0)
+            att_ref[slot, :, pair * 2 * HD : (pair + 1) * 2 * HD] = jnp.transpose(result).astype(jnp.bfloat16)
+
+
+def out_kernel(
+    where_ref, att_refs, own, near, mate_own, mate_near, lat_ref, teacher_ref, align_ref,
+    hidden_ref, loss_ref, att_s, weight_s,
+):
+    chip, core, ctx = where_ref[0], where_ref[1], where_ref[2]
+    rows, width = lat_ref.shape
+    part = att_refs[0].shape[1]
+    for span, piece in ordered(chip, core, (own, near, mate_own, mate_near)):
+        weight_s[span, :] = piece[...]
+    for j, att in enumerate(att_refs):
+        group = (ctx - j) & (len(att_refs) - 1)
+        att_s[:, pl.ds(pl.multiple_of(group * part, part), part)] = att[...]
+    branch = jnp.dot(att_s[...], weight_s[...], preferred_element_type=jnp.float32)
+    hidden = (lat_ref[...].astype(jnp.float32) + branch).astype(jnp.bfloat16)
+    hidden_ref[...] = hidden
+    source = lax.broadcasted_iota(jnp.int32, (rows, rows), 0) + ctx * rows
+    chosen = (source == align_ref[...]).astype(jnp.float32).astype(jnp.bfloat16)
+    picked = lax.dot_general(
+        chosen, hidden, (((0,), (0,)), ((), ())), preferred_element_type=jnp.float32
+    )
+    difference = picked - teacher_ref[...].astype(jnp.float32)
+    square = difference * difference
+    lanes = square[:, :128]
+    for start in range(128, width, 128):
+        lanes = lanes + square[:, start : start + 128]
+    loss_ref[...] = jnp.sum(jnp.transpose(lanes), axis=0, keepdims=True) * (1.0 / width)
+
+
+VMEM = pl.BlockSpec(memory_space=pltpu.VMEM)
+SMEM = pl.BlockSpec(memory_space=pltpu.SMEM)
+MIB = 1024 * 1024
+
+
+def call(kernel, name, mib, flops, in_specs, outs, scratch=()):
+    return pl.pallas_call(
+        kernel,
+        out_shape=tuple(jax.ShapeDtypeStruct(shape, dtype) for shape, dtype in outs),
+        in_specs=in_specs,
+        out_specs=(VMEM,) * len(outs),
+        scratch_shapes=[pltpu.VMEM(shape, dtype) for shape, dtype in scratch],
+        compiler_params=pltpu.CompilerParams(vmem_limit_bytes=mib * MIB),
+        cost_estimate=pl.CostEstimate(flops=flops, bytes_accessed=4 * MIB, transcendentals=0),
+        name=name,
+    )
+
+
+def head_body(sizes, byte_ids, byte_table, w_conv, w_qkv, w_out, norm_gain, teacher, align):
+    n_fsdp, n_ctx = sizes
+    me, ctx = lax.axis_index("fsdp"), lax.axis_index("ctx")
+    chip, core = me // 2, me % 2
+    rows = byte_ids.shape[1] // KW
+    length = rows * n_ctx
+    features = w_conv.shape[1]
+    q_width = GROUP * HD
+    part_width = q_width + 2 * HD
+    half = VOCAB // 2
+    bf16, f32 = jnp.bfloat16, jnp.float32
+    where = jnp.stack([chip, core, ctx]).astype(jnp.int32)
+
+    def swap(x, j):
+        return lax.ppermute(x, "fsdp", [(d, d ^ j) for d in range(n_fsdp)])
+
+    def along(x, d):
+        return lax.ppermute(x, "ctx", [(s, (s + d) % n_ctx) for s in range(n_ctx)])
+
+    def to_near(x):
+        return tuple(swap(x, 2 * j) for j in range(1, n_fsdp // 2))
+
+    mate_conv = swap(w_conv, 1)
+    total, part = call(
+        own_kernel, "own_rows", 8, 10**9, [SMEM, VMEM, VMEM, VMEM],
+        [((half, features), f32), ((w_qkv.shape[0], part_width), bf16)],
+    )(where, byte_table, w_conv, w_qkv)
+    (own,) = call(
+        mate_kernel, "tap_table", 8, 10**8, [SMEM, VMEM, VMEM, VMEM, VMEM],
+        [((half, features + part_width), bf16)],
+    )(where, byte_table, mate_conv, total, part)
+    near = to_near(own)
+
+    ids = jnp.transpose(byte_ids[0].reshape(rows, KW))
+    ids = jnp.pad(ids, ((0, 8 - KW), (0, 0)))
+    ids, unused = lax.optimization_barrier((ids, own))
+    ids_all = (ids,) + tuple(along(ids, d) for d in range(1, n_ctx))
+    last, ids_all = lax.optimization_barrier((near[-1], ids_all))
+    near = near[:-1] + (last,)
+    pieces = (own, near, swap(own, 1), tuple(swap(piece, 1) for piece in near))
+    out_own, unused = lax.optimization_barrier((w_out, near))
+    out_near = to_near(out_own)
+
+    cos, sin = rope_tables(length)
+    near_specs = (VMEM,) * (n_fsdp // 2 - 1)
+    piece_specs = [VMEM, near_specs, VMEM, near_specs]
+    att, latent = call(
+        attend_kernel, "attend", 24, 6 * 10**9,
+        [SMEM, (VMEM,) * n_ctx] + piece_specs + [VMEM, VMEM, VMEM],
+        [((n_ctx, rows, q_width), bf16), ((rows, features), bf16)],
+        [
+            ((KW * VOCAB, features), bf16),
+            ((features, part_width), bf16),
+            ((n_ctx, 8, rows), jnp.int32),
+            ((n_ctx, rows, features), bf16),
+            ((n_ctx, GROUP, rows, HD), bf16),
+            ((length, HD), bf16),
+            ((n_ctx, HD + 16, rows), bf16),
+        ],
+    )(where, ids_all, *pieces, norm_gain[None], jnp.asarray(cos), jnp.asarray(sin))
+
+    att, out_near = lax.optimization_barrier((att, out_near))
+    parts = (att[0],) + tuple(along(att[d], d) for d in range(1, n_ctx))
+    first, out_near = lax.optimization_barrier((parts[1], out_near))
+    parts = (parts[0], first) + parts[2:]
+    out_pieces = (out_own, out_near, swap(out_own, 1), tuple(swap(piece, 1) for piece in out_near))
+    hidden, loss = call(
+        out_kernel, "project_out", 16, 10**9,
+        [SMEM, (VMEM,) * n_ctx] + piece_specs + [VMEM, VMEM, VMEM],
+        [((rows, features), bf16), ((1, rows), f32)],
+        [((rows, features), bf16), ((features, features), bf16)],
+    )(where, parts, *out_pieces, latent, teacher[0], align)
+    return hidden[None], loss
+
+
 def solution(mesh):
     in_specs = (
         P("fsdp", "ctx"),
@@ -121,4 +371,6 @@
         P("fsdp", "ctx"),
     )
     out_specs = (P("fsdp", "ctx", None), P("fsdp", "ctx"))
+    sizes = (mesh.shape["fsdp"], mesh.shape["ctx"])
+    body = functools.partial(head_body, sizes) if sizes == (2 * KW, HK) else general_body
     return jax.shard_map(body, mesh=mesh, in_specs=in_specs, out_specs=out_specs, check_vma=False)

time: 195 us -> 63.1 us (0.32)
  waiting for transfers between devices: 71 us -> 27.2 us
  blocking collectives: 31.8 us -> 0 us
  matrix products: 31.1 us -> 0 us
  other arithmetic: 24.4 us -> 0.74 us
  Pallas kernels: 0 us -> 15.6 us
  local copies, waits for them, and re-layouts: 19.9 us -> 4.58 us
  starting transfers between devices: 0.11 us -> 13.4 us
  between operations: 14 us -> 0.82 us
    all_gather x3 -> x0, waiting for transfers between devices: 69 us -> none  [project(): lax.all_gather(weight, 'fsdp', axis=0, tiled=True)]
    all_gather x2 -> x0, blocking collectives: 31.8 us -> none  [the longest x1 16.3 us: body(): key_all = lax.all_gather(key_rows, 'ctx', axis=0, tiled=True)]
    dot_general x12 -> x0, matrix products: 31.1 us -> none  [the longest x4 10.9 us: one_block(): jnp.einsum('qkgd,skd->kgqs', grouped, key_block, preferred_element_type=j...]
    ppermute x0 -> x21, waiting for transfers between devices: none -> 27.2 us  [the longest x6 21.2 us: along(): return lax.ppermute(x, 'ctx', [(s, (s + d) % n_ctx) for s in range(n_ctx)])]
    pallas_call x0 -> x4, Pallas kernels: none -> 15.6 us  [the longest x1 11.5 us: head_body(): call(attend_kernel, 'attend', 24, 6 * 10 ** 9, [SMEM, (VMEM,) * n_ctx] +...]
    ppermute x0 -> x21, starting transfers between devices: none -> 13.4 us  [the longest x15 8.21 us: swap(): return lax.ppermute(x, 'fsdp', [(d, d ^ j) for d in range(n_fsdp)])]
    reduce_sum x5 -> x0, other arithmetic: 13.3 us -> none  [the longest x4 12.9 us: one_block(): row_mass = row_mass * shrink + jnp.sum(weights, axis=-1)]
    reshape x3 -> x0, local copies, waits for them, and re-layouts: 4.71 us -> none  [the longest x1 1.9 us: body(): stacked = embedded.reshape(lat_rows, KW * byte_table.shape[1])]
  transfers between devices with their start and end apart: 3 -> 21, of which waited for: 2 -> 7; matrix products, arithmetic and copies ran while one was open for 36% -> 2% of each run, Pallas kernels for 0% -> 20%
where the time goes in v1:
time: 63.1 us; the launch traced here: 62.4 us
  waiting for transfers between devices  27.2 us (43%)
  Pallas kernels  15.6 us (25%)
  starting transfers between devices  13.4 us (21%)
  local copies, waits for them, and re-layouts  4.58 us (7%)
  between operations  0.82 us (1%)
  other arithmetic  0.74 us (1%)
    ppermute x6, waiting for transfers between devices, along(): return lax.ppermute(x, 'ctx', [(s, (s + d) % n_ctx) for s in range(n_ctx)])  21.2 us
    pallas_call x1, Pallas kernels, head_body(): call(attend_kernel, 'attend', 24, 6 * 10 ** 9, [SMEM, (VMEM,) * n_ctx] +...  11.5 us
    ppermute x15, starting transfers between devices, swap(): return lax.ppermute(x, 'fsdp', [(d, d ^ j) for d in range(n_fsdp)])  8.21 us
    ppermute x15, waiting for transfers between devices, swap(): return lax.ppermute(x, 'fsdp', [(d, d ^ j) for d in range(n_fsdp)])  6.03 us
    ppermute x6, starting transfers between devices, along(): return lax.ppermute(x, 'ctx', [(s, (s + d) % n_ctx) for s in range(n_ctx)])  5.23 us
    unnamed x21, local copies, waits for them, and re-layouts  4.33 us
    pallas_call x1, Pallas kernels, head_body(): call(out_kernel, 'project_out', 16, 10 ** 9, [SMEM, (VMEM,) * n_ctx] + pi...  2.41 us
  transfers between devices with their start and end apart: 21, of which 7 were waited for; matrix products, arithmetic and copies ran while one was open for 2% of the time, Pallas kernels for 20%

profile of v1, /device:TPU:24, one launch (start us, length us, event | category | flops | bytes accessed | tf_op | source)
XLA Modules:
  0.0 62.4 jit_solution(3108862166537855842)
XLA Ops:
  0.6 0.1 collective-permute-start
  0.7 0.1 pad_add_fusion.where_ref
  0.8 1.0 %copy-done = bf16[256,768]{1,0:T(8,128)(2,1)S(1)} copy-done((bf16[256,768]{1,0:T(8,128)(2,1)S(1)}, bf16[256,768]{1,0:T(8,128)(2,1)}, u32[]{:S(2)}) %copy-start) | copy-done | bytes 393240
  1.8 1.1 %copy-done.1 = bf16[384,1024]{1,0:T(8,128)(2,1)S(1)} copy-done((bf16[384,1024]{1,0:T(8,128)(2,1)S(1)}, bf16[384,1024]{1,0:T(8,128)(2,1)}, u32[]{:S(2)}) %copy-start.1) | copy-done | bytes 786456
  2.9 1.0 %copy-done.3 = bf16[128,1536]{1,0:T(8,128)(2,1)S(1)} copy-done((bf16[128,1536]{1,0:T(8,128)(2,1)S(1)}, bf16[128,1536]{1,0:T(8,128)(2,1)}, u32[]{:S(2)}) %copy-start.3) | copy-done | bytes 393240
  3.9 0.8 %own_rows.1 = (f32[128,1024]{1,0:T(8,128)S(1)}, bf16[128,384]{1,0:T(8,128)(2,1)S(1)}) custom-call(s32[3]{0:T(128)S(1)} %pad_add_fusion.where_ref, bf16[256,768]{1,0:T(8,128)(2,1)S(1)} %copy-done, bf16[384,1024]{1,0:T(8,128)(2,1)S(1)} %copy-done.1, bf16[128,1536]{1,0:T(8,128)(2,1)S(1)} %copy-done.3), custom_call_target="tpu_custom_call" | custom-call | flops 1000000000 | bytes 4194304 | tf_op jit(solution)/shard_map/own_rows/pallas_call | solution.py:310
  4.8 0.0 collective-permute-done.conv_ref
  4.8 0.0 copy-start.8
  4.8 0.0 copy-start.6
  4.8 0.0 copy-start.7
  4.8 0.9 %tap_table.1.own = bf16[128,1408]{1,0:T(8,128)(2,1)S(1)} custom-call(s32[3]{0:T(128)S(1)} %pad_add_fusion.where_ref, bf16[256,768]{1,0:T(8,128)(2,1)S(1)} %copy-done, bf16[384,1024]{1,0:T(8,128)(2,1)S(1)} %collective-permute-done.conv_ref, f32[128,1024]{1,0:T(8,128)S(1)} %get-tuple-element.23.total_ref, bf16[128,384]{1,0:T(8,128)(2,1)S(1)} %get-tuple-element.24.part_ref), custom_call_target="tpu_custom_call" | custom-call | flops 100000000 | bytes 4194304 | tf_op jit(solution)/shard_map/tap_table/pallas_call | solution.py:314
  5.7 0.0 copy-start.4
  5.7 2.5 %collective-permute-start.1 = (bf16[128,1408]{1,0:T(8,128)(2,1)S(1)}, bf16[128,1408]{1,0:T(8,128)(2,1)S(1)}, u32[]{:S(2)}, u32[]{:S(2)}) collective-permute-start(bf16[128,1408]{1,0:T(8,128)(2,1)S(1)} %tap_table.1.own), channel_id=1, source_target_pairs={{0,24},{4,28},{8,16},{12,20},{16,8},{20,12},{24,0},{28,4},{1,25},{... | collective-permute-start | bytes 1081352 | tf_op jit(solution)/shard_map/ppermute | solution.py:301
  8.2 0.5 collective-permute-start.5
  8.7 0.5 collective-permute-start.6
  9.3 0.5 broadcast.7
  9.8 0.0 copy-done.8
  9.8 0.7 %reduce.3 = s32[1024]{0:T(1024)S(1)} reduce(s32[1,1024]{1,0:T(1,128)S(1)} %copy-done.8, s32[]{:T(128)} %broadcast.7), dimensions={0}, to_apply=%param.10.reduce_sub_computation.3 | reduce | bytes 8196 | tf_op args[0]
  10.4 0.1 reshape_squeeze.3
  10.6 0.1 copy.12
  10.7 0.1 collective-permute-start.2
  10.7 1.9 %collective-permute-start.3 = (s32[8,256]{1,0:T(8,128)S(1)}, s32[8,256]{1,0:T(8,128)S(1)}, u32[]{:S(2)}, u32[]{:S(2)}) collective-permute-start(s32[8,256]{1,0:T(8,128)S(1)} %pad.4.ids_refs_0_), channel_id=1, source_target_pairs={{0,2},{1,3},{2,0},{3,1},{4,6},{5,7},{6,4},{7,5},{8,10},{9,11},{10,... | collective-permute-start | bytes 24584 | tf_op jit(solution)/shard_map/ppermute | solution.py:304
  12.6 1.7 %collective-permute-done.2.ids_refs_1_ = s32[8,256]{1,0:T(8,128)S(1)} collective-permute-done((s32[8,256]{1,0:T(8,128)S(1)}, s32[8,256]{1,0:T(8,128)S(1)}, u32[]{:S(2)}, u32[]{:S(2)}) %collective-permute-start.2) | collective-permute-done | bytes 8224 | tf_op jit(solution)/shard_map/ppermute | solution.py:304
  14.4 0.4 collective-permute-start.4
  14.8 0.5 collective-permute-done.3.ids_refs_2_
  15.3 0.0 collective-permute-start.7
  15.4 4.5 %collective-permute-done.4.ids_refs_3_ = s32[8,256]{1,0:T(8,128)S(1)} collective-permute-done((s32[8,256]{1,0:T(8,128)S(1)}, s32[8,256]{1,0:T(8,128)S(1)}, u32[]{:S(2)}, u32[]{:S(2)}) %collective-permute-start.4) | collective-permute-done | bytes 8224 | tf_op jit(solution)/shard_map/ppermute | solution.py:304
  19.8 0.0 collective-permute-done.1.near_2_
  19.8 5.5 %collective-permute-done.5.near_0_ = bf16[128,1408]{1,0:T(8,128)(2,1)S(1)} collective-permute-done((bf16[128,1408]{1,0:T(8,128)(2,1)S(1)}, bf16[128,1408]{1,0:T(8,128)(2,1)S(1)}, u32[]{:S(2)}, u32[]{:S(2)}) %collective-permute-start.5) | collective-permute-done | bytes 360480 | tf_op jit(solution)/shard_map/ppermute | solution.py:301
  25.3 0.0 collective-permute-start.8
  25.3 0.0 collective-permute-done.6.near_1_
  25.3 0.5 collective-permute-start.9
  25.8 0.0 collective-permute-start.10
  25.8 0.0 copy-done.9
  25.8 0.0 copy-done.4
  25.8 1.6 %collective-permute-start.11 = (bf16[128,1024]{1,0:T(8,128)(2,1)S(1)}, bf16[128,1024]{1,0:T(8,128)(2,1)S(1)}, u32[]{:S(2)}, u32[]{:S(2)}) collective-permute-start(bf16[128,1024]{1,0:T(8,128)(2,1)S(1)} %copy-done.4), channel_id=1, source_target_pairs={{0,8},{4,12},{8,0},{12,4},{16,24},{20,28},{24,16},{28,20},{1,9},{5... | collective-permute-start | bytes 786440 | tf_op jit(solution)/shard_map/ppermute | solution.py:301
  27.4 0.0 collective-permute-done.7.mate_own
  27.4 1.4 %collective-permute-start.12 = (bf16[128,1024]{1,0:T(8,128)(2,1)S(1)}, bf16[128,1024]{1,0:T(8,128)(2,1)S(1)}, u32[]{:S(2)}, u32[]{:S(2)}) collective-permute-start(bf16[128,1024]{1,0:T(8,128)(2,1)S(1)} %copy-done.4), channel_id=1, source_target_pairs={{0,16},{4,20},{8,24},{12,28},{16,0},{20,4},{24,8},{28,12},{1,17},{... | collective-permute-start | bytes 786440 | tf_op jit(solution)/shard_map/ppermute | solution.py:301
  28.8 0.0 collective-permute-done.8.mate_near_0_
  28.8 0.6 collective-permute-start.13
  29.4 0.0 collective-permute-done.9.mate_near_1_
  29.4 0.0 collective-permute-done.10.mate_near_2_
  29.4 0.0 copy-done.6
  29.4 11.5 %attend.1 = (bf16[4,256,256]{2,1,0:T(8,128)(2,1)S(1)}, bf16[256,1024]{1,0:T(8,128)(2,1)S(1)}) custom-call(s32[3]{0:T(128)S(1)} %pad_add_fusion.where_ref, s32[8,256]{1,0:T(8,128)S(1)} %pad.4.ids_refs_0_, s32[8,256]{1,0:T(8,128)S(1)} %collective-permute-done.2.ids_refs_1_, s32[8,256]{1,0:T(8,128)S(1)} %collective-permute-done.3.ids_refs_2_, ...), custom_call_target="tpu_custom_call" | custom-call | flops 6000000000 | bytes 4194304 | tf_op jit(solution)/shard_map/attend/pallas_call | solution.py:333
  40.9 0.0 collective-permute-done.11.near_0_
  40.9 0.5 collective-permute-done.12.near_1_
  41.5 0.0 collective-permute-done.13.near_2_
  41.5 0.3 collective-permute-start.14
  41.8 0.0 collective-permute-start.17
  41.8 4.8 %collective-permute-done.14.att_refs_1_ = bf16[256,256]{1,0:T(8,128)(2,1)S(1)} collective-permute-done((bf16[256,256]{1,0:T(8,128)(2,1)S(1)}, bf16[256,256]{1,0:T(8,128)(2,1)S(1)}, u32[]{:S(2)}, u32[]{:S(2)}) %collective-permute-start.14) | collective-permute-done | bytes 131104 | tf_op jit(solution)/shard_map/ppermute | solution.py:304
  46.5 0.0 collective-permute-start.18
  46.5 0.5 collective-permute-start.19
  47.0 0.0 collective-permute-start.20
  47.0 0.3 collective-permute-start.15
  47.4 0.0 collective-permute-done.17.mate_own
  47.4 2.2 %collective-permute-start.16 = (bf16[256,256]{1,0:T(8,128)(2,1)S(1)}, bf16[256,256]{1,0:T(8,128)(2,1)S(1)}, u32[]{:S(2)}, u32[]{:S(2)}) collective-permute-start(bf16[256,256]{1,0:T(8,128)(2,1)S(1)} %get-tuple-element.44), channel_id=1, source_target_pairs={{0,3},{1,0},{2,1},{3,2},{4,7},{5,4},{6,5},{7,6},{8,11},{9,8},{10,9... | collective-permute-start | bytes 393224 | tf_op jit(solution)/shard_map/ppermute | solution.py:304
  49.6 9.7 %collective-permute-done.15.att_refs_2_ = bf16[256,256]{1,0:T(8,128)(2,1)S(1)} collective-permute-done((bf16[256,256]{1,0:T(8,128)(2,1)S(1)}, bf16[256,256]{1,0:T(8,128)(2,1)S(1)}, u32[]{:S(2)}, u32[]{:S(2)}) %collective-permute-start.15) | collective-permute-done | bytes 131104 | tf_op jit(solution)/shard_map/ppermute | solution.py:304
  59.3 0.0 collective-permute-done.16.att_refs_3_
  59.3 0.0 collective-permute-done.18.mate_near_0_
  59.3 0.0 collective-permute-done.19.mate_near_1_
  59.3 0.0 collective-permute-done.20.mate_near_2_
  59.3 0.0 copy-start.5
  59.4 0.7 %copy-done.5 = s32[1,256]{1,0:T(1,128)S(1)} copy-done((s32[1,256]{1,0:T(1,128)S(1)}, s32[1,256]{1,0:T(1,128)}, u32[]{:S(2)}) %copy-start.5) | copy-done | bytes 1048
  60.0 2.4 %project_out.1 = (bf16[256,1024]{1,0:T(8,128)(2,1)}, f32[1,256]{1,0:T(1,128)}) custom-call(s32[3]{0:T(128)S(1)} %pad_add_fusion.where_ref, bf16[256,256]{1,0:T(8,128)(2,1)S(1)} %get-tuple-element.47.att_refs_0_, bf16[256,256]{1,0:T(8,128)(2,1)S(1)} %collective-permute-done.14.att_refs_1_, bf16[256,256]{1,0:T(8,128)(2,1)S(1)} %collective-permute-done.15.att_refs_2_, ...), custom_call_target="tpu_custom_call" | custom-call | flops 1000000000 | bytes 4194304 | tf_op jit(solution)/shard_map/project_out/pallas_call | solution.py:353
  (10 shorter events, 0.1 us)
Async XLA Ops:
  0.6 4.2 %collective-permute-start = (bf16[384,1024]{1,0:T(8,128)(2,1)}, bf16[384,1024]{1,0:T(8,128)(2,1)S(1)}, u32[]{:S(2)}, u32[]{:S(2)}) collective-permute-start(bf16[384,1024]{1,0:T(8,128)(2,1)} %conv_ref.1), channel_id=1, source_target_pairs={{0,4},{4,0},{8,12},{12,8},{16,20},{20,16},{24,28},{28,24},{1,5},{5... | collective-permute-start | bytes 2359304 | tf_op jit(solution)/shard_map/ppermute | solution.py:301
  0.8 1.0 %copy-start = (bf16[256,768]{1,0:T(8,128)(2,1)S(1)}, bf16[256,768]{1,0:T(8,128)(2,1)}, u32[]{:S(2)}) copy-start(bf16[256,768]{1,0:T(8,128)(2,1)} %bytes_ref.3) | copy-start | bytes 1179652
  1.8 1.1 %copy-start.1 = (bf16[384,1024]{1,0:T(8,128)(2,1)S(1)}, bf16[384,1024]{1,0:T(8,128)(2,1)}, u32[]{:S(2)}) copy-start(bf16[384,1024]{1,0:T(8,128)(2,1)} %conv_ref.1) | copy-start | bytes 2359300
  2.9 1.0 %copy-start.3 = (bf16[128,1536]{1,0:T(8,128)(2,1)S(1)}, bf16[128,1536]{1,0:T(8,128)(2,1)}, u32[]{:S(2)}) copy-start(bf16[128,1536]{1,0:T(8,128)(2,1)} %qkv_ref.1) | copy-start | bytes 1179652
  4.8 5.0 %copy-start.8 = (s32[1,1024]{1,0:T(1,128)S(1)}, s32[1,1024]{1,0:T(1,128)}, u32[]{:S(2)}) copy-start(s32[1,1024]{1,0:T(1,128)} %param.10) | copy-start | bytes 12292
  4.8 24.6 %copy-start.6 = (f32[1024,128]{1,0:T(8,128)S(1)}, f32[1024,128]{1,0:T(8,128)}, u32[]{:S(2)}) copy-start(f32[1024,128]{1,0:T(8,128)} %constant.38.clone.cos_ref) | copy-start | bytes 1572868
  4.8 24.6 %copy-start.7 = (f32[1024,128]{1,0:T(8,128)S(1)}, f32[1024,128]{1,0:T(8,128)}, u32[]{:S(2)}) copy-start(f32[1024,128]{1,0:T(8,128)} %constant.39.clone.sin_ref) | copy-start | bytes 1572868
  5.7 20.1 %copy-start.4 = (bf16[128,1024]{1,0:T(8,128)(2,1)S(1)}, bf16[128,1024]{1,0:T(8,128)(2,1)}, u32[]{:S(2)}) copy-start(bf16[128,1024]{1,0:T(8,128)(2,1)} %own) | copy-start | bytes 786436
  5.7 14.1 %collective-permute-start.1 = (bf16[128,1408]{1,0:T(8,128)(2,1)S(1)}, bf16[128,1408]{1,0:T(8,128)(2,1)S(1)}, u32[]{:S(2)}, u32[]{:S(2)}) collective-permute-start(bf16[128,1408]{1,0:T(8,128)(2,1)S(1)} %tap_table.1.own), channel_id=1, source_target_pairs={{0,24},{4,28},{8,16},{12,20},{16,8},{20,12},{24,0},{28,4},{1,25},{... | collective-permute-start | bytes 1081352 | tf_op jit(solution)/shard_map/ppermute | solution.py:301
  8.2 17.1 %collective-permute-start.5 = (bf16[128,1408]{1,0:T(8,128)(2,1)S(1)}, bf16[128,1408]{1,0:T(8,128)(2,1)S(1)}, u32[]{:S(2)}, u32[]{:S(2)}) collective-permute-start(bf16[128,1408]{1,0:T(8,128)(2,1)S(1)} %tap_table.1.own), channel_id=1, source_target_pairs={{0,8},{4,12},{8,0},{12,4},{16,24},{20,28},{24,16},{28,20},{1,9},{5... | collective-permute-start | bytes 1081352 | tf_op jit(solution)/shard_map/ppermute | solution.py:301
  8.7 16.6 %collective-permute-start.6 = (bf16[128,1408]{1,0:T(8,128)(2,1)S(1)}, bf16[128,1408]{1,0:T(8,128)(2,1)S(1)}, u32[]{:S(2)}, u32[]{:S(2)}) collective-permute-start(bf16[128,1408]{1,0:T(8,128)(2,1)S(1)} %tap_table.1.own), channel_id=1, source_target_pairs={{0,16},{4,20},{8,24},{12,28},{16,0},{20,4},{24,8},{28,12},{1,17},{... | collective-permute-start | bytes 1081352 | tf_op jit(solution)/shard_map/ppermute | solution.py:301
  10.7 15.2 %copy-start.9 = (bf16[1024]{0:T(1024)(128)(2,1)S(1)}, bf16[1024]{0:T(1024)(128)(2,1)}, u32[]{:S(2)}) copy-start(bf16[1024]{0:T(1024)(128)(2,1)} %param.15) | copy-start | bytes 6148
  10.7 3.7 %collective-permute-start.2 = (s32[8,256]{1,0:T(8,128)S(1)}, s32[8,256]{1,0:T(8,128)S(1)}, u32[]{:S(2)}, u32[]{:S(2)}) collective-permute-start(s32[8,256]{1,0:T(8,128)S(1)} %pad.4.ids_refs_0_), channel_id=1, source_target_pairs={{0,1},{1,2},{2,3},{3,0},{4,5},{5,6},{6,7},{7,4},{8,9},{9,10},{10,1... | collective-permute-start | bytes 24584 | tf_op jit(solution)/shard_map/ppermute | solution.py:304
  10.7 4.6 %collective-permute-start.3 = (s32[8,256]{1,0:T(8,128)S(1)}, s32[8,256]{1,0:T(8,128)S(1)}, u32[]{:S(2)}, u32[]{:S(2)}) collective-permute-start(s32[8,256]{1,0:T(8,128)S(1)} %pad.4.ids_refs_0_), channel_id=1, source_target_pairs={{0,2},{1,3},{2,0},{3,1},{4,6},{5,7},{6,4},{7,5},{8,10},{9,11},{10,... | collective-permute-start | bytes 24584 | tf_op jit(solution)/shard_map/ppermute | solution.py:304
  14.4 5.4 %collective-permute-start.4 = (s32[8,256]{1,0:T(8,128)S(1)}, s32[8,256]{1,0:T(8,128)S(1)}, u32[]{:S(2)}, u32[]{:S(2)}) collective-permute-start(s32[8,256]{1,0:T(8,128)S(1)} %pad.4.ids_refs_0_), channel_id=1, source_target_pairs={{0,3},{1,0},{2,1},{3,2},{4,7},{5,4},{6,5},{7,6},{8,11},{9,8},{10,9... | collective-permute-start | bytes 24584 | tf_op jit(solution)/shard_map/ppermute | solution.py:304
  15.3 12.1 %collective-permute-start.7 = (bf16[128,1408]{1,0:T(8,128)(2,1)S(1)}, bf16[128,1408]{1,0:T(8,128)(2,1)S(1)}, u32[]{:S(2)}, u32[]{:S(2)}) collective-permute-start(bf16[128,1408]{1,0:T(8,128)(2,1)S(1)} %tap_table.1.own), channel_id=1, source_target_pairs={{0,4},{4,0},{8,12},{12,8},{16,20},{20,16},{24,28},{28,24},{1,5},{5... | collective-permute-start | bytes 1081352 | tf_op jit(solution)/shard_map/ppermute | solution.py:301
  25.3 3.5 %collective-permute-start.8 = (bf16[128,1408]{1,0:T(8,128)(2,1)S(1)}, bf16[128,1408]{1,0:T(8,128)(2,1)S(1)}, u32[]{:S(2)}, u32[]{:S(2)}) collective-permute-start(bf16[128,1408]{1,0:T(8,128)(2,1)S(1)} %collective-permute-done.5.near_0_), channel_id=1, source_target_pairs={{0,4},{4,0},{8,12},{12,8},{16,20},{20,16},{24,28},{28,24},{1,5},{5... | collective-permute-start | bytes 1081352 | tf_op jit(solution)/shard_map/ppermute | solution.py:301
  25.3 4.1 %collective-permute-start.9 = (bf16[128,1408]{1,0:T(8,128)(2,1)S(1)}, bf16[128,1408]{1,0:T(8,128)(2,1)S(1)}, u32[]{:S(2)}, u32[]{:S(2)}) collective-permute-start(bf16[128,1408]{1,0:T(8,128)(2,1)S(1)} %collective-permute-done.6.near_1_), channel_id=1, source_target_pairs={{0,4},{4,0},{8,12},{12,8},{16,20},{20,16},{24,28},{28,24},{1,5},{5... | collective-permute-start | bytes 1081352 | tf_op jit(solution)/shard_map/ppermute | solution.py:301
  25.8 3.6 %collective-permute-start.10 = (bf16[128,1408]{1,0:T(8,128)(2,1)S(1)}, bf16[128,1408]{1,0:T(8,128)(2,1)S(1)}, u32[]{:S(2)}, u32[]{:S(2)}) collective-permute-start(bf16[128,1408]{1,0:T(8,128)(2,1)S(1)} %collective-permute-done.1.near_2_), channel_id=1, source_target_pairs={{0,4},{4,0},{8,12},{12,8},{16,20},{20,16},{24,28},{28,24},{1,5},{5... | collective-permute-start | bytes 1081352 | tf_op jit(solution)/shard_map/ppermute | solution.py:301
  25.8 15.1 %collective-permute-start.11 = (bf16[128,1024]{1,0:T(8,128)(2,1)S(1)}, bf16[128,1024]{1,0:T(8,128)(2,1)S(1)}, u32[]{:S(2)}, u32[]{:S(2)}) collective-permute-start(bf16[128,1024]{1,0:T(8,128)(2,1)S(1)} %copy-done.4), channel_id=1, source_target_pairs={{0,8},{4,12},{8,0},{12,4},{16,24},{20,28},{24,16},{28,20},{1,9},{5... | collective-permute-start | bytes 786440 | tf_op jit(solution)/shard_map/ppermute | solution.py:301
  27.4 14.0 %collective-permute-start.12 = (bf16[128,1024]{1,0:T(8,128)(2,1)S(1)}, bf16[128,1024]{1,0:T(8,128)(2,1)S(1)}, u32[]{:S(2)}, u32[]{:S(2)}) collective-permute-start(bf16[128,1024]{1,0:T(8,128)(2,1)S(1)} %copy-done.4), channel_id=1, source_target_pairs={{0,16},{4,20},{8,24},{12,28},{16,0},{20,4},{24,8},{28,12},{1,17},{... | collective-permute-start | bytes 786440 | tf_op jit(solution)/shard_map/ppermute | solution.py:301
  28.8 12.6 %collective-permute-start.13 = (bf16[128,1024]{1,0:T(8,128)(2,1)S(1)}, bf16[128,1024]{1,0:T(8,128)(2,1)S(1)}, u32[]{:S(2)}, u32[]{:S(2)}) collective-permute-start(bf16[128,1024]{1,0:T(8,128)(2,1)S(1)} %copy-done.4), channel_id=1, source_target_pairs={{0,24},{4,28},{8,16},{12,20},{16,8},{20,12},{24,0},{28,4},{1,25},{... | collective-permute-start | bytes 786440 | tf_op jit(solution)/shard_map/ppermute | solution.py:301
  41.5 17.9 %copy-start.2 = (bf16[1,256,1024]{2,1,0:T(8,128)(2,1)S(1)}, bf16[1,256,1024]{2,1,0:T(8,128)(2,1)}, u32[]{:S(2)}) copy-start(bf16[1,256,1024]{2,1,0:T(8,128)(2,1)} %param.16) | copy-start | bytes 1572868
  41.5 5.0 %collective-permute-start.14 = (bf16[256,256]{1,0:T(8,128)(2,1)S(1)}, bf16[256,256]{1,0:T(8,128)(2,1)S(1)}, u32[]{:S(2)}, u32[]{:S(2)}) collective-permute-start(bf16[256,256]{1,0:T(8,128)(2,1)S(1)} %get-tuple-element.46), channel_id=1, source_target_pairs={{0,1},{1,2},{2,3},{3,0},{4,5},{5,6},{6,7},{7,4},{8,9},{9,10},{10,1... | collective-permute-start | bytes 393224 | tf_op jit(solution)/shard_map/ppermute | solution.py:304
  41.8 5.6 %collective-permute-start.17 = (bf16[128,1024]{1,0:T(8,128)(2,1)S(1)}, bf16[128,1024]{1,0:T(8,128)(2,1)S(1)}, u32[]{:S(2)}, u32[]{:S(2)}) collective-permute-start(bf16[128,1024]{1,0:T(8,128)(2,1)S(1)} %copy-done.4), channel_id=1, source_target_pairs={{0,4},{4,0},{8,12},{12,8},{16,20},{20,16},{24,28},{28,24},{1,5},{5... | collective-permute-start | bytes 786440 | tf_op jit(solution)/shard_map/ppermute | solution.py:301
  46.5 12.8 %collective-permute-start.18 = (bf16[128,1024]{1,0:T(8,128)(2,1)S(1)}, bf16[128,1024]{1,0:T(8,128)(2,1)S(1)}, u32[]{:S(2)}, u32[]{:S(2)}) collective-permute-start(bf16[128,1024]{1,0:T(8,128)(2,1)S(1)} %collective-permute-done.11.near_0_), channel_id=1, source_target_pairs={{0,4},{4,0},{8,12},{12,8},{16,20},{20,16},{24,28},{28,24},{1,5},{5... | collective-permute-start | bytes 786440 | tf_op jit(solution)/shard_map/ppermute | solution.py:301
  46.5 12.8 %collective-permute-start.19 = (bf16[128,1024]{1,0:T(8,128)(2,1)S(1)}, bf16[128,1024]{1,0:T(8,128)(2,1)S(1)}, u32[]{:S(2)}, u32[]{:S(2)}) collective-permute-start(bf16[128,1024]{1,0:T(8,128)(2,1)S(1)} %collective-permute-done.12.near_1_), channel_id=1, source_target_pairs={{0,4},{4,0},{8,12},{12,8},{16,20},{20,16},{24,28},{28,24},{1,5},{5... | collective-permute-start | bytes 786440 | tf_op jit(solution)/shard_map/ppermute | solution.py:301
  47.0 12.3 %collective-permute-start.20 = (bf16[128,1024]{1,0:T(8,128)(2,1)S(1)}, bf16[128,1024]{1,0:T(8,128)(2,1)S(1)}, u32[]{:S(2)}, u32[]{:S(2)}) collective-permute-start(bf16[128,1024]{1,0:T(8,128)(2,1)S(1)} %collective-permute-done.13.near_2_), channel_id=1, source_target_pairs={{0,4},{4,0},{8,12},{12,8},{16,20},{20,16},{24,28},{28,24},{1,5},{5... | collective-permute-start | bytes 786440 | tf_op jit(solution)/shard_map/ppermute | solution.py:301
  47.0 12.3 %collective-permute-start.15 = (bf16[256,256]{1,0:T(8,128)(2,1)S(1)}, bf16[256,256]{1,0:T(8,128)(2,1)S(1)}, u32[]{:S(2)}, u32[]{:S(2)}) collective-permute-start(bf16[256,256]{1,0:T(8,128)(2,1)S(1)} %get-tuple-element.45), channel_id=1, source_target_pairs={{0,2},{1,3},{2,0},{3,1},{4,6},{5,7},{6,4},{7,5},{8,10},{9,11},{10,... | collective-permute-start | bytes 393224 | tf_op jit(solution)/shard_map/ppermute | solution.py:304
  47.4 12.0 %collective-permute-start.16 = (bf16[256,256]{1,0:T(8,128)(2,1)S(1)}, bf16[256,256]{1,0:T(8,128)(2,1)S(1)}, u32[]{:S(2)}, u32[]{:S(2)}) collective-permute-start(bf16[256,256]{1,0:T(8,128)(2,1)S(1)} %get-tuple-element.44), channel_id=1, source_target_pairs={{0,3},{1,0},{2,1},{3,2},{4,7},{5,4},{6,5},{7,6},{8,11},{9,8},{10,9... | collective-permute-start | bytes 393224 | tf_op jit(solution)/shard_map/ppermute | solution.py:304
  59.3 0.7 %copy-start.5 = (s32[1,256]{1,0:T(1,128)S(1)}, s32[1,256]{1,0:T(1,128)}, u32[]{:S(2)}) copy-start(s32[1,256]{1,0:T(1,128)} %align_ref.1) | copy-start | bytes 3076

commit v2 on v0

--- a/solution.py
+++ b/solution.py
@@ -1,19 +1,25 @@
+import functools
 import math
 
 import jax
 import jax.numpy as jnp
+import numpy as np
 from jax import lax
+from jax.experimental import pallas as pl
+from jax.experimental.pallas import tpu as pltpu
 from jax.sharding import PartitionSpec as P
 
 KW = 4
 HQ = 16
 HK = 4
 HD = 64
-
+GROUP = HQ // HK
+VOCAB = 256
 
 theta_base = 500000.0
 norm_eps = 1e-05
 masked_score = -1e30
+score_scale = 1.0 / math.sqrt(HD)
 
 
 def rotate(values, positions):
@@ -33,8 +39,7 @@
     )
 
 
-def body(byte_ids, byte_table, w_conv, w_qkv, w_out, norm_gain, teacher, align):
-    score_scale = 1.0 / math.sqrt(HD)
+def general_body(byte_ids, byte_table, w_conv, w_qkv, w_out, norm_gain, teacher, align):
     seq_bytes = byte_ids.shape[1]
     lat_rows = seq_bytes // KW
     query_width = HQ * HD
@@ -109,6 +114,304 @@
     return (hidden_out[None], token_loss[None])
 
 
+def rope_tables(length):
+    half = HD // 2
+    frequency = np.float32(theta_base) ** (-np.arange(half, dtype=np.float32) * np.float32(2.0 / HD))
+    angles = np.arange(length, dtype=np.float32)[:, None] * frequency[None, :]
+    angles = angles.astype(np.float64)
+    cos, sin = np.cos(angles).astype(np.float32), np.sin(angles).astype(np.float32)
+    return np.concatenate([cos] * 4, axis=1), np.concatenate([-sin, sin] * 2, axis=1)
+
+
+def turn(x, cos, sin):
+    half = HD // 2
+    lane = lax.broadcasted_iota(jnp.int32, x.shape, 1)
+    low = (lane & half) == 0
+    swapped = jnp.where(low, pltpu.roll(x, 128 - half, axis=1), pltpu.roll(x, half, axis=1))
+    return x * cos + swapped * sin
+
+
+def part_kernel(where_ref, qkv_ref, align_ref, part_ref, align_out):
+    align_out[...] = align_ref[...]
+    side = where_ref[2] % 2
+    start = 0
+    for width in (HQ * HD, HK * HD, HK * HD):
+        own = width // 2
+        part_ref[:, start // 2 : start // 2 + own] = qkv_ref[
+            :, pl.ds(pl.multiple_of(start + side * own, own), own)
+        ]
+        start += width
+
+
+def table_kernel(where_ref, bytes_ref, conv_ref, total_ref, out_ref):
+    core = where_ref[1]
+    taps_in = conv_ref.shape[0]
+    half = total_ref.shape[0]
+    rows = pl.ds(pl.multiple_of(core * half, half), half)
+    mates = bytes_ref[rows, pl.ds(pl.multiple_of((1 - core) * taps_in, taps_in), taps_in)]
+    total = total_ref[...] + jnp.dot(mates, conv_ref[...], preferred_element_type=jnp.float32)
+    out_ref[...] = total.astype(jnp.bfloat16)
+
+
+def ordered(chip, core, pieces):
+    own, near, mate_own, mate_near = pieces
+    depth = own.shape[0]
+    for j, (mine, mates) in enumerate(zip((own,) + near, (mate_own,) + mate_near)):
+        base = (chip ^ j) * 2
+        for which, piece in ((core, mine), (1 - core, mates)):
+            yield pl.ds(pl.multiple_of((base + which) * depth, depth), depth), piece
+
+
+def attend(queries, key_slots, allowed, k_s, v_s, att_ref):
+    heads = HQ // 2
+
+    def one_head(h):
+        query = queries(h)
+        group = h // GROUP
+        scores = [
+            lax.dot_general(
+                k_s[slot, group], query, (((1,), (1,)), ((), ())), preferred_element_type=jnp.float32
+            )
+            for slot in key_slots
+        ]
+        scores[-1] = jnp.where(allowed, scores[-1], masked_score)
+        top = functools.reduce(jnp.maximum, [jnp.max(s, axis=0, keepdims=True) for s in scores])
+        total = None
+        for slot, s in zip(key_slots, scores):
+            probs = jnp.exp(s - top).astype(jnp.bfloat16)
+            term = jnp.dot(v_s[slot, group], probs, preferred_element_type=jnp.float32)
+            total = term if total is None else total + term
+        return total[:HD] / total[HD : HD + 1]
+
+    for pair in range(heads // 2):
+        result = jnp.concatenate([one_head(2 * pair), one_head(2 * pair + 1)], axis=0)
+        att_ref[:, pair * 2 * HD : (pair + 1) * 2 * HD] = jnp.transpose(result).astype(jnp.bfloat16)
+
+
+def causal(rows):
+    return lax.broadcasted_iota(jnp.int32, (rows, rows), 0) <= lax.broadcasted_iota(
+        jnp.int32, (rows, rows), 1
+    )
+
+
+def key_variants(ctx, which):
+    for block in range(2):
+        now = tuple(range(2, 3 + block))
+        yield (which == block) & (ctx < 2), block, now
+        yield (which == block) & (ctx >= 2), block, (0, 1) + now
+
+
+def lift_kernel(
+    where_ref, ids_ref, own_t, near_t, mate_own_t, mate_near_t, own_w, near_w, mate_own_w, mate_near_w,
+    gain_ref, cos_ref, sin_ref, att_ref, query_ref, k_s, v_s, lat_ref,
+    table_s, weight_s, ids_s, lat_s, q_s,
+):
+    chip, core, ctx = where_ref[0], where_ref[1], where_ref[2]
+    side, upper = ctx % 2, ctx // 2
+    rows, features = lat_ref.shape
+    q_width, k_width = HQ * HD // 2, HK * HD // 2
+    for span, piece in ordered(chip, core, (own_t, near_t, mate_own_t, mate_near_t)):
+        table_s[span, :] = piece[...]
+    for span, piece in ordered(chip, core, (own_w, near_w, mate_own_w, mate_near_w)):
+        weight_s[span, :] = piece[...]
+    for place, slot in enumerate((2 + side, 3 - side, side, 1 - side)):
+        ids_s[slot] = ids_ref[place]
+    gain = gain_ref[...].astype(jnp.float32)
+    v_s[:, :, HD:, :] = jnp.ones(v_s.shape[:2] + (v_s.shape[2] - HD, rows), jnp.bfloat16)
+
+    def lift(slot):
+        ids = jnp.transpose(ids_s[slot])
+        byte = lax.broadcasted_iota(jnp.int32, (rows, VOCAB), 1)
+        one_hot = jnp.concatenate(
+            [(ids[:, k : k + 1] == byte).astype(jnp.float32).astype(jnp.bfloat16) for k in range(KW)], axis=1
+        )
+        latent = jnp.dot(one_hot, table_s[...], preferred_element_type=jnp.float32).astype(jnp.bfloat16)
+        wide = latent.astype(jnp.float32)
+        scale = lax.rsqrt(jnp.mean(wide * wide, axis=1, keepdims=True) + norm_eps)
+        normed = (wide * scale * gain).astype(jnp.bfloat16)
+        block = slot if slot < 2 else 2 * upper + slot - 2
+        cos, sin = cos_ref[block], sin_ref[block]
+        if slot >= 2:
+            lat_s[slot - 2] = latent
+            asked = jnp.dot(normed, weight_s[:, :q_width], preferred_element_type=jnp.float32)
+            for pair in range(q_width // 128):
+                turned = turn(asked[:, pair * 128 : (pair + 1) * 128], cos, sin)
+                turned = (turned * score_scale).astype(jnp.bfloat16)
+                q_s[slot - 2, 2 * pair] = turned[:, :HD]
+                q_s[slot - 2, 2 * pair + 1] = turned[:, HD:]
+        kept = jnp.dot(normed, weight_s[:, q_width:], preferred_element_type=jnp.float32)
+        keys = turn(kept[:, :k_width], cos, sin).astype(jnp.bfloat16)
+        values = jnp.transpose(kept[:, k_width:]).astype(jnp.bfloat16)
+        for group in range(2):
+            k_s[slot, group] = keys[:, group * HD : (group + 1) * HD]
+            v_s[slot, group, :HD, :] = values[group * HD : (group + 1) * HD]
+
+    @pl.when(upper == 1)
+    def _():
+        lift(0)
+        lift(1)
+
+    lift(2)
+    lift(3)
+    lat_ref[...] = lat_s[side]
+    query_ref[...] = q_s[side]
+    allowed = causal(rows)
+    other = 1 - side
+    for condition, block, slots in key_variants(ctx, other):
+
+        @pl.when(condition)
+        def _(block=block, slots=slots):
+            attend(lambda h: q_s[block, h], slots, allowed, k_s, v_s, att_ref)
+
+
+def own_kernel(where_ref, query_ref, k_ref, v_ref, att_ref):
+    ctx = where_ref[2]
+    allowed = causal(att_ref.shape[0])
+    for condition, block, slots in key_variants(ctx, ctx % 2):
+
+        @pl.when(condition)
+        def _(slots=slots):
+            attend(lambda h: query_ref[h], slots, allowed, k_ref, v_ref, att_ref)
+
+
+def out_kernel(
+    where_ref, own_att, mate_att, own, near, mate_own, mate_near, lat_ref, teacher_ref, align_ref,
+    hidden_ref, loss_ref, att_s, weight_s,
+):
+    chip, core, ctx = where_ref[0], where_ref[1], where_ref[2]
+    side = ctx % 2
+    rows, width = lat_ref.shape
+    part = own_att.shape[1]
+    for span, piece in ordered(chip, core, (own, near, mate_own, mate_near)):
+        weight_s[span, :] = piece[...]
+    att_s[:, pl.ds(pl.multiple_of(side * part, part), part)] = own_att[...]
+    att_s[:, pl.ds(pl.multiple_of((1 - side) * part, part), part)] = mate_att[...]
+    branch = jnp.dot(att_s[...], weight_s[...], preferred_element_type=jnp.float32)
+    hidden = (lat_ref[...].astype(jnp.float32) + branch).astype(jnp.bfloat16)
+    hidden_ref[...] = hidden
+    source = lax.broadcasted_iota(jnp.int32, (rows, rows), 0) + ctx * rows
+    chosen = (source == align_ref[...]).astype(jnp.float32).astype(jnp.bfloat16)
+    picked = lax.dot_general(
+        chosen, hidden, (((0,), (0,)), ((), ())), preferred_element_type=jnp.float32
+    )
+    difference = picked - teacher_ref[...].astype(jnp.float32)
+    square = difference * difference
+    lanes = square[:, :128]
+    for start in range(128, width, 128):
+        lanes = lanes + square[:, start : start + 128]
+    loss_ref[...] = jnp.sum(jnp.transpose(lanes), axis=0, keepdims=True) * (1.0 / width)
+
+
+VMEM = pl.BlockSpec(memory_space=pltpu.VMEM)
+SMEM = pl.BlockSpec(memory_space=pltpu.SMEM)
+MIB = 1024 * 1024
+
+
+def call(kernel, name, mib, flops, in_specs, outs, scratch=()):
+    return pl.pallas_call(
+        kernel,
+        out_shape=tuple(jax.ShapeDtypeStruct(shape, dtype) for shape, dtype in outs),
+        in_specs=in_specs,
+        out_specs=(VMEM,) * len(outs),
+        scratch_shapes=[pltpu.VMEM(shape, dtype) for shape, dtype in scratch],
+        compiler_params=pltpu.CompilerParams(vmem_limit_bytes=mib * MIB),
+        cost_estimate=pl.CostEstimate(flops=flops, bytes_accessed=4 * MIB, transcendentals=0),
+        name=name,
+    )
+
+
+def head_body(sizes, byte_ids, byte_table, w_conv, w_qkv, w_out, norm_gain, teacher, align):
+    n_fsdp, n_ctx = sizes
+    me, ctx = lax.axis_index("fsdp"), lax.axis_index("ctx")
+    chip, core = me // 2, me % 2
+    rows = byte_ids.shape[1] // KW
+    features = w_conv.shape[1]
+    q_width = HQ * HD // 2
+    part_width = w_qkv.shape[1] // 2
+    half = VOCAB // 2
+    bf16, f32 = jnp.bfloat16, jnp.float32
+    where = jnp.stack([chip, core, ctx]).astype(jnp.int32)
+
+    def swap(x, j):
+        return lax.ppermute(x, "fsdp", [(d, d ^ j) for d in range(n_fsdp)])
+
+    def along(x, pairs):
+        return lax.ppermute(x, "ctx", pairs)
+
+    def to_near(x):
+        return tuple(swap(x, 2 * j) for j in range(1, n_fsdp // 2))
+
+    def to_mate(x, near):
+        return x, near, swap(x, 1), tuple(swap(piece, 1) for piece in near)
+
+    beside = [(z, z ^ 1) for z in range(n_ctx)]
+
+    mate_conv = swap(w_conv, 1)
+    part, align = call(
+        part_kernel, "qkv_part", 4, 10**8, [SMEM, VMEM, VMEM],
+        [((w_qkv.shape[0], part_width), bf16), (align.shape, jnp.int32)],
+    )(where, w_qkv, align)
+    near_w = to_near(part)
+
+    taps_in = w_conv.shape[0]
+    mine = lax.dynamic_slice(byte_table, (core * half, core * taps_in), (half, taps_in))
+    total = jnp.dot(mine, w_conv, preferred_element_type=f32)
+    (own_t,) = call(
+        table_kernel, "tap_table", 8, 10**8, [SMEM, VMEM, VMEM, VMEM], [((half, features), bf16)]
+    )(where, byte_table, mate_conv, total)
+    ids_all = (
+        byte_ids,
+        along(byte_ids, beside),
+        along(byte_ids, [(0, 2), (1, 3)]),
+        along(byte_ids, [(0, 3), (1, 2)]),
+    )
+    own_t, ids_all = lax.optimization_barrier((own_t, ids_all))
+    near_t = to_near(own_t)
+    ids_all = jnp.concatenate(ids_all, axis=0).reshape(4, rows, KW)
+    ids_all = jnp.pad(jnp.swapaxes(ids_all, 1, 2), ((0, 0), (0, 8 - KW), (0, 0)))
+    w_pieces, mate_own_t = to_mate(part, near_w), swap(own_t, 1)
+    near_t, w_pieces, mate_own_t = lax.optimization_barrier((near_t, w_pieces, mate_own_t))
+    t_pieces = (own_t, near_t, mate_own_t, tuple(swap(piece, 1) for piece in near_t))
+    out_own, unused = lax.optimization_barrier((w_out, near_t))
+    out_near = to_near(out_own)
+
+    cos, sin = (jnp.asarray(t.reshape(n_ctx, rows, 128)) for t in rope_tables(rows * n_ctx))
+    near_specs = (VMEM,) * (n_fsdp // 2 - 1)
+    piece_specs = [VMEM, near_specs, VMEM, near_specs]
+    att_shape = ((rows, q_width), bf16)
+    att_mate, query, keys, values, latent = call(
+        lift_kernel, "lift", 28, 5 * 10**9,
+        [SMEM, VMEM] + piece_specs + piece_specs + [VMEM, VMEM, VMEM],
+        [
+            att_shape,
+            ((HQ // 2, rows, HD), bf16),
+            ((4, 2, rows, HD), bf16),
+            ((4, 2, HD + 16, rows), bf16),
+            ((rows, features), bf16),
+        ],
+        [
+            ((KW * VOCAB, features), bf16),
+            ((features, part_width), bf16),
+            ((4, 8, rows), jnp.int32),
+            ((2, rows, features), bf16),
+            ((2, HQ // 2, rows, HD), bf16),
+        ],
+    )(where, ids_all, *t_pieces, *w_pieces, norm_gain[None], cos, sin)
+
+    att_mate, out_near = lax.optimization_barrier((att_mate, out_near))
+    att_back = along(att_mate, beside)
+    (att_own,) = call(
+        own_kernel, "own_block", 16, 3 * 10**9, [SMEM, VMEM, VMEM, VMEM], [att_shape]
+    )(where, query, keys, values)
+    hidden, loss = call(
+        out_kernel, "project_out", 16, 10**9,
+        [SMEM, VMEM, VMEM] + piece_specs + [VMEM, VMEM, VMEM],
+        [((rows, features), bf16), ((1, rows), f32)],
+        [((rows, features), bf16), ((features, features), bf16)],
+    )(where, att_own, att_back, *to_mate(out_own, out_near), latent, teacher[0], align)
+    return hidden[None], loss
+
+
 def solution(mesh):
     in_specs = (
         P("fsdp", "ctx"),
@@ -121,4 +424,6 @@
         P("fsdp", "ctx"),
     )
     out_specs = (P("fsdp", "ctx", None), P("fsdp", "ctx"))
+    sizes = (mesh.shape["fsdp"], mesh.shape["ctx"])
+    body = functools.partial(head_body, sizes) if sizes == (2 * KW, HK) else general_body
     return jax.shard_map(body, mesh=mesh, in_specs=in_specs, out_specs=out_specs, check_vma=False)

time: 195 us -> 73.1 us (0.37)
  waiting for transfers between devices: 71 us -> 22.3 us
  blocking collectives: 31.8 us -> 0 us
  matrix products: 31.1 us -> 1.43 us
  other arithmetic: 24.4 us -> 0.1 us
  Pallas kernels: 0 us -> 19.9 us
  starting transfers between devices: 0.11 us -> 16.9 us
  between operations: 14 us -> 0.87 us
  local copies, waits for them, and re-layouts: 19.9 us -> 11.2 us
    all_gather x3 -> x0, waiting for transfers between devices: 69 us -> none  [project(): lax.all_gather(weight, 'fsdp', axis=0, tiled=True)]
    all_gather x2 -> x0, blocking collectives: 31.8 us -> none  [the longest x1 16.3 us: body(): key_all = lax.all_gather(key_rows, 'ctx', axis=0, tiled=True)]
    dot_general x12 -> x1, matrix products: 31.1 us -> 1.43 us  [head_body(): total = jnp.dot(mine, w_conv, preferred_element_type=f32)]
    ppermute x0 -> x26, waiting for transfers between devices: none -> 22.3 us  [the longest x4 12.3 us: along(): return lax.ppermute(x, 'ctx', pairs)]
    pallas_call x0 -> x5, Pallas kernels: none -> 19.9 us  [the longest x1 11 us: head_body(): call(lift_kernel, 'lift', 28, 5 * 10 ** 9, [SMEM, VMEM] + piece_specs + p...]
    ppermute x0 -> x26, starting transfers between devices: none -> 16.9 us  [the longest x22 13.8 us: swap(): return lax.ppermute(x, 'fsdp', [(d, d ^ j) for d in range(n_fsdp)])]
    reduce_sum x5 -> x0, other arithmetic: 13.3 us -> none  [the longest x4 12.9 us: one_block(): row_mass = row_mass * shrink + jnp.sum(weights, axis=-1)]
    dynamic_slice x4 -> x0, local copies, waits for them, and re-layouts: 4.7 us -> none  [body(): lax.scan(one_block, start_state, (key_blocks, value_blocks, block_starts))]
  transfers between devices with their start and end apart: 3 -> 26, of which waited for: 2 -> 9; matrix products, arithmetic and copies ran while one was open for 36% -> 6% of each run, Pallas kernels for 0% -> 24%
where the time goes in v2:
time: 73.1 us; the launch traced here: 72.7 us
  waiting for transfers between devices  22.3 us (31%)
  Pallas kernels  19.9 us (27%)
  starting transfers between devices  16.9 us (23%)
  local copies, waits for them, and re-layouts  11.2 us (15%)
  matrix products  1.43 us (2%)
  between operations  0.87 us (1%)
    ppermute x22, starting transfers between devices, swap(): return lax.ppermute(x, 'fsdp', [(d, d ^ j) for d in range(n_fsdp)])  13.8 us
    ppermute x4, waiting for transfers between devices, along(): return lax.ppermute(x, 'ctx', pairs)  12.3 us
    pallas_call x1, Pallas kernels, head_body(): call(lift_kernel, 'lift', 28, 5 * 10 ** 9, [SMEM, VMEM] + piece_specs + p...  11 us
    ppermute x22, waiting for transfers between devices, swap(): return lax.ppermute(x, 'fsdp', [(d, d ^ j) for d in range(n_fsdp)])  9.99 us
    unnamed x30, local copies, waits for them, and re-layouts  8.58 us
    pallas_call x1, Pallas kernels, head_body(): call(own_kernel, 'own_block', 16, 3 * 10 ** 9, [SMEM, VMEM, VMEM, VMEM],...  5.06 us
    ppermute x4, starting transfers between devices, along(): return lax.ppermute(x, 'ctx', pairs)  3.09 us
    reshape x2, local copies, waits for them, and re-layouts, head_body(): ids_all = jnp.concatenate(ids_all, axis=0).reshape(4, rows, KW)  2.61 us
  transfers between devices with their start and end apart: 26, of which 9 were waited for; matrix products, arithmetic and copies ran while one was open for 6% of the time, Pallas kernels for 24%

profile of v2, /device:TPU:24, one launch (start us, length us, event | category | flops | bytes accessed | tf_op | source)
XLA Modules:
  0.0 72.7 jit_solution(15308463113421600310)
XLA Ops:
  0.6 0.1 collective-permute-start
  0.7 0.1 pad_add_fusion.1.where_ref
  0.8 1.0 %copy-done.1 = bf16[128,1536]{1,0:T(8,128)(2,1)S(1)} copy-done((bf16[128,1536]{1,0:T(8,128)(2,1)S(1)}, bf16[128,1536]{1,0:T(8,128)(2,1)}, u32[]{:S(2)}) %copy-start.1) | copy-done | bytes 393240
  1.8 0.7 copy-done.2
  2.5 0.6 qkv_part.1
  3.1 1.6 %collective-permute-start.7 = (bf16[128,768]{1,0:T(8,128)(2,1)S(1)}, bf16[128,768]{1,0:T(8,128)(2,1)S(1)}, u32[]{:S(2)}, u32[]{:S(2)}) collective-permute-start(bf16[128,768]{1,0:T(8,128)(2,1)S(1)} %get-tuple-element.43.own_w), channel_id=1, source_target_pairs={{0,8},{4,12},{8,0},{12,4},{16,24},{20,28},{24,16},{28,20},{1,9},{5... | collective-permute-start | bytes 589832 | tf_op jit(solution)/shard_map/ppermute | solution.py:336
  4.6 1.5 %collective-permute-start.8 = (bf16[128,768]{1,0:T(8,128)(2,1)S(1)}, bf16[128,768]{1,0:T(8,128)(2,1)S(1)}, u32[]{:S(2)}, u32[]{:S(2)}) collective-permute-start(bf16[128,768]{1,0:T(8,128)(2,1)S(1)} %get-tuple-element.43.own_w), channel_id=1, source_target_pairs={{0,16},{4,20},{8,24},{12,28},{16,0},{20,4},{24,8},{28,12},{1,17},{... | collective-permute-start | bytes 589832 | tf_op jit(solution)/shard_map/ppermute | solution.py:336
  6.2 0.4 collective-permute-start.1
  6.6 1.3 %collective-permute-start.2 = (s32[1,1024]{1,0:T(1,128)S(1)}, s32[1,1024]{1,0:T(1,128)S(1)}, u32[]{:S(2)}, u32[]{:S(2)}) collective-permute-start(s32[1,1024]{1,0:T(1,128)S(1)} %copy-done.13), channel_id=1, source_target_pairs={{0,2},{1,3},{4,6},{5,7},{8,10},{9,11},{12,14},{13,15},{16,18},{17,... | collective-permute-start | bytes 12296 | tf_op jit(solution)/shard_map/ppermute | solution.py:339
  7.9 1.9 %collective-permute-done.1 = s32[1,1024]{1,0:T(1,128)S(1)} collective-permute-done((s32[1,1024]{1,0:T(1,128)S(1)}, s32[1,1024]{1,0:T(1,128)S(1)}, u32[]{:S(2)}, u32[]{:S(2)}) %collective-permute-start.1) | collective-permute-done | bytes 4128 | tf_op jit(solution)/shard_map/ppermute | solution.py:339
  9.8 0.5 collective-permute-start.9
  10.2 2.8 %collective-permute-done.2 = s32[1,1024]{1,0:T(1,128)S(1)} collective-permute-done((s32[1,1024]{1,0:T(1,128)S(1)}, s32[1,1024]{1,0:T(1,128)S(1)}, u32[]{:S(2)}, u32[]{:S(2)}) %collective-permute-start.2) | collective-permute-done | bytes 4128 | tf_op jit(solution)/shard_map/ppermute | solution.py:339
  13.0 0.0 collective-permute-start.10
  13.0 0.0 collective-permute-done.7.near_w_0_
  13.0 0.5 collective-permute-start.11
  13.5 1.4 %collective-permute-done.8.near_w_1_ = bf16[128,768]{1,0:T(8,128)(2,1)S(1)} collective-permute-done((bf16[128,768]{1,0:T(8,128)(2,1)S(1)}, bf16[128,768]{1,0:T(8,128)(2,1)S(1)}, u32[]{:S(2)}, u32[]{:S(2)}) %collective-permute-start.8) | collective-permute-done | bytes 196640 | tf_op jit(solution)/shard_map/ppermute | solution.py:336
  14.9 1.4 %fusion.total_ref = f32[128,1024]{1,0:T(8,128)S(1)} fusion(bf16[384,1024]{1,0:T(8,128)(2,1)} %param.12, bf16[256,768]{1,0:T(8,128)(2,1)S(1)} %copy-done, s32[]{:T(128)S(6)} %select_n.19, s32[]{:T(128)S(6)} %select_n.20), kind=kOutput, calls=%fused_computation | convolution fusion | flops 100663296 | bytes 1409032 | tf_op jit(solution)/shard_map/dot_general | solution.py:358
  16.4 0.0 copy-start.14
  16.4 0.0 collective-permute-done.conv_ref
  16.4 1.3 %collective-permute-start.3 = (s32[1,1024]{1,0:T(1,128)S(1)}, s32[1,1024]{1,0:T(1,128)S(1)}, u32[]{:S(2)}, u32[]{:S(2)}) collective-permute-start(s32[1,1024]{1,0:T(1,128)S(1)} %copy-done.13), channel_id=1, source_target_pairs={{0,3},{1,2},{4,7},{5,6},{8,11},{9,10},{12,15},{13,14},{16,19},{17,... | collective-permute-start | bytes 12296 | tf_op jit(solution)/shard_map/ppermute | solution.py:339
  17.7 0.8 %tap_table.1.own_t = bf16[128,1024]{1,0:T(8,128)(2,1)S(1)} custom-call(s32[3]{0:T(128)S(1)} %pad_add_fusion.1.where_ref, bf16[256,768]{1,0:T(8,128)(2,1)S(1)} %copy-done, bf16[384,1024]{1,0:T(8,128)(2,1)S(1)} %collective-permute-done.conv_ref, f32[128,1024]{1,0:T(8,128)S(1)} %fusion.total_ref), custom_call_target="tpu_custom_call" | custom-call | flops 100000000 | bytes 4194304 | tf_op jit(solution)/shard_map/tap_table/pallas_call | solution.py:359
  18.5 5.1 %collective-permute-done.3 = s32[1,1024]{1,0:T(1,128)S(1)} collective-permute-done((s32[1,1024]{1,0:T(1,128)S(1)}, s32[1,1024]{1,0:T(1,128)S(1)}, u32[]{:S(2)}, u32[]{:S(2)}) %collective-permute-start.3) | collective-permute-done | bytes 4128 | tf_op jit(solution)/shard_map/ppermute | solution.py:339
  23.7 0.5 collective-permute-start.4
  24.2 2.4 %collective-permute-start.5 = (bf16[128,1024]{1,0:T(8,128)(2,1)S(1)}, bf16[128,1024]{1,0:T(8,128)(2,1)S(1)}, u32[]{:S(2)}, u32[]{:S(2)}) collective-permute-start(bf16[128,1024]{1,0:T(8,128)(2,1)S(1)} %tap_table.1.own_t), channel_id=1, source_target_pairs={{0,16},{4,20},{8,24},{12,28},{16,0},{20,4},{24,8},{28,12},{1,17},{... | collective-permute-start | bytes 786440 | tf_op jit(solution)/shard_map/ppermute | solution.py:336
  26.7 1.0 %collective-permute-start.6 = (bf16[128,1024]{1,0:T(8,128)(2,1)S(1)}, bf16[128,1024]{1,0:T(8,128)(2,1)S(1)}, u32[]{:S(2)}, u32[]{:S(2)}) collective-permute-start(bf16[128,1024]{1,0:T(8,128)(2,1)S(1)} %tap_table.1.own_t), channel_id=1, source_target_pairs={{0,24},{4,28},{8,16},{12,20},{16,8},{20,12},{24,0},{28,4},{1,25},{... | collective-permute-start | bytes 786440 | tf_op jit(solution)/shard_map/ppermute | solution.py:336
  27.7 0.7 copy-done.5
  28.3 0.0 collective-permute-start.14
  28.4 0.0 collective-permute-done.12.mate_near_w_1_
  28.4 0.7 copy-done.7
  29.0 0.5 collective-permute-start.13
  29.5 1.1 %collective-permute-done.13.mate_near_w_2_ = bf16[128,768]{1,0:T(8,128)(2,1)S(1)} collective-permute-done((bf16[128,768]{1,0:T(8,128)(2,1)S(1)}, bf16[128,768]{1,0:T(8,128)(2,1)S(1)}, u32[]{:S(2)}, u32[]{:S(2)}) %collective-permute-start.13) | collective-permute-done | bytes 196640 | tf_op jit(solution)/shard_map/ppermute | solution.py:336
  30.6 0.7 copy-done.9
  31.3 1.6 %collective-permute-done.4.near_t_0_ = bf16[128,1024]{1,0:T(8,128)(2,1)S(1)} collective-permute-done((bf16[128,1024]{1,0:T(8,128)(2,1)S(1)}, bf16[128,1024]{1,0:T(8,128)(2,1)S(1)}, u32[]{:S(2)}, u32[]{:S(2)}) %collective-permute-start.4) | collective-permute-done | bytes 262176 | tf_op jit(solution)/shard_map/ppermute | solution.py:336
  32.9 4.2 %collective-permute-done.5.near_t_1_ = bf16[128,1024]{1,0:T(8,128)(2,1)S(1)} collective-permute-done((bf16[128,1024]{1,0:T(8,128)(2,1)S(1)}, bf16[128,1024]{1,0:T(8,128)(2,1)S(1)}, u32[]{:S(2)}, u32[]{:S(2)}) %collective-permute-start.5) | collective-permute-done | bytes 262176 | tf_op jit(solution)/shard_map/ppermute | solution.py:336
  37.1 1.7 %collective-permute-done.6.near_t_2_ = bf16[128,1024]{1,0:T(8,128)(2,1)S(1)} collective-permute-done((bf16[128,1024]{1,0:T(8,128)(2,1)S(1)}, bf16[128,1024]{1,0:T(8,128)(2,1)S(1)}, u32[]{:S(2)}, u32[]{:S(2)}) %collective-permute-start.6) | collective-permute-done | bytes 262176 | tf_op jit(solution)/shard_map/ppermute | solution.py:336
  38.8 0.0 collective-permute-done.14.mate_own_t
  38.8 0.0 collective-permute-start.15
  38.8 0.5 collective-permute-start.16
  39.3 0.0 collective-permute-start.17
  39.3 1.3 %reshape.7 = s32[4,256,4]{2,1,0:T(8,128)} reshape(s32[4,1024]{1,0:T(4,128)S(1)} %pad_add_fusion) | data formatting | bytes 32768 | tf_op jit(solution)/shard_map/reshape | solution.py:370
  40.7 1.3 %copy.12 = s32[4,256,4]{1,2,0:T(4,128)S(1)} copy(s32[4,256,4]{2,1,0:T(8,128)} %reshape.7) | data formatting | bytes 32768 | tf_op jit(solution)/shard_map/reshape | solution.py:370
  41.9 0.0 copy-done.4
  42.0 0.6 collective-permute-start.18
  42.6 1.8 %collective-permute-start.19 = (bf16[128,1024]{1,0:T(8,128)(2,1)S(1)}, bf16[128,1024]{1,0:T(8,128)(2,1)S(1)}, u32[]{:S(2)}, u32[]{:S(2)}) collective-permute-start(bf16[128,1024]{1,0:T(8,128)(2,1)S(1)} %copy-done.4), channel_id=1, source_target_pairs={{0,16},{4,20},{8,24},{12,28},{16,0},{20,4},{24,8},{28,12},{1,17},{... | collective-permute-start | bytes 786440 | tf_op jit(solution)/shard_map/ppermute | solution.py:336
  44.4 0.0 collective-permute-done.15.mate_near_t_0_
  44.4 1.1 %collective-permute-start.20 = (bf16[128,1024]{1,0:T(8,128)(2,1)S(1)}, bf16[128,1024]{1,0:T(8,128)(2,1)S(1)}, u32[]{:S(2)}, u32[]{:S(2)}) collective-permute-start(bf16[128,1024]{1,0:T(8,128)(2,1)S(1)} %copy-done.4), channel_id=1, source_target_pairs={{0,24},{4,28},{8,16},{12,20},{16,8},{20,12},{24,0},{28,4},{1,25},{... | collective-permute-start | bytes 786440 | tf_op jit(solution)/shard_map/ppermute | solution.py:336
  45.5 0.0 collective-permute-done.16.mate_near_t_1_
  45.5 0.0 collective-permute-start.22
  45.5 0.0 collective-permute-done.17.mate_near_t_2_
  45.5 0.9 %copy-done.6 = bf16[128,768]{1,0:T(8,128)(2,1)S(1)} copy-done((bf16[128,768]{1,0:T(8,128)(2,1)S(1)}, bf16[128,768]{1,0:T(8,128)(2,1)}, u32[]{:S(2)}) %copy-start.6) | copy-done | bytes 196632
  46.5 0.9 %copy-done.8 = bf16[128,768]{1,0:T(8,128)(2,1)S(1)} copy-done((bf16[128,768]{1,0:T(8,128)(2,1)S(1)}, bf16[128,768]{1,0:T(8,128)(2,1)}, u32[]{:S(2)}) %copy-start.8) | copy-done | bytes 196632
  47.4 0.9 %copy-done.10 = bf16[128,768]{1,0:T(8,128)(2,1)S(1)} copy-done((bf16[128,768]{1,0:T(8,128)(2,1)S(1)}, bf16[128,768]{1,0:T(8,128)(2,1)}, u32[]{:S(2)}) %copy-start.10) | copy-done | bytes 196632
  48.3 1.0 %copy-done.11 = f32[4,256,128]{2,1,0:T(8,128)S(1)} copy-done((f32[4,256,128]{2,1,0:T(8,128)S(1)}, f32[4,256,128]{2,1,0:T(8,128)}, u32[]{:S(2)}) %copy-start.11) | copy-done | bytes 524312
  49.3 1.0 %copy-done.12 = f32[4,256,128]{2,1,0:T(8,128)S(1)} copy-done((f32[4,256,128]{2,1,0:T(8,128)S(1)}, f32[4,256,128]{2,1,0:T(8,128)}, u32[]{:S(2)}) %copy-start.12) | copy-done | bytes 524312
  50.4 11.0 %lift.1 = (bf16[256,512]{1,0:T(8,128)(2,1)S(1)}, bf16[8,256,64]{2,1,0:T(8,128)(2,1)S(1)}, bf16[4,2,256,64]{3,2,1,0:T(8,128)(2,1)S(1)}, bf16[4,2,80,256]{3,2,1,0:T(8,128)(2,1)S(1)}, bf16[256,1024]{1,0:T(8,128)(2,1)S(1)}) custom-call(s32[3]{0:T(128)S(1)} %pad_add_fusion.1.where_ref, s32[4,8,256]{2,1,0:T(8,128)S(1)} %pad.4.ids_ref, ...), custom_call_target="tpu_custom_call" | custom-call | flops 5000000000 | bytes 4194304 | tf_op jit(solution)/shard_map/lift/pallas_call | solution.py:382
  61.4 0.0 collective-permute-done.18.near_0_
  61.4 0.1 collective-permute-start.21
  61.5 0.6 collective-permute-start.23
  62.1 0.1 collective-permute-start.24
  62.1 0.4 collective-permute-start.25
  62.6 5.1 %own_block.1.own_att = bf16[256,512]{1,0:T(8,128)(2,1)S(1)} custom-call(s32[3]{0:T(128)S(1)} %pad_add_fusion.1.where_ref, bf16[8,256,64]{2,1,0:T(8,128)(2,1)S(1)} %get-tuple-element.51.query_ref, bf16[4,2,256,64]{3,2,1,0:T(8,128)(2,1)S(1)} %get-tuple-element.52.k_ref, bf16[4,2,80,256]{3,2,1,0:T(8,128)(2,1)S(1)} %get-tuple-element.53.v_ref), custom_call_target="tpu_custom_call" | custom-call | flops 3000000000 | bytes 4194304 | tf_op jit(solution)/shard_map/own_block/pallas_call | solution.py:403
  67.7 2.5 %collective-permute-done.21.mate_att = bf16[256,512]{1,0:T(8,128)(2,1)S(1)} collective-permute-done((bf16[256,512]{1,0:T(8,128)(2,1)S(1)}, bf16[256,512]{1,0:T(8,128)(2,1)S(1)}, u32[]{:S(2)}, u32[]{:S(2)}) %collective-permute-start.21) | collective-permute-done | bytes 262176 | tf_op jit(solution)/shard_map/ppermute | solution.py:339
  70.2 0.0 collective-permute-done.23.mate_near_0_
  70.2 2.4 %project_out.1 = (bf16[256,1024]{1,0:T(8,128)(2,1)}, f32[1,256]{1,0:T(1,128)}) custom-call(s32[3]{0:T(128)S(1)} %pad_add_fusion.1.where_ref, bf16[256,512]{1,0:T(8,128)(2,1)S(1)} %own_block.1.own_att, bf16[256,512]{1,0:T(8,128)(2,1)S(1)} %collective-permute-done.21.mate_att, bf16[128,1024]{1,0:T(8,128)(2,1)S(1)} %copy-done.4, ...), custom_call_target="tpu_custom_call" | custom-call | flops 1000000000 | bytes 4194304 | tf_op jit(solution)/shard_map/project_out/pallas_call | solution.py:406
  (30 shorter events, 0.1 us)
Async XLA Ops:
  0.6 14.3 %copy-start = (bf16[256,768]{1,0:T(8,128)(2,1)S(1)}, bf16[256,768]{1,0:T(8,128)(2,1)}, u32[]{:S(2)}) copy-start(bf16[256,768]{1,0:T(8,128)(2,1)} %bytes_ref.1) | copy-start | bytes 1179652
  0.6 15.7 %collective-permute-start = (bf16[384,1024]{1,0:T(8,128)(2,1)}, bf16[384,1024]{1,0:T(8,128)(2,1)S(1)}, u32[]{:S(2)}, u32[]{:S(2)}) collective-permute-start(bf16[384,1024]{1,0:T(8,128)(2,1)} %param.12), channel_id=1, source_target_pairs={{0,4},{4,0},{8,12},{12,8},{16,20},{20,16},{24,28},{28,24},{1,5},{5... | collective-permute-start | bytes 2359304 | tf_op jit(solution)/shard_map/ppermute | solution.py:336
  0.8 1.0 %copy-start.1 = (bf16[128,1536]{1,0:T(8,128)(2,1)S(1)}, bf16[128,1536]{1,0:T(8,128)(2,1)}, u32[]{:S(2)}) copy-start(bf16[128,1536]{1,0:T(8,128)(2,1)} %qkv_ref.1) | copy-start | bytes 1179652
  1.8 0.7 copy-start.2
  2.5 3.7 %copy-start.13 = (s32[1,1024]{1,0:T(1,128)S(1)}, s32[1,1024]{1,0:T(1,128)}, u32[]{:S(2)}) copy-start(s32[1,1024]{1,0:T(1,128)} %param.10) | copy-start | bytes 12292
  3.1 9.9 %collective-permute-start.7 = (bf16[128,768]{1,0:T(8,128)(2,1)S(1)}, bf16[128,768]{1,0:T(8,128)(2,1)S(1)}, u32[]{:S(2)}, u32[]{:S(2)}) collective-permute-start(bf16[128,768]{1,0:T(8,128)(2,1)S(1)} %get-tuple-element.43.own_w), channel_id=1, source_target_pairs={{0,8},{4,12},{8,0},{12,4},{16,24},{20,28},{24,16},{28,20},{1,9},{5... | collective-permute-start | bytes 589832 | tf_op jit(solution)/shard_map/ppermute | solution.py:336
  4.6 10.3 %collective-permute-start.8 = (bf16[128,768]{1,0:T(8,128)(2,1)S(1)}, bf16[128,768]{1,0:T(8,128)(2,1)S(1)}, u32[]{:S(2)}, u32[]{:S(2)}) collective-permute-start(bf16[128,768]{1,0:T(8,128)(2,1)S(1)} %get-tuple-element.43.own_w), channel_id=1, source_target_pairs={{0,16},{4,20},{8,24},{12,28},{16,0},{20,4},{24,8},{28,12},{1,17},{... | collective-permute-start | bytes 589832 | tf_op jit(solution)/shard_map/ppermute | solution.py:336
  6.2 3.6 %collective-permute-start.1 = (s32[1,1024]{1,0:T(1,128)S(1)}, s32[1,1024]{1,0:T(1,128)S(1)}, u32[]{:S(2)}, u32[]{:S(2)}) collective-permute-start(s32[1,1024]{1,0:T(1,128)S(1)} %copy-done.13), channel_id=1, source_target_pairs={{0,1},{1,0},{2,3},{3,2},{4,5},{5,4},{6,7},{7,6},{8,9},{9,8},{10,11... | collective-permute-start | bytes 12296 | tf_op jit(solution)/shard_map/ppermute | solution.py:339
  6.6 6.4 %collective-permute-start.2 = (s32[1,1024]{1,0:T(1,128)S(1)}, s32[1,1024]{1,0:T(1,128)S(1)}, u32[]{:S(2)}, u32[]{:S(2)}) collective-permute-start(s32[1,1024]{1,0:T(1,128)S(1)} %copy-done.13), channel_id=1, source_target_pairs={{0,2},{1,3},{4,6},{5,7},{8,10},{9,11},{12,14},{13,15},{16,18},{17,... | collective-permute-start | bytes 12296 | tf_op jit(solution)/shard_map/ppermute | solution.py:339
  9.8 14.5 %collective-permute-start.9 = (bf16[128,768]{1,0:T(8,128)(2,1)S(1)}, bf16[128,768]{1,0:T(8,128)(2,1)S(1)}, u32[]{:S(2)}, u32[]{:S(2)}) collective-permute-start(bf16[128,768]{1,0:T(8,128)(2,1)S(1)} %get-tuple-element.43.own_w), channel_id=1, source_target_pairs={{0,24},{4,28},{8,16},{12,20},{16,8},{20,12},{24,0},{28,4},{1,25},{... | collective-permute-start | bytes 589832 | tf_op jit(solution)/shard_map/ppermute | solution.py:336
  13.0 13.7 %collective-permute-start.10 = (bf16[128,768]{1,0:T(8,128)(2,1)S(1)}, bf16[128,768]{1,0:T(8,128)(2,1)S(1)}, u32[]{:S(2)}, u32[]{:S(2)}) collective-permute-start(bf16[128,768]{1,0:T(8,128)(2,1)S(1)} %get-tuple-element.43.own_w), channel_id=1, source_target_pairs={{0,4},{4,0},{8,12},{12,8},{16,20},{20,16},{24,28},{28,24},{1,5},{5... | collective-permute-start | bytes 589832 | tf_op jit(solution)/shard_map/ppermute | solution.py:336
  13.0 14.7 %collective-permute-start.11 = (bf16[128,768]{1,0:T(8,128)(2,1)S(1)}, bf16[128,768]{1,0:T(8,128)(2,1)S(1)}, u32[]{:S(2)}, u32[]{:S(2)}) collective-permute-start(bf16[128,768]{1,0:T(8,128)(2,1)S(1)} %collective-permute-done.7.near_w_0_), channel_id=1, source_target_pairs={{0,4},{4,0},{8,12},{12,8},{16,20},{20,16},{24,28},{28,24},{1,5},{5... | collective-permute-start | bytes 589832 | tf_op jit(solution)/shard_map/ppermute | solution.py:336
  14.9 13.4 %collective-permute-start.12 = (bf16[128,768]{1,0:T(8,128)(2,1)S(1)}, bf16[128,768]{1,0:T(8,128)(2,1)S(1)}, u32[]{:S(2)}, u32[]{:S(2)}) collective-permute-start(bf16[128,768]{1,0:T(8,128)(2,1)S(1)} %collective-permute-done.8.near_w_1_), channel_id=1, source_target_pairs={{0,4},{4,0},{8,12},{12,8},{16,20},{20,16},{24,28},{28,24},{1,5},{5... | collective-permute-start | bytes 589832 | tf_op jit(solution)/shard_map/ppermute | solution.py:336
  16.4 22.9 %copy-start.14 = (bf16[1024]{0:T(1024)(128)(2,1)S(1)}, bf16[1024]{0:T(1024)(128)(2,1)}, u32[]{:S(2)}) copy-start(bf16[1024]{0:T(1024)(128)(2,1)} %param.15) | copy-start | bytes 6148
  16.4 7.3 %collective-permute-start.3 = (s32[1,1024]{1,0:T(1,128)S(1)}, s32[1,1024]{1,0:T(1,128)S(1)}, u32[]{:S(2)}, u32[]{:S(2)}) collective-permute-start(s32[1,1024]{1,0:T(1,128)S(1)} %copy-done.13), channel_id=1, source_target_pairs={{0,3},{1,2},{4,7},{5,6},{8,11},{9,10},{12,15},{13,14},{16,19},{17,... | collective-permute-start | bytes 12296 | tf_op jit(solution)/shard_map/ppermute | solution.py:339
  23.7 9.2 %collective-permute-start.4 = (bf16[128,1024]{1,0:T(8,128)(2,1)S(1)}, bf16[128,1024]{1,0:T(8,128)(2,1)S(1)}, u32[]{:S(2)}, u32[]{:S(2)}) collective-permute-start(bf16[128,1024]{1,0:T(8,128)(2,1)S(1)} %tap_table.1.own_t), channel_id=1, source_target_pairs={{0,8},{4,12},{8,0},{12,4},{16,24},{20,28},{24,16},{28,20},{1,9},{5... | collective-permute-start | bytes 786440 | tf_op jit(solution)/shard_map/ppermute | solution.py:336
  24.2 12.9 %collective-permute-start.5 = (bf16[128,1024]{1,0:T(8,128)(2,1)S(1)}, bf16[128,1024]{1,0:T(8,128)(2,1)S(1)}, u32[]{:S(2)}, u32[]{:S(2)}) collective-permute-start(bf16[128,1024]{1,0:T(8,128)(2,1)S(1)} %tap_table.1.own_t), channel_id=1, source_target_pairs={{0,16},{4,20},{8,24},{12,28},{16,0},{20,4},{24,8},{28,12},{1,17},{... | collective-permute-start | bytes 786440 | tf_op jit(solution)/shard_map/ppermute | solution.py:336
  26.7 12.1 %collective-permute-start.6 = (bf16[128,1024]{1,0:T(8,128)(2,1)S(1)}, bf16[128,1024]{1,0:T(8,128)(2,1)S(1)}, u32[]{:S(2)}, u32[]{:S(2)}) collective-permute-start(bf16[128,1024]{1,0:T(8,128)(2,1)S(1)} %tap_table.1.own_t), channel_id=1, source_target_pairs={{0,24},{4,28},{8,16},{12,20},{16,8},{20,12},{24,0},{28,4},{1,25},{... | collective-permute-start | bytes 786440 | tf_op jit(solution)/shard_map/ppermute | solution.py:336
  27.7 0.7 copy-start.5
  28.3 10.4 %collective-permute-start.14 = (bf16[128,1024]{1,0:T(8,128)(2,1)S(1)}, bf16[128,1024]{1,0:T(8,128)(2,1)S(1)}, u32[]{:S(2)}, u32[]{:S(2)}) collective-permute-start(bf16[128,1024]{1,0:T(8,128)(2,1)S(1)} %tap_table.1.own_t), channel_id=1, source_target_pairs={{0,4},{4,0},{8,12},{12,8},{16,20},{20,16},{24,28},{28,24},{1,5},{5... | collective-permute-start | bytes 786440 | tf_op jit(solution)/shard_map/ppermute | solution.py:336
  28.4 0.7 copy-start.7
  29.0 1.6 %collective-permute-start.13 = (bf16[128,768]{1,0:T(8,128)(2,1)S(1)}, bf16[128,768]{1,0:T(8,128)(2,1)S(1)}, u32[]{:S(2)}, u32[]{:S(2)}) collective-permute-start(bf16[128,768]{1,0:T(8,128)(2,1)S(1)} %collective-permute-done.9.near_w_2_), channel_id=1, source_target_pairs={{0,4},{4,0},{8,12},{12,8},{16,20},{20,16},{24,28},{28,24},{1,5},{5... | collective-permute-start | bytes 589832 | tf_op jit(solution)/shard_map/ppermute | solution.py:336
  30.6 0.7 copy-start.9
  38.8 5.6 %collective-permute-start.15 = (bf16[128,1024]{1,0:T(8,128)(2,1)S(1)}, bf16[128,1024]{1,0:T(8,128)(2,1)S(1)}, u32[]{:S(2)}, u32[]{:S(2)}) collective-permute-start(bf16[128,1024]{1,0:T(8,128)(2,1)S(1)} %collective-permute-done.4.near_t_0_), channel_id=1, source_target_pairs={{0,4},{4,0},{8,12},{12,8},{16,20},{20,16},{24,28},{28,24},{1,5},{5... | collective-permute-start | bytes 786440 | tf_op jit(solution)/shard_map/ppermute | solution.py:336
  38.8 6.7 %collective-permute-start.16 = (bf16[128,1024]{1,0:T(8,128)(2,1)S(1)}, bf16[128,1024]{1,0:T(8,128)(2,1)S(1)}, u32[]{:S(2)}, u32[]{:S(2)}) collective-permute-start(bf16[128,1024]{1,0:T(8,128)(2,1)S(1)} %collective-permute-done.5.near_t_1_), channel_id=1, source_target_pairs={{0,4},{4,0},{8,12},{12,8},{16,20},{20,16},{24,28},{28,24},{1,5},{5... | collective-permute-start | bytes 786440 | tf_op jit(solution)/shard_map/ppermute | solution.py:336
  39.3 6.2 %collective-permute-start.17 = (bf16[128,1024]{1,0:T(8,128)(2,1)S(1)}, bf16[128,1024]{1,0:T(8,128)(2,1)S(1)}, u32[]{:S(2)}, u32[]{:S(2)}) collective-permute-start(bf16[128,1024]{1,0:T(8,128)(2,1)S(1)} %collective-permute-done.6.near_t_2_), channel_id=1, source_target_pairs={{0,4},{4,0},{8,12},{12,8},{16,20},{20,16},{24,28},{28,24},{1,5},{5... | collective-permute-start | bytes 786440 | tf_op jit(solution)/shard_map/ppermute | solution.py:336
  40.7 1.3 %copy-start.4 = (bf16[128,1024]{1,0:T(8,128)(2,1)S(1)}, bf16[128,1024]{1,0:T(8,128)(2,1)}, u32[]{:S(2)}) copy-start(bf16[128,1024]{1,0:T(8,128)(2,1)} %own) | copy-start | bytes 786436
  42.0 19.4 %collective-permute-start.18 = (bf16[128,1024]{1,0:T(8,128)(2,1)S(1)}, bf16[128,1024]{1,0:T(8,128)(2,1)S(1)}, u32[]{:S(2)}, u32[]{:S(2)}) collective-permute-start(bf16[128,1024]{1,0:T(8,128)(2,1)S(1)} %copy-done.4), channel_id=1, source_target_pairs={{0,8},{4,12},{8,0},{12,4},{16,24},{20,28},{24,16},{28,20},{1,9},{5... | collective-permute-start | bytes 786440 | tf_op jit(solution)/shard_map/ppermute | solution.py:336
  42.6 18.8 %collective-permute-start.19 = (bf16[128,1024]{1,0:T(8,128)(2,1)S(1)}, bf16[128,1024]{1,0:T(8,128)(2,1)S(1)}, u32[]{:S(2)}, u32[]{:S(2)}) collective-permute-start(bf16[128,1024]{1,0:T(8,128)(2,1)S(1)} %copy-done.4), channel_id=1, source_target_pairs={{0,16},{4,20},{8,24},{12,28},{16,0},{20,4},{24,8},{28,12},{1,17},{... | collective-permute-start | bytes 786440 | tf_op jit(solution)/shard_map/ppermute | solution.py:336
  44.4 17.0 %collective-permute-start.20 = (bf16[128,1024]{1,0:T(8,128)(2,1)S(1)}, bf16[128,1024]{1,0:T(8,128)(2,1)S(1)}, u32[]{:S(2)}, u32[]{:S(2)}) collective-permute-start(bf16[128,1024]{1,0:T(8,128)(2,1)S(1)} %copy-done.4), channel_id=1, source_target_pairs={{0,24},{4,28},{8,16},{12,20},{16,8},{20,12},{24,0},{28,4},{1,25},{... | collective-permute-start | bytes 786440 | tf_op jit(solution)/shard_map/ppermute | solution.py:336
  45.5 22.1 %collective-permute-start.22 = (bf16[128,1024]{1,0:T(8,128)(2,1)S(1)}, bf16[128,1024]{1,0:T(8,128)(2,1)S(1)}, u32[]{:S(2)}, u32[]{:S(2)}) collective-permute-start(bf16[128,1024]{1,0:T(8,128)(2,1)S(1)} %copy-done.4), channel_id=1, source_target_pairs={{0,4},{4,0},{8,12},{12,8},{16,20},{20,16},{24,28},{28,24},{1,5},{5... | collective-permute-start | bytes 786440 | tf_op jit(solution)/shard_map/ppermute | solution.py:336
  45.5 0.9 %copy-start.6 = (bf16[128,768]{1,0:T(8,128)(2,1)S(1)}, bf16[128,768]{1,0:T(8,128)(2,1)}, u32[]{:S(2)}) copy-start(bf16[128,768]{1,0:T(8,128)(2,1)} %copy-done.5) | copy-start | bytes 589828
  46.5 0.9 %copy-start.8 = (bf16[128,768]{1,0:T(8,128)(2,1)S(1)}, bf16[128,768]{1,0:T(8,128)(2,1)}, u32[]{:S(2)}) copy-start(bf16[128,768]{1,0:T(8,128)(2,1)} %copy-done.7) | copy-start | bytes 589828
  47.4 0.9 %copy-start.10 = (bf16[128,768]{1,0:T(8,128)(2,1)S(1)}, bf16[128,768]{1,0:T(8,128)(2,1)}, u32[]{:S(2)}) copy-start(bf16[128,768]{1,0:T(8,128)(2,1)} %copy-done.9) | copy-start | bytes 589828
  48.3 1.0 %copy-start.11 = (f32[4,256,128]{2,1,0:T(8,128)S(1)}, f32[4,256,128]{2,1,0:T(8,128)}, u32[]{:S(2)}) copy-start(f32[4,256,128]{2,1,0:T(8,128)} %constant.46.clone.cos_ref) | copy-start | bytes 1572868
  49.3 1.0 %copy-start.12 = (f32[4,256,128]{2,1,0:T(8,128)S(1)}, f32[4,256,128]{2,1,0:T(8,128)}, u32[]{:S(2)}) copy-start(f32[4,256,128]{2,1,0:T(8,128)} %constant.47.clone.sin_ref) | copy-start | bytes 1572868
  61.4 8.8 %collective-permute-start.21 = (bf16[256,512]{1,0:T(8,128)(2,1)S(1)}, bf16[256,512]{1,0:T(8,128)(2,1)S(1)}, u32[]{:S(2)}, u32[]{:S(2)}) collective-permute-start(bf16[256,512]{1,0:T(8,128)(2,1)S(1)} %get-tuple-element.56), channel_id=1, source_target_pairs={{0,1},{1,0},{2,3},{3,2},{4,5},{5,4},{6,7},{7,6},{8,9},{9,8},{10,11... | collective-permute-start | bytes 786440 | tf_op jit(solution)/shard_map/ppermute | solution.py:339
  61.5 8.7 %collective-permute-start.23 = (bf16[128,1024]{1,0:T(8,128)(2,1)S(1)}, bf16[128,1024]{1,0:T(8,128)(2,1)S(1)}, u32[]{:S(2)}, u32[]{:S(2)}) collective-permute-start(bf16[128,1024]{1,0:T(8,128)(2,1)S(1)} %collective-permute-done.18.near_0_), channel_id=1, source_target_pairs={{0,4},{4,0},{8,12},{12,8},{16,20},{20,16},{24,28},{28,24},{1,5},{5... | collective-permute-start | bytes 786440 | tf_op jit(solution)/shard_map/ppermute | solution.py:336
  62.1 8.1 %collective-permute-start.24 = (bf16[128,1024]{1,0:T(8,128)(2,1)S(1)}, bf16[128,1024]{1,0:T(8,128)(2,1)S(1)}, u32[]{:S(2)}, u32[]{:S(2)}) collective-permute-start(bf16[128,1024]{1,0:T(8,128)(2,1)S(1)} %collective-permute-done.19.near_1_), channel_id=1, source_target_pairs={{0,4},{4,0},{8,12},{12,8},{16,20},{20,16},{24,28},{28,24},{1,5},{5... | collective-permute-start | bytes 786440 | tf_op jit(solution)/shard_map/ppermute | solution.py:336
  62.1 8.1 %collective-permute-start.25 = (bf16[128,1024]{1,0:T(8,128)(2,1)S(1)}, bf16[128,1024]{1,0:T(8,128)(2,1)S(1)}, u32[]{:S(2)}, u32[]{:S(2)}) collective-permute-start(bf16[128,1024]{1,0:T(8,128)(2,1)S(1)} %collective-permute-done.20.near_2_), channel_id=1, source_target_pairs={{0,4},{4,0},{8,12},{12,8},{16,20},{20,16},{24,28},{28,24},{1,5},{5... | collective-permute-start | bytes 786440 | tf_op jit(solution)/shard_map/ppermute | solution.py:336
  62.6 7.6 %copy-start.3 = (bf16[1,256,1024]{2,1,0:T(8,128)(2,1)S(1)}, bf16[1,256,1024]{2,1,0:T(8,128)(2,1)}, u32[]{:S(2)}) copy-start(bf16[1,256,1024]{2,1,0:T(8,128)(2,1)} %param.16) | copy-start | bytes 1572868

commit v3 on v2

--- a/solution.py
+++ b/solution.py
@@ -131,8 +131,7 @@
     return x * cos + swapped * sin
 
 
-def part_kernel(where_ref, qkv_ref, align_ref, part_ref, align_out):
-    align_out[...] = align_ref[...]
+def part_kernel(where_ref, qkv_ref, part_ref):
     side = where_ref[2] % 2
     start = 0
     for width in (HQ * HD, HK * HD, HK * HD):
@@ -143,7 +142,8 @@
         start += width
 
 
-def table_kernel(where_ref, bytes_ref, conv_ref, total_ref, out_ref):
+def table_kernel(where_ref, bytes_ref, conv_ref, total_ref, part_ref, align_ref, out_ref, both_ref, align_out):
+    align_out[...] = align_ref[...]
     core = where_ref[1]
     taps_in = conv_ref.shape[0]
     half = total_ref.shape[0]
@@ -151,6 +151,8 @@
     mates = bytes_ref[rows, pl.ds(pl.multiple_of((1 - core) * taps_in, taps_in), taps_in)]
     total = total_ref[...] + jnp.dot(mates, conv_ref[...], preferred_element_type=jnp.float32)
     out_ref[...] = total.astype(jnp.bfloat16)
+    both_ref[:, : total.shape[1]] = total.astype(jnp.bfloat16)
+    both_ref[:, total.shape[1] :] = part_ref[...]
 
 
 def ordered(chip, core, pieces):
@@ -202,7 +204,7 @@
 
 
 def lift_kernel(
-    where_ref, ids_ref, own_t, near_t, mate_own_t, mate_near_t, own_w, near_w, mate_own_w, mate_near_w,
+    where_ref, ids_refs, own_t, near_t, mate_own_t, mate_near_t, own_w, near_w, mate_own_w, mate_near_w,
     gain_ref, cos_ref, sin_ref, att_ref, query_ref, k_s, v_s, lat_ref,
     table_s, weight_s, ids_s, lat_s, q_s,
 ):
@@ -211,11 +213,15 @@
     rows, features = lat_ref.shape
     q_width, k_width = HQ * HD // 2, HK * HD // 2
     for span, piece in ordered(chip, core, (own_t, near_t, mate_own_t, mate_near_t)):
-        table_s[span, :] = piece[...]
+        table_s[span, :] = piece[:, :features]
+    near_w, mate_near_w = near_w + (near_t[-1],), mate_near_w + (mate_near_t[-1],)
     for span, piece in ordered(chip, core, (own_w, near_w, mate_own_w, mate_near_w)):
-        weight_s[span, :] = piece[...]
-    for place, slot in enumerate((2 + side, 3 - side, side, 1 - side)):
-        ids_s[slot] = ids_ref[place]
+        weight_s[span, :] = piece[:, -weight_s.shape[1] :]
+    own_ids, pair_ids, past_ids, cross_ids = ids_refs
+    ids_s[side] = past_ids[...]
+    ids_s[1 - side] = cross_ids[...]
+    ids_s[2 + side] = own_ids[...]
+    ids_s[3 - side] = pair_ids[...]
     gain = gain_ref[...].astype(jnp.float32)
     v_s[:, :, HD:, :] = jnp.ones(v_s.shape[:2] + (v_s.shape[2] - HD, rows), jnp.bfloat16)
 
@@ -347,31 +353,32 @@
     beside = [(z, z ^ 1) for z in range(n_ctx)]
 
     mate_conv = swap(w_conv, 1)
-    part, align = call(
-        part_kernel, "qkv_part", 4, 10**8, [SMEM, VMEM, VMEM],
-        [((w_qkv.shape[0], part_width), bf16), (align.shape, jnp.int32)],
-    )(where, w_qkv, align)
-    near_w = to_near(part)
+    (part,) = call(
+        part_kernel, "qkv_part", 4, 10**8, [SMEM, VMEM], [((w_qkv.shape[0], part_width), bf16)]
+    )(where, w_qkv)
+    near_w = tuple(swap(part, 2 * j) for j in (1, 2))
 
     taps_in = w_conv.shape[0]
     mine = lax.dynamic_slice(byte_table, (core * half, core * taps_in), (half, taps_in))
     total = jnp.dot(mine, w_conv, preferred_element_type=f32)
-    (own_t,) = call(
-        table_kernel, "tap_table", 8, 10**8, [SMEM, VMEM, VMEM, VMEM], [((half, features), bf16)]
-    )(where, byte_table, mate_conv, total)
+    own_t, both, align = call(
+        table_kernel, "tap_table", 8, 10**8, [SMEM] + [VMEM] * 5,
+        [((half, features), bf16), ((half, features + part_width), bf16), (align.shape, jnp.int32)],
+    )(where, byte_table, mate_conv, total, part, align)
+    (own_t, both), near_w = lax.optimization_barrier(((own_t, both), near_w))
+    near_t = (swap(own_t, 2), swap(own_t, 4), swap(both, 6))
+    ids = jnp.transpose(byte_ids[0].reshape(rows, KW))
+    ids = jnp.pad(ids, ((0, 8 - KW), (0, 0)))
+    ids, unused = lax.optimization_barrier((ids, own_t))
     ids_all = (
-        byte_ids,
-        along(byte_ids, beside),
-        along(byte_ids, [(0, 2), (1, 3)]),
-        along(byte_ids, [(0, 3), (1, 2)]),
-    )
-    own_t, ids_all = lax.optimization_barrier((own_t, ids_all))
-    near_t = to_near(own_t)
-    ids_all = jnp.concatenate(ids_all, axis=0).reshape(4, rows, KW)
-    ids_all = jnp.pad(jnp.swapaxes(ids_all, 1, 2), ((0, 0), (0, 8 - KW), (0, 0)))
-    w_pieces, mate_own_t = to_mate(part, near_w), swap(own_t, 1)
-    near_t, w_pieces, mate_own_t = lax.optimization_barrier((near_t, w_pieces, mate_own_t))
-    t_pieces = (own_t, near_t, mate_own_t, tuple(swap(piece, 1) for piece in near_t))
+        ids,
+        along(ids, beside),
+        along(ids, [(0, 2), (1, 3)]),
+        along(ids, [(0, 3), (1, 2)]),
+    )
+    last, ids_all = lax.optimization_barrier((near_t[-1], ids_all))
+    near_t = near_t[:-1] + (last,)
+    t_pieces, w_pieces = to_mate(own_t, near_t), to_mate(part, near_w)
     out_own, unused = lax.optimization_barrier((w_out, near_t))
     out_near = to_near(out_own)
 
@@ -380,8 +387,8 @@
     piece_specs = [VMEM, near_specs, VMEM, near_specs]
     att_shape = ((rows, q_width), bf16)
     att_mate, query, keys, values, latent = call(
-        lift_kernel, "lift", 28, 5 * 10**9,
-        [SMEM, VMEM] + piece_specs + piece_specs + [VMEM, VMEM, VMEM],
+        lift_kernel, "lift", 18, 5 * 10**9,
+        [SMEM, (VMEM,) * 4] + piece_specs + [VMEM, (VMEM,) * 2] * 2 + [VMEM, VMEM, VMEM],
         [
             att_shape,
             ((HQ // 2, rows, HD), bf16),
@@ -401,10 +408,10 @@
     att_mate, out_near = lax.optimization_barrier((att_mate, out_near))
     att_back = along(att_mate, beside)
     (att_own,) = call(
-        own_kernel, "own_block", 16, 3 * 10**9, [SMEM, VMEM, VMEM, VMEM], [att_shape]
+        own_kernel, "own_block", 12, 3 * 10**9, [SMEM, VMEM, VMEM, VMEM], [att_shape]
     )(where, query, keys, values)
     hidden, loss = call(
-        out_kernel, "project_out", 16, 10**9,
+        out_kernel, "project_out", 12, 10**9,
         [SMEM, VMEM, VMEM] + piece_specs + [VMEM, VMEM, VMEM],
         [((rows, features), bf16), ((1, rows), f32)],
         [((rows, features), bf16), ((features, features), bf16)],

time: 73.1 us -> 59.3 us (0.81)
  local copies, waits for them, and re-layouts: 11.2 us -> 2.79 us
  waiting for transfers between devices: 22.3 us -> 16.4 us
    unnamed x30 -> x19, local copies, waits for them, and re-layouts: 8.58 us -> 2.58 us
    ppermute x22 -> x20, waiting for transfers between devices: 9.99 us -> 6.68 us  [swap(): return lax.ppermute(x, 'fsdp', [(d, d ^ j) for d in range(n_fsdp)])]
    reshape x2 -> x0, local copies, waits for them, and re-layouts: 2.61 us -> none  [head_body(): ids_all = jnp.concatenate(ids_all, axis=0).reshape(4, rows, KW)]
    ppermute x4, waiting for transfers between devices: 12.3 us -> 9.69 us  [along(): return lax.ppermute(x, 'ctx', pairs)]
    ppermute x22 -> x20, starting transfers between devices: 13.8 us -> 12 us  [swap(): return lax.ppermute(x, 'fsdp', [(d, d ^ j) for d in range(n_fsdp)])]
    ppermute x4, starting transfers between devices: 3.09 us -> 4.3 us  [along(): return lax.ppermute(x, 'ctx', pairs)]
  transfers between devices with their start and end apart: 26 -> 24, of which waited for: 9 -> 8; matrix products, arithmetic and copies ran while one was open for 6% -> 5% of each run, Pallas kernels for 24% -> 30%
where the time goes in v3:
time: 59.3 us; the launch traced here: 58.4 us
  Pallas kernels  19.9 us (34%)
  waiting for transfers between devices  16.4 us (28%)
  starting transfers between devices  16.3 us (27%)
  local copies, waits for them, and re-layouts  2.79 us (5%)
  matrix products  1.45 us (2%)
  between operations  0.87 us (1%)
  other arithmetic  0.74 us (1%)
    ppermute x20, starting transfers between devices, swap(): return lax.ppermute(x, 'fsdp', [(d, d ^ j) for d in range(n_fsdp)])  12 us
    pallas_call x1, Pallas kernels, head_body(): call(lift_kernel, 'lift', 18, 5 * 10 ** 9, [SMEM, (VMEM,) * 4] + piece_sp...  11 us
    ppermute x4, waiting for transfers between devices, along(): return lax.ppermute(x, 'ctx', pairs)  9.69 us
    ppermute x20, waiting for transfers between devices, swap(): return lax.ppermute(x, 'fsdp', [(d, d ^ j) for d in range(n_fsdp)])  6.68 us
    pallas_call x1, Pallas kernels, head_body(): call(own_kernel, 'own_block', 12, 3 * 10 ** 9, [SMEM, VMEM, VMEM, VMEM],...  5.06 us
    ppermute x4, starting transfers between devices, along(): return lax.ppermute(x, 'ctx', pairs)  4.3 us
    unnamed x19, local copies, waits for them, and re-layouts  2.58 us
    pallas_call x1, Pallas kernels, head_body(): call(out_kernel, 'project_out', 12, 10 ** 9, [SMEM, VMEM, VMEM] + piece_s...  2.44 us
  transfers between devices with their start and end apart: 24, of which 8 were waited for; matrix products, arithmetic and copies ran while one was open for 5% of the time, Pallas kernels for 30%

profile of v3, /device:TPU:24, one launch (start us, length us, event | category | flops | bytes accessed | tf_op | source)
XLA Modules:
  0.0 58.4 jit_solution(1830365575522445805)
XLA Ops:
  0.6 0.1 collective-permute-start
  0.7 0.1 pad_add_fusion.where_ref
  0.8 1.0 %copy-done.1 = bf16[128,1536]{1,0:T(8,128)(2,1)S(1)} copy-done((bf16[128,1536]{1,0:T(8,128)(2,1)S(1)}, bf16[128,1536]{1,0:T(8,128)(2,1)}, u32[]{:S(2)}) %copy-start.1) | copy-done | bytes 393240
  1.8 0.6 qkv_part.1.part_ref.own_w
  2.4 1.6 %collective-permute-start.1 = (bf16[128,768]{1,0:T(8,128)(2,1)S(1)}, bf16[128,768]{1,0:T(8,128)(2,1)S(1)}, u32[]{:S(2)}, u32[]{:S(2)}) collective-permute-start(bf16[128,768]{1,0:T(8,128)(2,1)S(1)} %qkv_part.1.part_ref.own_w), channel_id=1, source_target_pairs={{0,8},{4,12},{8,0},{12,4},{16,24},{20,28},{24,16},{28,20},{1,9},{5... | collective-permute-start | bytes 589832 | tf_op jit(solution)/shard_map/ppermute | solution.py:342
  3.9 1.5 %collective-permute-start.2 = (bf16[128,768]{1,0:T(8,128)(2,1)S(1)}, bf16[128,768]{1,0:T(8,128)(2,1)S(1)}, u32[]{:S(2)}, u32[]{:S(2)}) collective-permute-start(bf16[128,768]{1,0:T(8,128)(2,1)S(1)} %qkv_part.1.part_ref.own_w), channel_id=1, source_target_pairs={{0,16},{4,20},{8,24},{12,28},{16,0},{20,4},{24,8},{28,12},{1,17},{... | collective-permute-start | bytes 589832 | tf_op jit(solution)/shard_map/ppermute | solution.py:342
  5.5 1.4 %fusion.total_ref = f32[128,1024]{1,0:T(8,128)S(1)} fusion(bf16[384,1024]{1,0:T(8,128)(2,1)} %param.12, bf16[256,768]{1,0:T(8,128)(2,1)S(1)} %copy-done, s32[]{:T(128)S(6)} %select_n.19, s32[]{:T(128)S(6)} %select_n.20), kind=kOutput, calls=%fused_computation | convolution fusion | flops 100663296 | bytes 1409032 | tf_op jit(solution)/shard_map/dot_general | solution.py:363
  6.9 0.0 copy-start.5
  6.9 0.0 collective-permute-done.conv_ref
  7.0 0.0 copy-start.7
  7.0 0.9 %tap_table.1 = (bf16[128,1024]{1,0:T(8,128)(2,1)S(1)}, bf16[128,1792]{1,0:T(8,128)(2,1)S(1)}, s32[1,256]{1,0:T(1,128)S(1)}) custom-call(s32[3]{0:T(128)S(1)} %pad_add_fusion.where_ref, bf16[256,768]{1,0:T(8,128)(2,1)S(1)} %copy-done, bf16[384,1024]{1,0:T(8,128)(2,1)S(1)} %collective-permute-done.conv_ref, f32[128,1024]{1,0:T(8,128)S(1)} %fusion.total_ref, ...), custom_call_target="tpu_custom_call" | custom-call | flops 100000000 | bytes 4194304 | tf_op jit(solution)/shard_map/tap_table/pallas_call | solution.py:364
  7.8 0.0 copy-start.4
  7.8 1.9 %collective-permute-done.1.near_w_0_ = bf16[128,768]{1,0:T(8,128)(2,1)S(1)} collective-permute-done((bf16[128,768]{1,0:T(8,128)(2,1)S(1)}, bf16[128,768]{1,0:T(8,128)(2,1)S(1)}, u32[]{:S(2)}, u32[]{:S(2)}) %collective-permute-start.1) | collective-permute-done | bytes 196640 | tf_op jit(solution)/shard_map/ppermute | solution.py:342
  9.7 1.2 %collective-permute-done.2.near_w_1_ = bf16[128,768]{1,0:T(8,128)(2,1)S(1)} collective-permute-done((bf16[128,768]{1,0:T(8,128)(2,1)S(1)}, bf16[128,768]{1,0:T(8,128)(2,1)S(1)}, u32[]{:S(2)}, u32[]{:S(2)}) %collective-permute-start.2) | collective-permute-done | bytes 196640 | tf_op jit(solution)/shard_map/ppermute | solution.py:342
  10.9 1.5 %collective-permute-start.3 = (bf16[128,1792]{1,0:T(8,128)(2,1)S(1)}, bf16[128,1792]{1,0:T(8,128)(2,1)S(1)}, u32[]{:S(2)}, u32[]{:S(2)}) collective-permute-start(bf16[128,1792]{1,0:T(8,128)(2,1)S(1)} %get-tuple-element.29), channel_id=1, source_target_pairs={{0,24},{4,28},{8,16},{12,20},{16,8},{20,12},{24,0},{28,4},{1,25},{... | collective-permute-start | bytes 1376264 | tf_op jit(solution)/shard_map/ppermute | solution.py:342
  12.4 1.5 %collective-permute-start.7 = (bf16[128,1024]{1,0:T(8,128)(2,1)S(1)}, bf16[128,1024]{1,0:T(8,128)(2,1)S(1)}, u32[]{:S(2)}, u32[]{:S(2)}) collective-permute-start(bf16[128,1024]{1,0:T(8,128)(2,1)S(1)} %get-tuple-element.30.own_t), channel_id=1, source_target_pairs={{0,8},{4,12},{8,0},{12,4},{16,24},{20,28},{24,16},{28,20},{1,9},{5... | collective-permute-start | bytes 786440 | tf_op jit(solution)/shard_map/ppermute | solution.py:342
  13.9 0.5 collective-permute-start.8
  14.4 0.5 broadcast.7
  15.0 0.7 %reduce.3 = s32[1024]{0:T(1024)S(1)} reduce(s32[1,1024]{1,0:T(1,128)S(1)} %copy-done.7, s32[]{:T(128)} %broadcast.7), dimensions={0}, to_apply=%param.10.reduce_sub_computation.3 | reduce | bytes 8196 | tf_op args[0]
  15.6 0.1 reshape_squeeze.3
  15.8 0.1 copy.12
  15.8 0.5 collective-permute-start.4
  16.4 1.3 %collective-permute-start.5 = (s32[8,256]{1,0:T(8,128)S(1)}, s32[8,256]{1,0:T(8,128)S(1)}, u32[]{:S(2)}, u32[]{:S(2)}) collective-permute-start(s32[8,256]{1,0:T(8,128)S(1)} %pad.4.ids_refs_0_), channel_id=1, source_target_pairs={{0,2},{1,3},{4,6},{5,7},{8,10},{9,11},{12,14},{13,15},{16,18},{17,... | collective-permute-start | bytes 24584 | tf_op jit(solution)/shard_map/ppermute | solution.py:345
  17.6 1.9 %collective-permute-done.4.ids_refs_1_ = s32[8,256]{1,0:T(8,128)S(1)} collective-permute-done((s32[8,256]{1,0:T(8,128)S(1)}, s32[8,256]{1,0:T(8,128)S(1)}, u32[]{:S(2)}, u32[]{:S(2)}) %collective-permute-start.4) | collective-permute-done | bytes 8224 | tf_op jit(solution)/shard_map/ppermute | solution.py:345
  19.6 1.3 %collective-permute-start.6 = (s32[8,256]{1,0:T(8,128)S(1)}, s32[8,256]{1,0:T(8,128)S(1)}, u32[]{:S(2)}, u32[]{:S(2)}) collective-permute-start(s32[8,256]{1,0:T(8,128)S(1)} %pad.4.ids_refs_0_), channel_id=1, source_target_pairs={{0,3},{1,2},{4,7},{5,6},{8,11},{9,10},{12,15},{13,14},{16,19},{17,... | collective-permute-start | bytes 24584 | tf_op jit(solution)/shard_map/ppermute | solution.py:345
  20.9 1.9 %collective-permute-done.5.ids_refs_2_ = s32[8,256]{1,0:T(8,128)S(1)} collective-permute-done((s32[8,256]{1,0:T(8,128)S(1)}, s32[8,256]{1,0:T(8,128)S(1)}, u32[]{:S(2)}, u32[]{:S(2)}) %collective-permute-start.5) | collective-permute-done | bytes 8224 | tf_op jit(solution)/shard_map/ppermute | solution.py:345
  22.8 0.0 collective-permute-start.13
  22.8 4.1 %collective-permute-done.6.ids_refs_3_ = s32[8,256]{1,0:T(8,128)S(1)} collective-permute-done((s32[8,256]{1,0:T(8,128)S(1)}, s32[8,256]{1,0:T(8,128)S(1)}, u32[]{:S(2)}, u32[]{:S(2)}) %collective-permute-start.6) | collective-permute-done | bytes 8224 | tf_op jit(solution)/shard_map/ppermute | solution.py:345
  26.9 0.0 collective-permute-done.3.near_t_2_
  26.9 0.0 collective-permute-start.12
  26.9 0.5 collective-permute-start.14
  27.4 0.0 collective-permute-done.13.mate_own_w
  27.4 0.0 collective-permute-start.9
  27.4 1.9 %collective-permute-done.7.near_t_0_ = bf16[128,1024]{1,0:T(8,128)(2,1)S(1)} collective-permute-done((bf16[128,1024]{1,0:T(8,128)(2,1)S(1)}, bf16[128,1024]{1,0:T(8,128)(2,1)S(1)}, u32[]{:S(2)}, u32[]{:S(2)}) %collective-permute-start.7) | collective-permute-done | bytes 262176 | tf_op jit(solution)/shard_map/ppermute | solution.py:342
  29.4 0.0 collective-permute-start.10
  29.4 0.0 collective-permute-done.8.near_t_1_
  29.4 0.5 collective-permute-start.11
  29.9 0.0 collective-permute-done.14.mate_near_w_0_
  29.9 0.1 collective-permute-start.15
  30.0 1.6 %collective-permute-done.15.mate_near_w_1_ = bf16[128,768]{1,0:T(8,128)(2,1)S(1)} collective-permute-done((bf16[128,768]{1,0:T(8,128)(2,1)S(1)}, bf16[128,768]{1,0:T(8,128)(2,1)S(1)}, u32[]{:S(2)}, u32[]{:S(2)}) %collective-permute-start.15) | collective-permute-done | bytes 196640 | tf_op jit(solution)/shard_map/ppermute | solution.py:342
  31.6 0.6 %collective-permute-start.16 = (bf16[128,1024]{1,0:T(8,128)(2,1)S(1)}, bf16[128,1024]{1,0:T(8,128)(2,1)S(1)}, u32[]{:S(2)}, u32[]{:S(2)}) collective-permute-start(bf16[128,1024]{1,0:T(8,128)(2,1)S(1)} %copy-done.4), channel_id=1, source_target_pairs={{0,8},{4,12},{8,0},{12,4},{16,24},{20,28},{24,16},{28,20},{1,9},{5... | collective-permute-start | bytes 786440 | tf_op jit(solution)/shard_map/ppermute | solution.py:342
  32.2 0.0 collective-permute-done.9.mate_own_t
  32.2 1.0 %collective-permute-start.17 = (bf16[128,1024]{1,0:T(8,128)(2,1)S(1)}, bf16[128,1024]{1,0:T(8,128)(2,1)S(1)}, u32[]{:S(2)}, u32[]{:S(2)}) collective-permute-start(bf16[128,1024]{1,0:T(8,128)(2,1)S(1)} %copy-done.4), channel_id=1, source_target_pairs={{0,16},{4,20},{8,24},{12,28},{16,0},{20,4},{24,8},{28,12},{1,17},{... | collective-permute-start | bytes 786440 | tf_op jit(solution)/shard_map/ppermute | solution.py:342
  33.2 0.0 collective-permute-done.10.mate_near_t_0_
  33.2 1.8 %collective-permute-start.18 = (bf16[128,1024]{1,0:T(8,128)(2,1)S(1)}, bf16[128,1024]{1,0:T(8,128)(2,1)S(1)}, u32[]{:S(2)}, u32[]{:S(2)}) collective-permute-start(bf16[128,1024]{1,0:T(8,128)(2,1)S(1)} %copy-done.4), channel_id=1, source_target_pairs={{0,24},{4,28},{8,16},{12,20},{16,8},{20,12},{24,0},{28,4},{1,25},{... | collective-permute-start | bytes 786440 | tf_op jit(solution)/shard_map/ppermute | solution.py:342
  35.1 0.0 collective-permute-done.11.mate_near_t_1_
  35.1 0.0 collective-permute-start.20
  35.1 0.0 collective-permute-done.12.mate_near_t_2_
  35.1 0.0 copy-start.6
  35.1 1.0 %copy-done.6 = f32[4,256,128]{2,1,0:T(8,128)S(1)} copy-done((f32[4,256,128]{2,1,0:T(8,128)S(1)}, f32[4,256,128]{2,1,0:T(8,128)}, u32[]{:S(2)}) %copy-start.6) | copy-done | bytes 524312
  36.1 11.0 %lift.1 = (bf16[256,512]{1,0:T(8,128)(2,1)S(1)}, bf16[8,256,64]{2,1,0:T(8,128)(2,1)S(1)}, bf16[4,2,256,64]{3,2,1,0:T(8,128)(2,1)S(1)}, bf16[4,2,80,256]{3,2,1,0:T(8,128)(2,1)S(1)}, bf16[256,1024]{1,0:T(8,128)(2,1)S(1)}) custom-call(s32[3]{0:T(128)S(1)} %pad_add_fusion.where_ref, s32[8,256]{1,0:T(8,128)S(1)} %pad.4.ids_refs_0_, ...), custom_call_target="tpu_custom_call" | custom-call | flops 5000000000 | bytes 4194304 | tf_op jit(solution)/shard_map/lift/pallas_call | solution.py:389
  47.1 0.0 collective-permute-done.16.near_0_
  47.1 0.0 collective-permute-done.17.near_1_
  47.1 0.0 collective-permute-done.18.near_2_
  47.1 1.2 %collective-permute-start.19 = (bf16[256,512]{1,0:T(8,128)(2,1)S(1)}, bf16[256,512]{1,0:T(8,128)(2,1)S(1)}, u32[]{:S(2)}, u32[]{:S(2)}) collective-permute-start(bf16[256,512]{1,0:T(8,128)(2,1)S(1)} %get-tuple-element.44), channel_id=1, source_target_pairs={{0,1},{1,0},{2,3},{3,2},{4,5},{5,4},{6,7},{7,6},{8,9},{9,8},{10,11... | collective-permute-start | bytes 786440 | tf_op jit(solution)/shard_map/ppermute | solution.py:345
  48.4 0.2 collective-permute-start.21
  48.6 0.3 collective-permute-start.22
  48.9 0.2 collective-permute-start.23
  49.1 5.1 %own_block.1.own_att = bf16[256,512]{1,0:T(8,128)(2,1)S(1)} custom-call(s32[3]{0:T(128)S(1)} %pad_add_fusion.where_ref, bf16[8,256,64]{2,1,0:T(8,128)(2,1)S(1)} %get-tuple-element.39.query_ref, bf16[4,2,256,64]{3,2,1,0:T(8,128)(2,1)S(1)} %get-tuple-element.40.k_ref, bf16[4,2,80,256]{3,2,1,0:T(8,128)(2,1)S(1)} %get-tuple-element.41.v_ref), custom_call_target="tpu_custom_call" | custom-call | flops 3000000000 | bytes 4194304 | tf_op jit(solution)/shard_map/own_block/pallas_call | solution.py:410
  54.2 0.0 collective-permute-done.20.mate_own
  54.2 1.7 %collective-permute-done.19.mate_att = bf16[256,512]{1,0:T(8,128)(2,1)S(1)} collective-permute-done((bf16[256,512]{1,0:T(8,128)(2,1)S(1)}, bf16[256,512]{1,0:T(8,128)(2,1)S(1)}, u32[]{:S(2)}, u32[]{:S(2)}) %collective-permute-start.19) | collective-permute-done | bytes 262176 | tf_op jit(solution)/shard_map/ppermute | solution.py:345
  55.9 0.0 collective-permute-done.21.mate_near_0_
  55.9 0.0 collective-permute-done.22.mate_near_1_
  55.9 2.4 %project_out.1 = (bf16[256,1024]{1,0:T(8,128)(2,1)}, f32[1,256]{1,0:T(1,128)}) custom-call(s32[3]{0:T(128)S(1)} %pad_add_fusion.where_ref, bf16[256,512]{1,0:T(8,128)(2,1)S(1)} %own_block.1.own_att, bf16[256,512]{1,0:T(8,128)(2,1)S(1)} %collective-permute-done.19.mate_att, bf16[128,1024]{1,0:T(8,128)(2,1)S(1)} %copy-done.4, ...), custom_call_target="tpu_custom_call" | custom-call | flops 1000000000 | bytes 4194304 | tf_op jit(solution)/shard_map/project_out/pallas_call | solution.py:413
  (15 shorter events, 0.0 us)
Async XLA Ops:
  0.6 4.8 %copy-start = (bf16[256,768]{1,0:T(8,128)(2,1)S(1)}, bf16[256,768]{1,0:T(8,128)(2,1)}, u32[]{:S(2)}) copy-start(bf16[256,768]{1,0:T(8,128)(2,1)} %bytes_ref.1) | copy-start | bytes 1179652
  0.6 6.3 %collective-permute-start = (bf16[384,1024]{1,0:T(8,128)(2,1)}, bf16[384,1024]{1,0:T(8,128)(2,1)S(1)}, u32[]{:S(2)}, u32[]{:S(2)}) collective-permute-start(bf16[384,1024]{1,0:T(8,128)(2,1)} %param.12), channel_id=1, source_target_pairs={{0,4},{4,0},{8,12},{12,8},{16,20},{20,16},{24,28},{28,24},{1,5},{5... | collective-permute-start | bytes 2359304 | tf_op jit(solution)/shard_map/ppermute | solution.py:342
  0.8 1.0 %copy-start.1 = (bf16[128,1536]{1,0:T(8,128)(2,1)S(1)}, bf16[128,1536]{1,0:T(8,128)(2,1)}, u32[]{:S(2)}) copy-start(bf16[128,1536]{1,0:T(8,128)(2,1)} %qkv_ref.1) | copy-start | bytes 1179652
  2.4 7.3 %collective-permute-start.1 = (bf16[128,768]{1,0:T(8,128)(2,1)S(1)}, bf16[128,768]{1,0:T(8,128)(2,1)S(1)}, u32[]{:S(2)}, u32[]{:S(2)}) collective-permute-start(bf16[128,768]{1,0:T(8,128)(2,1)S(1)} %qkv_part.1.part_ref.own_w), channel_id=1, source_target_pairs={{0,8},{4,12},{8,0},{12,4},{16,24},{20,28},{24,16},{28,20},{1,9},{5... | collective-permute-start | bytes 589832 | tf_op jit(solution)/shard_map/ppermute | solution.py:342
  3.9 7.0 %collective-permute-start.2 = (bf16[128,768]{1,0:T(8,128)(2,1)S(1)}, bf16[128,768]{1,0:T(8,128)(2,1)S(1)}, u32[]{:S(2)}, u32[]{:S(2)}) collective-permute-start(bf16[128,768]{1,0:T(8,128)(2,1)S(1)} %qkv_part.1.part_ref.own_w), channel_id=1, source_target_pairs={{0,16},{4,20},{8,24},{12,28},{16,0},{20,4},{24,8},{28,12},{1,17},{... | collective-permute-start | bytes 589832 | tf_op jit(solution)/shard_map/ppermute | solution.py:342
  5.5 1.5 %copy-start.2 = (s32[1,256]{1,0:T(1,128)S(1)}, s32[1,256]{1,0:T(1,128)}, u32[]{:S(2)}) copy-start(s32[1,256]{1,0:T(1,128)} %align_ref.1) | copy-start | bytes 3076
  6.9 28.1 %copy-start.5 = (f32[4,256,128]{2,1,0:T(8,128)S(1)}, f32[4,256,128]{2,1,0:T(8,128)}, u32[]{:S(2)}) copy-start(f32[4,256,128]{2,1,0:T(8,128)} %constant.46.clone.cos_ref) | copy-start | bytes 1572868
  7.0 8.0 %copy-start.7 = (s32[1,1024]{1,0:T(1,128)S(1)}, s32[1,1024]{1,0:T(1,128)}, u32[]{:S(2)}) copy-start(s32[1,1024]{1,0:T(1,128)} %param.10) | copy-start | bytes 12292
  7.8 23.7 %copy-start.4 = (bf16[128,1024]{1,0:T(8,128)(2,1)S(1)}, bf16[128,1024]{1,0:T(8,128)(2,1)}, u32[]{:S(2)}) copy-start(bf16[128,1024]{1,0:T(8,128)(2,1)} %own) | copy-start | bytes 786436
  10.9 15.9 %collective-permute-start.3 = (bf16[128,1792]{1,0:T(8,128)(2,1)S(1)}, bf16[128,1792]{1,0:T(8,128)(2,1)S(1)}, u32[]{:S(2)}, u32[]{:S(2)}) collective-permute-start(bf16[128,1792]{1,0:T(8,128)(2,1)S(1)} %get-tuple-element.29), channel_id=1, source_target_pairs={{0,24},{4,28},{8,16},{12,20},{16,8},{20,12},{24,0},{28,4},{1,25},{... | collective-permute-start | bytes 1376264 | tf_op jit(solution)/shard_map/ppermute | solution.py:342
  12.4 16.9 %collective-permute-start.7 = (bf16[128,1024]{1,0:T(8,128)(2,1)S(1)}, bf16[128,1024]{1,0:T(8,128)(2,1)S(1)}, u32[]{:S(2)}, u32[]{:S(2)}) collective-permute-start(bf16[128,1024]{1,0:T(8,128)(2,1)S(1)} %get-tuple-element.30.own_t), channel_id=1, source_target_pairs={{0,8},{4,12},{8,0},{12,4},{16,24},{20,28},{24,16},{28,20},{1,9},{5... | collective-permute-start | bytes 786440 | tf_op jit(solution)/shard_map/ppermute | solution.py:342
  13.9 15.4 %collective-permute-start.8 = (bf16[128,1024]{1,0:T(8,128)(2,1)S(1)}, bf16[128,1024]{1,0:T(8,128)(2,1)S(1)}, u32[]{:S(2)}, u32[]{:S(2)}) collective-permute-start(bf16[128,1024]{1,0:T(8,128)(2,1)S(1)} %get-tuple-element.30.own_t), channel_id=1, source_target_pairs={{0,16},{4,20},{8,24},{12,28},{16,0},{20,4},{24,8},{28,12},{1,17},{... | collective-permute-start | bytes 786440 | tf_op jit(solution)/shard_map/ppermute | solution.py:342
  15.8 14.1 %copy-start.8 = (bf16[1024]{0:T(1024)(128)(2,1)S(1)}, bf16[1024]{0:T(1024)(128)(2,1)}, u32[]{:S(2)}) copy-start(bf16[1024]{0:T(1024)(128)(2,1)} %param.15) | copy-start | bytes 6148
  15.8 3.7 %collective-permute-start.4 = (s32[8,256]{1,0:T(8,128)S(1)}, s32[8,256]{1,0:T(8,128)S(1)}, u32[]{:S(2)}, u32[]{:S(2)}) collective-permute-start(s32[8,256]{1,0:T(8,128)S(1)} %pad.4.ids_refs_0_), channel_id=1, source_target_pairs={{0,1},{1,0},{2,3},{3,2},{4,5},{5,4},{6,7},{7,6},{8,9},{9,8},{10,11... | collective-permute-start | bytes 24584 | tf_op jit(solution)/shard_map/ppermute | solution.py:345
  16.4 6.4 %collective-permute-start.5 = (s32[8,256]{1,0:T(8,128)S(1)}, s32[8,256]{1,0:T(8,128)S(1)}, u32[]{:S(2)}, u32[]{:S(2)}) collective-permute-start(s32[8,256]{1,0:T(8,128)S(1)} %pad.4.ids_refs_0_), channel_id=1, source_target_pairs={{0,2},{1,3},{4,6},{5,7},{8,10},{9,11},{12,14},{13,15},{16,18},{17,... | collective-permute-start | bytes 24584 | tf_op jit(solution)/shard_map/ppermute | solution.py:345
  19.6 7.3 %collective-permute-start.6 = (s32[8,256]{1,0:T(8,128)S(1)}, s32[8,256]{1,0:T(8,128)S(1)}, u32[]{:S(2)}, u32[]{:S(2)}) collective-permute-start(s32[8,256]{1,0:T(8,128)S(1)} %pad.4.ids_refs_0_), channel_id=1, source_target_pairs={{0,3},{1,2},{4,7},{5,6},{8,11},{9,10},{12,15},{13,14},{16,19},{17,... | collective-permute-start | bytes 24584 | tf_op jit(solution)/shard_map/ppermute | solution.py:345
  22.8 4.6 %collective-permute-start.13 = (bf16[128,768]{1,0:T(8,128)(2,1)S(1)}, bf16[128,768]{1,0:T(8,128)(2,1)S(1)}, u32[]{:S(2)}, u32[]{:S(2)}) collective-permute-start(bf16[128,768]{1,0:T(8,128)(2,1)S(1)} %qkv_part.1.part_ref.own_w), channel_id=1, source_target_pairs={{0,4},{4,0},{8,12},{12,8},{16,20},{20,16},{24,28},{28,24},{1,5},{5... | collective-permute-start | bytes 589832 | tf_op jit(solution)/shard_map/ppermute | solution.py:342
  26.9 8.2 %collective-permute-start.12 = (bf16[128,1792]{1,0:T(8,128)(2,1)S(1)}, bf16[128,1792]{1,0:T(8,128)(2,1)S(1)}, u32[]{:S(2)}, u32[]{:S(2)}) collective-permute-start(bf16[128,1792]{1,0:T(8,128)(2,1)S(1)} %collective-permute-done.3.near_t_2_), channel_id=1, source_target_pairs={{0,4},{4,0},{8,12},{12,8},{16,20},{20,16},{24,28},{28,24},{1,5},{5... | collective-permute-start | bytes 1376264 | tf_op jit(solution)/shard_map/ppermute | solution.py:342
  26.9 3.0 %collective-permute-start.14 = (bf16[128,768]{1,0:T(8,128)(2,1)S(1)}, bf16[128,768]{1,0:T(8,128)(2,1)S(1)}, u32[]{:S(2)}, u32[]{:S(2)}) collective-permute-start(bf16[128,768]{1,0:T(8,128)(2,1)S(1)} %collective-permute-done.1.near_w_0_), channel_id=1, source_target_pairs={{0,4},{4,0},{8,12},{12,8},{16,20},{20,16},{24,28},{28,24},{1,5},{5... | collective-permute-start | bytes 589832 | tf_op jit(solution)/shard_map/ppermute | solution.py:342
  27.4 4.7 %collective-permute-start.9 = (bf16[128,1024]{1,0:T(8,128)(2,1)S(1)}, bf16[128,1024]{1,0:T(8,128)(2,1)S(1)}, u32[]{:S(2)}, u32[]{:S(2)}) collective-permute-start(bf16[128,1024]{1,0:T(8,128)(2,1)S(1)} %get-tuple-element.30.own_t), channel_id=1, source_target_pairs={{0,4},{4,0},{8,12},{12,8},{16,20},{20,16},{24,28},{28,24},{1,5},{5... | collective-permute-start | bytes 786440 | tf_op jit(solution)/shard_map/ppermute | solution.py:342
  29.4 3.8 %collective-permute-start.10 = (bf16[128,1024]{1,0:T(8,128)(2,1)S(1)}, bf16[128,1024]{1,0:T(8,128)(2,1)S(1)}, u32[]{:S(2)}, u32[]{:S(2)}) collective-permute-start(bf16[128,1024]{1,0:T(8,128)(2,1)S(1)} %collective-permute-done.7.near_t_0_), channel_id=1, source_target_pairs={{0,4},{4,0},{8,12},{12,8},{16,20},{20,16},{24,28},{28,24},{1,5},{5... | collective-permute-start | bytes 786440 | tf_op jit(solution)/shard_map/ppermute | solution.py:342
  29.4 5.7 %collective-permute-start.11 = (bf16[128,1024]{1,0:T(8,128)(2,1)S(1)}, bf16[128,1024]{1,0:T(8,128)(2,1)S(1)}, u32[]{:S(2)}, u32[]{:S(2)}) collective-permute-start(bf16[128,1024]{1,0:T(8,128)(2,1)S(1)} %collective-permute-done.8.near_t_1_), channel_id=1, source_target_pairs={{0,4},{4,0},{8,12},{12,8},{16,20},{20,16},{24,28},{28,24},{1,5},{5... | collective-permute-start | bytes 786440 | tf_op jit(solution)/shard_map/ppermute | solution.py:342
  29.9 1.7 %collective-permute-start.15 = (bf16[128,768]{1,0:T(8,128)(2,1)S(1)}, bf16[128,768]{1,0:T(8,128)(2,1)S(1)}, u32[]{:S(2)}, u32[]{:S(2)}) collective-permute-start(bf16[128,768]{1,0:T(8,128)(2,1)S(1)} %collective-permute-done.2.near_w_1_), channel_id=1, source_target_pairs={{0,4},{4,0},{8,12},{12,8},{16,20},{20,16},{24,28},{28,24},{1,5},{5... | collective-permute-start | bytes 589832 | tf_op jit(solution)/shard_map/ppermute | solution.py:342
  31.6 15.6 %collective-permute-start.16 = (bf16[128,1024]{1,0:T(8,128)(2,1)S(1)}, bf16[128,1024]{1,0:T(8,128)(2,1)S(1)}, u32[]{:S(2)}, u32[]{:S(2)}) collective-permute-start(bf16[128,1024]{1,0:T(8,128)(2,1)S(1)} %copy-done.4), channel_id=1, source_target_pairs={{0,8},{4,12},{8,0},{12,4},{16,24},{20,28},{24,16},{28,20},{1,9},{5... | collective-permute-start | bytes 786440 | tf_op jit(solution)/shard_map/ppermute | solution.py:342
  32.2 15.0 %collective-permute-start.17 = (bf16[128,1024]{1,0:T(8,128)(2,1)S(1)}, bf16[128,1024]{1,0:T(8,128)(2,1)S(1)}, u32[]{:S(2)}, u32[]{:S(2)}) collective-permute-start(bf16[128,1024]{1,0:T(8,128)(2,1)S(1)} %copy-done.4), channel_id=1, source_target_pairs={{0,16},{4,20},{8,24},{12,28},{16,0},{20,4},{24,8},{28,12},{1,17},{... | collective-permute-start | bytes 786440 | tf_op jit(solution)/shard_map/ppermute | solution.py:342
  33.2 13.9 %collective-permute-start.18 = (bf16[128,1024]{1,0:T(8,128)(2,1)S(1)}, bf16[128,1024]{1,0:T(8,128)(2,1)S(1)}, u32[]{:S(2)}, u32[]{:S(2)}) collective-permute-start(bf16[128,1024]{1,0:T(8,128)(2,1)S(1)} %copy-done.4), channel_id=1, source_target_pairs={{0,24},{4,28},{8,16},{12,20},{16,8},{20,12},{24,0},{28,4},{1,25},{... | collective-permute-start | bytes 786440 | tf_op jit(solution)/shard_map/ppermute | solution.py:342
  35.1 19.1 %collective-permute-start.20 = (bf16[128,1024]{1,0:T(8,128)(2,1)S(1)}, bf16[128,1024]{1,0:T(8,128)(2,1)S(1)}, u32[]{:S(2)}, u32[]{:S(2)}) collective-permute-start(bf16[128,1024]{1,0:T(8,128)(2,1)S(1)} %copy-done.4), channel_id=1, source_target_pairs={{0,4},{4,0},{8,12},{12,8},{16,20},{20,16},{24,28},{28,24},{1,5},{5... | collective-permute-start | bytes 786440 | tf_op jit(solution)/shard_map/ppermute | solution.py:342
  35.1 1.0 %copy-start.6 = (f32[4,256,128]{2,1,0:T(8,128)S(1)}, f32[4,256,128]{2,1,0:T(8,128)}, u32[]{:S(2)}) copy-start(f32[4,256,128]{2,1,0:T(8,128)} %constant.47.clone.sin_ref) | copy-start | bytes 1572868
  47.1 8.8 %collective-permute-start.19 = (bf16[256,512]{1,0:T(8,128)(2,1)S(1)}, bf16[256,512]{1,0:T(8,128)(2,1)S(1)}, u32[]{:S(2)}, u32[]{:S(2)}) collective-permute-start(bf16[256,512]{1,0:T(8,128)(2,1)S(1)} %get-tuple-element.44), channel_id=1, source_target_pairs={{0,1},{1,0},{2,3},{3,2},{4,5},{5,4},{6,7},{7,6},{8,9},{9,8},{10,11... | collective-permute-start | bytes 786440 | tf_op jit(solution)/shard_map/ppermute | solution.py:345
  48.4 7.5 %collective-permute-start.21 = (bf16[128,1024]{1,0:T(8,128)(2,1)S(1)}, bf16[128,1024]{1,0:T(8,128)(2,1)S(1)}, u32[]{:S(2)}, u32[]{:S(2)}) collective-permute-start(bf16[128,1024]{1,0:T(8,128)(2,1)S(1)} %collective-permute-done.16.near_0_), channel_id=1, source_target_pairs={{0,4},{4,0},{8,12},{12,8},{16,20},{20,16},{24,28},{28,24},{1,5},{5... | collective-permute-start | bytes 786440 | tf_op jit(solution)/shard_map/ppermute | solution.py:342
  48.6 7.3 %collective-permute-start.22 = (bf16[128,1024]{1,0:T(8,128)(2,1)S(1)}, bf16[128,1024]{1,0:T(8,128)(2,1)S(1)}, u32[]{:S(2)}, u32[]{:S(2)}) collective-permute-start(bf16[128,1024]{1,0:T(8,128)(2,1)S(1)} %collective-permute-done.17.near_1_), channel_id=1, source_target_pairs={{0,4},{4,0},{8,12},{12,8},{16,20},{20,16},{24,28},{28,24},{1,5},{5... | collective-permute-start | bytes 786440 | tf_op jit(solution)/shard_map/ppermute | solution.py:342
  48.9 7.0 %collective-permute-start.23 = (bf16[128,1024]{1,0:T(8,128)(2,1)S(1)}, bf16[128,1024]{1,0:T(8,128)(2,1)S(1)}, u32[]{:S(2)}, u32[]{:S(2)}) collective-permute-start(bf16[128,1024]{1,0:T(8,128)(2,1)S(1)} %collective-permute-done.18.near_2_), channel_id=1, source_target_pairs={{0,4},{4,0},{8,12},{12,8},{16,20},{20,16},{24,28},{28,24},{1,5},{5... | collective-permute-start | bytes 786440 | tf_op jit(solution)/shard_map/ppermute | solution.py:342
  49.1 6.8 %copy-start.3 = (bf16[1,256,1024]{2,1,0:T(8,128)(2,1)S(1)}, bf16[1,256,1024]{2,1,0:T(8,128)(2,1)}, u32[]{:S(2)}) copy-start(bf16[1,256,1024]{2,1,0:T(8,128)(2,1)} %param.16) | copy-start | bytes 1572868

commit v4 on v3

--- a/solution.py
+++ b/solution.py
@@ -114,13 +114,26 @@
     return (hidden_out[None], token_loss[None])
 
 
-def rope_tables(length):
+def rope_tables(blocks, rows):
     half = HD // 2
     frequency = np.float32(theta_base) ** (-np.arange(half, dtype=np.float32) * np.float32(2.0 / HD))
-    angles = np.arange(length, dtype=np.float32)[:, None] * frequency[None, :]
-    angles = angles.astype(np.float64)
-    cos, sin = np.cos(angles).astype(np.float32), np.sin(angles).astype(np.float32)
-    return np.concatenate([cos] * 4, axis=1), np.concatenate([-sin, sin] * 2, axis=1)
+    places = [np.arange(rows), np.arange(blocks) * rows]
+    angles = [np.concatenate([p[:, None] * frequency[None, :].astype(np.float64)] * 4, axis=1) for p in places]
+    parts = [f(angles[0]) for f in (np.cos, np.sin)] + [f(angles[1]) for f in (np.cos, np.sin)]
+    return np.concatenate(parts, axis=0).astype(np.float32)
+
+
+def rope_at(rope_ref, rows, block):
+    blocks = (rope_ref.shape[0] - 2 * rows) // 2
+    cos, sin = rope_ref[:rows, :], rope_ref[rows : 2 * rows, :]
+    cos_start = rope_ref[pl.ds(2 * rows + block, 1), :]
+    sin_start = rope_ref[pl.ds(2 * rows + blocks + block, 1), :]
+    lane = lax.broadcasted_iota(jnp.int32, (1, 128), 1)
+    sign = jnp.where((lane & (HD // 2)) == 0, -1.0, 1.0)
+    return (
+        cos * cos_start - sin * sin_start,
+        sin * (cos_start * sign) + cos * (sin_start * sign),
+    )
 
 
 def turn(x, cos, sin):
@@ -142,8 +155,9 @@
         start += width
 
 
-def table_kernel(where_ref, bytes_ref, conv_ref, total_ref, part_ref, align_ref, out_ref, both_ref, align_out):
+def table_kernel(where_ref, bytes_ref, conv_ref, total_ref, align_ref, rope_ref, out_ref, align_out, rope_out):
     align_out[...] = align_ref[...]
+    rope_out[...] = rope_ref[...]
     core = where_ref[1]
     taps_in = conv_ref.shape[0]
     half = total_ref.shape[0]
@@ -151,8 +165,6 @@
     mates = bytes_ref[rows, pl.ds(pl.multiple_of((1 - core) * taps_in, taps_in), taps_in)]
     total = total_ref[...] + jnp.dot(mates, conv_ref[...], preferred_element_type=jnp.float32)
     out_ref[...] = total.astype(jnp.bfloat16)
-    both_ref[:, : total.shape[1]] = total.astype(jnp.bfloat16)
-    both_ref[:, total.shape[1] :] = part_ref[...]
 
 
 def ordered(chip, core, pieces):
@@ -164,30 +176,29 @@
             yield pl.ds(pl.multiple_of((base + which) * depth, depth), depth), piece
 
 
-def attend(queries, key_slots, allowed, k_s, v_s, att_ref):
+def attend(queries, slots, allowed, k_s, v_s, att_ref):
     heads = HQ // 2
-
-    def one_head(h):
-        query = queries(h)
-        group = h // GROUP
-        scores = [
-            lax.dot_general(
-                k_s[slot, group], query, (((1,), (1,)), ((), ())), preferred_element_type=jnp.float32
-            )
-            for slot in key_slots
-        ]
-        scores[-1] = jnp.where(allowed, scores[-1], masked_score)
-        top = functools.reduce(jnp.maximum, [jnp.max(s, axis=0, keepdims=True) for s in scores])
-        total = None
-        for slot, s in zip(key_slots, scores):
-            probs = jnp.exp(s - top).astype(jnp.bfloat16)
-            term = jnp.dot(v_s[slot, group], probs, preferred_element_type=jnp.float32)
-            total = term if total is None else total + term
-        return total[:HD] / total[HD : HD + 1]
-
-    for pair in range(heads // 2):
-        result = jnp.concatenate([one_head(2 * pair), one_head(2 * pair + 1)], axis=0)
-        att_ref[:, pair * 2 * HD : (pair + 1) * 2 * HD] = jnp.transpose(result).astype(jnp.bfloat16)
+    rows = att_ref.shape[0]
+    keys = slice(slots[0] * rows, (slots[-1] + 1) * rows)
+
+    def score(h):
+        scores = lax.dot_general(
+            k_s[h // GROUP, keys, :], queries(h), (((1,), (1,)), ((), ())), preferred_element_type=jnp.float32
+        )
+        last = jnp.where(allowed, scores[-rows:], masked_score)
+        return last if len(slots) == 1 else jnp.concatenate([scores[:-rows], last], axis=0)
+
+    coming, results = score(0), []
+    for h in range(heads):
+        scores = coming
+        if h + 1 < heads:
+            coming = score(h + 1)
+        probs = jnp.exp(scores - jnp.max(scores, axis=0, keepdims=True)).astype(jnp.bfloat16)
+        total = jnp.dot(v_s[h // GROUP, :, keys], probs, preferred_element_type=jnp.float32)
+        results.append(total[:HD] / total[HD : HD + 1])
+        if h % 2 == 1:
+            pair = jnp.transpose(jnp.concatenate(results[-2:], axis=0))
+            att_ref[:, (h - 1) * HD : (h + 1) * HD] = pair.astype(jnp.bfloat16)
 
 
 def causal(rows):
@@ -205,7 +216,7 @@
 
 def lift_kernel(
     where_ref, ids_refs, own_t, near_t, mate_own_t, mate_near_t, own_w, near_w, mate_own_w, mate_near_w,
-    gain_ref, cos_ref, sin_ref, att_ref, query_ref, k_s, v_s, lat_ref,
+    gain_ref, rope_ref, att_ref, query_ref, k_s, v_s, lat_ref,
     table_s, weight_s, ids_s, lat_s, q_s,
 ):
     chip, core, ctx = where_ref[0], where_ref[1], where_ref[2]
@@ -213,17 +224,16 @@
     rows, features = lat_ref.shape
     q_width, k_width = HQ * HD // 2, HK * HD // 2
     for span, piece in ordered(chip, core, (own_t, near_t, mate_own_t, mate_near_t)):
-        table_s[span, :] = piece[:, :features]
-    near_w, mate_near_w = near_w + (near_t[-1],), mate_near_w + (mate_near_t[-1],)
+        table_s[span, :] = piece[...]
     for span, piece in ordered(chip, core, (own_w, near_w, mate_own_w, mate_near_w)):
-        weight_s[span, :] = piece[:, -weight_s.shape[1] :]
+        weight_s[span, :] = piece[...]
     own_ids, pair_ids, past_ids, cross_ids = ids_refs
     ids_s[side] = past_ids[...]
     ids_s[1 - side] = cross_ids[...]
     ids_s[2 + side] = own_ids[...]
     ids_s[3 - side] = pair_ids[...]
     gain = gain_ref[...].astype(jnp.float32)
-    v_s[:, :, HD:, :] = jnp.ones(v_s.shape[:2] + (v_s.shape[2] - HD, rows), jnp.bfloat16)
+    v_s[:, HD:, :] = jnp.ones((v_s.shape[0], v_s.shape[1] - HD, v_s.shape[2]), jnp.bfloat16)
 
     def lift(slot):
         ids = jnp.transpose(ids_s[slot])
@@ -236,7 +246,7 @@
         scale = lax.rsqrt(jnp.mean(wide * wide, axis=1, keepdims=True) + norm_eps)
         normed = (wide * scale * gain).astype(jnp.bfloat16)
         block = slot if slot < 2 else 2 * upper + slot - 2
-        cos, sin = cos_ref[block], sin_ref[block]
+        cos, sin = rope_at(rope_ref, rows, block)
         if slot >= 2:
             lat_s[slot - 2] = latent
             asked = jnp.dot(normed, weight_s[:, :q_width], preferred_element_type=jnp.float32)
@@ -249,8 +259,8 @@
         keys = turn(kept[:, :k_width], cos, sin).astype(jnp.bfloat16)
         values = jnp.transpose(kept[:, k_width:]).astype(jnp.bfloat16)
         for group in range(2):
-            k_s[slot, group] = keys[:, group * HD : (group + 1) * HD]
-            v_s[slot, group, :HD, :] = values[group * HD : (group + 1) * HD]
+            k_s[group, slot * rows : (slot + 1) * rows, :] = keys[:, group * HD : (group + 1) * HD]
+            v_s[group, :HD, slot * rows : (slot + 1) * rows] = values[group * HD : (group + 1) * HD]
 
     @pl.when(upper == 1)
     def _():
@@ -356,17 +366,19 @@
     (part,) = call(
         part_kernel, "qkv_part", 4, 10**8, [SMEM, VMEM], [((w_qkv.shape[0], part_width), bf16)]
     )(where, w_qkv)
-    near_w = tuple(swap(part, 2 * j) for j in (1, 2))
+    near_w = to_near(part)
 
     taps_in = w_conv.shape[0]
     mine = lax.dynamic_slice(byte_table, (core * half, core * taps_in), (half, taps_in))
     total = jnp.dot(mine, w_conv, preferred_element_type=f32)
-    own_t, both, align = call(
+    rope = jnp.asarray(rope_tables(n_ctx, rows))
+    own_t, align, rope = call(
         table_kernel, "tap_table", 8, 10**8, [SMEM] + [VMEM] * 5,
-        [((half, features), bf16), ((half, features + part_width), bf16), (align.shape, jnp.int32)],
-    )(where, byte_table, mate_conv, total, part, align)
-    (own_t, both), near_w = lax.optimization_barrier(((own_t, both), near_w))
-    near_t = (swap(own_t, 2), swap(own_t, 4), swap(both, 6))
+        [((half, features), bf16), (align.shape, jnp.int32), (rope.shape, f32)],
+    )(where, byte_table, mate_conv, total, align, rope)
+    own_t, first = lax.optimization_barrier((own_t, near_w[0]))
+    near_w = (first,) + near_w[1:]
+    near_t = to_near(own_t)
     ids = jnp.transpose(byte_ids[0].reshape(rows, KW))
     ids = jnp.pad(ids, ((0, 8 - KW), (0, 0)))
     ids, unused = lax.optimization_barrier((ids, own_t))
@@ -382,18 +394,17 @@
     out_own, unused = lax.optimization_barrier((w_out, near_t))
     out_near = to_near(out_own)
 
-    cos, sin = (jnp.asarray(t.reshape(n_ctx, rows, 128)) for t in rope_tables(rows * n_ctx))
     near_specs = (VMEM,) * (n_fsdp // 2 - 1)
     piece_specs = [VMEM, near_specs, VMEM, near_specs]
     att_shape = ((rows, q_width), bf16)
     att_mate, query, keys, values, latent = call(
         lift_kernel, "lift", 18, 5 * 10**9,
-        [SMEM, (VMEM,) * 4] + piece_specs + [VMEM, (VMEM,) * 2] * 2 + [VMEM, VMEM, VMEM],
+        [SMEM, (VMEM,) * 4] + piece_specs + piece_specs + [VMEM, VMEM],
         [
             att_shape,
             ((HQ // 2, rows, HD), bf16),
-            ((4, 2, rows, HD), bf16),
-            ((4, 2, HD + 16, rows), bf16),
+            ((2, 4 * rows, HD), bf16),
+            ((2, HD + 16, 4 * rows), bf16),
             ((rows, features), bf16),
         ],
         [
@@ -403,7 +414,7 @@
             ((2, rows, features), bf16),
             ((2, HQ // 2, rows, HD), bf16),
         ],
-    )(where, ids_all, *t_pieces, *w_pieces, norm_gain[None], cos, sin)
+    )(where, ids_all, *t_pieces, *w_pieces, norm_gain[None], rope)
 
     att_mate, out_near = lax.optimization_barrier((att_mate, out_near))
     att_back = along(att_mate, beside)

time: 59.3 us -> 62.3 us (1.051)
  waiting for transfers between devices: 16.4 us -> 21.9 us
  Pallas kernels: 19.9 us -> 18.5 us
  local copies, waits for them, and re-layouts: 2.79 us -> 1.75 us
    ppermute x20 -> x22, waiting for transfers between devices: 6.68 us -> 11.1 us  [swap(): return lax.ppermute(x, 'fsdp', [(d, d ^ j) for d in range(n_fsdp)])]
    ppermute x4, starting transfers between devices: 4.3 us -> 3.01 us  [along(): return lax.ppermute(x, 'ctx', pairs)]
    ppermute x4, waiting for transfers between devices: 9.69 us -> 10.7 us  [along(): return lax.ppermute(x, 'ctx', pairs)]
    unnamed x19 -> x17, local copies, waits for them, and re-layouts: 2.58 us -> 1.54 us
    ppermute x20 -> x22, starting transfers between devices: 12 us -> 12.9 us  [swap(): return lax.ppermute(x, 'fsdp', [(d, d ^ j) for d in range(n_fsdp)])]
    pallas_call x1, Pallas kernels: 5.06 us -> 4.3 us  [head_body(): call(own_kernel, 'own_block', 12, 3 * 10 ** 9, [SMEM, VMEM, VMEM, VMEM],...]
    pallas_call x1, Pallas kernels: 11 us -> 10.3 us  [head_body(): call(lift_kernel, 'lift', 18, 5 * 10 ** 9, [SMEM, (VMEM,) * 4] + piece_sp...]
  transfers between devices with their start and end apart: 24 -> 26, of which waited for: 8 -> 10; matrix products, arithmetic and copies ran while one was open for 5% -> 5% of each run, Pallas kernels for 30% -> 26%
where the time goes in v4:
time: 62.3 us; the launch traced here: 61.1 us
  waiting for transfers between devices  21.9 us (35%)
  Pallas kernels  18.5 us (30%)
  starting transfers between devices  15.9 us (26%)
  local copies, waits for them, and re-layouts  1.75 us (3%)
  matrix products  1.47 us (2%)
  between operations  0.85 us (1%)
  other arithmetic  0.74 us (1%)
    ppermute x22, starting transfers between devices, swap(): return lax.ppermute(x, 'fsdp', [(d, d ^ j) for d in range(n_fsdp)])  12.9 us
    ppermute x22, waiting for transfers between devices, swap(): return lax.ppermute(x, 'fsdp', [(d, d ^ j) for d in range(n_fsdp)])  11.1 us
    ppermute x4, waiting for transfers between devices, along(): return lax.ppermute(x, 'ctx', pairs)  10.7 us
    pallas_call x1, Pallas kernels, head_body(): call(lift_kernel, 'lift', 18, 5 * 10 ** 9, [SMEM, (VMEM,) * 4] + piece_sp...  10.3 us
    pallas_call x1, Pallas kernels, head_body(): call(own_kernel, 'own_block', 12, 3 * 10 ** 9, [SMEM, VMEM, VMEM, VMEM],...  4.3 us
    ppermute x4, starting transfers between devices, along(): return lax.ppermute(x, 'ctx', pairs)  3.01 us
    pallas_call x1, Pallas kernels, head_body(): call(out_kernel, 'project_out', 12, 10 ** 9, [SMEM, VMEM, VMEM] + piece_s...  2.44 us
    unnamed x17, local copies, waits for them, and re-layouts  1.54 us
  transfers between devices with their start and end apart: 26, of which 10 were waited for; matrix products, arithmetic and copies ran while one was open for 5% of the time, Pallas kernels for 26%

profile of v4, /device:TPU:24, one launch (start us, length us, event | category | flops | bytes accessed | tf_op | source)
XLA Modules:
  0.0 61.1 jit_solution(702224498299001594)
XLA Ops:
  0.6 0.1 collective-permute-start
  0.7 0.1 pad_add_fusion.where_ref
  0.8 1.0 %copy-done.1 = bf16[128,1536]{1,0:T(8,128)(2,1)S(1)} copy-done((bf16[128,1536]{1,0:T(8,128)(2,1)S(1)}, bf16[128,1536]{1,0:T(8,128)(2,1)}, u32[]{:S(2)}) %copy-start.1) | copy-done | bytes 393240
  1.8 0.6 qkv_part.1.own_w
  2.4 1.6 %collective-permute-start.1 = (bf16[128,768]{1,0:T(8,128)(2,1)S(1)}, bf16[128,768]{1,0:T(8,128)(2,1)S(1)}, u32[]{:S(2)}, u32[]{:S(2)}) collective-permute-start(bf16[128,768]{1,0:T(8,128)(2,1)S(1)} %qkv_part.1.own_w), channel_id=1, source_target_pairs={{0,8},{4,12},{8,0},{12,4},{16,24},{20,28},{24,16},{28,20},{1,9},{5... | collective-permute-start | bytes 589832 | tf_op jit(solution)/shard_map/ppermute | solution.py:352
  3.9 1.5 %collective-permute-start.12 = (bf16[128,768]{1,0:T(8,128)(2,1)S(1)}, bf16[128,768]{1,0:T(8,128)(2,1)S(1)}, u32[]{:S(2)}, u32[]{:S(2)}) collective-permute-start(bf16[128,768]{1,0:T(8,128)(2,1)S(1)} %qkv_part.1.own_w), channel_id=1, source_target_pairs={{0,16},{4,20},{8,24},{12,28},{16,0},{20,4},{24,8},{28,12},{1,17},{... | collective-permute-start | bytes 589832 | tf_op jit(solution)/shard_map/ppermute | solution.py:352
  5.5 0.5 collective-permute-start.13
  6.0 1.5 %fusion.total_ref = f32[128,1024]{1,0:T(8,128)S(1)} fusion(bf16[384,1024]{1,0:T(8,128)(2,1)} %param.11, bf16[256,768]{1,0:T(8,128)(2,1)S(1)} %copy-done, s32[]{:T(128)S(6)} %select_n.19, s32[]{:T(128)S(6)} %select_n.20), kind=kOutput, calls=%fused_computation | convolution fusion | flops 100663296 | bytes 1409032 | tf_op jit(solution)/shard_map/dot_general | solution.py:373
  7.4 0.0 collective-permute-done.conv_ref
  7.5 0.0 copy-start.6
  7.5 0.9 %tap_table.1 = (bf16[128,1024]{1,0:T(8,128)(2,1)S(1)}, s32[1,256]{1,0:T(1,128)S(1)}, f32[520,128]{1,0:T(8,128)S(1)}) custom-call(s32[3]{0:T(128)S(1)} %pad_add_fusion.where_ref, bf16[256,768]{1,0:T(8,128)(2,1)S(1)} %copy-done, bf16[384,1024]{1,0:T(8,128)(2,1)S(1)} %collective-permute-done.conv_ref, f32[128,1024]{1,0:T(8,128)S(1)} %fusion.total_ref, ...), custom_call_target="tpu_custom_call" | custom-call | flops 100000000 | bytes 4194304 | tf_op jit(solution)/shard_map/tap_table/pallas_call | solution.py:375
  8.4 0.0 copy-start.5
  8.4 1.8 %collective-permute-done.1.near_w_0_ = bf16[128,768]{1,0:T(8,128)(2,1)S(1)} collective-permute-done((bf16[128,768]{1,0:T(8,128)(2,1)S(1)}, bf16[128,768]{1,0:T(8,128)(2,1)S(1)}, u32[]{:S(2)}, u32[]{:S(2)}) %collective-permute-start.1) | collective-permute-done | bytes 196640 | tf_op jit(solution)/shard_map/ppermute | solution.py:352
  10.2 2.4 %collective-permute-start.2 = (bf16[128,1024]{1,0:T(8,128)(2,1)S(1)}, bf16[128,1024]{1,0:T(8,128)(2,1)S(1)}, u32[]{:S(2)}, u32[]{:S(2)}) collective-permute-start(bf16[128,1024]{1,0:T(8,128)(2,1)S(1)} %get-tuple-element.26.own_t), channel_id=1, source_target_pairs={{0,24},{4,28},{8,16},{12,20},{16,8},{20,12},{24,0},{28,4},{1,25},{... | collective-permute-start | bytes 786440 | tf_op jit(solution)/shard_map/ppermute | solution.py:352
  12.6 0.5 collective-permute-start.6
  13.1 0.5 collective-permute-start.7
  13.7 0.5 broadcast.7
  14.2 0.7 %reduce.3 = s32[1024]{0:T(1024)S(1)} reduce(s32[1,1024]{1,0:T(1,128)S(1)} %copy-done.6, s32[]{:T(128)} %broadcast.7), dimensions={0}, to_apply=%param.9.reduce_sub_computation.3 | reduce | bytes 8196 | tf_op args[0]
  14.8 0.1 reshape_squeeze.3
  15.0 0.1 copy.11
  15.1 5.7 %collective-permute-done.12.near_w_1_ = bf16[128,768]{1,0:T(8,128)(2,1)S(1)} collective-permute-done((bf16[128,768]{1,0:T(8,128)(2,1)S(1)}, bf16[128,768]{1,0:T(8,128)(2,1)S(1)}, u32[]{:S(2)}, u32[]{:S(2)}) %collective-permute-start.12) | collective-permute-done | bytes 196640 | tf_op jit(solution)/shard_map/ppermute | solution.py:352
  20.7 0.4 collective-permute-start.3
  21.2 0.0 collective-permute-done.13.near_w_2_
  21.2 1.3 %collective-permute-start.4 = (s32[8,256]{1,0:T(8,128)S(1)}, s32[8,256]{1,0:T(8,128)S(1)}, u32[]{:S(2)}, u32[]{:S(2)}) collective-permute-start(s32[8,256]{1,0:T(8,128)S(1)} %pad.4.ids_refs_0_), channel_id=1, source_target_pairs={{0,2},{1,3},{4,6},{5,7},{8,10},{9,11},{12,14},{13,15},{16,18},{17,... | collective-permute-start | bytes 24584 | tf_op jit(solution)/shard_map/ppermute | solution.py:355
  22.5 1.9 %collective-permute-done.3.ids_refs_1_ = s32[8,256]{1,0:T(8,128)S(1)} collective-permute-done((s32[8,256]{1,0:T(8,128)S(1)}, s32[8,256]{1,0:T(8,128)S(1)}, u32[]{:S(2)}, u32[]{:S(2)}) %collective-permute-start.3) | collective-permute-done | bytes 8224 | tf_op jit(solution)/shard_map/ppermute | solution.py:355
  24.4 1.3 %collective-permute-start.5 = (s32[8,256]{1,0:T(8,128)S(1)}, s32[8,256]{1,0:T(8,128)S(1)}, u32[]{:S(2)}, u32[]{:S(2)}) collective-permute-start(s32[8,256]{1,0:T(8,128)S(1)} %pad.4.ids_refs_0_), channel_id=1, source_target_pairs={{0,3},{1,2},{4,7},{5,6},{8,11},{9,10},{12,15},{13,14},{16,19},{17,... | collective-permute-start | bytes 24584 | tf_op jit(solution)/shard_map/ppermute | solution.py:355
  25.7 2.0 %collective-permute-done.4.ids_refs_2_ = s32[8,256]{1,0:T(8,128)S(1)} collective-permute-done((s32[8,256]{1,0:T(8,128)S(1)}, s32[8,256]{1,0:T(8,128)S(1)}, u32[]{:S(2)}, u32[]{:S(2)}) %collective-permute-start.4) | collective-permute-done | bytes 8224 | tf_op jit(solution)/shard_map/ppermute | solution.py:355
  27.7 0.0 collective-permute-start.14
  27.7 4.0 %collective-permute-done.5.ids_refs_3_ = s32[8,256]{1,0:T(8,128)S(1)} collective-permute-done((s32[8,256]{1,0:T(8,128)S(1)}, s32[8,256]{1,0:T(8,128)S(1)}, u32[]{:S(2)}, u32[]{:S(2)}) %collective-permute-start.5) | collective-permute-done | bytes 8224 | tf_op jit(solution)/shard_map/ppermute | solution.py:355
  31.7 0.0 collective-permute-start.16
  31.7 0.0 collective-permute-done.2.near_t_2_
  31.7 0.5 collective-permute-start.17
  32.2 0.0 collective-permute-done.14.mate_own_w
  32.2 0.1 collective-permute-start.8
  32.3 0.0 collective-permute-done.6.near_t_0_
  32.3 0.4 collective-permute-start.9
  32.8 0.0 collective-permute-done.7.near_t_1_
  32.8 0.1 collective-permute-start.10
  32.8 0.3 collective-permute-done.16.mate_near_w_1_
  33.2 0.1 collective-permute-start.11
  33.3 0.1 collective-permute-done.17.mate_near_w_2_
  33.4 0.2 collective-permute-start.15
  33.7 1.5 %collective-permute-done.15.mate_near_w_0_ = bf16[128,768]{1,0:T(8,128)(2,1)S(1)} collective-permute-done((bf16[128,768]{1,0:T(8,128)(2,1)S(1)}, bf16[128,768]{1,0:T(8,128)(2,1)S(1)}, u32[]{:S(2)}, u32[]{:S(2)}) %collective-permute-start.15) | collective-permute-done | bytes 196640 | tf_op jit(solution)/shard_map/ppermute | solution.py:352
  35.2 0.0 collective-permute-start.18
  35.2 0.0 collective-permute-done.8.mate_own_t
  35.2 2.4 %collective-permute-start.19 = (bf16[128,1024]{1,0:T(8,128)(2,1)S(1)}, bf16[128,1024]{1,0:T(8,128)(2,1)S(1)}, u32[]{:S(2)}, u32[]{:S(2)}) collective-permute-start(bf16[128,1024]{1,0:T(8,128)(2,1)S(1)} %copy-done.5), channel_id=1, source_target_pairs={{0,16},{4,20},{8,24},{12,28},{16,0},{20,4},{24,8},{28,12},{1,17},{... | collective-permute-start | bytes 786440 | tf_op jit(solution)/shard_map/ppermute | solution.py:352
  37.6 0.0 collective-permute-done.9.mate_near_t_0_
  37.6 1.5 %collective-permute-start.20 = (bf16[128,1024]{1,0:T(8,128)(2,1)S(1)}, bf16[128,1024]{1,0:T(8,128)(2,1)S(1)}, u32[]{:S(2)}, u32[]{:S(2)}) collective-permute-start(bf16[128,1024]{1,0:T(8,128)(2,1)S(1)} %copy-done.5), channel_id=1, source_target_pairs={{0,24},{4,28},{8,16},{12,20},{16,8},{20,12},{24,0},{28,4},{1,25},{... | collective-permute-start | bytes 786440 | tf_op jit(solution)/shard_map/ppermute | solution.py:352
  39.1 0.0 collective-permute-done.10.mate_near_t_1_
  39.1 0.0 collective-permute-start.22
  39.1 0.0 collective-permute-done.11.mate_near_t_2_
  39.1 10.3 %lift.1 = (bf16[256,512]{1,0:T(8,128)(2,1)S(1)}, bf16[8,256,64]{2,1,0:T(8,128)(2,1)S(1)}, bf16[2,1024,64]{2,1,0:T(8,128)(2,1)S(1)}, bf16[2,80,1024]{2,1,0:T(8,128)(2,1)S(1)}, bf16[256,1024]{1,0:T(8,128)(2,1)S(1)}) custom-call(s32[3]{0:T(128)S(1)} %pad_add_fusion.where_ref, s32[8,256]{1,0:T(8,128)S(1)} %pad.4.ids_refs_0_, ...), custom_call_target="tpu_custom_call" | custom-call | flops 5000000000 | bytes 4194304 | tf_op jit(solution)/shard_map/lift/pallas_call | solution.py:400
  49.4 0.0 collective-permute-done.18.near_0_
  49.4 1.6 %collective-permute-done.20.near_2_ = bf16[128,1024]{1,0:T(8,128)(2,1)S(1)} collective-permute-done((bf16[128,1024]{1,0:T(8,128)(2,1)S(1)}, bf16[128,1024]{1,0:T(8,128)(2,1)S(1)}, u32[]{:S(2)}, u32[]{:S(2)}) %collective-permute-start.20) | collective-permute-done | bytes 262176 | tf_op jit(solution)/shard_map/ppermute | solution.py:352
  51.0 0.0 collective-permute-start.21
  51.0 0.0 collective-permute-start.23
  51.0 0.5 collective-permute-start.24
  51.5 0.0 collective-permute-start.25
  51.6 4.3 %own_block.1.own_att = bf16[256,512]{1,0:T(8,128)(2,1)S(1)} custom-call(s32[3]{0:T(128)S(1)} %pad_add_fusion.where_ref, bf16[8,256,64]{2,1,0:T(8,128)(2,1)S(1)} %get-tuple-element.35.query_ref, bf16[2,1024,64]{2,1,0:T(8,128)(2,1)S(1)} %get-tuple-element.36.k_ref, bf16[2,80,1024]{2,1,0:T(8,128)(2,1)S(1)} %get-tuple-element.37.v_ref), custom_call_target="tpu_custom_call" | custom-call | flops 3000000000 | bytes 4194304 | tf_op jit(solution)/shard_map/own_block/pallas_call | solution.py:421
  55.9 0.0 collective-permute-done.22.mate_own
  55.9 2.8 %collective-permute-done.21.mate_att = bf16[256,512]{1,0:T(8,128)(2,1)S(1)} collective-permute-done((bf16[256,512]{1,0:T(8,128)(2,1)S(1)}, bf16[256,512]{1,0:T(8,128)(2,1)S(1)}, u32[]{:S(2)}, u32[]{:S(2)}) %collective-permute-start.21) | collective-permute-done | bytes 262176 | tf_op jit(solution)/shard_map/ppermute | solution.py:355
  58.7 0.0 collective-permute-done.23.mate_near_0_
  58.7 0.0 collective-permute-done.24.mate_near_1_
  58.7 2.4 %project_out.1 = (bf16[256,1024]{1,0:T(8,128)(2,1)}, f32[1,256]{1,0:T(1,128)}) custom-call(s32[3]{0:T(128)S(1)} %pad_add_fusion.where_ref, bf16[256,512]{1,0:T(8,128)(2,1)S(1)} %own_block.1.own_att, bf16[256,512]{1,0:T(8,128)(2,1)S(1)} %collective-permute-done.21.mate_att, bf16[128,1024]{1,0:T(8,128)(2,1)S(1)} %copy-done.5, ...), custom_call_target="tpu_custom_call" | custom-call | flops 1000000000 | bytes 4194304 | tf_op jit(solution)/shard_map/project_out/pallas_call | solution.py:424
  (17 shorter events, 0.0 us)
Async XLA Ops:
  0.6 5.3 %copy-start = (bf16[256,768]{1,0:T(8,128)(2,1)S(1)}, bf16[256,768]{1,0:T(8,128)(2,1)}, u32[]{:S(2)}) copy-start(bf16[256,768]{1,0:T(8,128)(2,1)} %bytes_ref.1) | copy-start | bytes 1179652
  0.6 6.8 %collective-permute-start = (bf16[384,1024]{1,0:T(8,128)(2,1)}, bf16[384,1024]{1,0:T(8,128)(2,1)S(1)}, u32[]{:S(2)}, u32[]{:S(2)}) collective-permute-start(bf16[384,1024]{1,0:T(8,128)(2,1)} %param.11), channel_id=1, source_target_pairs={{0,4},{4,0},{8,12},{12,8},{16,20},{20,16},{24,28},{28,24},{1,5},{5... | collective-permute-start | bytes 2359304 | tf_op jit(solution)/shard_map/ppermute | solution.py:352
  0.8 1.0 %copy-start.1 = (bf16[128,1536]{1,0:T(8,128)(2,1)S(1)}, bf16[128,1536]{1,0:T(8,128)(2,1)}, u32[]{:S(2)}) copy-start(bf16[128,1536]{1,0:T(8,128)(2,1)} %qkv_ref.1) | copy-start | bytes 1179652
  2.4 7.8 %collective-permute-start.1 = (bf16[128,768]{1,0:T(8,128)(2,1)S(1)}, bf16[128,768]{1,0:T(8,128)(2,1)S(1)}, u32[]{:S(2)}, u32[]{:S(2)}) collective-permute-start(bf16[128,768]{1,0:T(8,128)(2,1)S(1)} %qkv_part.1.own_w), channel_id=1, source_target_pairs={{0,8},{4,12},{8,0},{12,4},{16,24},{20,28},{24,16},{28,20},{1,9},{5... | collective-permute-start | bytes 589832 | tf_op jit(solution)/shard_map/ppermute | solution.py:352
  3.9 16.8 %collective-permute-start.12 = (bf16[128,768]{1,0:T(8,128)(2,1)S(1)}, bf16[128,768]{1,0:T(8,128)(2,1)S(1)}, u32[]{:S(2)}, u32[]{:S(2)}) collective-permute-start(bf16[128,768]{1,0:T(8,128)(2,1)S(1)} %qkv_part.1.own_w), channel_id=1, source_target_pairs={{0,16},{4,20},{8,24},{12,28},{16,0},{20,4},{24,8},{28,12},{1,17},{... | collective-permute-start | bytes 589832 | tf_op jit(solution)/shard_map/ppermute | solution.py:352
  5.5 15.7 %collective-permute-start.13 = (bf16[128,768]{1,0:T(8,128)(2,1)S(1)}, bf16[128,768]{1,0:T(8,128)(2,1)S(1)}, u32[]{:S(2)}, u32[]{:S(2)}) collective-permute-start(bf16[128,768]{1,0:T(8,128)(2,1)S(1)} %qkv_part.1.own_w), channel_id=1, source_target_pairs={{0,24},{4,28},{8,16},{12,20},{16,8},{20,12},{24,0},{28,4},{1,25},{... | collective-permute-start | bytes 589832 | tf_op jit(solution)/shard_map/ppermute | solution.py:352
  5.9 1.5 %copy-start.2 = (f32[520,128]{1,0:T(8,128)S(1)}, f32[520,128]{1,0:T(8,128)}, u32[]{:S(2)}) copy-start(f32[520,128]{1,0:T(8,128)} %constant.44.clone.rope_ref) | copy-start | bytes 798724
  6.0 1.5 %copy-start.3 = (s32[1,256]{1,0:T(1,128)S(1)}, s32[1,256]{1,0:T(1,128)}, u32[]{:S(2)}) copy-start(s32[1,256]{1,0:T(1,128)} %align_ref.1) | copy-start | bytes 3076
  7.5 6.7 %copy-start.6 = (s32[1,1024]{1,0:T(1,128)S(1)}, s32[1,1024]{1,0:T(1,128)}, u32[]{:S(2)}) copy-start(s32[1,1024]{1,0:T(1,128)} %param.9) | copy-start | bytes 12292
  8.4 26.9 %copy-start.5 = (bf16[128,1024]{1,0:T(8,128)(2,1)S(1)}, bf16[128,1024]{1,0:T(8,128)(2,1)}, u32[]{:S(2)}) copy-start(bf16[128,1024]{1,0:T(8,128)(2,1)} %own) | copy-start | bytes 786436
  10.2 21.6 %collective-permute-start.2 = (bf16[128,1024]{1,0:T(8,128)(2,1)S(1)}, bf16[128,1024]{1,0:T(8,128)(2,1)S(1)}, u32[]{:S(2)}, u32[]{:S(2)}) collective-permute-start(bf16[128,1024]{1,0:T(8,128)(2,1)S(1)} %get-tuple-element.26.own_t), channel_id=1, source_target_pairs={{0,24},{4,28},{8,16},{12,20},{16,8},{20,12},{24,0},{28,4},{1,25},{... | collective-permute-start | bytes 786440 | tf_op jit(solution)/shard_map/ppermute | solution.py:352
  12.6 19.7 %collective-permute-start.6 = (bf16[128,1024]{1,0:T(8,128)(2,1)S(1)}, bf16[128,1024]{1,0:T(8,128)(2,1)S(1)}, u32[]{:S(2)}, u32[]{:S(2)}) collective-permute-start(bf16[128,1024]{1,0:T(8,128)(2,1)S(1)} %get-tuple-element.26.own_t), channel_id=1, source_target_pairs={{0,8},{4,12},{8,0},{12,4},{16,24},{20,28},{24,16},{28,20},{1,9},{5... | collective-permute-start | bytes 786440 | tf_op jit(solution)/shard_map/ppermute | solution.py:352
  13.1 19.6 %collective-permute-start.7 = (bf16[128,1024]{1,0:T(8,128)(2,1)S(1)}, bf16[128,1024]{1,0:T(8,128)(2,1)S(1)}, u32[]{:S(2)}, u32[]{:S(2)}) collective-permute-start(bf16[128,1024]{1,0:T(8,128)(2,1)S(1)} %get-tuple-element.26.own_t), channel_id=1, source_target_pairs={{0,16},{4,20},{8,24},{12,28},{16,0},{20,4},{24,8},{28,12},{1,17},{... | collective-permute-start | bytes 786440 | tf_op jit(solution)/shard_map/ppermute | solution.py:352
  15.0 18.6 %copy-start.7 = (bf16[1024]{0:T(1024)(128)(2,1)S(1)}, bf16[1024]{0:T(1024)(128)(2,1)}, u32[]{:S(2)}) copy-start(bf16[1024]{0:T(1024)(128)(2,1)} %param.14) | copy-start | bytes 6148
  20.7 3.7 %collective-permute-start.3 = (s32[8,256]{1,0:T(8,128)S(1)}, s32[8,256]{1,0:T(8,128)S(1)}, u32[]{:S(2)}, u32[]{:S(2)}) collective-permute-start(s32[8,256]{1,0:T(8,128)S(1)} %pad.4.ids_refs_0_), channel_id=1, source_target_pairs={{0,1},{1,0},{2,3},{3,2},{4,5},{5,4},{6,7},{7,6},{8,9},{9,8},{10,11... | collective-permute-start | bytes 24584 | tf_op jit(solution)/shard_map/ppermute | solution.py:355
  21.2 6.5 %collective-permute-start.4 = (s32[8,256]{1,0:T(8,128)S(1)}, s32[8,256]{1,0:T(8,128)S(1)}, u32[]{:S(2)}, u32[]{:S(2)}) collective-permute-start(s32[8,256]{1,0:T(8,128)S(1)} %pad.4.ids_refs_0_), channel_id=1, source_target_pairs={{0,2},{1,3},{4,6},{5,7},{8,10},{9,11},{12,14},{13,15},{16,18},{17,... | collective-permute-start | bytes 24584 | tf_op jit(solution)/shard_map/ppermute | solution.py:355
  24.4 7.3 %collective-permute-start.5 = (s32[8,256]{1,0:T(8,128)S(1)}, s32[8,256]{1,0:T(8,128)S(1)}, u32[]{:S(2)}, u32[]{:S(2)}) collective-permute-start(s32[8,256]{1,0:T(8,128)S(1)} %pad.4.ids_refs_0_), channel_id=1, source_target_pairs={{0,3},{1,2},{4,7},{5,6},{8,11},{9,10},{12,15},{13,14},{16,19},{17,... | collective-permute-start | bytes 24584 | tf_op jit(solution)/shard_map/ppermute | solution.py:355
  27.7 4.6 %collective-permute-start.14 = (bf16[128,768]{1,0:T(8,128)(2,1)S(1)}, bf16[128,768]{1,0:T(8,128)(2,1)S(1)}, u32[]{:S(2)}, u32[]{:S(2)}) collective-permute-start(bf16[128,768]{1,0:T(8,128)(2,1)S(1)} %qkv_part.1.own_w), channel_id=1, source_target_pairs={{0,4},{4,0},{8,12},{12,8},{16,20},{20,16},{24,28},{28,24},{1,5},{5... | collective-permute-start | bytes 589832 | tf_op jit(solution)/shard_map/ppermute | solution.py:352
  31.7 1.4 %collective-permute-start.16 = (bf16[128,768]{1,0:T(8,128)(2,1)S(1)}, bf16[128,768]{1,0:T(8,128)(2,1)S(1)}, u32[]{:S(2)}, u32[]{:S(2)}) collective-permute-start(bf16[128,768]{1,0:T(8,128)(2,1)S(1)} %collective-permute-done.12.near_w_1_), channel_id=1, source_target_pairs={{0,4},{4,0},{8,12},{12,8},{16,20},{20,16},{24,28},{28,24},{1,5},{5... | collective-permute-start | bytes 589832 | tf_op jit(solution)/shard_map/ppermute | solution.py:352
  31.7 1.7 %collective-permute-start.17 = (bf16[128,768]{1,0:T(8,128)(2,1)S(1)}, bf16[128,768]{1,0:T(8,128)(2,1)S(1)}, u32[]{:S(2)}, u32[]{:S(2)}) collective-permute-start(bf16[128,768]{1,0:T(8,128)(2,1)S(1)} %collective-permute-done.13.near_w_2_), channel_id=1, source_target_pairs={{0,4},{4,0},{8,12},{12,8},{16,20},{20,16},{24,28},{28,24},{1,5},{5... | collective-permute-start | bytes 589832 | tf_op jit(solution)/shard_map/ppermute | solution.py:352
  32.2 3.0 %collective-permute-start.8 = (bf16[128,1024]{1,0:T(8,128)(2,1)S(1)}, bf16[128,1024]{1,0:T(8,128)(2,1)S(1)}, u32[]{:S(2)}, u32[]{:S(2)}) collective-permute-start(bf16[128,1024]{1,0:T(8,128)(2,1)S(1)} %get-tuple-element.26.own_t), channel_id=1, source_target_pairs={{0,4},{4,0},{8,12},{12,8},{16,20},{20,16},{24,28},{28,24},{1,5},{5... | collective-permute-start | bytes 786440 | tf_op jit(solution)/shard_map/ppermute | solution.py:352
  32.3 5.3 %collective-permute-start.9 = (bf16[128,1024]{1,0:T(8,128)(2,1)S(1)}, bf16[128,1024]{1,0:T(8,128)(2,1)S(1)}, u32[]{:S(2)}, u32[]{:S(2)}) collective-permute-start(bf16[128,1024]{1,0:T(8,128)(2,1)S(1)} %collective-permute-done.6.near_t_0_), channel_id=1, source_target_pairs={{0,4},{4,0},{8,12},{12,8},{16,20},{20,16},{24,28},{28,24},{1,5},{5... | collective-permute-start | bytes 786440 | tf_op jit(solution)/shard_map/ppermute | solution.py:352
  32.8 6.3 %collective-permute-start.10 = (bf16[128,1024]{1,0:T(8,128)(2,1)S(1)}, bf16[128,1024]{1,0:T(8,128)(2,1)S(1)}, u32[]{:S(2)}, u32[]{:S(2)}) collective-permute-start(bf16[128,1024]{1,0:T(8,128)(2,1)S(1)} %collective-permute-done.7.near_t_1_), channel_id=1, source_target_pairs={{0,4},{4,0},{8,12},{12,8},{16,20},{20,16},{24,28},{28,24},{1,5},{5... | collective-permute-start | bytes 786440 | tf_op jit(solution)/shard_map/ppermute | solution.py:352
  33.2 5.9 %collective-permute-start.11 = (bf16[128,1024]{1,0:T(8,128)(2,1)S(1)}, bf16[128,1024]{1,0:T(8,128)(2,1)S(1)}, u32[]{:S(2)}, u32[]{:S(2)}) collective-permute-start(bf16[128,1024]{1,0:T(8,128)(2,1)S(1)} %collective-permute-done.2.near_t_2_), channel_id=1, source_target_pairs={{0,4},{4,0},{8,12},{12,8},{16,20},{20,16},{24,28},{28,24},{1,5},{5... | collective-permute-start | bytes 786440 | tf_op jit(solution)/shard_map/ppermute | solution.py:352
  33.4 1.8 %collective-permute-start.15 = (bf16[128,768]{1,0:T(8,128)(2,1)S(1)}, bf16[128,768]{1,0:T(8,128)(2,1)S(1)}, u32[]{:S(2)}, u32[]{:S(2)}) collective-permute-start(bf16[128,768]{1,0:T(8,128)(2,1)S(1)} %collective-permute-done.1.near_w_0_), channel_id=1, source_target_pairs={{0,4},{4,0},{8,12},{12,8},{16,20},{20,16},{24,28},{28,24},{1,5},{5... | collective-permute-start | bytes 589832 | tf_op jit(solution)/shard_map/ppermute | solution.py:352
  35.2 14.2 %collective-permute-start.18 = (bf16[128,1024]{1,0:T(8,128)(2,1)S(1)}, bf16[128,1024]{1,0:T(8,128)(2,1)S(1)}, u32[]{:S(2)}, u32[]{:S(2)}) collective-permute-start(bf16[128,1024]{1,0:T(8,128)(2,1)S(1)} %copy-done.5), channel_id=1, source_target_pairs={{0,8},{4,12},{8,0},{12,4},{16,24},{20,28},{24,16},{28,20},{1,9},{5... | collective-permute-start | bytes 786440 | tf_op jit(solution)/shard_map/ppermute | solution.py:352
  35.2 14.2 %collective-permute-start.19 = (bf16[128,1024]{1,0:T(8,128)(2,1)S(1)}, bf16[128,1024]{1,0:T(8,128)(2,1)S(1)}, u32[]{:S(2)}, u32[]{:S(2)}) collective-permute-start(bf16[128,1024]{1,0:T(8,128)(2,1)S(1)} %copy-done.5), channel_id=1, source_target_pairs={{0,16},{4,20},{8,24},{12,28},{16,0},{20,4},{24,8},{28,12},{1,17},{... | collective-permute-start | bytes 786440 | tf_op jit(solution)/shard_map/ppermute | solution.py:352
  37.6 13.4 %collective-permute-start.20 = (bf16[128,1024]{1,0:T(8,128)(2,1)S(1)}, bf16[128,1024]{1,0:T(8,128)(2,1)S(1)}, u32[]{:S(2)}, u32[]{:S(2)}) collective-permute-start(bf16[128,1024]{1,0:T(8,128)(2,1)S(1)} %copy-done.5), channel_id=1, source_target_pairs={{0,24},{4,28},{8,16},{12,20},{16,8},{20,12},{24,0},{28,4},{1,25},{... | collective-permute-start | bytes 786440 | tf_op jit(solution)/shard_map/ppermute | solution.py:352
  39.1 16.8 %collective-permute-start.22 = (bf16[128,1024]{1,0:T(8,128)(2,1)S(1)}, bf16[128,1024]{1,0:T(8,128)(2,1)S(1)}, u32[]{:S(2)}, u32[]{:S(2)}) collective-permute-start(bf16[128,1024]{1,0:T(8,128)(2,1)S(1)} %copy-done.5), channel_id=1, source_target_pairs={{0,4},{4,0},{8,12},{12,8},{16,20},{20,16},{24,28},{28,24},{1,5},{5... | collective-permute-start | bytes 786440 | tf_op jit(solution)/shard_map/ppermute | solution.py:352
  51.0 7.6 %collective-permute-start.21 = (bf16[256,512]{1,0:T(8,128)(2,1)S(1)}, bf16[256,512]{1,0:T(8,128)(2,1)S(1)}, u32[]{:S(2)}, u32[]{:S(2)}) collective-permute-start(bf16[256,512]{1,0:T(8,128)(2,1)S(1)} %get-tuple-element.40), channel_id=1, source_target_pairs={{0,1},{1,0},{2,3},{3,2},{4,5},{5,4},{6,7},{7,6},{8,9},{9,8},{10,11... | collective-permute-start | bytes 786440 | tf_op jit(solution)/shard_map/ppermute | solution.py:355
  51.0 7.6 %collective-permute-start.23 = (bf16[128,1024]{1,0:T(8,128)(2,1)S(1)}, bf16[128,1024]{1,0:T(8,128)(2,1)S(1)}, u32[]{:S(2)}, u32[]{:S(2)}) collective-permute-start(bf16[128,1024]{1,0:T(8,128)(2,1)S(1)} %collective-permute-done.18.near_0_), channel_id=1, source_target_pairs={{0,4},{4,0},{8,12},{12,8},{16,20},{20,16},{24,28},{28,24},{1,5},{5... | collective-permute-start | bytes 786440 | tf_op jit(solution)/shard_map/ppermute | solution.py:352
  51.0 7.6 %collective-permute-start.24 = (bf16[128,1024]{1,0:T(8,128)(2,1)S(1)}, bf16[128,1024]{1,0:T(8,128)(2,1)S(1)}, u32[]{:S(2)}, u32[]{:S(2)}) collective-permute-start(bf16[128,1024]{1,0:T(8,128)(2,1)S(1)} %collective-permute-done.19.near_1_), channel_id=1, source_target_pairs={{0,4},{4,0},{8,12},{12,8},{16,20},{20,16},{24,28},{28,24},{1,5},{5... | collective-permute-start | bytes 786440 | tf_op jit(solution)/shard_map/ppermute | solution.py:352
  51.5 7.1 %collective-permute-start.25 = (bf16[128,1024]{1,0:T(8,128)(2,1)S(1)}, bf16[128,1024]{1,0:T(8,128)(2,1)S(1)}, u32[]{:S(2)}, u32[]{:S(2)}) collective-permute-start(bf16[128,1024]{1,0:T(8,128)(2,1)S(1)} %collective-permute-done.20.near_2_), channel_id=1, source_target_pairs={{0,4},{4,0},{8,12},{12,8},{16,20},{20,16},{24,28},{28,24},{1,5},{5... | collective-permute-start | bytes 786440 | tf_op jit(solution)/shard_map/ppermute | solution.py:352
  51.5 7.1 %copy-start.4 = (bf16[1,256,1024]{2,1,0:T(8,128)(2,1)S(1)}, bf16[1,256,1024]{2,1,0:T(8,128)(2,1)}, u32[]{:S(2)}) copy-start(bf16[1,256,1024]{2,1,0:T(8,128)(2,1)} %param.15) | copy-start | bytes 1572868

commit v5 on v4

--- a/solution.py
+++ b/solution.py
@@ -215,9 +215,9 @@
 
 
 def lift_kernel(
-    where_ref, ids_refs, own_t, near_t, mate_own_t, mate_near_t, own_w, near_w, mate_own_w, mate_near_w,
+    where_ref, ids_ref, own_t, near_t, mate_own_t, mate_near_t, own_w, near_w, mate_own_w, mate_near_w,
     gain_ref, rope_ref, att_ref, query_ref, k_s, v_s, lat_ref,
-    table_s, weight_s, ids_s, lat_s, q_s,
+    table_s, weight_s, lat_s, q_s,
 ):
     chip, core, ctx = where_ref[0], where_ref[1], where_ref[2]
     side, upper = ctx % 2, ctx // 2
@@ -227,16 +227,12 @@
         table_s[span, :] = piece[...]
     for span, piece in ordered(chip, core, (own_w, near_w, mate_own_w, mate_near_w)):
         weight_s[span, :] = piece[...]
-    own_ids, pair_ids, past_ids, cross_ids = ids_refs
-    ids_s[side] = past_ids[...]
-    ids_s[1 - side] = cross_ids[...]
-    ids_s[2 + side] = own_ids[...]
-    ids_s[3 - side] = pair_ids[...]
     gain = gain_ref[...].astype(jnp.float32)
     v_s[:, HD:, :] = jnp.ones((v_s.shape[0], v_s.shape[1] - HD, v_s.shape[2]), jnp.bfloat16)
 
     def lift(slot):
-        ids = jnp.transpose(ids_s[slot])
+        block = slot if slot < 2 else 2 * upper + slot - 2
+        ids = jnp.transpose(ids_ref[block])
         byte = lax.broadcasted_iota(jnp.int32, (rows, VOCAB), 1)
         one_hot = jnp.concatenate(
             [(ids[:, k : k + 1] == byte).astype(jnp.float32).astype(jnp.bfloat16) for k in range(KW)], axis=1
@@ -245,7 +241,6 @@
         wide = latent.astype(jnp.float32)
         scale = lax.rsqrt(jnp.mean(wide * wide, axis=1, keepdims=True) + norm_eps)
         normed = (wide * scale * gain).astype(jnp.bfloat16)
-        block = slot if slot < 2 else 2 * upper + slot - 2
         cos, sin = rope_at(rope_ref, rows, block)
         if slot >= 2:
             lat_s[slot - 2] = latent
@@ -376,19 +371,13 @@
         table_kernel, "tap_table", 8, 10**8, [SMEM] + [VMEM] * 5,
         [((half, features), bf16), (align.shape, jnp.int32), (rope.shape, f32)],
     )(where, byte_table, mate_conv, total, align, rope)
-    own_t, first = lax.optimization_barrier((own_t, near_w[0]))
-    near_w = (first,) + near_w[1:]
+    ids = jnp.broadcast_to(byte_ids, (n_ctx, byte_ids.shape[1]))
+    ids = lax.all_to_all(ids, "ctx", 0, 0, tiled=True)
+    own_t, near_w, ids = lax.optimization_barrier((own_t, near_w, ids))
     near_t = to_near(own_t)
-    ids = jnp.transpose(byte_ids[0].reshape(rows, KW))
-    ids = jnp.pad(ids, ((0, 8 - KW), (0, 0)))
-    ids, unused = lax.optimization_barrier((ids, own_t))
-    ids_all = (
-        ids,
-        along(ids, beside),
-        along(ids, [(0, 2), (1, 3)]),
-        along(ids, [(0, 3), (1, 2)]),
-    )
-    last, ids_all = lax.optimization_barrier((near_t[-1], ids_all))
+    ids = jnp.swapaxes(ids.reshape(n_ctx, rows, KW), 1, 2)
+    ids = jnp.pad(ids, ((0, 0), (0, 8 - KW), (0, 0)))
+    last, ids = lax.optimization_barrier((near_t[-1], ids))
     near_t = near_t[:-1] + (last,)
     t_pieces, w_pieces = to_mate(own_t, near_t), to_mate(part, near_w)
     out_own, unused = lax.optimization_barrier((w_out, near_t))
@@ -399,7 +388,7 @@
     att_shape = ((rows, q_width), bf16)
     att_mate, query, keys, values, latent = call(
         lift_kernel, "lift", 18, 5 * 10**9,
-        [SMEM, (VMEM,) * 4] + piece_specs + piece_specs + [VMEM, VMEM],
+        [SMEM, VMEM] + piece_specs + piece_specs + [VMEM, VMEM],
         [
             att_shape,
             ((HQ // 2, rows, HD), bf16),
@@ -410,11 +399,10 @@
         [
             ((KW * VOCAB, features), bf16),
             ((features, part_width), bf16),
-            ((4, 8, rows), jnp.int32),
             ((2, rows, features), bf16),
             ((2, HQ // 2, rows, HD), bf16),
         ],
-    )(where, ids_all, *t_pieces, *w_pieces, norm_gain[None], rope)
+    )(where, ids, *t_pieces, *w_pieces, norm_gain[None], rope)
 
     att_mate, out_near = lax.optimization_barrier((att_mate, out_near))
     att_back = along(att_mate, beside)

time: 62.3 us -> 61 us (0.979)
  waiting for transfers between devices: 21.9 us -> 13.6 us
  local copies, waits for them, and re-layouts: 1.75 us -> 5.58 us
  starting transfers between devices: 15.9 us -> 19.7 us
  other arithmetic: 0.74 us -> 0.08 us
    ppermute x4 -> x1, waiting for transfers between devices: 10.7 us -> 2.54 us  [along(): return lax.ppermute(x, 'ctx', pairs)]
    all_to_all x0 -> x1, starting transfers between devices: none -> 5.09 us  [head_body(): ids = lax.all_to_all(ids, 'ctx', 0, 0, tiled=True)]
    unnamed x17 -> x25, local copies, waits for them, and re-layouts: 1.54 us -> 4.23 us
    ppermute x4 -> x1, starting transfers between devices: 3.01 us -> 1.18 us  [along(): return lax.ppermute(x, 'ctx', pairs)]
    ppermute x22, waiting for transfers between devices: 11.1 us -> 10.2 us  [swap(): return lax.ppermute(x, 'fsdp', [(d, d ^ j) for d in range(n_fsdp)])]
    all_to_all x0 -> x1, waiting for transfers between devices: none -> 0.9 us  [head_body(): ids = lax.all_to_all(ids, 'ctx', 0, 0, tiled=True)]
    reshape x0 -> x2, local copies, waits for them, and re-layouts: none -> 0.72 us  [head_body(): ids = jnp.swapaxes(ids.reshape(n_ctx, rows, KW), 1, 2)]
    unnamed x1 -> x0, other arithmetic: 0.66 us -> none
  transfers between devices with their start and end apart: 26 -> 24, of which waited for: 10 -> 6; matrix products, arithmetic and copies ran while one was open for 5% -> 5% of each run, Pallas kernels for 26% -> 27%
where the time goes in v5:
time: 61 us; the launch traced here: 59.8 us
  starting transfers between devices  19.7 us (32%)
  Pallas kernels  18.5 us (30%)
  waiting for transfers between devices  13.6 us (22%)
  local copies, waits for them, and re-layouts  5.58 us (9%)
  matrix products  1.47 us (2%)
  between operations  0.86 us (1%)
    ppermute x22, starting transfers between devices, swap(): return lax.ppermute(x, 'fsdp', [(d, d ^ j) for d in range(n_fsdp)])  13.5 us
    pallas_call x1, Pallas kernels, head_body(): call(lift_kernel, 'lift', 18, 5 * 10 ** 9, [SMEM, VMEM] + piece_specs + p...  10.3 us
    ppermute x22, waiting for transfers between devices, swap(): return lax.ppermute(x, 'fsdp', [(d, d ^ j) for d in range(n_fsdp)])  10.2 us
    all_to_all x1, starting transfers between devices, head_body(): ids = lax.all_to_all(ids, 'ctx', 0, 0, tiled=True)  5.09 us
    pallas_call x1, Pallas kernels, head_body(): call(own_kernel, 'own_block', 12, 3 * 10 ** 9, [SMEM, VMEM, VMEM, VMEM],...  4.31 us
    unnamed x25, local copies, waits for them, and re-layouts  4.23 us
    ppermute x1, waiting for transfers between devices, along(): return lax.ppermute(x, 'ctx', pairs)  2.54 us
    pallas_call x1, Pallas kernels, head_body(): call(out_kernel, 'project_out', 12, 10 ** 9, [SMEM, VMEM, VMEM] + piece_s...  2.43 us
  transfers between devices with their start and end apart: 24, of which 6 were waited for; matrix products, arithmetic and copies ran while one was open for 5% of the time, Pallas kernels for 27%

profile of v5, /device:TPU:24, one launch (start us, length us, event | category | flops | bytes accessed | tf_op | source)
XLA Modules:
  0.0 59.8 jit_solution(16546460487818507781)
XLA Ops:
  0.6 0.1 collective-permute-start
  0.7 0.1 pad_add_fusion.where_ref
  0.8 1.0 %copy-done.1 = bf16[128,1536]{1,0:T(8,128)(2,1)S(1)} copy-done((bf16[128,1536]{1,0:T(8,128)(2,1)S(1)}, bf16[128,1536]{1,0:T(8,128)(2,1)}, u32[]{:S(2)}) %copy-start.1) | copy-done | bytes 393240
  1.8 0.6 qkv_part.1.own_w
  2.4 1.6 %collective-permute-start.1 = (bf16[128,768]{1,0:T(8,128)(2,1)S(1)}, bf16[128,768]{1,0:T(8,128)(2,1)S(1)}, u32[]{:S(2)}, u32[]{:S(2)}) collective-permute-start(bf16[128,768]{1,0:T(8,128)(2,1)S(1)} %qkv_part.1.own_w), channel_id=1, source_target_pairs={{0,8},{4,12},{8,0},{12,4},{16,24},{20,28},{24,16},{28,20},{1,9},{5... | collective-permute-start | bytes 589832 | tf_op jit(solution)/shard_map/ppermute | solution.py:347
  4.0 1.5 %collective-permute-start.2 = (bf16[128,768]{1,0:T(8,128)(2,1)S(1)}, bf16[128,768]{1,0:T(8,128)(2,1)S(1)}, u32[]{:S(2)}, u32[]{:S(2)}) collective-permute-start(bf16[128,768]{1,0:T(8,128)(2,1)S(1)} %qkv_part.1.own_w), channel_id=1, source_target_pairs={{0,16},{4,20},{8,24},{12,28},{16,0},{20,4},{24,8},{28,12},{1,17},{... | collective-permute-start | bytes 589832 | tf_op jit(solution)/shard_map/ppermute | solution.py:347
  5.5 0.5 collective-permute-start.3
  6.0 0.6 %broadcast_in_dim.11 = s32[4,1,1024]{2,1,0:T(1,128)} broadcast(s32[1024]{0:T(1024)S(1)} %bitcast.14), dimensions={2} | broadcast | bytes 20480 | tf_op jit(solution)/shard_map/broadcast_in_dim | solution.py:374
  6.6 5.1 %all-to-all-start = ((s32[4,1,1024]{2,1,0:T(1,128)}), s32[4,1,1024]{2,1,0:T(1,128)S(1)}, u32[]{:S(2)}, u32[]{:S(2)}) async-start(s32[4,1,1024]{2,1,0:T(1,128)} %broadcast_in_dim.11), calls=%async_computation | async-start | bytes 32768 | tf_op jit(solution)/shard_map/all_to_all | solution.py:375
  11.7 1.5 %fusion.total_ref = f32[128,1024]{1,0:T(8,128)S(1)} fusion(bf16[384,1024]{1,0:T(8,128)(2,1)} %param.11, bf16[256,768]{1,0:T(8,128)(2,1)S(1)} %copy-done, s32[]{:T(128)S(6)} %select_n.19, s32[]{:T(128)S(6)} %select_n.20), kind=kOutput, calls=%fused_computation | convolution fusion | flops 100663296 | bytes 1409032 | tf_op jit(solution)/shard_map/dot_general | solution.py:368
  13.1 0.0 copy-start.3
  13.2 0.9 %all-to-all-done = s32[4,1,1024]{2,1,0:T(1,128)S(1)} async-done(((s32[4,1,1024]{2,1,0:T(1,128)}), s32[4,1,1024]{2,1,0:T(1,128)S(1)}, u32[]{:S(2)}, u32[]{:S(2)}) %all-to-all-start) | async-done | bytes 16416 | tf_op jit(solution)/shard_map/all_to_all | solution.py:375
  14.1 0.0 collective-permute-done.conv_ref
  14.1 0.9 %tap_table.1 = (bf16[128,1024]{1,0:T(8,128)(2,1)S(1)}, s32[1,256]{1,0:T(1,128)S(1)}, f32[520,128]{1,0:T(8,128)S(1)}) custom-call(s32[3]{0:T(128)S(1)} %pad_add_fusion.where_ref, bf16[256,768]{1,0:T(8,128)(2,1)S(1)} %copy-done, bf16[384,1024]{1,0:T(8,128)(2,1)S(1)} %collective-permute-done.conv_ref, f32[128,1024]{1,0:T(8,128)S(1)} %fusion.total_ref, ...), custom_call_target="tpu_custom_call" | custom-call | flops 100000000 | bytes 4194304 | tf_op jit(solution)/shard_map/tap_table/pallas_call | solution.py:370
  15.0 0.0 collective-permute-done.1.near_w_0_
  15.0 0.2 collective-permute-done.2.near_w_1_
  15.2 0.0 collective-permute-done.3.near_w_2_
  15.2 2.3 %collective-permute-start.4 = (bf16[128,1024]{1,0:T(8,128)(2,1)S(1)}, bf16[128,1024]{1,0:T(8,128)(2,1)S(1)}, u32[]{:S(2)}, u32[]{:S(2)}) collective-permute-start(bf16[128,1024]{1,0:T(8,128)(2,1)S(1)} %get-tuple-element.25.own_t), channel_id=1, source_target_pairs={{0,24},{4,28},{8,16},{12,20},{16,8},{20,12},{24,0},{28,4},{1,25},{... | collective-permute-start | bytes 786440 | tf_op jit(solution)/shard_map/ppermute | solution.py:347
  17.5 0.6 %collective-permute-start.5 = (bf16[128,1024]{1,0:T(8,128)(2,1)S(1)}, bf16[128,1024]{1,0:T(8,128)(2,1)S(1)}, u32[]{:S(2)}, u32[]{:S(2)}) collective-permute-start(bf16[128,1024]{1,0:T(8,128)(2,1)S(1)} %get-tuple-element.25.own_t), channel_id=1, source_target_pairs={{0,8},{4,12},{8,0},{12,4},{16,24},{20,28},{24,16},{28,20},{1,9},{5... | collective-permute-start | bytes 786440 | tf_op jit(solution)/shard_map/ppermute | solution.py:347
  18.2 0.5 collective-permute-start.6
  18.7 0.0 collective-permute-start.11
  18.7 0.5 collective-permute-start.12
  19.2 6.2 %collective-permute-done.4.near_t_2_ = bf16[128,1024]{1,0:T(8,128)(2,1)S(1)} collective-permute-done((bf16[128,1024]{1,0:T(8,128)(2,1)S(1)}, bf16[128,1024]{1,0:T(8,128)(2,1)S(1)}, u32[]{:S(2)}, u32[]{:S(2)}) %collective-permute-start.4) | collective-permute-done | bytes 262176 | tf_op jit(solution)/shard_map/ppermute | solution.py:347
  25.4 0.0 collective-permute-start.13
  25.4 0.5 reshape.13
  25.9 0.0 copy-start.5
  25.9 0.2 copy.12
  26.1 0.0 collective-permute-done.11.mate_own_w
  26.1 0.6 collective-permute-start.7
  26.7 2.7 %collective-permute-done.5.near_t_0_ = bf16[128,1024]{1,0:T(8,128)(2,1)S(1)} collective-permute-done((bf16[128,1024]{1,0:T(8,128)(2,1)S(1)}, bf16[128,1024]{1,0:T(8,128)(2,1)S(1)}, u32[]{:S(2)}, u32[]{:S(2)}) %collective-permute-start.5) | collective-permute-done | bytes 262176 | tf_op jit(solution)/shard_map/ppermute | solution.py:347
  29.4 0.0 collective-permute-start.8
  29.4 0.0 collective-permute-done.6.near_t_1_
  29.4 0.5 collective-permute-start.9
  29.9 0.0 collective-permute-done.12.mate_near_w_0_
  29.9 0.7 %copy-done.6 = bf16[128,768]{1,0:T(8,128)(2,1)} copy-done((bf16[128,768]{1,0:T(8,128)(2,1)}, bf16[128,768]{1,0:T(8,128)(2,1)S(1)}, u32[]{:S(2)}) %copy-start.6) | copy-done | bytes 196632
  30.6 0.0 collective-permute-start.10
  30.6 0.0 collective-permute-done.13.mate_near_w_1_
  30.6 0.7 %copy-done.8 = bf16[128,768]{1,0:T(8,128)(2,1)} copy-done((bf16[128,768]{1,0:T(8,128)(2,1)}, bf16[128,768]{1,0:T(8,128)(2,1)S(1)}, u32[]{:S(2)}) %copy-start.8) | copy-done | bytes 196632
  31.2 0.5 collective-permute-start.14
  31.8 1.1 %collective-permute-done.14.mate_near_w_2_ = bf16[128,768]{1,0:T(8,128)(2,1)S(1)} collective-permute-done((bf16[128,768]{1,0:T(8,128)(2,1)S(1)}, bf16[128,768]{1,0:T(8,128)(2,1)S(1)}, u32[]{:S(2)}, u32[]{:S(2)}) %collective-permute-start.14) | collective-permute-done | bytes 196640 | tf_op jit(solution)/shard_map/ppermute | solution.py:347
  32.8 1.3 %collective-permute-start.15 = (bf16[128,1024]{1,0:T(8,128)(2,1)S(1)}, bf16[128,1024]{1,0:T(8,128)(2,1)S(1)}, u32[]{:S(2)}, u32[]{:S(2)}) collective-permute-start(bf16[128,1024]{1,0:T(8,128)(2,1)S(1)} %copy-done.5), channel_id=1, source_target_pairs={{0,8},{4,12},{8,0},{12,4},{16,24},{20,28},{24,16},{28,20},{1,9},{5... | collective-permute-start | bytes 786440 | tf_op jit(solution)/shard_map/ppermute | solution.py:347
  34.1 0.0 collective-permute-done.7.mate_own_t
  34.1 0.8 %collective-permute-start.16 = (bf16[128,1024]{1,0:T(8,128)(2,1)S(1)}, bf16[128,1024]{1,0:T(8,128)(2,1)S(1)}, u32[]{:S(2)}, u32[]{:S(2)}) collective-permute-start(bf16[128,1024]{1,0:T(8,128)(2,1)S(1)} %copy-done.5), channel_id=1, source_target_pairs={{0,16},{4,20},{8,24},{12,28},{16,0},{20,4},{24,8},{28,12},{1,17},{... | collective-permute-start | bytes 786440 | tf_op jit(solution)/shard_map/ppermute | solution.py:347
  34.9 0.0 collective-permute-done.8.mate_near_t_0_
  34.9 1.4 %collective-permute-start.17 = (bf16[128,1024]{1,0:T(8,128)(2,1)S(1)}, bf16[128,1024]{1,0:T(8,128)(2,1)S(1)}, u32[]{:S(2)}, u32[]{:S(2)}) collective-permute-start(bf16[128,1024]{1,0:T(8,128)(2,1)S(1)} %copy-done.5), channel_id=1, source_target_pairs={{0,24},{4,28},{8,16},{12,20},{16,8},{20,12},{24,0},{28,4},{1,25},{... | collective-permute-start | bytes 786440 | tf_op jit(solution)/shard_map/ppermute | solution.py:347
  36.3 0.0 collective-permute-done.9.mate_near_t_1_
  36.3 0.0 collective-permute-start.19
  36.3 0.0 collective-permute-done.10.mate_near_t_2_
  36.3 0.0 copy-start.7
  36.4 0.9 %copy-done.7 = bf16[128,768]{1,0:T(8,128)(2,1)S(1)} copy-done((bf16[128,768]{1,0:T(8,128)(2,1)S(1)}, bf16[128,768]{1,0:T(8,128)(2,1)}, u32[]{:S(2)}) %copy-start.7) | copy-done | bytes 196632
  37.3 0.9 %copy-done.9 = bf16[128,768]{1,0:T(8,128)(2,1)S(1)} copy-done((bf16[128,768]{1,0:T(8,128)(2,1)S(1)}, bf16[128,768]{1,0:T(8,128)(2,1)}, u32[]{:S(2)}) %copy-start.9) | copy-done | bytes 196632
  38.2 10.3 %lift.1 = (bf16[256,512]{1,0:T(8,128)(2,1)S(1)}, bf16[8,256,64]{2,1,0:T(8,128)(2,1)S(1)}, bf16[2,1024,64]{2,1,0:T(8,128)(2,1)S(1)}, bf16[2,80,1024]{2,1,0:T(8,128)(2,1)S(1)}, bf16[256,1024]{1,0:T(8,128)(2,1)S(1)}) custom-call(s32[3]{0:T(128)S(1)} %pad_add_fusion.where_ref, s32[4,8,256]{2,1,0:T(8,128)S(1)} %pad.4.ids_ref, ...), custom_call_target="tpu_custom_call" | custom-call | flops 5000000000 | bytes 4194304 | tf_op jit(solution)/shard_map/lift/pallas_call | solution.py:389
  48.5 0.0 collective-permute-done.15.near_0_
  48.5 0.0 collective-permute-done.16.near_1_
  48.5 0.0 collective-permute-done.17.near_2_
  48.5 1.2 %collective-permute-start.18 = (bf16[256,512]{1,0:T(8,128)(2,1)S(1)}, bf16[256,512]{1,0:T(8,128)(2,1)S(1)}, u32[]{:S(2)}, u32[]{:S(2)}) collective-permute-start(bf16[256,512]{1,0:T(8,128)(2,1)S(1)} %get-tuple-element.38), channel_id=1, source_target_pairs={{0,1},{1,0},{2,3},{3,2},{4,5},{5,4},{6,7},{7,6},{8,9},{9,8},{10,11... | collective-permute-start | bytes 786440 | tf_op jit(solution)/shard_map/ppermute | solution.py:350
  49.7 0.2 collective-permute-start.20
  49.9 0.3 collective-permute-start.21
  50.2 0.2 collective-permute-start.22
  50.5 4.3 %own_block.1.own_att = bf16[256,512]{1,0:T(8,128)(2,1)S(1)} custom-call(s32[3]{0:T(128)S(1)} %pad_add_fusion.where_ref, bf16[8,256,64]{2,1,0:T(8,128)(2,1)S(1)} %get-tuple-element.33.query_ref, bf16[2,1024,64]{2,1,0:T(8,128)(2,1)S(1)} %get-tuple-element.34.k_ref, bf16[2,80,1024]{2,1,0:T(8,128)(2,1)S(1)} %get-tuple-element.35.v_ref), custom_call_target="tpu_custom_call" | custom-call | flops 3000000000 | bytes 4194304 | tf_op jit(solution)/shard_map/own_block/pallas_call | solution.py:409
  54.8 0.0 collective-permute-done.19.mate_own
  54.8 2.5 %collective-permute-done.18.mate_att = bf16[256,512]{1,0:T(8,128)(2,1)S(1)} collective-permute-done((bf16[256,512]{1,0:T(8,128)(2,1)S(1)}, bf16[256,512]{1,0:T(8,128)(2,1)S(1)}, u32[]{:S(2)}, u32[]{:S(2)}) %collective-permute-start.18) | collective-permute-done | bytes 262176 | tf_op jit(solution)/shard_map/ppermute | solution.py:350
  57.3 0.0 collective-permute-done.20.mate_near_0_
  57.3 2.4 %project_out.1 = (bf16[256,1024]{1,0:T(8,128)(2,1)}, f32[1,256]{1,0:T(1,128)}) custom-call(s32[3]{0:T(128)S(1)} %pad_add_fusion.where_ref, bf16[256,512]{1,0:T(8,128)(2,1)S(1)} %own_block.1.own_att, bf16[256,512]{1,0:T(8,128)(2,1)S(1)} %collective-permute-done.18.mate_att, bf16[128,1024]{1,0:T(8,128)(2,1)S(1)} %copy-done.5, ...), custom_call_target="tpu_custom_call" | custom-call | flops 1000000000 | bytes 4194304 | tf_op jit(solution)/shard_map/project_out/pallas_call | solution.py:412
  (21 shorter events, 0.1 us)
Async XLA Ops:
  0.6 11.0 %copy-start = (bf16[256,768]{1,0:T(8,128)(2,1)S(1)}, bf16[256,768]{1,0:T(8,128)(2,1)}, u32[]{:S(2)}) copy-start(bf16[256,768]{1,0:T(8,128)(2,1)} %bytes_ref.1) | copy-start | bytes 1179652
  0.6 13.4 %collective-permute-start = (bf16[384,1024]{1,0:T(8,128)(2,1)}, bf16[384,1024]{1,0:T(8,128)(2,1)S(1)}, u32[]{:S(2)}, u32[]{:S(2)}) collective-permute-start(bf16[384,1024]{1,0:T(8,128)(2,1)} %param.11), channel_id=1, source_target_pairs={{0,4},{4,0},{8,12},{12,8},{16,20},{20,16},{24,28},{28,24},{1,5},{5... | collective-permute-start | bytes 2359304 | tf_op jit(solution)/shard_map/ppermute | solution.py:347
  0.8 1.0 %copy-start.1 = (bf16[128,1536]{1,0:T(8,128)(2,1)S(1)}, bf16[128,1536]{1,0:T(8,128)(2,1)}, u32[]{:S(2)}) copy-start(bf16[128,1536]{1,0:T(8,128)(2,1)} %qkv_ref.1) | copy-start | bytes 1179652
  1.8 4.1 %copy-start.10 = (s32[1,1024]{1,0:T(1,128)S(1)}, s32[1,1024]{1,0:T(1,128)}, u32[]{:S(2)}) copy-start(s32[1,1024]{1,0:T(1,128)} %param.9) | copy-start | bytes 12292
  2.4 12.6 %collective-permute-start.1 = (bf16[128,768]{1,0:T(8,128)(2,1)S(1)}, bf16[128,768]{1,0:T(8,128)(2,1)S(1)}, u32[]{:S(2)}, u32[]{:S(2)}) collective-permute-start(bf16[128,768]{1,0:T(8,128)(2,1)S(1)} %qkv_part.1.own_w), channel_id=1, source_target_pairs={{0,8},{4,12},{8,0},{12,4},{16,24},{20,28},{24,16},{28,20},{1,9},{5... | collective-permute-start | bytes 589832 | tf_op jit(solution)/shard_map/ppermute | solution.py:347
  4.0 11.2 %collective-permute-start.2 = (bf16[128,768]{1,0:T(8,128)(2,1)S(1)}, bf16[128,768]{1,0:T(8,128)(2,1)S(1)}, u32[]{:S(2)}, u32[]{:S(2)}) collective-permute-start(bf16[128,768]{1,0:T(8,128)(2,1)S(1)} %qkv_part.1.own_w), channel_id=1, source_target_pairs={{0,16},{4,20},{8,24},{12,28},{16,0},{20,4},{24,8},{28,12},{1,17},{... | collective-permute-start | bytes 589832 | tf_op jit(solution)/shard_map/ppermute | solution.py:347
  5.5 9.7 %collective-permute-start.3 = (bf16[128,768]{1,0:T(8,128)(2,1)S(1)}, bf16[128,768]{1,0:T(8,128)(2,1)S(1)}, u32[]{:S(2)}, u32[]{:S(2)}) collective-permute-start(bf16[128,768]{1,0:T(8,128)(2,1)S(1)} %qkv_part.1.own_w), channel_id=1, source_target_pairs={{0,24},{4,28},{8,16},{12,20},{16,8},{20,12},{24,0},{28,4},{1,25},{... | collective-permute-start | bytes 589832 | tf_op jit(solution)/shard_map/ppermute | solution.py:347
  6.6 7.5 %all-to-all-start = ((s32[4,1,1024]{2,1,0:T(1,128)}), s32[4,1,1024]{2,1,0:T(1,128)S(1)}, u32[]{:S(2)}, u32[]{:S(2)}) async-start(s32[4,1,1024]{2,1,0:T(1,128)} %broadcast_in_dim.11), calls=%async_computation | async-start | bytes 32768 | tf_op jit(solution)/shard_map/all_to_all | solution.py:375
  11.7 2.4 %copy-start.2 = (f32[520,128]{1,0:T(8,128)S(1)}, f32[520,128]{1,0:T(8,128)}, u32[]{:S(2)}) copy-start(f32[520,128]{1,0:T(8,128)} %constant.44.clone.rope_ref) | copy-start | bytes 798724
  13.1 0.9 %copy-start.3 = (s32[1,256]{1,0:T(1,128)S(1)}, s32[1,256]{1,0:T(1,128)}, u32[]{:S(2)}) copy-start(s32[1,256]{1,0:T(1,128)} %align_ref.1) | copy-start | bytes 3076
  15.2 10.2 %collective-permute-start.4 = (bf16[128,1024]{1,0:T(8,128)(2,1)S(1)}, bf16[128,1024]{1,0:T(8,128)(2,1)S(1)}, u32[]{:S(2)}, u32[]{:S(2)}) collective-permute-start(bf16[128,1024]{1,0:T(8,128)(2,1)S(1)} %get-tuple-element.25.own_t), channel_id=1, source_target_pairs={{0,24},{4,28},{8,16},{12,20},{16,8},{20,12},{24,0},{28,4},{1,25},{... | collective-permute-start | bytes 786440 | tf_op jit(solution)/shard_map/ppermute | solution.py:347
  17.5 11.9 %collective-permute-start.5 = (bf16[128,1024]{1,0:T(8,128)(2,1)S(1)}, bf16[128,1024]{1,0:T(8,128)(2,1)S(1)}, u32[]{:S(2)}, u32[]{:S(2)}) collective-permute-start(bf16[128,1024]{1,0:T(8,128)(2,1)S(1)} %get-tuple-element.25.own_t), channel_id=1, source_target_pairs={{0,8},{4,12},{8,0},{12,4},{16,24},{20,28},{24,16},{28,20},{1,9},{5... | collective-permute-start | bytes 786440 | tf_op jit(solution)/shard_map/ppermute | solution.py:347
  18.2 11.2 %collective-permute-start.6 = (bf16[128,1024]{1,0:T(8,128)(2,1)S(1)}, bf16[128,1024]{1,0:T(8,128)(2,1)S(1)}, u32[]{:S(2)}, u32[]{:S(2)}) collective-permute-start(bf16[128,1024]{1,0:T(8,128)(2,1)S(1)} %get-tuple-element.25.own_t), channel_id=1, source_target_pairs={{0,16},{4,20},{8,24},{12,28},{16,0},{20,4},{24,8},{28,12},{1,17},{... | collective-permute-start | bytes 786440 | tf_op jit(solution)/shard_map/ppermute | solution.py:347
  18.7 7.5 %collective-permute-start.11 = (bf16[128,768]{1,0:T(8,128)(2,1)S(1)}, bf16[128,768]{1,0:T(8,128)(2,1)S(1)}, u32[]{:S(2)}, u32[]{:S(2)}) collective-permute-start(bf16[128,768]{1,0:T(8,128)(2,1)S(1)} %qkv_part.1.own_w), channel_id=1, source_target_pairs={{0,4},{4,0},{8,12},{12,8},{16,20},{20,16},{24,28},{28,24},{1,5},{5... | collective-permute-start | bytes 589832 | tf_op jit(solution)/shard_map/ppermute | solution.py:347
  18.7 11.2 %collective-permute-start.12 = (bf16[128,768]{1,0:T(8,128)(2,1)S(1)}, bf16[128,768]{1,0:T(8,128)(2,1)S(1)}, u32[]{:S(2)}, u32[]{:S(2)}) collective-permute-start(bf16[128,768]{1,0:T(8,128)(2,1)S(1)} %collective-permute-done.1.near_w_0_), channel_id=1, source_target_pairs={{0,4},{4,0},{8,12},{12,8},{16,20},{20,16},{24,28},{28,24},{1,5},{5... | collective-permute-start | bytes 589832 | tf_op jit(solution)/shard_map/ppermute | solution.py:347
  25.4 5.2 %collective-permute-start.13 = (bf16[128,768]{1,0:T(8,128)(2,1)S(1)}, bf16[128,768]{1,0:T(8,128)(2,1)S(1)}, u32[]{:S(2)}, u32[]{:S(2)}) collective-permute-start(bf16[128,768]{1,0:T(8,128)(2,1)S(1)} %collective-permute-done.2.near_w_1_), channel_id=1, source_target_pairs={{0,4},{4,0},{8,12},{12,8},{16,20},{20,16},{24,28},{28,24},{1,5},{5... | collective-permute-start | bytes 589832 | tf_op jit(solution)/shard_map/ppermute | solution.py:347
  25.9 6.9 %copy-start.5 = (bf16[128,1024]{1,0:T(8,128)(2,1)S(1)}, bf16[128,1024]{1,0:T(8,128)(2,1)}, u32[]{:S(2)}) copy-start(bf16[128,1024]{1,0:T(8,128)(2,1)} %own) | copy-start | bytes 786436
  26.1 5.6 %copy-start.11 = (bf16[1024]{0:T(1024)(128)(2,1)S(1)}, bf16[1024]{0:T(1024)(128)(2,1)}, u32[]{:S(2)}) copy-start(bf16[1024]{0:T(1024)(128)(2,1)} %param.14) | copy-start | bytes 6148
  26.1 8.0 %collective-permute-start.7 = (bf16[128,1024]{1,0:T(8,128)(2,1)S(1)}, bf16[128,1024]{1,0:T(8,128)(2,1)S(1)}, u32[]{:S(2)}, u32[]{:S(2)}) collective-permute-start(bf16[128,1024]{1,0:T(8,128)(2,1)S(1)} %get-tuple-element.25.own_t), channel_id=1, source_target_pairs={{0,4},{4,0},{8,12},{12,8},{16,20},{20,16},{24,28},{28,24},{1,5},{5... | collective-permute-start | bytes 786440 | tf_op jit(solution)/shard_map/ppermute | solution.py:347
  29.4 5.6 %collective-permute-start.8 = (bf16[128,1024]{1,0:T(8,128)(2,1)S(1)}, bf16[128,1024]{1,0:T(8,128)(2,1)S(1)}, u32[]{:S(2)}, u32[]{:S(2)}) collective-permute-start(bf16[128,1024]{1,0:T(8,128)(2,1)S(1)} %collective-permute-done.5.near_t_0_), channel_id=1, source_target_pairs={{0,4},{4,0},{8,12},{12,8},{16,20},{20,16},{24,28},{28,24},{1,5},{5... | collective-permute-start | bytes 786440 | tf_op jit(solution)/shard_map/ppermute | solution.py:347
  29.4 7.0 %collective-permute-start.9 = (bf16[128,1024]{1,0:T(8,128)(2,1)S(1)}, bf16[128,1024]{1,0:T(8,128)(2,1)S(1)}, u32[]{:S(2)}, u32[]{:S(2)}) collective-permute-start(bf16[128,1024]{1,0:T(8,128)(2,1)S(1)} %collective-permute-done.6.near_t_1_), channel_id=1, source_target_pairs={{0,4},{4,0},{8,12},{12,8},{16,20},{20,16},{24,28},{28,24},{1,5},{5... | collective-permute-start | bytes 786440 | tf_op jit(solution)/shard_map/ppermute | solution.py:347
  29.9 0.7 %copy-start.6 = (bf16[128,768]{1,0:T(8,128)(2,1)}, bf16[128,768]{1,0:T(8,128)(2,1)S(1)}, u32[]{:S(2)}) copy-start(bf16[128,768]{1,0:T(8,128)(2,1)S(1)} %collective-permute-done.12.mate_near_w_0_) | copy-start | bytes 589828
  30.6 5.8 %collective-permute-start.10 = (bf16[128,1024]{1,0:T(8,128)(2,1)S(1)}, bf16[128,1024]{1,0:T(8,128)(2,1)S(1)}, u32[]{:S(2)}, u32[]{:S(2)}) collective-permute-start(bf16[128,1024]{1,0:T(8,128)(2,1)S(1)} %collective-permute-done.4.near_t_2_), channel_id=1, source_target_pairs={{0,4},{4,0},{8,12},{12,8},{16,20},{20,16},{24,28},{28,24},{1,5},{5... | collective-permute-start | bytes 786440 | tf_op jit(solution)/shard_map/ppermute | solution.py:347
  30.6 0.7 %copy-start.8 = (bf16[128,768]{1,0:T(8,128)(2,1)}, bf16[128,768]{1,0:T(8,128)(2,1)S(1)}, u32[]{:S(2)}) copy-start(bf16[128,768]{1,0:T(8,128)(2,1)S(1)} %collective-permute-done.13.mate_near_w_1_) | copy-start | bytes 589828
  31.2 1.6 %collective-permute-start.14 = (bf16[128,768]{1,0:T(8,128)(2,1)S(1)}, bf16[128,768]{1,0:T(8,128)(2,1)S(1)}, u32[]{:S(2)}, u32[]{:S(2)}) collective-permute-start(bf16[128,768]{1,0:T(8,128)(2,1)S(1)} %collective-permute-done.3.near_w_2_), channel_id=1, source_target_pairs={{0,4},{4,0},{8,12},{12,8},{16,20},{20,16},{24,28},{28,24},{1,5},{5... | collective-permute-start | bytes 589832 | tf_op jit(solution)/shard_map/ppermute | solution.py:347
  32.8 15.7 %collective-permute-start.15 = (bf16[128,1024]{1,0:T(8,128)(2,1)S(1)}, bf16[128,1024]{1,0:T(8,128)(2,1)S(1)}, u32[]{:S(2)}, u32[]{:S(2)}) collective-permute-start(bf16[128,1024]{1,0:T(8,128)(2,1)S(1)} %copy-done.5), channel_id=1, source_target_pairs={{0,8},{4,12},{8,0},{12,4},{16,24},{20,28},{24,16},{28,20},{1,9},{5... | collective-permute-start | bytes 786440 | tf_op jit(solution)/shard_map/ppermute | solution.py:347
  34.1 14.4 %collective-permute-start.16 = (bf16[128,1024]{1,0:T(8,128)(2,1)S(1)}, bf16[128,1024]{1,0:T(8,128)(2,1)S(1)}, u32[]{:S(2)}, u32[]{:S(2)}) collective-permute-start(bf16[128,1024]{1,0:T(8,128)(2,1)S(1)} %copy-done.5), channel_id=1, source_target_pairs={{0,16},{4,20},{8,24},{12,28},{16,0},{20,4},{24,8},{28,12},{1,17},{... | collective-permute-start | bytes 786440 | tf_op jit(solution)/shard_map/ppermute | solution.py:347
  34.9 13.6 %collective-permute-start.17 = (bf16[128,1024]{1,0:T(8,128)(2,1)S(1)}, bf16[128,1024]{1,0:T(8,128)(2,1)S(1)}, u32[]{:S(2)}, u32[]{:S(2)}) collective-permute-start(bf16[128,1024]{1,0:T(8,128)(2,1)S(1)} %copy-done.5), channel_id=1, source_target_pairs={{0,24},{4,28},{8,16},{12,20},{16,8},{20,12},{24,0},{28,4},{1,25},{... | collective-permute-start | bytes 786440 | tf_op jit(solution)/shard_map/ppermute | solution.py:347
  36.3 18.4 %collective-permute-start.19 = (bf16[128,1024]{1,0:T(8,128)(2,1)S(1)}, bf16[128,1024]{1,0:T(8,128)(2,1)S(1)}, u32[]{:S(2)}, u32[]{:S(2)}) collective-permute-start(bf16[128,1024]{1,0:T(8,128)(2,1)S(1)} %copy-done.5), channel_id=1, source_target_pairs={{0,4},{4,0},{8,12},{12,8},{16,20},{20,16},{24,28},{28,24},{1,5},{5... | collective-permute-start | bytes 786440 | tf_op jit(solution)/shard_map/ppermute | solution.py:347
  36.3 0.9 %copy-start.7 = (bf16[128,768]{1,0:T(8,128)(2,1)S(1)}, bf16[128,768]{1,0:T(8,128)(2,1)}, u32[]{:S(2)}) copy-start(bf16[128,768]{1,0:T(8,128)(2,1)} %copy-done.6) | copy-start | bytes 589828
  37.3 0.9 %copy-start.9 = (bf16[128,768]{1,0:T(8,128)(2,1)S(1)}, bf16[128,768]{1,0:T(8,128)(2,1)}, u32[]{:S(2)}) copy-start(bf16[128,768]{1,0:T(8,128)(2,1)} %copy-done.8) | copy-start | bytes 589828
  48.5 8.8 %collective-permute-start.18 = (bf16[256,512]{1,0:T(8,128)(2,1)S(1)}, bf16[256,512]{1,0:T(8,128)(2,1)S(1)}, u32[]{:S(2)}, u32[]{:S(2)}) collective-permute-start(bf16[256,512]{1,0:T(8,128)(2,1)S(1)} %get-tuple-element.38), channel_id=1, source_target_pairs={{0,1},{1,0},{2,3},{3,2},{4,5},{5,4},{6,7},{7,6},{8,9},{9,8},{10,11... | collective-permute-start | bytes 786440 | tf_op jit(solution)/shard_map/ppermute | solution.py:350
  49.7 7.6 %collective-permute-start.20 = (bf16[128,1024]{1,0:T(8,128)(2,1)S(1)}, bf16[128,1024]{1,0:T(8,128)(2,1)S(1)}, u32[]{:S(2)}, u32[]{:S(2)}) collective-permute-start(bf16[128,1024]{1,0:T(8,128)(2,1)S(1)} %collective-permute-done.15.near_0_), channel_id=1, source_target_pairs={{0,4},{4,0},{8,12},{12,8},{16,20},{20,16},{24,28},{28,24},{1,5},{5... | collective-permute-start | bytes 786440 | tf_op jit(solution)/shard_map/ppermute | solution.py:347
  49.9 7.4 %collective-permute-start.21 = (bf16[128,1024]{1,0:T(8,128)(2,1)S(1)}, bf16[128,1024]{1,0:T(8,128)(2,1)S(1)}, u32[]{:S(2)}, u32[]{:S(2)}) collective-permute-start(bf16[128,1024]{1,0:T(8,128)(2,1)S(1)} %collective-permute-done.16.near_1_), channel_id=1, source_target_pairs={{0,4},{4,0},{8,12},{12,8},{16,20},{20,16},{24,28},{28,24},{1,5},{5... | collective-permute-start | bytes 786440 | tf_op jit(solution)/shard_map/ppermute | solution.py:347
  50.2 7.1 %collective-permute-start.22 = (bf16[128,1024]{1,0:T(8,128)(2,1)S(1)}, bf16[128,1024]{1,0:T(8,128)(2,1)S(1)}, u32[]{:S(2)}, u32[]{:S(2)}) collective-permute-start(bf16[128,1024]{1,0:T(8,128)(2,1)S(1)} %collective-permute-done.17.near_2_), channel_id=1, source_target_pairs={{0,4},{4,0},{8,12},{12,8},{16,20},{20,16},{24,28},{28,24},{1,5},{5... | collective-permute-start | bytes 786440 | tf_op jit(solution)/shard_map/ppermute | solution.py:347
  50.5 6.9 %copy-start.4 = (bf16[1,256,1024]{2,1,0:T(8,128)(2,1)S(1)}, bf16[1,256,1024]{2,1,0:T(8,128)(2,1)}, u32[]{:S(2)}) copy-start(bf16[1,256,1024]{2,1,0:T(8,128)(2,1)} %param.15) | copy-start | bytes 1572868

commit v6 on v5

--- a/solution.py
+++ b/solution.py
@@ -144,7 +144,9 @@
     return x * cos + swapped * sin
 
 
-def part_kernel(where_ref, qkv_ref, part_ref):
+def part_kernel(where_ref, qkv_ref, align_ref, rope_ref, part_ref, align_out, rope_out):
+    align_out[...] = align_ref[...]
+    rope_out[...] = rope_ref[...]
     side = where_ref[2] % 2
     start = 0
     for width in (HQ * HD, HK * HD, HK * HD):
@@ -155,9 +157,7 @@
         start += width
 
 
-def table_kernel(where_ref, bytes_ref, conv_ref, total_ref, align_ref, rope_ref, out_ref, align_out, rope_out):
-    align_out[...] = align_ref[...]
-    rope_out[...] = rope_ref[...]
+def table_kernel(where_ref, bytes_ref, conv_ref, total_ref, out_ref):
     core = where_ref[1]
     taps_in = conv_ref.shape[0]
     half = total_ref.shape[0]
@@ -165,6 +165,25 @@
     mates = bytes_ref[rows, pl.ds(pl.multiple_of((1 - core) * taps_in, taps_in), taps_in)]
     total = total_ref[...] + jnp.dot(mates, conv_ref[...], preferred_element_type=jnp.float32)
     out_ref[...] = total.astype(jnp.bfloat16)
+
+
+def one_hot_kernel(where_ref, ids_refs, hot_ref):
+    side = where_ref[2] % 2
+    length = ids_refs[0].shape[1]
+    rows = length // KW
+    row = lax.broadcasted_iota(jnp.int32, (rows, length), 0)
+    mine = lax.broadcasted_iota(jnp.int32, (rows, length), 1) // KW == row
+    tap = lax.broadcasted_iota(jnp.int32, (length, 128), 0) % KW
+    pick = (tap == lax.broadcasted_iota(jnp.int32, (length, 128), 1)).astype(jnp.float32).astype(jnp.bfloat16)
+    byte = lax.broadcasted_iota(jnp.int32, (rows, VOCAB), 1).astype(jnp.float32)
+    for ids_ref, slot in zip(ids_refs, (2 + side, 3 - side, side, 1 - side)):
+        ids = ids_ref[...].astype(jnp.float32)
+        apart = jnp.where(mine, ids, 0.0).astype(jnp.bfloat16)
+        columns = jnp.dot(apart, pick, preferred_element_type=jnp.float32)
+        for k in range(KW):
+            hot_ref[slot, :, k * VOCAB : (k + 1) * VOCAB] = (
+                (columns[:, k : k + 1] == byte).astype(jnp.float32).astype(jnp.bfloat16)
+            )
 
 
 def ordered(chip, core, pieces):
@@ -214,36 +233,48 @@
         yield (which == block) & (ctx >= 2), block, (0, 1) + now
 
 
+def latent_kernel(
+    where_ref, hot_ref, own, near, mate_own, mate_near, gain_ref, normed_ref, lat_ref, table_s, lat_s,
+):
+    chip, core, ctx = where_ref[0], where_ref[1], where_ref[2]
+    for span, piece in ordered(chip, core, (own, near, mate_own, mate_near)):
+        table_s[span, :] = piece[...]
+    gain = gain_ref[...].astype(jnp.float32)
+
+    def latent_of(slot):
+        latent = jnp.dot(hot_ref[slot], table_s[...], preferred_element_type=jnp.float32).astype(jnp.bfloat16)
+        if slot >= 2:
+            lat_s[slot - 2] = latent
+        wide = latent.astype(jnp.float32)
+        scale = lax.rsqrt(jnp.mean(wide * wide, axis=1, keepdims=True) + norm_eps)
+        normed_ref[slot] = (wide * scale * gain).astype(jnp.bfloat16)
+
+    @pl.when(ctx >= 2)
+    def _():
+        latent_of(0)
+        latent_of(1)
+
+    latent_of(2)
+    latent_of(3)
+    lat_ref[...] = lat_s[ctx % 2]
+
+
 def lift_kernel(
-    where_ref, ids_ref, own_t, near_t, mate_own_t, mate_near_t, own_w, near_w, mate_own_w, mate_near_w,
-    gain_ref, rope_ref, att_ref, query_ref, k_s, v_s, lat_ref,
-    table_s, weight_s, lat_s, q_s,
+    where_ref, normed_ref, own, near, mate_own, mate_near, rope_ref, att_ref, query_ref, k_s, v_s, weight_s, q_s,
 ):
     chip, core, ctx = where_ref[0], where_ref[1], where_ref[2]
     side, upper = ctx % 2, ctx // 2
-    rows, features = lat_ref.shape
+    rows = att_ref.shape[0]
     q_width, k_width = HQ * HD // 2, HK * HD // 2
-    for span, piece in ordered(chip, core, (own_t, near_t, mate_own_t, mate_near_t)):
-        table_s[span, :] = piece[...]
-    for span, piece in ordered(chip, core, (own_w, near_w, mate_own_w, mate_near_w)):
+    for span, piece in ordered(chip, core, (own, near, mate_own, mate_near)):
         weight_s[span, :] = piece[...]
-    gain = gain_ref[...].astype(jnp.float32)
     v_s[:, HD:, :] = jnp.ones((v_s.shape[0], v_s.shape[1] - HD, v_s.shape[2]), jnp.bfloat16)
 
     def lift(slot):
         block = slot if slot < 2 else 2 * upper + slot - 2
-        ids = jnp.transpose(ids_ref[block])
-        byte = lax.broadcasted_iota(jnp.int32, (rows, VOCAB), 1)
-        one_hot = jnp.concatenate(
-            [(ids[:, k : k + 1] == byte).astype(jnp.float32).astype(jnp.bfloat16) for k in range(KW)], axis=1
-        )
-        latent = jnp.dot(one_hot, table_s[...], preferred_element_type=jnp.float32).astype(jnp.bfloat16)
-        wide = latent.astype(jnp.float32)
-        scale = lax.rsqrt(jnp.mean(wide * wide, axis=1, keepdims=True) + norm_eps)
-        normed = (wide * scale * gain).astype(jnp.bfloat16)
+        normed = normed_ref[slot]
         cos, sin = rope_at(rope_ref, rows, block)
         if slot >= 2:
-            lat_s[slot - 2] = latent
             asked = jnp.dot(normed, weight_s[:, :q_width], preferred_element_type=jnp.float32)
             for pair in range(q_width // 128):
                 turned = turn(asked[:, pair * 128 : (pair + 1) * 128], cos, sin)
@@ -264,7 +295,6 @@
 
     lift(2)
     lift(3)
-    lat_ref[...] = lat_s[side]
     query_ref[...] = q_s[side]
     allowed = causal(rows)
     other = 1 - side
@@ -358,51 +388,58 @@
     beside = [(z, z ^ 1) for z in range(n_ctx)]
 
     mate_conv = swap(w_conv, 1)
-    (part,) = call(
-        part_kernel, "qkv_part", 4, 10**8, [SMEM, VMEM], [((w_qkv.shape[0], part_width), bf16)]
-    )(where, w_qkv)
-    near_w = to_near(part)
-
     taps_in = w_conv.shape[0]
     mine = lax.dynamic_slice(byte_table, (core * half, core * taps_in), (half, taps_in))
     total = jnp.dot(mine, w_conv, preferred_element_type=f32)
     rope = jnp.asarray(rope_tables(n_ctx, rows))
-    own_t, align, rope = call(
-        table_kernel, "tap_table", 8, 10**8, [SMEM] + [VMEM] * 5,
-        [((half, features), bf16), (align.shape, jnp.int32), (rope.shape, f32)],
-    )(where, byte_table, mate_conv, total, align, rope)
-    ids = jnp.broadcast_to(byte_ids, (n_ctx, byte_ids.shape[1]))
-    ids = lax.all_to_all(ids, "ctx", 0, 0, tiled=True)
-    own_t, near_w, ids = lax.optimization_barrier((own_t, near_w, ids))
+    (own_t,) = call(
+        table_kernel, "tap_table", 8, 10**8, [SMEM, VMEM, VMEM, VMEM], [((half, features), bf16)]
+    )(where, byte_table, mate_conv, total)
     near_t = to_near(own_t)
-    ids = jnp.swapaxes(ids.reshape(n_ctx, rows, KW), 1, 2)
-    ids = jnp.pad(ids, ((0, 0), (0, 8 - KW), (0, 0)))
-    last, ids = lax.optimization_barrier((near_t[-1], ids))
+
+    ids, late_qkv, unused = lax.optimization_barrier((byte_ids, w_qkv, own_t))
+    ids_all = (
+        ids,
+        along(ids, beside),
+        along(ids, [(0, 2), (1, 3)]),
+        along(ids, [(0, 3), (1, 2)]),
+    )
+    (hot,) = call(
+        one_hot_kernel, "one_hot", 8, 10**9, [SMEM, (VMEM,) * 4], [((n_ctx, rows, KW * VOCAB), bf16)]
+    )(where, ids_all)
+    part, align, rope = call(
+        part_kernel, "qkv_part", 6, 10**8, [SMEM, VMEM, VMEM, VMEM],
+        [((w_qkv.shape[0], part_width), bf16), (align.shape, jnp.int32), (rope.shape, f32)],
+    )(where, late_qkv, align, rope)
+    last, hot, part = lax.optimization_barrier((near_t[-1], hot, part))
     near_t = near_t[:-1] + (last,)
-    t_pieces, w_pieces = to_mate(own_t, near_t), to_mate(part, near_w)
-    out_own, unused = lax.optimization_barrier((w_out, near_t))
-    out_near = to_near(out_own)
+    part, unused = lax.optimization_barrier((part, near_t))
+    near_w = to_near(part)
 
     near_specs = (VMEM,) * (n_fsdp // 2 - 1)
     piece_specs = [VMEM, near_specs, VMEM, near_specs]
+    normed, latent = call(
+        latent_kernel, "latents", 18, 2 * 10**9,
+        [SMEM, VMEM] + piece_specs + [VMEM],
+        [((n_ctx, rows, features), bf16), ((rows, features), bf16)],
+        [((KW * VOCAB, features), bf16), ((2, rows, features), bf16)],
+    )(where, hot, *to_mate(own_t, near_t), norm_gain[None])
+    near_w, normed = lax.optimization_barrier((near_w, normed))
+    out_own, unused = lax.optimization_barrier((w_out, near_w))
+    out_near = to_near(out_own)
+
     att_shape = ((rows, q_width), bf16)
-    att_mate, query, keys, values, latent = call(
-        lift_kernel, "lift", 18, 5 * 10**9,
-        [SMEM, VMEM] + piece_specs + piece_specs + [VMEM, VMEM],
+    att_mate, query, keys, values = call(
+        lift_kernel, "lift", 16, 4 * 10**9,
+        [SMEM, VMEM] + piece_specs + [VMEM],
         [
             att_shape,
             ((HQ // 2, rows, HD), bf16),
             ((2, 4 * rows, HD), bf16),
             ((2, HD + 16, 4 * rows), bf16),
-            ((rows, features), bf16),
         ],
-        [
-            ((KW * VOCAB, features), bf16),
-            ((features, part_width), bf16),
-            ((2, rows, features), bf16),
-            ((2, HQ // 2, rows, HD), bf16),
-        ],
-    )(where, ids, *t_pieces, *w_pieces, norm_gain[None], rope)
+        [((features, part_width), bf16), ((2, HQ // 2, rows, HD), bf16)],
+    )(where, normed, *to_mate(part, near_w), rope)
 
     att_mate, out_near = lax.optimization_barrier((att_mate, out_near))
     att_back = along(att_mate, beside)

time: 61 us -> 61.9 us (1.015)
  waiting for transfers between devices: 13.6 us -> 21.9 us
  local copies, waits for them, and re-layouts: 5.58 us -> 1.03 us
  starting transfers between devices: 19.7 us -> 15.4 us
  Pallas kernels: 18.5 us -> 19.9 us
    ppermute x1 -> x4, waiting for transfers between devices: 2.54 us -> 10.3 us  [along(): return lax.ppermute(x, 'ctx', pairs)]
    all_to_all x1 -> x0, starting transfers between devices: 5.09 us -> none  [head_body(): ids = lax.all_to_all(ids, 'ctx', 0, 0, tiled=True)]
    unnamed x25 -> x16, local copies, waits for them, and re-layouts: 4.23 us -> 1.03 us
    ppermute x1 -> x4, starting transfers between devices: 1.18 us -> 3 us  [along(): return lax.ppermute(x, 'ctx', pairs)]
    pallas_call x3 -> x5, Pallas kernels: 11.7 us -> 13.2 us  [the longest x1 6.12 us: head_body(): call(lift_kernel, 'lift', 16, 4 * 10 ** 9, [SMEM, VMEM] + piece_specs + [...]
    ppermute x22, waiting for transfers between devices: 10.2 us -> 11.6 us  [swap(): return lax.ppermute(x, 'fsdp', [(d, d ^ j) for d in range(n_fsdp)])]
    ppermute x22, starting transfers between devices: 13.5 us -> 12.4 us  [swap(): return lax.ppermute(x, 'fsdp', [(d, d ^ j) for d in range(n_fsdp)])]
    all_to_all x1 -> x0, waiting for transfers between devices: 0.9 us -> none  [head_body(): ids = lax.all_to_all(ids, 'ctx', 0, 0, tiled=True)]
  transfers between devices with their start and end apart: 24 -> 26, of which waited for: 6 -> 9; matrix products, arithmetic and copies ran while one was open for 5% -> 3% of each run, Pallas kernels for 27% -> 27%
where the time goes in v6:
time: 61.9 us; the launch traced here: 60.7 us
  waiting for transfers between devices  21.9 us (35%)
  Pallas kernels  19.9 us (32%)
  starting transfers between devices  15.4 us (25%)
  matrix products  1.49 us (2%)
  local copies, waits for them, and re-layouts  1.03 us (2%)
  between operations  0.91 us (1%)
    ppermute x22, starting transfers between devices, swap(): return lax.ppermute(x, 'fsdp', [(d, d ^ j) for d in range(n_fsdp)])  12.4 us
    ppermute x22, waiting for transfers between devices, swap(): return lax.ppermute(x, 'fsdp', [(d, d ^ j) for d in range(n_fsdp)])  11.6 us
    ppermute x4, waiting for transfers between devices, along(): return lax.ppermute(x, 'ctx', pairs)  10.3 us
    pallas_call x1, Pallas kernels, head_body(): call(lift_kernel, 'lift', 16, 4 * 10 ** 9, [SMEM, VMEM] + piece_specs + [...  6.12 us
    pallas_call x1, Pallas kernels, head_body(): call(own_kernel, 'own_block', 12, 3 * 10 ** 9, [SMEM, VMEM, VMEM, VMEM],...  4.31 us
    pallas_call x1, Pallas kernels, head_body(): call(latent_kernel, 'latents', 18, 2 * 10 ** 9, [SMEM, VMEM] + piece_spec...  4.03 us
    ppermute x4, starting transfers between devices, along(): return lax.ppermute(x, 'ctx', pairs)  3 us
    pallas_call x1, Pallas kernels, head_body(): call(out_kernel, 'project_out', 12, 10 ** 9, [SMEM, VMEM, VMEM] + piece_s...  2.45 us
  transfers between devices with their start and end apart: 26, of which 9 were waited for; matrix products, arithmetic and copies ran while one was open for 3% of the time, Pallas kernels for 27%

profile of v6, /device:TPU:24, one launch (start us, length us, event | category | flops | bytes accessed | tf_op | source)
XLA Modules:
  0.0 60.7 jit_solution(12388145750399528234)
XLA Ops:
  0.6 0.0 copy-start.2
  0.7 0.1 collective-permute-start
  0.8 0.1 pad_add_fusion.where_ref
  0.9 1.5 %fusion.total_ref = f32[128,1024]{1,0:T(8,128)S(1)} fusion(bf16[384,1024]{1,0:T(8,128)(2,1)} %param.11, bf16[256,768]{1,0:T(8,128)(2,1)} %bytes_ref.1, s32[]{:T(128)S(6)} %select_n.19, s32[]{:T(128)S(6)} %select_n.20), kind=kOutput, calls=%fused_computation | convolution fusion | flops 100663296 | bytes 1409032 | tf_op jit(solution)/shard_map/dot_general | solution.py:393
  2.4 0.9 %collective-permute-done.conv_ref = bf16[384,1024]{1,0:T(8,128)(2,1)S(1)} collective-permute-done((bf16[384,1024]{1,0:T(8,128)(2,1)}, bf16[384,1024]{1,0:T(8,128)(2,1)S(1)}, u32[]{:S(2)}, u32[]{:S(2)}) %collective-permute-start) | collective-permute-done | bytes 786464 | tf_op jit(solution)/shard_map/ppermute | solution.py:377
  3.2 1.0 %copy-done = bf16[256,768]{1,0:T(8,128)(2,1)S(1)} copy-done((bf16[256,768]{1,0:T(8,128)(2,1)S(1)}, bf16[256,768]{1,0:T(8,128)(2,1)}, u32[]{:S(2)}) %copy-start) | copy-done | bytes 393240
  4.2 0.9 %tap_table.1.own = bf16[128,1024]{1,0:T(8,128)(2,1)S(1)} custom-call(s32[3]{0:T(128)S(1)} %pad_add_fusion.where_ref, bf16[256,768]{1,0:T(8,128)(2,1)S(1)} %copy-done, bf16[384,1024]{1,0:T(8,128)(2,1)S(1)} %collective-permute-done.conv_ref, f32[128,1024]{1,0:T(8,128)S(1)} %fusion.total_ref), custom_call_target="tpu_custom_call" | custom-call | flops 100000000 | bytes 4194304 | tf_op jit(solution)/shard_map/tap_table/pallas_call | solution.py:395
  5.1 0.0 copy-start.7
  5.1 2.5 %collective-permute-start.1 = (bf16[128,1024]{1,0:T(8,128)(2,1)S(1)}, bf16[128,1024]{1,0:T(8,128)(2,1)S(1)}, u32[]{:S(2)}, u32[]{:S(2)}) collective-permute-start(bf16[128,1024]{1,0:T(8,128)(2,1)S(1)} %tap_table.1.own), channel_id=1, source_target_pairs={{0,24},{4,28},{8,16},{12,20},{16,8},{20,12},{24,0},{28,4},{1,25},{... | collective-permute-start | bytes 786440 | tf_op jit(solution)/shard_map/ppermute | solution.py:377
  7.6 0.5 collective-permute-start.5
  8.1 0.5 collective-permute-start.6
  8.7 0.4 collective-permute-start.2
  9.1 1.3 %collective-permute-start.3 = (s32[1,1024]{1,0:T(1,128)S(1)}, s32[1,1024]{1,0:T(1,128)S(1)}, u32[]{:S(2)}, u32[]{:S(2)}) collective-permute-start(s32[1,1024]{1,0:T(1,128)S(1)} %copy-done.6), channel_id=1, source_target_pairs={{0,2},{1,3},{4,6},{5,7},{8,10},{9,11},{12,14},{13,15},{16,18},{17,... | collective-permute-start | bytes 12296 | tf_op jit(solution)/shard_map/ppermute | solution.py:380
  10.4 1.9 %collective-permute-done.2.ids_refs_1_ = s32[1,1024]{1,0:T(1,128)S(1)} collective-permute-done((s32[1,1024]{1,0:T(1,128)S(1)}, s32[1,1024]{1,0:T(1,128)S(1)}, u32[]{:S(2)}, u32[]{:S(2)}) %collective-permute-start.2) | collective-permute-done | bytes 4128 | tf_op jit(solution)/shard_map/ppermute | solution.py:380
  12.3 1.3 %collective-permute-start.4 = (s32[1,1024]{1,0:T(1,128)S(1)}, s32[1,1024]{1,0:T(1,128)S(1)}, u32[]{:S(2)}, u32[]{:S(2)}) collective-permute-start(s32[1,1024]{1,0:T(1,128)S(1)} %copy-done.6), channel_id=1, source_target_pairs={{0,3},{1,2},{4,7},{5,6},{8,11},{9,10},{12,15},{13,14},{16,19},{17,... | collective-permute-start | bytes 12296 | tf_op jit(solution)/shard_map/ppermute | solution.py:380
  13.6 0.6 qkv_part.1
  14.2 1.3 %collective-permute-done.3.ids_refs_2_ = s32[1,1024]{1,0:T(1,128)S(1)} collective-permute-done((s32[1,1024]{1,0:T(1,128)S(1)}, s32[1,1024]{1,0:T(1,128)S(1)}, u32[]{:S(2)}, u32[]{:S(2)}) %collective-permute-start.3) | collective-permute-done | bytes 4128 | tf_op jit(solution)/shard_map/ppermute | solution.py:380
  15.5 0.0 collective-permute-start.10
  15.5 4.1 %collective-permute-done.4.ids_refs_3_ = s32[1,1024]{1,0:T(1,128)S(1)} collective-permute-done((s32[1,1024]{1,0:T(1,128)S(1)}, s32[1,1024]{1,0:T(1,128)S(1)}, u32[]{:S(2)}, u32[]{:S(2)}) %collective-permute-start.4) | collective-permute-done | bytes 4128 | tf_op jit(solution)/shard_map/ppermute | solution.py:380
  19.6 1.6 %one_hot.1.hot_ref = bf16[4,256,1024]{2,1,0:T(8,128)(2,1)S(1)} custom-call(s32[3]{0:T(128)S(1)} %pad_add_fusion.where_ref, s32[1,1024]{1,0:T(1,128)S(1)} %copy-done.6, s32[1,1024]{1,0:T(1,128)S(1)} %collective-permute-done.2.ids_refs_1_, s32[1,1024]{1,0:T(1,128)S(1)} %collective-permute-done.3.ids_refs_2_, s32[1,1024]{1,0:T(1,128)S(1)} %collective-permute-done.4.ids_refs_3_), custom_call_target="tpu_custom_call" | custom-call | flops 1000000000 | bytes 4194304 | tf_op jit(solution)/shard_map/one_hot/pallas_call | solution.py:407
  21.1 0.0 collective-permute-done.1.near_2_
  21.1 0.1 collective-permute-start.13
  21.2 0.0 collective-permute-done.5.near_0_
  21.2 0.5 collective-permute-start.11
  21.7 0.0 collective-permute-done.6.near_1_
  21.7 0.1 collective-permute-start.12
  21.8 1.5 %collective-permute-start.7 = (bf16[128,768]{1,0:T(8,128)(2,1)S(1)}, bf16[128,768]{1,0:T(8,128)(2,1)S(1)}, u32[]{:S(2)}, u32[]{:S(2)}) collective-permute-start(bf16[128,768]{1,0:T(8,128)(2,1)S(1)} %get-tuple-element.33.own), channel_id=1, source_target_pairs={{0,8},{4,12},{8,0},{12,4},{16,24},{20,28},{24,16},{28,20},{1,9},{5... | collective-permute-start | bytes 589832 | tf_op jit(solution)/shard_map/ppermute | solution.py:377
  23.3 0.0 collective-permute-done.10.mate_own
  23.3 1.5 %collective-permute-start.8 = (bf16[128,768]{1,0:T(8,128)(2,1)S(1)}, bf16[128,768]{1,0:T(8,128)(2,1)S(1)}, u32[]{:S(2)}, u32[]{:S(2)}) collective-permute-start(bf16[128,768]{1,0:T(8,128)(2,1)S(1)} %get-tuple-element.33.own), channel_id=1, source_target_pairs={{0,16},{4,20},{8,24},{12,28},{16,0},{20,4},{24,8},{28,12},{1,17},{... | collective-permute-start | bytes 589832 | tf_op jit(solution)/shard_map/ppermute | solution.py:377
  24.8 0.0 collective-permute-done.13.mate_near_2_
  24.8 0.5 collective-permute-start.9
  25.3 0.0 collective-permute-done.11.mate_near_0_
  25.3 0.1 collective-permute-start.14
  25.4 0.0 collective-permute-done.12.mate_near_1_
  25.4 4.0 %latents.1 = (bf16[4,256,1024]{2,1,0:T(8,128)(2,1)S(1)}, bf16[256,1024]{1,0:T(8,128)(2,1)S(1)}) custom-call(s32[3]{0:T(128)S(1)} %pad_add_fusion.where_ref, bf16[4,256,1024]{2,1,0:T(8,128)(2,1)S(1)} %one_hot.1.hot_ref, bf16[128,1024]{1,0:T(8,128)(2,1)S(1)} %tap_table.1.own, bf16[128,1024]{1,0:T(8,128)(2,1)S(1)} %collective-permute-done.5.near_0_, ...), custom_call_target="tpu_custom_call" | custom-call | flops 2000000000 | bytes 4194304 | tf_op jit(solution)/shard_map/latents/pallas_call | solution.py:421
  29.5 0.1 collective-permute-done.7.near_0_
  29.5 5.0 %collective-permute-done.8.near_1_ = bf16[128,768]{1,0:T(8,128)(2,1)S(1)} collective-permute-done((bf16[128,768]{1,0:T(8,128)(2,1)S(1)}, bf16[128,768]{1,0:T(8,128)(2,1)S(1)}, u32[]{:S(2)}, u32[]{:S(2)}) %collective-permute-start.8) | collective-permute-done | bytes 196640 | tf_op jit(solution)/shard_map/ppermute | solution.py:377
  34.5 0.0 collective-permute-done.9.near_2_
  34.5 0.0 collective-permute-start.15
  34.5 0.5 collective-permute-start.16
  35.0 0.0 collective-permute-start.17
  35.0 1.2 %collective-permute-start.18 = (bf16[128,1024]{1,0:T(8,128)(2,1)S(1)}, bf16[128,1024]{1,0:T(8,128)(2,1)S(1)}, u32[]{:S(2)}, u32[]{:S(2)}) collective-permute-start(bf16[128,1024]{1,0:T(8,128)(2,1)S(1)} %copy-done.5), channel_id=1, source_target_pairs={{0,8},{4,12},{8,0},{12,4},{16,24},{20,28},{24,16},{28,20},{1,9},{5... | collective-permute-start | bytes 786440 | tf_op jit(solution)/shard_map/ppermute | solution.py:377
  36.2 0.0 collective-permute-done.14.mate_own
  36.2 0.8 %collective-permute-start.19 = (bf16[128,1024]{1,0:T(8,128)(2,1)S(1)}, bf16[128,1024]{1,0:T(8,128)(2,1)S(1)}, u32[]{:S(2)}, u32[]{:S(2)}) collective-permute-start(bf16[128,1024]{1,0:T(8,128)(2,1)S(1)} %copy-done.5), channel_id=1, source_target_pairs={{0,16},{4,20},{8,24},{12,28},{16,0},{20,4},{24,8},{28,12},{1,17},{... | collective-permute-start | bytes 786440 | tf_op jit(solution)/shard_map/ppermute | solution.py:377
  37.0 0.0 collective-permute-done.15.mate_near_0_
  37.1 1.4 %collective-permute-start.20 = (bf16[128,1024]{1,0:T(8,128)(2,1)S(1)}, bf16[128,1024]{1,0:T(8,128)(2,1)S(1)}, u32[]{:S(2)}, u32[]{:S(2)}) collective-permute-start(bf16[128,1024]{1,0:T(8,128)(2,1)S(1)} %copy-done.5), channel_id=1, source_target_pairs={{0,24},{4,28},{8,16},{12,20},{16,8},{20,12},{24,0},{28,4},{1,25},{... | collective-permute-start | bytes 786440 | tf_op jit(solution)/shard_map/ppermute | solution.py:377
  38.5 0.0 collective-permute-done.16.mate_near_1_
  38.5 0.0 collective-permute-start.22
  38.5 0.0 collective-permute-done.17.mate_near_2_
  38.5 6.1 %lift.1 = (bf16[256,512]{1,0:T(8,128)(2,1)S(1)}, bf16[8,256,64]{2,1,0:T(8,128)(2,1)S(1)}, bf16[2,1024,64]{2,1,0:T(8,128)(2,1)S(1)}, bf16[2,80,1024]{2,1,0:T(8,128)(2,1)S(1)}) custom-call(s32[3]{0:T(128)S(1)} %pad_add_fusion.where_ref, bf16[4,256,1024]{2,1,0:T(8,128)(2,1)S(1)} %get-tuple-element.36.normed_ref, bf16[128,768]{1,0:T(8,128)(2,1)S(1)} %get-tuple-element.33.own, ...), custom_call_target="tpu_custom_call" | custom-call | flops 4000000000 | bytes 4194304 | tf_op jit(solution)/shard_map/lift/pallas_call | solution.py:432
  44.6 0.0 collective-permute-done.18.near_0_
  44.6 4.0 %collective-permute-done.19.near_1_ = bf16[128,1024]{1,0:T(8,128)(2,1)S(1)} collective-permute-done((bf16[128,1024]{1,0:T(8,128)(2,1)S(1)}, bf16[128,1024]{1,0:T(8,128)(2,1)S(1)}, u32[]{:S(2)}, u32[]{:S(2)}) %collective-permute-start.19) | collective-permute-done | bytes 262176 | tf_op jit(solution)/shard_map/ppermute | solution.py:377
  48.7 1.6 %collective-permute-done.20.near_2_ = bf16[128,1024]{1,0:T(8,128)(2,1)S(1)} collective-permute-done((bf16[128,1024]{1,0:T(8,128)(2,1)S(1)}, bf16[128,1024]{1,0:T(8,128)(2,1)S(1)}, u32[]{:S(2)}, u32[]{:S(2)}) %collective-permute-start.20) | collective-permute-done | bytes 262176 | tf_op jit(solution)/shard_map/ppermute | solution.py:377
  50.3 0.0 collective-permute-start.21
  50.3 0.0 collective-permute-start.23
  50.3 0.5 collective-permute-start.24
  50.8 0.0 collective-permute-start.25
  50.8 4.3 %own_block.1.own_att = bf16[256,512]{1,0:T(8,128)(2,1)S(1)} custom-call(s32[3]{0:T(128)S(1)} %pad_add_fusion.where_ref, bf16[8,256,64]{2,1,0:T(8,128)(2,1)S(1)} %get-tuple-element.41.query_ref, bf16[2,1024,64]{2,1,0:T(8,128)(2,1)S(1)} %get-tuple-element.42.k_ref, bf16[2,80,1024]{2,1,0:T(8,128)(2,1)S(1)} %get-tuple-element.43.v_ref), custom_call_target="tpu_custom_call" | custom-call | flops 3000000000 | bytes 4194304 | tf_op jit(solution)/shard_map/own_block/pallas_call | solution.py:446
  55.1 0.0 collective-permute-done.22.mate_own
  55.1 3.1 %collective-permute-done.21.mate_att = bf16[256,512]{1,0:T(8,128)(2,1)S(1)} collective-permute-done((bf16[256,512]{1,0:T(8,128)(2,1)S(1)}, bf16[256,512]{1,0:T(8,128)(2,1)S(1)}, u32[]{:S(2)}, u32[]{:S(2)}) %collective-permute-start.21) | collective-permute-done | bytes 262176 | tf_op jit(solution)/shard_map/ppermute | solution.py:380
  58.2 0.0 collective-permute-done.23.mate_near_0_
  58.2 0.0 collective-permute-done.24.mate_near_1_
  58.2 0.0 collective-permute-done.25.mate_near_2_
  58.2 2.4 %project_out.1 = (bf16[256,1024]{1,0:T(8,128)(2,1)}, f32[1,256]{1,0:T(1,128)}) custom-call(s32[3]{0:T(128)S(1)} %pad_add_fusion.where_ref, bf16[256,512]{1,0:T(8,128)(2,1)S(1)} %own_block.1.own_att, bf16[256,512]{1,0:T(8,128)(2,1)S(1)} %collective-permute-done.21.mate_att, bf16[128,1024]{1,0:T(8,128)(2,1)S(1)} %copy-done.5, ...), custom_call_target="tpu_custom_call" | custom-call | flops 1000000000 | bytes 4194304 | tf_op jit(solution)/shard_map/project_out/pallas_call | solution.py:449
  (14 shorter events, 0.0 us)
Async XLA Ops:
  0.6 12.9 %copy-start.2 = (f32[520,128]{1,0:T(8,128)S(1)}, f32[520,128]{1,0:T(8,128)}, u32[]{:S(2)}) copy-start(f32[520,128]{1,0:T(8,128)} %constant.44.clone.rope_ref) | copy-start | bytes 798724
  0.6 12.9 %copy-start.1 = (bf16[128,1536]{1,0:T(8,128)(2,1)S(1)}, bf16[128,1536]{1,0:T(8,128)(2,1)}, u32[]{:S(2)}) copy-start(bf16[128,1536]{1,0:T(8,128)(2,1)} %qkv_ref) | copy-start | bytes 1179652
  0.7 8.0 %copy-start.6 = (s32[1,1024]{1,0:T(1,128)S(1)}, s32[1,1024]{1,0:T(1,128)}, u32[]{:S(2)}) copy-start(s32[1,1024]{1,0:T(1,128)} %ids_refs_0_) | copy-start | bytes 12292
  0.7 12.9 %copy-start.3 = (s32[1,256]{1,0:T(1,128)S(1)}, s32[1,256]{1,0:T(1,128)}, u32[]{:S(2)}) copy-start(s32[1,256]{1,0:T(1,128)} %align_ref.1) | copy-start | bytes 3076
  0.7 2.6 %collective-permute-start = (bf16[384,1024]{1,0:T(8,128)(2,1)}, bf16[384,1024]{1,0:T(8,128)(2,1)S(1)}, u32[]{:S(2)}, u32[]{:S(2)}) collective-permute-start(bf16[384,1024]{1,0:T(8,128)(2,1)} %param.11), channel_id=1, source_target_pairs={{0,4},{4,0},{8,12},{12,8},{16,20},{20,16},{24,28},{28,24},{1,5},{5... | collective-permute-start | bytes 2359304 | tf_op jit(solution)/shard_map/ppermute | solution.py:377
  3.2 1.0 %copy-start = (bf16[256,768]{1,0:T(8,128)(2,1)S(1)}, bf16[256,768]{1,0:T(8,128)(2,1)}, u32[]{:S(2)}) copy-start(bf16[256,768]{1,0:T(8,128)(2,1)} %bytes_ref.1) | copy-start | bytes 1179652
  5.1 20.2 %copy-start.7 = (bf16[1024]{0:T(1024)(128)(2,1)S(1)}, bf16[1024]{0:T(1024)(128)(2,1)}, u32[]{:S(2)}) copy-start(bf16[1024]{0:T(1024)(128)(2,1)} %param.14) | copy-start | bytes 6148
  5.1 16.0 %collective-permute-start.1 = (bf16[128,1024]{1,0:T(8,128)(2,1)S(1)}, bf16[128,1024]{1,0:T(8,128)(2,1)S(1)}, u32[]{:S(2)}, u32[]{:S(2)}) collective-permute-start(bf16[128,1024]{1,0:T(8,128)(2,1)S(1)} %tap_table.1.own), channel_id=1, source_target_pairs={{0,24},{4,28},{8,16},{12,20},{16,8},{20,12},{24,0},{28,4},{1,25},{... | collective-permute-start | bytes 786440 | tf_op jit(solution)/shard_map/ppermute | solution.py:377
  7.6 13.6 %collective-permute-start.5 = (bf16[128,1024]{1,0:T(8,128)(2,1)S(1)}, bf16[128,1024]{1,0:T(8,128)(2,1)S(1)}, u32[]{:S(2)}, u32[]{:S(2)}) collective-permute-start(bf16[128,1024]{1,0:T(8,128)(2,1)S(1)} %tap_table.1.own), channel_id=1, source_target_pairs={{0,8},{4,12},{8,0},{12,4},{16,24},{20,28},{24,16},{28,20},{1,9},{5... | collective-permute-start | bytes 786440 | tf_op jit(solution)/shard_map/ppermute | solution.py:377
  8.1 13.6 %collective-permute-start.6 = (bf16[128,1024]{1,0:T(8,128)(2,1)S(1)}, bf16[128,1024]{1,0:T(8,128)(2,1)S(1)}, u32[]{:S(2)}, u32[]{:S(2)}) collective-permute-start(bf16[128,1024]{1,0:T(8,128)(2,1)S(1)} %tap_table.1.own), channel_id=1, source_target_pairs={{0,16},{4,20},{8,24},{12,28},{16,0},{20,4},{24,8},{28,12},{1,17},{... | collective-permute-start | bytes 786440 | tf_op jit(solution)/shard_map/ppermute | solution.py:377
  8.7 3.6 %collective-permute-start.2 = (s32[1,1024]{1,0:T(1,128)S(1)}, s32[1,1024]{1,0:T(1,128)S(1)}, u32[]{:S(2)}, u32[]{:S(2)}) collective-permute-start(s32[1,1024]{1,0:T(1,128)S(1)} %copy-done.6), channel_id=1, source_target_pairs={{0,1},{1,0},{2,3},{3,2},{4,5},{5,4},{6,7},{7,6},{8,9},{9,8},{10,11... | collective-permute-start | bytes 12296 | tf_op jit(solution)/shard_map/ppermute | solution.py:380
  9.1 6.4 %collective-permute-start.3 = (s32[1,1024]{1,0:T(1,128)S(1)}, s32[1,1024]{1,0:T(1,128)S(1)}, u32[]{:S(2)}, u32[]{:S(2)}) collective-permute-start(s32[1,1024]{1,0:T(1,128)S(1)} %copy-done.6), channel_id=1, source_target_pairs={{0,2},{1,3},{4,6},{5,7},{8,10},{9,11},{12,14},{13,15},{16,18},{17,... | collective-permute-start | bytes 12296 | tf_op jit(solution)/shard_map/ppermute | solution.py:380
  12.3 7.3 %collective-permute-start.4 = (s32[1,1024]{1,0:T(1,128)S(1)}, s32[1,1024]{1,0:T(1,128)S(1)}, u32[]{:S(2)}, u32[]{:S(2)}) collective-permute-start(s32[1,1024]{1,0:T(1,128)S(1)} %copy-done.6), channel_id=1, source_target_pairs={{0,3},{1,2},{4,7},{5,6},{8,11},{9,10},{12,15},{13,14},{16,19},{17,... | collective-permute-start | bytes 12296 | tf_op jit(solution)/shard_map/ppermute | solution.py:380
  15.5 7.8 %collective-permute-start.10 = (bf16[128,1024]{1,0:T(8,128)(2,1)S(1)}, bf16[128,1024]{1,0:T(8,128)(2,1)S(1)}, u32[]{:S(2)}, u32[]{:S(2)}) collective-permute-start(bf16[128,1024]{1,0:T(8,128)(2,1)S(1)} %tap_table.1.own), channel_id=1, source_target_pairs={{0,4},{4,0},{8,12},{12,8},{16,20},{20,16},{24,28},{28,24},{1,5},{5... | collective-permute-start | bytes 786440 | tf_op jit(solution)/shard_map/ppermute | solution.py:377
  21.1 3.7 %collective-permute-start.13 = (bf16[128,1024]{1,0:T(8,128)(2,1)S(1)}, bf16[128,1024]{1,0:T(8,128)(2,1)S(1)}, u32[]{:S(2)}, u32[]{:S(2)}) collective-permute-start(bf16[128,1024]{1,0:T(8,128)(2,1)S(1)} %collective-permute-done.1.near_2_), channel_id=1, source_target_pairs={{0,4},{4,0},{8,12},{12,8},{16,20},{20,16},{24,28},{28,24},{1,5},{5... | collective-permute-start | bytes 786440 | tf_op jit(solution)/shard_map/ppermute | solution.py:377
  21.2 4.1 %collective-permute-start.11 = (bf16[128,1024]{1,0:T(8,128)(2,1)S(1)}, bf16[128,1024]{1,0:T(8,128)(2,1)S(1)}, u32[]{:S(2)}, u32[]{:S(2)}) collective-permute-start(bf16[128,1024]{1,0:T(8,128)(2,1)S(1)} %collective-permute-done.5.near_0_), channel_id=1, source_target_pairs={{0,4},{4,0},{8,12},{12,8},{16,20},{20,16},{24,28},{28,24},{1,5},{5... | collective-permute-start | bytes 786440 | tf_op jit(solution)/shard_map/ppermute | solution.py:377
  21.7 3.7 %collective-permute-start.12 = (bf16[128,1024]{1,0:T(8,128)(2,1)S(1)}, bf16[128,1024]{1,0:T(8,128)(2,1)S(1)}, u32[]{:S(2)}, u32[]{:S(2)}) collective-permute-start(bf16[128,1024]{1,0:T(8,128)(2,1)S(1)} %collective-permute-done.6.near_1_), channel_id=1, source_target_pairs={{0,4},{4,0},{8,12},{12,8},{16,20},{20,16},{24,28},{28,24},{1,5},{5... | collective-permute-start | bytes 786440 | tf_op jit(solution)/shard_map/ppermute | solution.py:377
  21.8 7.7 %collective-permute-start.7 = (bf16[128,768]{1,0:T(8,128)(2,1)S(1)}, bf16[128,768]{1,0:T(8,128)(2,1)S(1)}, u32[]{:S(2)}, u32[]{:S(2)}) collective-permute-start(bf16[128,768]{1,0:T(8,128)(2,1)S(1)} %get-tuple-element.33.own), channel_id=1, source_target_pairs={{0,8},{4,12},{8,0},{12,4},{16,24},{20,28},{24,16},{28,20},{1,9},{5... | collective-permute-start | bytes 589832 | tf_op jit(solution)/shard_map/ppermute | solution.py:377
  23.3 11.2 %collective-permute-start.8 = (bf16[128,768]{1,0:T(8,128)(2,1)S(1)}, bf16[128,768]{1,0:T(8,128)(2,1)S(1)}, u32[]{:S(2)}, u32[]{:S(2)}) collective-permute-start(bf16[128,768]{1,0:T(8,128)(2,1)S(1)} %get-tuple-element.33.own), channel_id=1, source_target_pairs={{0,16},{4,20},{8,24},{12,28},{16,0},{20,4},{24,8},{28,12},{1,17},{... | collective-permute-start | bytes 589832 | tf_op jit(solution)/shard_map/ppermute | solution.py:377
  24.8 9.7 %collective-permute-start.9 = (bf16[128,768]{1,0:T(8,128)(2,1)S(1)}, bf16[128,768]{1,0:T(8,128)(2,1)S(1)}, u32[]{:S(2)}, u32[]{:S(2)}) collective-permute-start(bf16[128,768]{1,0:T(8,128)(2,1)S(1)} %get-tuple-element.33.own), channel_id=1, source_target_pairs={{0,24},{4,28},{8,16},{12,20},{16,8},{20,12},{24,0},{28,4},{1,25},{... | collective-permute-start | bytes 589832 | tf_op jit(solution)/shard_map/ppermute | solution.py:377
  25.3 9.7 %copy-start.5 = (bf16[128,1024]{1,0:T(8,128)(2,1)S(1)}, bf16[128,1024]{1,0:T(8,128)(2,1)}, u32[]{:S(2)}) copy-start(bf16[128,1024]{1,0:T(8,128)(2,1)} %own) | copy-start | bytes 786436
  25.3 10.9 %collective-permute-start.14 = (bf16[128,768]{1,0:T(8,128)(2,1)S(1)}, bf16[128,768]{1,0:T(8,128)(2,1)S(1)}, u32[]{:S(2)}, u32[]{:S(2)}) collective-permute-start(bf16[128,768]{1,0:T(8,128)(2,1)S(1)} %get-tuple-element.33.own), channel_id=1, source_target_pairs={{0,4},{4,0},{8,12},{12,8},{16,20},{20,16},{24,28},{28,24},{1,5},{5... | collective-permute-start | bytes 589832 | tf_op jit(solution)/shard_map/ppermute | solution.py:377
  34.5 2.6 %collective-permute-start.15 = (bf16[128,768]{1,0:T(8,128)(2,1)S(1)}, bf16[128,768]{1,0:T(8,128)(2,1)S(1)}, u32[]{:S(2)}, u32[]{:S(2)}) collective-permute-start(bf16[128,768]{1,0:T(8,128)(2,1)S(1)} %collective-permute-done.7.near_0_), channel_id=1, source_target_pairs={{0,4},{4,0},{8,12},{12,8},{16,20},{20,16},{24,28},{28,24},{1,5},{5... | collective-permute-start | bytes 589832 | tf_op jit(solution)/shard_map/ppermute | solution.py:377
  34.5 4.0 %collective-permute-start.16 = (bf16[128,768]{1,0:T(8,128)(2,1)S(1)}, bf16[128,768]{1,0:T(8,128)(2,1)S(1)}, u32[]{:S(2)}, u32[]{:S(2)}) collective-permute-start(bf16[128,768]{1,0:T(8,128)(2,1)S(1)} %collective-permute-done.8.near_1_), channel_id=1, source_target_pairs={{0,4},{4,0},{8,12},{12,8},{16,20},{20,16},{24,28},{28,24},{1,5},{5... | collective-permute-start | bytes 589832 | tf_op jit(solution)/shard_map/ppermute | solution.py:377
  35.0 3.5 %collective-permute-start.17 = (bf16[128,768]{1,0:T(8,128)(2,1)S(1)}, bf16[128,768]{1,0:T(8,128)(2,1)S(1)}, u32[]{:S(2)}, u32[]{:S(2)}) collective-permute-start(bf16[128,768]{1,0:T(8,128)(2,1)S(1)} %collective-permute-done.9.near_2_), channel_id=1, source_target_pairs={{0,4},{4,0},{8,12},{12,8},{16,20},{20,16},{24,28},{28,24},{1,5},{5... | collective-permute-start | bytes 589832 | tf_op jit(solution)/shard_map/ppermute | solution.py:377
  35.0 9.6 %collective-permute-start.18 = (bf16[128,1024]{1,0:T(8,128)(2,1)S(1)}, bf16[128,1024]{1,0:T(8,128)(2,1)S(1)}, u32[]{:S(2)}, u32[]{:S(2)}) collective-permute-start(bf16[128,1024]{1,0:T(8,128)(2,1)S(1)} %copy-done.5), channel_id=1, source_target_pairs={{0,8},{4,12},{8,0},{12,4},{16,24},{20,28},{24,16},{28,20},{1,9},{5... | collective-permute-start | bytes 786440 | tf_op jit(solution)/shard_map/ppermute | solution.py:377
  36.2 12.4 %collective-permute-start.19 = (bf16[128,1024]{1,0:T(8,128)(2,1)S(1)}, bf16[128,1024]{1,0:T(8,128)(2,1)S(1)}, u32[]{:S(2)}, u32[]{:S(2)}) collective-permute-start(bf16[128,1024]{1,0:T(8,128)(2,1)S(1)} %copy-done.5), channel_id=1, source_target_pairs={{0,16},{4,20},{8,24},{12,28},{16,0},{20,4},{24,8},{28,12},{1,17},{... | collective-permute-start | bytes 786440 | tf_op jit(solution)/shard_map/ppermute | solution.py:377
  37.1 13.2 %collective-permute-start.20 = (bf16[128,1024]{1,0:T(8,128)(2,1)S(1)}, bf16[128,1024]{1,0:T(8,128)(2,1)S(1)}, u32[]{:S(2)}, u32[]{:S(2)}) collective-permute-start(bf16[128,1024]{1,0:T(8,128)(2,1)S(1)} %copy-done.5), channel_id=1, source_target_pairs={{0,24},{4,28},{8,16},{12,20},{16,8},{20,12},{24,0},{28,4},{1,25},{... | collective-permute-start | bytes 786440 | tf_op jit(solution)/shard_map/ppermute | solution.py:377
  38.5 16.6 %collective-permute-start.22 = (bf16[128,1024]{1,0:T(8,128)(2,1)S(1)}, bf16[128,1024]{1,0:T(8,128)(2,1)S(1)}, u32[]{:S(2)}, u32[]{:S(2)}) collective-permute-start(bf16[128,1024]{1,0:T(8,128)(2,1)S(1)} %copy-done.5), channel_id=1, source_target_pairs={{0,4},{4,0},{8,12},{12,8},{16,20},{20,16},{24,28},{28,24},{1,5},{5... | collective-permute-start | bytes 786440 | tf_op jit(solution)/shard_map/ppermute | solution.py:377
  50.3 7.9 %collective-permute-start.21 = (bf16[256,512]{1,0:T(8,128)(2,1)S(1)}, bf16[256,512]{1,0:T(8,128)(2,1)S(1)}, u32[]{:S(2)}, u32[]{:S(2)}) collective-permute-start(bf16[256,512]{1,0:T(8,128)(2,1)S(1)} %get-tuple-element.46), channel_id=1, source_target_pairs={{0,1},{1,0},{2,3},{3,2},{4,5},{5,4},{6,7},{7,6},{8,9},{9,8},{10,11... | collective-permute-start | bytes 786440 | tf_op jit(solution)/shard_map/ppermute | solution.py:380
  50.3 7.9 %collective-permute-start.23 = (bf16[128,1024]{1,0:T(8,128)(2,1)S(1)}, bf16[128,1024]{1,0:T(8,128)(2,1)S(1)}, u32[]{:S(2)}, u32[]{:S(2)}) collective-permute-start(bf16[128,1024]{1,0:T(8,128)(2,1)S(1)} %collective-permute-done.18.near_0_), channel_id=1, source_target_pairs={{0,4},{4,0},{8,12},{12,8},{16,20},{20,16},{24,28},{28,24},{1,5},{5... | collective-permute-start | bytes 786440 | tf_op jit(solution)/shard_map/ppermute | solution.py:377
  50.3 7.9 %collective-permute-start.24 = (bf16[128,1024]{1,0:T(8,128)(2,1)S(1)}, bf16[128,1024]{1,0:T(8,128)(2,1)S(1)}, u32[]{:S(2)}, u32[]{:S(2)}) collective-permute-start(bf16[128,1024]{1,0:T(8,128)(2,1)S(1)} %collective-permute-done.19.near_1_), channel_id=1, source_target_pairs={{0,4},{4,0},{8,12},{12,8},{16,20},{20,16},{24,28},{28,24},{1,5},{5... | collective-permute-start | bytes 786440 | tf_op jit(solution)/shard_map/ppermute | solution.py:377
  50.8 7.4 %collective-permute-start.25 = (bf16[128,1024]{1,0:T(8,128)(2,1)S(1)}, bf16[128,1024]{1,0:T(8,128)(2,1)S(1)}, u32[]{:S(2)}, u32[]{:S(2)}) collective-permute-start(bf16[128,1024]{1,0:T(8,128)(2,1)S(1)} %collective-permute-done.20.near_2_), channel_id=1, source_target_pairs={{0,4},{4,0},{8,12},{12,8},{16,20},{20,16},{24,28},{28,24},{1,5},{5... | collective-permute-start | bytes 786440 | tf_op jit(solution)/shard_map/ppermute | solution.py:377
  50.8 7.4 %copy-start.4 = (bf16[1,256,1024]{2,1,0:T(8,128)(2,1)S(1)}, bf16[1,256,1024]{2,1,0:T(8,128)(2,1)}, u32[]{:S(2)}) copy-start(bf16[1,256,1024]{2,1,0:T(8,128)(2,1)} %param.15) | copy-start | bytes 1572868

commit v7 on v6

--- a/solution.py
+++ b/solution.py
@@ -441,11 +441,11 @@
         [((features, part_width), bf16), ((2, HQ // 2, rows, HD), bf16)],
     )(where, normed, *to_mate(part, near_w), rope)
 
-    att_mate, out_near = lax.optimization_barrier((att_mate, out_near))
     att_back = along(att_mate, beside)
     (att_own,) = call(
         own_kernel, "own_block", 12, 3 * 10**9, [SMEM, VMEM, VMEM, VMEM], [att_shape]
     )(where, query, keys, values)
+    att_own, out_near = lax.optimization_barrier((att_own, out_near))
     hidden, loss = call(
         out_kernel, "project_out", 12, 10**9,
         [SMEM, VMEM, VMEM] + piece_specs + [VMEM, VMEM, VMEM],

time: 61.9 us -> 56.2 us (0.908); the launches traced: 60.7 us -> 55.9 us
  waiting for transfers between devices: 21.9 us -> 17 us
    ppermute x22, waiting for transfers between devices: 11.6 us -> 7.16 us  [swap(): return lax.ppermute(x, 'fsdp', [(d, d ^ j) for d in range(n_fsdp)])]
  transfers between devices with their start and end apart: 26 -> 26, of which waited for: 9 -> 8; matrix products, arithmetic and copies ran while one was open for 3% -> 3% of each run, Pallas kernels for 27% -> 30%
where the time goes in v7:
time: 56.2 us; the launch traced here: 55.9 us
  Pallas kernels  19.9 us (35%)
  waiting for transfers between devices  17 us (30%)
  starting transfers between devices  15.4 us (27%)
  matrix products  1.49 us (3%)
  local copies, waits for them, and re-layouts  1.04 us (2%)
  between operations  0.92 us (2%)
    ppermute x22, starting transfers between devices, swap(): return lax.ppermute(x, 'fsdp', [(d, d ^ j) for d in range(n_fsdp)])  12.4 us
    ppermute x4, waiting for transfers between devices, along(): return lax.ppermute(x, 'ctx', pairs)  9.87 us
    ppermute x22, waiting for transfers between devices, swap(): return lax.ppermute(x, 'fsdp', [(d, d ^ j) for d in range(n_fsdp)])  7.16 us
    pallas_call x1, Pallas kernels, head_body(): call(lift_kernel, 'lift', 16, 4 * 10 ** 9, [SMEM, VMEM] + piece_specs + [...  6.12 us
    pallas_call x1, Pallas kernels, head_body(): call(own_kernel, 'own_block', 12, 3 * 10 ** 9, [SMEM, VMEM, VMEM, VMEM],...  4.3 us
    pallas_call x1, Pallas kernels, head_body(): call(latent_kernel, 'latents', 18, 2 * 10 ** 9, [SMEM, VMEM] + piece_spec...  4.03 us
    ppermute x4, starting transfers between devices, along(): return lax.ppermute(x, 'ctx', pairs)  3.07 us
    pallas_call x1, Pallas kernels, head_body(): call(out_kernel, 'project_out', 12, 10 ** 9, [SMEM, VMEM, VMEM] + piece_s...  2.44 us
  transfers between devices with their start and end apart: 26, of which 8 were waited for; matrix products, arithmetic and copies ran while one was open for 3% of the time, Pallas kernels for 30%

profile of v7, /device:TPU:24, one launch (start us, length us, event | category | flops | bytes accessed | tf_op | source)
XLA Modules:
  0.0 55.9 jit_solution(15772396125259079685)
XLA Ops:
  0.6 0.0 copy-start.2
  0.7 0.1 collective-permute-start
  0.8 0.1 pad_add_fusion.where_ref
  0.9 1.5 %fusion.total_ref = f32[128,1024]{1,0:T(8,128)S(1)} fusion(bf16[384,1024]{1,0:T(8,128)(2,1)} %param.11, bf16[256,768]{1,0:T(8,128)(2,1)} %bytes_ref.1, s32[]{:T(128)S(6)} %select_n.19, s32[]{:T(128)S(6)} %select_n.20), kind=kOutput, calls=%fused_computation | convolution fusion | flops 100663296 | bytes 1409032 | tf_op jit(solution)/shard_map/dot_general | solution.py:393
  2.4 0.9 %collective-permute-done.conv_ref = bf16[384,1024]{1,0:T(8,128)(2,1)S(1)} collective-permute-done((bf16[384,1024]{1,0:T(8,128)(2,1)}, bf16[384,1024]{1,0:T(8,128)(2,1)S(1)}, u32[]{:S(2)}, u32[]{:S(2)}) %collective-permute-start) | collective-permute-done | bytes 786464 | tf_op jit(solution)/shard_map/ppermute | solution.py:377
  3.2 1.0 %copy-done = bf16[256,768]{1,0:T(8,128)(2,1)S(1)} copy-done((bf16[256,768]{1,0:T(8,128)(2,1)S(1)}, bf16[256,768]{1,0:T(8,128)(2,1)}, u32[]{:S(2)}) %copy-start) | copy-done | bytes 393240
  4.2 0.9 %tap_table.1.own = bf16[128,1024]{1,0:T(8,128)(2,1)S(1)} custom-call(s32[3]{0:T(128)S(1)} %pad_add_fusion.where_ref, bf16[256,768]{1,0:T(8,128)(2,1)S(1)} %copy-done, bf16[384,1024]{1,0:T(8,128)(2,1)S(1)} %collective-permute-done.conv_ref, f32[128,1024]{1,0:T(8,128)S(1)} %fusion.total_ref), custom_call_target="tpu_custom_call" | custom-call | flops 100000000 | bytes 4194304 | tf_op jit(solution)/shard_map/tap_table/pallas_call | solution.py:395
  5.1 0.0 copy-start.7
  5.1 2.5 %collective-permute-start.1 = (bf16[128,1024]{1,0:T(8,128)(2,1)S(1)}, bf16[128,1024]{1,0:T(8,128)(2,1)S(1)}, u32[]{:S(2)}, u32[]{:S(2)}) collective-permute-start(bf16[128,1024]{1,0:T(8,128)(2,1)S(1)} %tap_table.1.own), channel_id=1, source_target_pairs={{0,24},{4,28},{8,16},{12,20},{16,8},{20,12},{24,0},{28,4},{1,25},{... | collective-permute-start | bytes 786440 | tf_op jit(solution)/shard_map/ppermute | solution.py:377
  7.6 0.5 collective-permute-start.5
  8.1 0.5 collective-permute-start.6
  8.7 0.4 collective-permute-start.2
  9.1 1.3 %collective-permute-start.3 = (s32[1,1024]{1,0:T(1,128)S(1)}, s32[1,1024]{1,0:T(1,128)S(1)}, u32[]{:S(2)}, u32[]{:S(2)}) collective-permute-start(s32[1,1024]{1,0:T(1,128)S(1)} %copy-done.6), channel_id=1, source_target_pairs={{0,2},{1,3},{4,6},{5,7},{8,10},{9,11},{12,14},{13,15},{16,18},{17,... | collective-permute-start | bytes 12296 | tf_op jit(solution)/shard_map/ppermute | solution.py:380
  10.4 1.9 %collective-permute-done.2.ids_refs_1_ = s32[1,1024]{1,0:T(1,128)S(1)} collective-permute-done((s32[1,1024]{1,0:T(1,128)S(1)}, s32[1,1024]{1,0:T(1,128)S(1)}, u32[]{:S(2)}, u32[]{:S(2)}) %collective-permute-start.2) | collective-permute-done | bytes 4128 | tf_op jit(solution)/shard_map/ppermute | solution.py:380
  12.3 1.3 %collective-permute-start.4 = (s32[1,1024]{1,0:T(1,128)S(1)}, s32[1,1024]{1,0:T(1,128)S(1)}, u32[]{:S(2)}, u32[]{:S(2)}) collective-permute-start(s32[1,1024]{1,0:T(1,128)S(1)} %copy-done.6), channel_id=1, source_target_pairs={{0,3},{1,2},{4,7},{5,6},{8,11},{9,10},{12,15},{13,14},{16,19},{17,... | collective-permute-start | bytes 12296 | tf_op jit(solution)/shard_map/ppermute | solution.py:380
  13.6 0.6 %qkv_part.1 = (bf16[128,768]{1,0:T(8,128)(2,1)S(1)}, s32[1,256]{1,0:T(1,128)S(1)}, f32[520,128]{1,0:T(8,128)S(1)}) custom-call(s32[3]{0:T(128)S(1)} %pad_add_fusion.where_ref, bf16[128,1536]{1,0:T(8,128)(2,1)S(1)} %copy-done.1, s32[1,256]{1,0:T(1,128)S(1)} %copy-done.3, f32[520,128]{1,0:T(8,128)S(1)} %copy-done.2), custom_call_target="tpu_custom_call" | custom-call | flops 100000000 | bytes 4194304 | tf_op jit(solution)/shard_map/qkv_part/pallas_call | solution.py:410
  14.2 1.3 %collective-permute-done.3.ids_refs_2_ = s32[1,1024]{1,0:T(1,128)S(1)} collective-permute-done((s32[1,1024]{1,0:T(1,128)S(1)}, s32[1,1024]{1,0:T(1,128)S(1)}, u32[]{:S(2)}, u32[]{:S(2)}) %collective-permute-start.3) | collective-permute-done | bytes 4128 | tf_op jit(solution)/shard_map/ppermute | solution.py:380
  15.5 0.0 collective-permute-start.10
  15.5 4.1 %collective-permute-done.4.ids_refs_3_ = s32[1,1024]{1,0:T(1,128)S(1)} collective-permute-done((s32[1,1024]{1,0:T(1,128)S(1)}, s32[1,1024]{1,0:T(1,128)S(1)}, u32[]{:S(2)}, u32[]{:S(2)}) %collective-permute-start.4) | collective-permute-done | bytes 4128 | tf_op jit(solution)/shard_map/ppermute | solution.py:380
  19.6 1.6 %one_hot.1.hot_ref = bf16[4,256,1024]{2,1,0:T(8,128)(2,1)S(1)} custom-call(s32[3]{0:T(128)S(1)} %pad_add_fusion.where_ref, s32[1,1024]{1,0:T(1,128)S(1)} %copy-done.6, s32[1,1024]{1,0:T(1,128)S(1)} %collective-permute-done.2.ids_refs_1_, s32[1,1024]{1,0:T(1,128)S(1)} %collective-permute-done.3.ids_refs_2_, s32[1,1024]{1,0:T(1,128)S(1)} %collective-permute-done.4.ids_refs_3_), custom_call_target="tpu_custom_call" | custom-call | flops 1000000000 | bytes 4194304 | tf_op jit(solution)/shard_map/one_hot/pallas_call | solution.py:407
  21.1 0.0 collective-permute-done.1.near_2_
  21.1 0.1 collective-permute-start.13
  21.2 0.0 collective-permute-done.5.near_0_
  21.2 0.5 collective-permute-start.11
  21.7 0.0 collective-permute-done.6.near_1_
  21.7 0.1 collective-permute-start.12
  21.8 1.5 %collective-permute-start.7 = (bf16[128,768]{1,0:T(8,128)(2,1)S(1)}, bf16[128,768]{1,0:T(8,128)(2,1)S(1)}, u32[]{:S(2)}, u32[]{:S(2)}) collective-permute-start(bf16[128,768]{1,0:T(8,128)(2,1)S(1)} %get-tuple-element.33.own), channel_id=1, source_target_pairs={{0,8},{4,12},{8,0},{12,4},{16,24},{20,28},{24,16},{28,20},{1,9},{5... | collective-permute-start | bytes 589832 | tf_op jit(solution)/shard_map/ppermute | solution.py:377
  23.3 0.0 collective-permute-done.10.mate_own
  23.3 1.5 %collective-permute-start.8 = (bf16[128,768]{1,0:T(8,128)(2,1)S(1)}, bf16[128,768]{1,0:T(8,128)(2,1)S(1)}, u32[]{:S(2)}, u32[]{:S(2)}) collective-permute-start(bf16[128,768]{1,0:T(8,128)(2,1)S(1)} %get-tuple-element.33.own), channel_id=1, source_target_pairs={{0,16},{4,20},{8,24},{12,28},{16,0},{20,4},{24,8},{28,12},{1,17},{... | collective-permute-start | bytes 589832 | tf_op jit(solution)/shard_map/ppermute | solution.py:377
  24.8 0.0 collective-permute-done.13.mate_near_2_
  24.8 0.5 collective-permute-start.9
  25.3 0.0 collective-permute-done.11.mate_near_0_
  25.3 0.1 collective-permute-start.14
  25.4 0.0 collective-permute-done.12.mate_near_1_
  25.4 4.0 %latents.1 = (bf16[4,256,1024]{2,1,0:T(8,128)(2,1)S(1)}, bf16[256,1024]{1,0:T(8,128)(2,1)S(1)}) custom-call(s32[3]{0:T(128)S(1)} %pad_add_fusion.where_ref, bf16[4,256,1024]{2,1,0:T(8,128)(2,1)S(1)} %one_hot.1.hot_ref, bf16[128,1024]{1,0:T(8,128)(2,1)S(1)} %tap_table.1.own, bf16[128,1024]{1,0:T(8,128)(2,1)S(1)} %collective-permute-done.5.near_0_, ...), custom_call_target="tpu_custom_call" | custom-call | flops 2000000000 | bytes 4194304 | tf_op jit(solution)/shard_map/latents/pallas_call | solution.py:421
  29.5 0.1 collective-permute-done.7.near_0_
  29.5 5.0 %collective-permute-done.8.near_1_ = bf16[128,768]{1,0:T(8,128)(2,1)S(1)} collective-permute-done((bf16[128,768]{1,0:T(8,128)(2,1)S(1)}, bf16[128,768]{1,0:T(8,128)(2,1)S(1)}, u32[]{:S(2)}, u32[]{:S(2)}) %collective-permute-start.8) | collective-permute-done | bytes 196640 | tf_op jit(solution)/shard_map/ppermute | solution.py:377
  34.5 0.0 collective-permute-done.9.near_2_
  34.5 0.0 collective-permute-start.15
  34.5 0.5 collective-permute-start.16
  35.0 0.0 collective-permute-start.17
  35.0 1.2 %collective-permute-start.18 = (bf16[128,1024]{1,0:T(8,128)(2,1)S(1)}, bf16[128,1024]{1,0:T(8,128)(2,1)S(1)}, u32[]{:S(2)}, u32[]{:S(2)}) collective-permute-start(bf16[128,1024]{1,0:T(8,128)(2,1)S(1)} %copy-done.5), channel_id=1, source_target_pairs={{0,8},{4,12},{8,0},{12,4},{16,24},{20,28},{24,16},{28,20},{1,9},{5... | collective-permute-start | bytes 786440 | tf_op jit(solution)/shard_map/ppermute | solution.py:377
  36.2 0.0 collective-permute-done.14.mate_own
  36.2 0.8 %collective-permute-start.19 = (bf16[128,1024]{1,0:T(8,128)(2,1)S(1)}, bf16[128,1024]{1,0:T(8,128)(2,1)S(1)}, u32[]{:S(2)}, u32[]{:S(2)}) collective-permute-start(bf16[128,1024]{1,0:T(8,128)(2,1)S(1)} %copy-done.5), channel_id=1, source_target_pairs={{0,16},{4,20},{8,24},{12,28},{16,0},{20,4},{24,8},{28,12},{1,17},{... | collective-permute-start | bytes 786440 | tf_op jit(solution)/shard_map/ppermute | solution.py:377
  37.0 0.0 collective-permute-done.15.mate_near_0_
  37.1 1.4 %collective-permute-start.20 = (bf16[128,1024]{1,0:T(8,128)(2,1)S(1)}, bf16[128,1024]{1,0:T(8,128)(2,1)S(1)}, u32[]{:S(2)}, u32[]{:S(2)}) collective-permute-start(bf16[128,1024]{1,0:T(8,128)(2,1)S(1)} %copy-done.5), channel_id=1, source_target_pairs={{0,24},{4,28},{8,16},{12,20},{16,8},{20,12},{24,0},{28,4},{1,25},{... | collective-permute-start | bytes 786440 | tf_op jit(solution)/shard_map/ppermute | solution.py:377
  38.5 0.0 collective-permute-done.16.mate_near_1_
  38.5 0.0 collective-permute-start.22
  38.5 0.0 collective-permute-done.17.mate_near_2_
  38.5 6.1 %lift.1 = (bf16[256,512]{1,0:T(8,128)(2,1)S(1)}, bf16[8,256,64]{2,1,0:T(8,128)(2,1)S(1)}, bf16[2,1024,64]{2,1,0:T(8,128)(2,1)S(1)}, bf16[2,80,1024]{2,1,0:T(8,128)(2,1)S(1)}) custom-call(s32[3]{0:T(128)S(1)} %pad_add_fusion.where_ref, bf16[4,256,1024]{2,1,0:T(8,128)(2,1)S(1)} %get-tuple-element.36.normed_ref, bf16[128,768]{1,0:T(8,128)(2,1)S(1)} %get-tuple-element.33.own, ...), custom_call_target="tpu_custom_call" | custom-call | flops 4000000000 | bytes 4194304 | tf_op jit(solution)/shard_map/lift/pallas_call | solution.py:432
  44.6 0.1 collective-permute-start.21
  44.7 0.0 copy-start.4
  44.7 4.3 %own_block.1.own_att = bf16[256,512]{1,0:T(8,128)(2,1)S(1)} custom-call(s32[3]{0:T(128)S(1)} %pad_add_fusion.where_ref, bf16[8,256,64]{2,1,0:T(8,128)(2,1)S(1)} %get-tuple-element.41.query_ref, bf16[2,1024,64]{2,1,0:T(8,128)(2,1)S(1)} %get-tuple-element.42.k_ref, bf16[2,80,1024]{2,1,0:T(8,128)(2,1)S(1)} %get-tuple-element.43.v_ref), custom_call_target="tpu_custom_call" | custom-call | flops 3000000000 | bytes 4194304 | tf_op jit(solution)/shard_map/own_block/pallas_call | solution.py:445
  49.0 0.0 collective-permute-done.18.near_0_
  49.0 0.0 collective-permute-done.19.near_1_
  49.1 1.2 %collective-permute-done.20.near_2_ = bf16[128,1024]{1,0:T(8,128)(2,1)S(1)} collective-permute-done((bf16[128,1024]{1,0:T(8,128)(2,1)S(1)}, bf16[128,1024]{1,0:T(8,128)(2,1)S(1)}, u32[]{:S(2)}, u32[]{:S(2)}) %collective-permute-start.20) | collective-permute-done | bytes 262176 | tf_op jit(solution)/shard_map/ppermute | solution.py:377
  50.3 0.0 collective-permute-start.23
  50.3 0.5 collective-permute-start.24
  50.8 0.0 collective-permute-start.25
  50.8 2.6 %collective-permute-done.21.mate_att = bf16[256,512]{1,0:T(8,128)(2,1)S(1)} collective-permute-done((bf16[256,512]{1,0:T(8,128)(2,1)S(1)}, bf16[256,512]{1,0:T(8,128)(2,1)S(1)}, u32[]{:S(2)}, u32[]{:S(2)}) %collective-permute-start.21) | collective-permute-done | bytes 262176 | tf_op jit(solution)/shard_map/ppermute | solution.py:380
  53.4 0.0 collective-permute-done.23.mate_near_0_
  53.4 0.0 collective-permute-done.24.mate_near_1_
  53.4 0.0 collective-permute-done.25.mate_near_2_
  53.4 2.4 %project_out.1 = (bf16[256,1024]{1,0:T(8,128)(2,1)}, f32[1,256]{1,0:T(1,128)}) custom-call(s32[3]{0:T(128)S(1)} %pad_add_fusion.where_ref, bf16[256,512]{1,0:T(8,128)(2,1)S(1)} %own_block.1.own_att, bf16[256,512]{1,0:T(8,128)(2,1)S(1)} %collective-permute-done.21.mate_att, bf16[128,1024]{1,0:T(8,128)(2,1)S(1)} %copy-done.5, ...), custom_call_target="tpu_custom_call" | custom-call | flops 1000000000 | bytes 4194304 | tf_op jit(solution)/shard_map/project_out/pallas_call | solution.py:449
  (14 shorter events, 0.0 us)
Async XLA Ops:
  0.6 12.9 %copy-start.2 = (f32[520,128]{1,0:T(8,128)S(1)}, f32[520,128]{1,0:T(8,128)}, u32[]{:S(2)}) copy-start(f32[520,128]{1,0:T(8,128)} %constant.44.clone.rope_ref) | copy-start | bytes 798724
  0.6 12.9 %copy-start.1 = (bf16[128,1536]{1,0:T(8,128)(2,1)S(1)}, bf16[128,1536]{1,0:T(8,128)(2,1)}, u32[]{:S(2)}) copy-start(bf16[128,1536]{1,0:T(8,128)(2,1)} %qkv_ref) | copy-start | bytes 1179652
  0.7 8.0 %copy-start.6 = (s32[1,1024]{1,0:T(1,128)S(1)}, s32[1,1024]{1,0:T(1,128)}, u32[]{:S(2)}) copy-start(s32[1,1024]{1,0:T(1,128)} %ids_refs_0_) | copy-start | bytes 12292
  0.7 12.9 %copy-start.3 = (s32[1,256]{1,0:T(1,128)S(1)}, s32[1,256]{1,0:T(1,128)}, u32[]{:S(2)}) copy-start(s32[1,256]{1,0:T(1,128)} %align_ref.1) | copy-start | bytes 3076
  0.7 2.6 %collective-permute-start = (bf16[384,1024]{1,0:T(8,128)(2,1)}, bf16[384,1024]{1,0:T(8,128)(2,1)S(1)}, u32[]{:S(2)}, u32[]{:S(2)}) collective-permute-start(bf16[384,1024]{1,0:T(8,128)(2,1)} %param.11), channel_id=1, source_target_pairs={{0,4},{4,0},{8,12},{12,8},{16,20},{20,16},{24,28},{28,24},{1,5},{5... | collective-permute-start | bytes 2359304 | tf_op jit(solution)/shard_map/ppermute | solution.py:377
  3.2 1.0 %copy-start = (bf16[256,768]{1,0:T(8,128)(2,1)S(1)}, bf16[256,768]{1,0:T(8,128)(2,1)}, u32[]{:S(2)}) copy-start(bf16[256,768]{1,0:T(8,128)(2,1)} %bytes_ref.1) | copy-start | bytes 1179652
  5.1 20.2 %copy-start.7 = (bf16[1024]{0:T(1024)(128)(2,1)S(1)}, bf16[1024]{0:T(1024)(128)(2,1)}, u32[]{:S(2)}) copy-start(bf16[1024]{0:T(1024)(128)(2,1)} %param.14) | copy-start | bytes 6148
  5.1 16.0 %collective-permute-start.1 = (bf16[128,1024]{1,0:T(8,128)(2,1)S(1)}, bf16[128,1024]{1,0:T(8,128)(2,1)S(1)}, u32[]{:S(2)}, u32[]{:S(2)}) collective-permute-start(bf16[128,1024]{1,0:T(8,128)(2,1)S(1)} %tap_table.1.own), channel_id=1, source_target_pairs={{0,24},{4,28},{8,16},{12,20},{16,8},{20,12},{24,0},{28,4},{1,25},{... | collective-permute-start | bytes 786440 | tf_op jit(solution)/shard_map/ppermute | solution.py:377
  7.6 13.6 %collective-permute-start.5 = (bf16[128,1024]{1,0:T(8,128)(2,1)S(1)}, bf16[128,1024]{1,0:T(8,128)(2,1)S(1)}, u32[]{:S(2)}, u32[]{:S(2)}) collective-permute-start(bf16[128,1024]{1,0:T(8,128)(2,1)S(1)} %tap_table.1.own), channel_id=1, source_target_pairs={{0,8},{4,12},{8,0},{12,4},{16,24},{20,28},{24,16},{28,20},{1,9},{5... | collective-permute-start | bytes 786440 | tf_op jit(solution)/shard_map/ppermute | solution.py:377
  8.1 13.6 %collective-permute-start.6 = (bf16[128,1024]{1,0:T(8,128)(2,1)S(1)}, bf16[128,1024]{1,0:T(8,128)(2,1)S(1)}, u32[]{:S(2)}, u32[]{:S(2)}) collective-permute-start(bf16[128,1024]{1,0:T(8,128)(2,1)S(1)} %tap_table.1.own), channel_id=1, source_target_pairs={{0,16},{4,20},{8,24},{12,28},{16,0},{20,4},{24,8},{28,12},{1,17},{... | collective-permute-start | bytes 786440 | tf_op jit(solution)/shard_map/ppermute | solution.py:377
  8.7 3.6 %collective-permute-start.2 = (s32[1,1024]{1,0:T(1,128)S(1)}, s32[1,1024]{1,0:T(1,128)S(1)}, u32[]{:S(2)}, u32[]{:S(2)}) collective-permute-start(s32[1,1024]{1,0:T(1,128)S(1)} %copy-done.6), channel_id=1, source_target_pairs={{0,1},{1,0},{2,3},{3,2},{4,5},{5,4},{6,7},{7,6},{8,9},{9,8},{10,11... | collective-permute-start | bytes 12296 | tf_op jit(solution)/shard_map/ppermute | solution.py:380
  9.1 6.4 %collective-permute-start.3 = (s32[1,1024]{1,0:T(1,128)S(1)}, s32[1,1024]{1,0:T(1,128)S(1)}, u32[]{:S(2)}, u32[]{:S(2)}) collective-permute-start(s32[1,1024]{1,0:T(1,128)S(1)} %copy-done.6), channel_id=1, source_target_pairs={{0,2},{1,3},{4,6},{5,7},{8,10},{9,11},{12,14},{13,15},{16,18},{17,... | collective-permute-start | bytes 12296 | tf_op jit(solution)/shard_map/ppermute | solution.py:380
  12.3 7.3 %collective-permute-start.4 = (s32[1,1024]{1,0:T(1,128)S(1)}, s32[1,1024]{1,0:T(1,128)S(1)}, u32[]{:S(2)}, u32[]{:S(2)}) collective-permute-start(s32[1,1024]{1,0:T(1,128)S(1)} %copy-done.6), channel_id=1, source_target_pairs={{0,3},{1,2},{4,7},{5,6},{8,11},{9,10},{12,15},{13,14},{16,19},{17,... | collective-permute-start | bytes 12296 | tf_op jit(solution)/shard_map/ppermute | solution.py:380
  15.5 7.8 %collective-permute-start.10 = (bf16[128,1024]{1,0:T(8,128)(2,1)S(1)}, bf16[128,1024]{1,0:T(8,128)(2,1)S(1)}, u32[]{:S(2)}, u32[]{:S(2)}) collective-permute-start(bf16[128,1024]{1,0:T(8,128)(2,1)S(1)} %tap_table.1.own), channel_id=1, source_target_pairs={{0,4},{4,0},{8,12},{12,8},{16,20},{20,16},{24,28},{28,24},{1,5},{5... | collective-permute-start | bytes 786440 | tf_op jit(solution)/shard_map/ppermute | solution.py:377
  21.1 3.7 %collective-permute-start.13 = (bf16[128,1024]{1,0:T(8,128)(2,1)S(1)}, bf16[128,1024]{1,0:T(8,128)(2,1)S(1)}, u32[]{:S(2)}, u32[]{:S(2)}) collective-permute-start(bf16[128,1024]{1,0:T(8,128)(2,1)S(1)} %collective-permute-done.1.near_2_), channel_id=1, source_target_pairs={{0,4},{4,0},{8,12},{12,8},{16,20},{20,16},{24,28},{28,24},{1,5},{5... | collective-permute-start | bytes 786440 | tf_op jit(solution)/shard_map/ppermute | solution.py:377
  21.2 4.1 %collective-permute-start.11 = (bf16[128,1024]{1,0:T(8,128)(2,1)S(1)}, bf16[128,1024]{1,0:T(8,128)(2,1)S(1)}, u32[]{:S(2)}, u32[]{:S(2)}) collective-permute-start(bf16[128,1024]{1,0:T(8,128)(2,1)S(1)} %collective-permute-done.5.near_0_), channel_id=1, source_target_pairs={{0,4},{4,0},{8,12},{12,8},{16,20},{20,16},{24,28},{28,24},{1,5},{5... | collective-permute-start | bytes 786440 | tf_op jit(solution)/shard_map/ppermute | solution.py:377
  21.7 3.7 %collective-permute-start.12 = (bf16[128,1024]{1,0:T(8,128)(2,1)S(1)}, bf16[128,1024]{1,0:T(8,128)(2,1)S(1)}, u32[]{:S(2)}, u32[]{:S(2)}) collective-permute-start(bf16[128,1024]{1,0:T(8,128)(2,1)S(1)} %collective-permute-done.6.near_1_), channel_id=1, source_target_pairs={{0,4},{4,0},{8,12},{12,8},{16,20},{20,16},{24,28},{28,24},{1,5},{5... | collective-permute-start | bytes 786440 | tf_op jit(solution)/shard_map/ppermute | solution.py:377
  21.8 7.7 %collective-permute-start.7 = (bf16[128,768]{1,0:T(8,128)(2,1)S(1)}, bf16[128,768]{1,0:T(8,128)(2,1)S(1)}, u32[]{:S(2)}, u32[]{:S(2)}) collective-permute-start(bf16[128,768]{1,0:T(8,128)(2,1)S(1)} %get-tuple-element.33.own), channel_id=1, source_target_pairs={{0,8},{4,12},{8,0},{12,4},{16,24},{20,28},{24,16},{28,20},{1,9},{5... | collective-permute-start | bytes 589832 | tf_op jit(solution)/shard_map/ppermute | solution.py:377
  23.3 11.2 %collective-permute-start.8 = (bf16[128,768]{1,0:T(8,128)(2,1)S(1)}, bf16[128,768]{1,0:T(8,128)(2,1)S(1)}, u32[]{:S(2)}, u32[]{:S(2)}) collective-permute-start(bf16[128,768]{1,0:T(8,128)(2,1)S(1)} %get-tuple-element.33.own), channel_id=1, source_target_pairs={{0,16},{4,20},{8,24},{12,28},{16,0},{20,4},{24,8},{28,12},{1,17},{... | collective-permute-start | bytes 589832 | tf_op jit(solution)/shard_map/ppermute | solution.py:377
  24.8 9.7 %collective-permute-start.9 = (bf16[128,768]{1,0:T(8,128)(2,1)S(1)}, bf16[128,768]{1,0:T(8,128)(2,1)S(1)}, u32[]{:S(2)}, u32[]{:S(2)}) collective-permute-start(bf16[128,768]{1,0:T(8,128)(2,1)S(1)} %get-tuple-element.33.own), channel_id=1, source_target_pairs={{0,24},{4,28},{8,16},{12,20},{16,8},{20,12},{24,0},{28,4},{1,25},{... | collective-permute-start | bytes 589832 | tf_op jit(solution)/shard_map/ppermute | solution.py:377
  25.3 9.7 %copy-start.5 = (bf16[128,1024]{1,0:T(8,128)(2,1)S(1)}, bf16[128,1024]{1,0:T(8,128)(2,1)}, u32[]{:S(2)}) copy-start(bf16[128,1024]{1,0:T(8,128)(2,1)} %own) | copy-start | bytes 786436
  25.3 10.9 %collective-permute-start.14 = (bf16[128,768]{1,0:T(8,128)(2,1)S(1)}, bf16[128,768]{1,0:T(8,128)(2,1)S(1)}, u32[]{:S(2)}, u32[]{:S(2)}) collective-permute-start(bf16[128,768]{1,0:T(8,128)(2,1)S(1)} %get-tuple-element.33.own), channel_id=1, source_target_pairs={{0,4},{4,0},{8,12},{12,8},{16,20},{20,16},{24,28},{28,24},{1,5},{5... | collective-permute-start | bytes 589832 | tf_op jit(solution)/shard_map/ppermute | solution.py:377
  34.5 2.6 %collective-permute-start.15 = (bf16[128,768]{1,0:T(8,128)(2,1)S(1)}, bf16[128,768]{1,0:T(8,128)(2,1)S(1)}, u32[]{:S(2)}, u32[]{:S(2)}) collective-permute-start(bf16[128,768]{1,0:T(8,128)(2,1)S(1)} %collective-permute-done.7.near_0_), channel_id=1, source_target_pairs={{0,4},{4,0},{8,12},{12,8},{16,20},{20,16},{24,28},{28,24},{1,5},{5... | collective-permute-start | bytes 589832 | tf_op jit(solution)/shard_map/ppermute | solution.py:377
  34.5 4.0 %collective-permute-start.16 = (bf16[128,768]{1,0:T(8,128)(2,1)S(1)}, bf16[128,768]{1,0:T(8,128)(2,1)S(1)}, u32[]{:S(2)}, u32[]{:S(2)}) collective-permute-start(bf16[128,768]{1,0:T(8,128)(2,1)S(1)} %collective-permute-done.8.near_1_), channel_id=1, source_target_pairs={{0,4},{4,0},{8,12},{12,8},{16,20},{20,16},{24,28},{28,24},{1,5},{5... | collective-permute-start | bytes 589832 | tf_op jit(solution)/shard_map/ppermute | solution.py:377
  35.0 3.5 %collective-permute-start.17 = (bf16[128,768]{1,0:T(8,128)(2,1)S(1)}, bf16[128,768]{1,0:T(8,128)(2,1)S(1)}, u32[]{:S(2)}, u32[]{:S(2)}) collective-permute-start(bf16[128,768]{1,0:T(8,128)(2,1)S(1)} %collective-permute-done.9.near_2_), channel_id=1, source_target_pairs={{0,4},{4,0},{8,12},{12,8},{16,20},{20,16},{24,28},{28,24},{1,5},{5... | collective-permute-start | bytes 589832 | tf_op jit(solution)/shard_map/ppermute | solution.py:377
  35.0 14.0 %collective-permute-start.18 = (bf16[128,1024]{1,0:T(8,128)(2,1)S(1)}, bf16[128,1024]{1,0:T(8,128)(2,1)S(1)}, u32[]{:S(2)}, u32[]{:S(2)}) collective-permute-start(bf16[128,1024]{1,0:T(8,128)(2,1)S(1)} %copy-done.5), channel_id=1, source_target_pairs={{0,8},{4,12},{8,0},{12,4},{16,24},{20,28},{24,16},{28,20},{1,9},{5... | collective-permute-start | bytes 786440 | tf_op jit(solution)/shard_map/ppermute | solution.py:377
  36.2 12.8 %collective-permute-start.19 = (bf16[128,1024]{1,0:T(8,128)(2,1)S(1)}, bf16[128,1024]{1,0:T(8,128)(2,1)S(1)}, u32[]{:S(2)}, u32[]{:S(2)}) collective-permute-start(bf16[128,1024]{1,0:T(8,128)(2,1)S(1)} %copy-done.5), channel_id=1, source_target_pairs={{0,16},{4,20},{8,24},{12,28},{16,0},{20,4},{24,8},{28,12},{1,17},{... | collective-permute-start | bytes 786440 | tf_op jit(solution)/shard_map/ppermute | solution.py:377
  37.1 13.2 %collective-permute-start.20 = (bf16[128,1024]{1,0:T(8,128)(2,1)S(1)}, bf16[128,1024]{1,0:T(8,128)(2,1)S(1)}, u32[]{:S(2)}, u32[]{:S(2)}) collective-permute-start(bf16[128,1024]{1,0:T(8,128)(2,1)S(1)} %copy-done.5), channel_id=1, source_target_pairs={{0,24},{4,28},{8,16},{12,20},{16,8},{20,12},{24,0},{28,4},{1,25},{... | collective-permute-start | bytes 786440 | tf_op jit(solution)/shard_map/ppermute | solution.py:377
  38.5 12.3 %collective-permute-start.22 = (bf16[128,1024]{1,0:T(8,128)(2,1)S(1)}, bf16[128,1024]{1,0:T(8,128)(2,1)S(1)}, u32[]{:S(2)}, u32[]{:S(2)}) collective-permute-start(bf16[128,1024]{1,0:T(8,128)(2,1)S(1)} %copy-done.5), channel_id=1, source_target_pairs={{0,4},{4,0},{8,12},{12,8},{16,20},{20,16},{24,28},{28,24},{1,5},{5... | collective-permute-start | bytes 786440 | tf_op jit(solution)/shard_map/ppermute | solution.py:377
  44.6 8.8 %collective-permute-start.21 = (bf16[256,512]{1,0:T(8,128)(2,1)S(1)}, bf16[256,512]{1,0:T(8,128)(2,1)S(1)}, u32[]{:S(2)}, u32[]{:S(2)}) collective-permute-start(bf16[256,512]{1,0:T(8,128)(2,1)S(1)} %get-tuple-element.46), channel_id=1, source_target_pairs={{0,1},{1,0},{2,3},{3,2},{4,5},{5,4},{6,7},{7,6},{8,9},{9,8},{10,11... | collective-permute-start | bytes 786440 | tf_op jit(solution)/shard_map/ppermute | solution.py:380
  44.7 8.7 %copy-start.4 = (bf16[1,256,1024]{2,1,0:T(8,128)(2,1)S(1)}, bf16[1,256,1024]{2,1,0:T(8,128)(2,1)}, u32[]{:S(2)}) copy-start(bf16[1,256,1024]{2,1,0:T(8,128)(2,1)} %param.15) | copy-start | bytes 1572868
  50.3 3.1 %collective-permute-start.23 = (bf16[128,1024]{1,0:T(8,128)(2,1)S(1)}, bf16[128,1024]{1,0:T(8,128)(2,1)S(1)}, u32[]{:S(2)}, u32[]{:S(2)}) collective-permute-start(bf16[128,1024]{1,0:T(8,128)(2,1)S(1)} %collective-permute-done.18.near_0_), channel_id=1, source_target_pairs={{0,4},{4,0},{8,12},{12,8},{16,20},{20,16},{24,28},{28,24},{1,5},{5... | collective-permute-start | bytes 786440 | tf_op jit(solution)/shard_map/ppermute | solution.py:377
  50.3 3.1 %collective-permute-start.24 = (bf16[128,1024]{1,0:T(8,128)(2,1)S(1)}, bf16[128,1024]{1,0:T(8,128)(2,1)S(1)}, u32[]{:S(2)}, u32[]{:S(2)}) collective-permute-start(bf16[128,1024]{1,0:T(8,128)(2,1)S(1)} %collective-permute-done.19.near_1_), channel_id=1, source_target_pairs={{0,4},{4,0},{8,12},{12,8},{16,20},{20,16},{24,28},{28,24},{1,5},{5... | collective-permute-start | bytes 786440 | tf_op jit(solution)/shard_map/ppermute | solution.py:377
  50.8 2.6 %collective-permute-start.25 = (bf16[128,1024]{1,0:T(8,128)(2,1)S(1)}, bf16[128,1024]{1,0:T(8,128)(2,1)S(1)}, u32[]{:S(2)}, u32[]{:S(2)}) collective-permute-start(bf16[128,1024]{1,0:T(8,128)(2,1)S(1)} %collective-permute-done.20.near_2_), channel_id=1, source_target_pairs={{0,4},{4,0},{8,12},{12,8},{16,20},{20,16},{24,28},{28,24},{1,5},{5... | collective-permute-start | bytes 786440 | tf_op jit(solution)/shard_map/ppermute | solution.py:377

commit v8 on v7

--- a/solution.py
+++ b/solution.py
@@ -404,18 +404,18 @@
         along(ids, [(0, 2), (1, 3)]),
         along(ids, [(0, 3), (1, 2)]),
     )
-    (hot,) = call(
-        one_hot_kernel, "one_hot", 8, 10**9, [SMEM, (VMEM,) * 4], [((n_ctx, rows, KW * VOCAB), bf16)]
-    )(where, ids_all)
     part, align, rope = call(
         part_kernel, "qkv_part", 6, 10**8, [SMEM, VMEM, VMEM, VMEM],
         [((w_qkv.shape[0], part_width), bf16), (align.shape, jnp.int32), (rope.shape, f32)],
     )(where, late_qkv, align, rope)
-    last, hot, part = lax.optimization_barrier((near_t[-1], hot, part))
+    last, ids_all, part = lax.optimization_barrier((near_t[-1], ids_all, part))
     near_t = near_t[:-1] + (last,)
     part, unused = lax.optimization_barrier((part, near_t))
     near_w = to_near(part)
 
+    (hot,) = call(
+        one_hot_kernel, "one_hot", 8, 10**9, [SMEM, (VMEM,) * 4], [((n_ctx, rows, KW * VOCAB), bf16)]
+    )(where, ids_all)
     near_specs = (VMEM,) * (n_fsdp // 2 - 1)
     piece_specs = [VMEM, near_specs, VMEM, near_specs]
     normed, latent = call(

time: 56.2 us -> 55.3 us (0.984); the launches traced: 55.9 us -> 54.4 us
  waiting for transfers between devices: 17 us -> 14.2 us
  starting transfers between devices: 15.4 us -> 16.7 us
    ppermute x22, waiting for transfers between devices: 7.16 us -> 4.55 us  [swap(): return lax.ppermute(x, 'fsdp', [(d, d ^ j) for d in range(n_fsdp)])]
    ppermute x4, starting transfers between devices: 3.07 us -> 4.2 us  [along(): return lax.ppermute(x, 'ctx', pairs)]
  transfers between devices with their start and end apart: 26 -> 26, of which waited for: 8 -> 7; matrix products, arithmetic and copies ran while one was open for 3% -> 3% of each run, Pallas kernels for 30% -> 31%
where the time goes in v8:
time: 55.3 us; the launch traced here: 54.4 us
  Pallas kernels  19.9 us (36%)
  starting transfers between devices  16.7 us (30%)
  waiting for transfers between devices  14.2 us (26%)
  matrix products  1.5 us (3%)
  local copies, waits for them, and re-layouts  1.03 us (2%)
  between operations  0.89 us (2%)
    ppermute x22, starting transfers between devices, swap(): return lax.ppermute(x, 'fsdp', [(d, d ^ j) for d in range(n_fsdp)])  12.5 us
    ppermute x4, waiting for transfers between devices, along(): return lax.ppermute(x, 'ctx', pairs)  9.68 us
    pallas_call x1, Pallas kernels, head_body(): call(lift_kernel, 'lift', 16, 4 * 10 ** 9, [SMEM, VMEM] + piece_specs + [...  6.12 us
    ppermute x22, waiting for transfers between devices, swap(): return lax.ppermute(x, 'fsdp', [(d, d ^ j) for d in range(n_fsdp)])  4.55 us
    pallas_call x1, Pallas kernels, head_body(): call(own_kernel, 'own_block', 12, 3 * 10 ** 9, [SMEM, VMEM, VMEM, VMEM],...  4.31 us
    ppermute x4, starting transfers between devices, along(): return lax.ppermute(x, 'ctx', pairs)  4.2 us
    pallas_call x1, Pallas kernels, head_body(): call(latent_kernel, 'latents', 18, 2 * 10 ** 9, [SMEM, VMEM] + piece_spec...  4.04 us
    pallas_call x1, Pallas kernels, head_body(): call(out_kernel, 'project_out', 12, 10 ** 9, [SMEM, VMEM, VMEM] + piece_s...  2.44 us
  transfers between devices with their start and end apart: 26, of which 7 were waited for; matrix products, arithmetic and copies ran while one was open for 3% of the time, Pallas kernels for 31%

profile of v8, /device:TPU:24, one launch (start us, length us, event | category | flops | bytes accessed | tf_op | source)
XLA Modules:
  0.0 54.4 jit_solution(15690114626535750268)
XLA Ops:
  0.6 0.0 copy-start.2
  0.7 0.1 collective-permute-start
  0.8 0.1 pad_add_fusion.where_ref
  0.9 1.5 %fusion.total_ref = f32[128,1024]{1,0:T(8,128)S(1)} fusion(bf16[384,1024]{1,0:T(8,128)(2,1)} %param.11, bf16[256,768]{1,0:T(8,128)(2,1)} %bytes_ref.1, s32[]{:T(128)S(6)} %select_n.19, s32[]{:T(128)S(6)} %select_n.20), kind=kOutput, calls=%fused_computation | convolution fusion | flops 100663296 | bytes 1409032 | tf_op jit(solution)/shard_map/dot_general | solution.py:393
  2.4 0.9 %collective-permute-done.conv_ref = bf16[384,1024]{1,0:T(8,128)(2,1)S(1)} collective-permute-done((bf16[384,1024]{1,0:T(8,128)(2,1)}, bf16[384,1024]{1,0:T(8,128)(2,1)S(1)}, u32[]{:S(2)}, u32[]{:S(2)}) %collective-permute-start) | collective-permute-done | bytes 786464 | tf_op jit(solution)/shard_map/ppermute | solution.py:377
  3.2 1.0 %copy-done = bf16[256,768]{1,0:T(8,128)(2,1)S(1)} copy-done((bf16[256,768]{1,0:T(8,128)(2,1)S(1)}, bf16[256,768]{1,0:T(8,128)(2,1)}, u32[]{:S(2)}) %copy-start) | copy-done | bytes 393240
  4.2 0.8 %tap_table.1.own = bf16[128,1024]{1,0:T(8,128)(2,1)S(1)} custom-call(s32[3]{0:T(128)S(1)} %pad_add_fusion.where_ref, bf16[256,768]{1,0:T(8,128)(2,1)S(1)} %copy-done, bf16[384,1024]{1,0:T(8,128)(2,1)S(1)} %collective-permute-done.conv_ref, f32[128,1024]{1,0:T(8,128)S(1)} %fusion.total_ref), custom_call_target="tpu_custom_call" | custom-call | flops 100000000 | bytes 4194304 | tf_op jit(solution)/shard_map/tap_table/pallas_call | solution.py:395
  5.1 2.5 %collective-permute-start.1 = (bf16[128,1024]{1,0:T(8,128)(2,1)S(1)}, bf16[128,1024]{1,0:T(8,128)(2,1)S(1)}, u32[]{:S(2)}, u32[]{:S(2)}) collective-permute-start(bf16[128,1024]{1,0:T(8,128)(2,1)S(1)} %tap_table.1.own), channel_id=1, source_target_pairs={{0,24},{4,28},{8,16},{12,20},{16,8},{20,12},{24,0},{28,4},{1,25},{... | collective-permute-start | bytes 786440 | tf_op jit(solution)/shard_map/ppermute | solution.py:377
  7.6 0.5 collective-permute-start.5
  8.1 0.5 collective-permute-start.6
  8.7 0.4 collective-permute-start.2
  9.1 1.3 %collective-permute-start.3 = (s32[1,1024]{1,0:T(1,128)S(1)}, s32[1,1024]{1,0:T(1,128)S(1)}, u32[]{:S(2)}, u32[]{:S(2)}) collective-permute-start(s32[1,1024]{1,0:T(1,128)S(1)} %copy-done.6), channel_id=1, source_target_pairs={{0,2},{1,3},{4,6},{5,7},{8,10},{9,11},{12,14},{13,15},{16,18},{17,... | collective-permute-start | bytes 12296 | tf_op jit(solution)/shard_map/ppermute | solution.py:380
  10.4 1.9 %collective-permute-done.2.ids_refs_1_ = s32[1,1024]{1,0:T(1,128)S(1)} collective-permute-done((s32[1,1024]{1,0:T(1,128)S(1)}, s32[1,1024]{1,0:T(1,128)S(1)}, u32[]{:S(2)}, u32[]{:S(2)}) %collective-permute-start.2) | collective-permute-done | bytes 4128 | tf_op jit(solution)/shard_map/ppermute | solution.py:380
  12.3 1.3 %collective-permute-start.4 = (s32[1,1024]{1,0:T(1,128)S(1)}, s32[1,1024]{1,0:T(1,128)S(1)}, u32[]{:S(2)}, u32[]{:S(2)}) collective-permute-start(s32[1,1024]{1,0:T(1,128)S(1)} %copy-done.6), channel_id=1, source_target_pairs={{0,3},{1,2},{4,7},{5,6},{8,11},{9,10},{12,15},{13,14},{16,19},{17,... | collective-permute-start | bytes 12296 | tf_op jit(solution)/shard_map/ppermute | solution.py:380
  13.6 0.6 %qkv_part.1 = (bf16[128,768]{1,0:T(8,128)(2,1)S(1)}, s32[1,256]{1,0:T(1,128)S(1)}, f32[520,128]{1,0:T(8,128)S(1)}) custom-call(s32[3]{0:T(128)S(1)} %pad_add_fusion.where_ref, bf16[128,1536]{1,0:T(8,128)(2,1)S(1)} %copy-done.1, s32[1,256]{1,0:T(1,128)S(1)} %copy-done.3, f32[520,128]{1,0:T(8,128)S(1)} %copy-done.2), custom_call_target="tpu_custom_call" | custom-call | flops 100000000 | bytes 4194304 | tf_op jit(solution)/shard_map/qkv_part/pallas_call | solution.py:407
  14.2 1.3 %collective-permute-done.3.ids_refs_2_ = s32[1,1024]{1,0:T(1,128)S(1)} collective-permute-done((s32[1,1024]{1,0:T(1,128)S(1)}, s32[1,1024]{1,0:T(1,128)S(1)}, u32[]{:S(2)}, u32[]{:S(2)}) %collective-permute-start.3) | collective-permute-done | bytes 4128 | tf_op jit(solution)/shard_map/ppermute | solution.py:380
  15.5 0.0 collective-permute-start.10
  15.5 4.1 %collective-permute-done.4.ids_refs_3_ = s32[1,1024]{1,0:T(1,128)S(1)} collective-permute-done((s32[1,1024]{1,0:T(1,128)S(1)}, s32[1,1024]{1,0:T(1,128)S(1)}, u32[]{:S(2)}, u32[]{:S(2)}) %collective-permute-start.4) | collective-permute-done | bytes 4128 | tf_op jit(solution)/shard_map/ppermute | solution.py:380
  19.5 0.0 collective-permute-done.1.near_2_
  19.6 0.0 collective-permute-start.13
  19.6 0.6 %collective-permute-done.5.near_0_ = bf16[128,1024]{1,0:T(8,128)(2,1)S(1)} collective-permute-done((bf16[128,1024]{1,0:T(8,128)(2,1)S(1)}, bf16[128,1024]{1,0:T(8,128)(2,1)S(1)}, u32[]{:S(2)}, u32[]{:S(2)}) %collective-permute-start.5) | collective-permute-done | bytes 262176 | tf_op jit(solution)/shard_map/ppermute | solution.py:377
  20.1 0.0 collective-permute-start.11
  20.1 0.0 collective-permute-done.6.near_1_
  20.1 0.5 collective-permute-start.12
  20.7 1.5 %collective-permute-start.7 = (bf16[128,768]{1,0:T(8,128)(2,1)S(1)}, bf16[128,768]{1,0:T(8,128)(2,1)S(1)}, u32[]{:S(2)}, u32[]{:S(2)}) collective-permute-start(bf16[128,768]{1,0:T(8,128)(2,1)S(1)} %get-tuple-element.36.own), channel_id=1, source_target_pairs={{0,8},{4,12},{8,0},{12,4},{16,24},{20,28},{24,16},{28,20},{1,9},{5... | collective-permute-start | bytes 589832 | tf_op jit(solution)/shard_map/ppermute | solution.py:377
  22.2 0.0 collective-permute-done.10.mate_own
  22.2 1.0 %collective-permute-start.8 = (bf16[128,768]{1,0:T(8,128)(2,1)S(1)}, bf16[128,768]{1,0:T(8,128)(2,1)S(1)}, u32[]{:S(2)}, u32[]{:S(2)}) collective-permute-start(bf16[128,768]{1,0:T(8,128)(2,1)S(1)} %get-tuple-element.36.own), channel_id=1, source_target_pairs={{0,16},{4,20},{8,24},{12,28},{16,0},{20,4},{24,8},{28,12},{1,17},{... | collective-permute-start | bytes 589832 | tf_op jit(solution)/shard_map/ppermute | solution.py:377
  23.2 0.0 collective-permute-done.13.mate_near_2_
  23.2 1.0 %collective-permute-start.9 = (bf16[128,768]{1,0:T(8,128)(2,1)S(1)}, bf16[128,768]{1,0:T(8,128)(2,1)S(1)}, u32[]{:S(2)}, u32[]{:S(2)}) collective-permute-start(bf16[128,768]{1,0:T(8,128)(2,1)S(1)} %get-tuple-element.36.own), channel_id=1, source_target_pairs={{0,24},{4,28},{8,16},{12,20},{16,8},{20,12},{24,0},{28,4},{1,25},{... | collective-permute-start | bytes 589832 | tf_op jit(solution)/shard_map/ppermute | solution.py:377
  24.2 1.6 %one_hot.1.hot_ref = bf16[4,256,1024]{2,1,0:T(8,128)(2,1)S(1)} custom-call(s32[3]{0:T(128)S(1)} %pad_add_fusion.where_ref, s32[1,1024]{1,0:T(1,128)S(1)} %copy-done.6, s32[1,1024]{1,0:T(1,128)S(1)} %collective-permute-done.2.ids_refs_1_, s32[1,1024]{1,0:T(1,128)S(1)} %collective-permute-done.3.ids_refs_2_, s32[1,1024]{1,0:T(1,128)S(1)} %collective-permute-done.4.ids_refs_3_), custom_call_target="tpu_custom_call" | custom-call | flops 1000000000 | bytes 4194304 | tf_op jit(solution)/shard_map/one_hot/pallas_call | solution.py:416
  25.8 0.0 copy-start.5
  25.8 0.0 collective-permute-done.11.mate_near_0_
  25.8 0.1 collective-permute-start.14
  25.9 0.0 collective-permute-done.12.mate_near_1_
  25.9 4.0 %latents.1 = (bf16[4,256,1024]{2,1,0:T(8,128)(2,1)S(1)}, bf16[256,1024]{1,0:T(8,128)(2,1)S(1)}) custom-call(s32[3]{0:T(128)S(1)} %pad_add_fusion.where_ref, bf16[4,256,1024]{2,1,0:T(8,128)(2,1)S(1)} %one_hot.1.hot_ref, bf16[128,1024]{1,0:T(8,128)(2,1)S(1)} %tap_table.1.own, bf16[128,1024]{1,0:T(8,128)(2,1)S(1)} %collective-permute-done.5.near_0_, ...), custom_call_target="tpu_custom_call" | custom-call | flops 2000000000 | bytes 4194304 | tf_op jit(solution)/shard_map/latents/pallas_call | solution.py:421
  29.9 0.0 collective-permute-done.7.near_0_
  29.9 3.0 %collective-permute-done.8.near_1_ = bf16[128,768]{1,0:T(8,128)(2,1)S(1)} collective-permute-done((bf16[128,768]{1,0:T(8,128)(2,1)S(1)}, bf16[128,768]{1,0:T(8,128)(2,1)S(1)}, u32[]{:S(2)}, u32[]{:S(2)}) %collective-permute-start.8) | collective-permute-done | bytes 196640 | tf_op jit(solution)/shard_map/ppermute | solution.py:377
  33.0 0.0 collective-permute-done.9.near_2_
  33.0 0.0 collective-permute-start.15
  33.0 0.5 collective-permute-start.16
  33.5 0.0 collective-permute-start.17
  33.5 1.2 %collective-permute-start.18 = (bf16[128,1024]{1,0:T(8,128)(2,1)S(1)}, bf16[128,1024]{1,0:T(8,128)(2,1)S(1)}, u32[]{:S(2)}, u32[]{:S(2)}) collective-permute-start(bf16[128,1024]{1,0:T(8,128)(2,1)S(1)} %copy-done.5), channel_id=1, source_target_pairs={{0,8},{4,12},{8,0},{12,4},{16,24},{20,28},{24,16},{28,20},{1,9},{5... | collective-permute-start | bytes 786440 | tf_op jit(solution)/shard_map/ppermute | solution.py:377
  34.6 0.0 collective-permute-done.14.mate_own
  34.6 0.8 %collective-permute-start.19 = (bf16[128,1024]{1,0:T(8,128)(2,1)S(1)}, bf16[128,1024]{1,0:T(8,128)(2,1)S(1)}, u32[]{:S(2)}, u32[]{:S(2)}) collective-permute-start(bf16[128,1024]{1,0:T(8,128)(2,1)S(1)} %copy-done.5), channel_id=1, source_target_pairs={{0,16},{4,20},{8,24},{12,28},{16,0},{20,4},{24,8},{28,12},{1,17},{... | collective-permute-start | bytes 786440 | tf_op jit(solution)/shard_map/ppermute | solution.py:377
  35.5 0.0 collective-permute-done.15.mate_near_0_
  35.5 1.5 %collective-permute-start.20 = (bf16[128,1024]{1,0:T(8,128)(2,1)S(1)}, bf16[128,1024]{1,0:T(8,128)(2,1)S(1)}, u32[]{:S(2)}, u32[]{:S(2)}) collective-permute-start(bf16[128,1024]{1,0:T(8,128)(2,1)S(1)} %copy-done.5), channel_id=1, source_target_pairs={{0,24},{4,28},{8,16},{12,20},{16,8},{20,12},{24,0},{28,4},{1,25},{... | collective-permute-start | bytes 786440 | tf_op jit(solution)/shard_map/ppermute | solution.py:377
  37.0 0.0 collective-permute-done.16.mate_near_1_
  37.0 0.0 collective-permute-start.22
  37.0 0.0 collective-permute-done.17.mate_near_2_
  37.0 6.1 %lift.1 = (bf16[256,512]{1,0:T(8,128)(2,1)S(1)}, bf16[8,256,64]{2,1,0:T(8,128)(2,1)S(1)}, bf16[2,1024,64]{2,1,0:T(8,128)(2,1)S(1)}, bf16[2,80,1024]{2,1,0:T(8,128)(2,1)S(1)}) custom-call(s32[3]{0:T(128)S(1)} %pad_add_fusion.where_ref, bf16[4,256,1024]{2,1,0:T(8,128)(2,1)S(1)} %get-tuple-element.42.normed_ref, bf16[128,768]{1,0:T(8,128)(2,1)S(1)} %get-tuple-element.36.own, ...), custom_call_target="tpu_custom_call" | custom-call | flops 4000000000 | bytes 4194304 | tf_op jit(solution)/shard_map/lift/pallas_call | solution.py:432
  43.1 1.2 %collective-permute-start.21 = (bf16[256,512]{1,0:T(8,128)(2,1)S(1)}, bf16[256,512]{1,0:T(8,128)(2,1)S(1)}, u32[]{:S(2)}, u32[]{:S(2)}) collective-permute-start(bf16[256,512]{1,0:T(8,128)(2,1)S(1)} %get-tuple-element.52), channel_id=1, source_target_pairs={{0,1},{1,0},{2,3},{3,2},{4,5},{5,4},{6,7},{7,6},{8,9},{9,8},{10,11... | collective-permute-start | bytes 786440 | tf_op jit(solution)/shard_map/ppermute | solution.py:380
  44.3 4.3 %own_block.1.own_att = bf16[256,512]{1,0:T(8,128)(2,1)S(1)} custom-call(s32[3]{0:T(128)S(1)} %pad_add_fusion.where_ref, bf16[8,256,64]{2,1,0:T(8,128)(2,1)S(1)} %get-tuple-element.47.query_ref, bf16[2,1024,64]{2,1,0:T(8,128)(2,1)S(1)} %get-tuple-element.48.k_ref, bf16[2,80,1024]{2,1,0:T(8,128)(2,1)S(1)} %get-tuple-element.49.v_ref), custom_call_target="tpu_custom_call" | custom-call | flops 3000000000 | bytes 4194304 | tf_op jit(solution)/shard_map/own_block/pallas_call | solution.py:445
  48.6 0.0 collective-permute-done.18.near_0_
  48.6 0.0 collective-permute-done.19.near_1_
  48.7 0.0 collective-permute-done.20.near_2_
  48.7 0.3 collective-permute-start.23
  49.0 0.3 collective-permute-start.24
  49.2 0.2 collective-permute-start.25
  49.5 0.0 collective-permute-done.22.mate_own
  49.5 2.4 %collective-permute-done.21.mate_att = bf16[256,512]{1,0:T(8,128)(2,1)S(1)} collective-permute-done((bf16[256,512]{1,0:T(8,128)(2,1)S(1)}, bf16[256,512]{1,0:T(8,128)(2,1)S(1)}, u32[]{:S(2)}, u32[]{:S(2)}) %collective-permute-start.21) | collective-permute-done | bytes 262176 | tf_op jit(solution)/shard_map/ppermute | solution.py:380
  51.9 0.0 collective-permute-done.23.mate_near_0_
  51.9 0.0 collective-permute-done.24.mate_near_1_
  51.9 0.0 collective-permute-done.25.mate_near_2_
  51.9 2.4 %project_out.1 = (bf16[256,1024]{1,0:T(8,128)(2,1)}, f32[1,256]{1,0:T(1,128)}) custom-call(s32[3]{0:T(128)S(1)} %pad_add_fusion.where_ref, bf16[256,512]{1,0:T(8,128)(2,1)S(1)} %own_block.1.own_att, bf16[256,512]{1,0:T(8,128)(2,1)S(1)} %collective-permute-done.21.mate_att, bf16[128,1024]{1,0:T(8,128)(2,1)S(1)} %copy-done.5, ...), custom_call_target="tpu_custom_call" | custom-call | flops 1000000000 | bytes 4194304 | tf_op jit(solution)/shard_map/project_out/pallas_call | solution.py:449
  (14 shorter events, 0.0 us)
Async XLA Ops:
  0.6 12.9 %copy-start.2 = (f32[520,128]{1,0:T(8,128)S(1)}, f32[520,128]{1,0:T(8,128)}, u32[]{:S(2)}) copy-start(f32[520,128]{1,0:T(8,128)} %constant.44.clone.rope_ref) | copy-start | bytes 798724
  0.6 12.9 %copy-start.1 = (bf16[128,1536]{1,0:T(8,128)(2,1)S(1)}, bf16[128,1536]{1,0:T(8,128)(2,1)}, u32[]{:S(2)}) copy-start(bf16[128,1536]{1,0:T(8,128)(2,1)} %qkv_ref) | copy-start | bytes 1179652
  0.7 8.0 %copy-start.6 = (s32[1,1024]{1,0:T(1,128)S(1)}, s32[1,1024]{1,0:T(1,128)}, u32[]{:S(2)}) copy-start(s32[1,1024]{1,0:T(1,128)} %ids_refs_0_) | copy-start | bytes 12292
  0.7 12.9 %copy-start.3 = (s32[1,256]{1,0:T(1,128)S(1)}, s32[1,256]{1,0:T(1,128)}, u32[]{:S(2)}) copy-start(s32[1,256]{1,0:T(1,128)} %align_ref.1) | copy-start | bytes 3076
  0.7 20.0 %copy-start.7 = (bf16[1024]{0:T(1024)(128)(2,1)S(1)}, bf16[1024]{0:T(1024)(128)(2,1)}, u32[]{:S(2)}) copy-start(bf16[1024]{0:T(1024)(128)(2,1)} %param.14) | copy-start | bytes 6148
  0.7 2.6 %collective-permute-start = (bf16[384,1024]{1,0:T(8,128)(2,1)}, bf16[384,1024]{1,0:T(8,128)(2,1)S(1)}, u32[]{:S(2)}, u32[]{:S(2)}) collective-permute-start(bf16[384,1024]{1,0:T(8,128)(2,1)} %param.11), channel_id=1, source_target_pairs={{0,4},{4,0},{8,12},{12,8},{16,20},{20,16},{24,28},{28,24},{1,5},{5... | collective-permute-start | bytes 2359304 | tf_op jit(solution)/shard_map/ppermute | solution.py:377
  3.2 1.0 %copy-start = (bf16[256,768]{1,0:T(8,128)(2,1)S(1)}, bf16[256,768]{1,0:T(8,128)(2,1)}, u32[]{:S(2)}) copy-start(bf16[256,768]{1,0:T(8,128)(2,1)} %bytes_ref.1) | copy-start | bytes 1179652
  5.1 14.5 %collective-permute-start.1 = (bf16[128,1024]{1,0:T(8,128)(2,1)S(1)}, bf16[128,1024]{1,0:T(8,128)(2,1)S(1)}, u32[]{:S(2)}, u32[]{:S(2)}) collective-permute-start(bf16[128,1024]{1,0:T(8,128)(2,1)S(1)} %tap_table.1.own), channel_id=1, source_target_pairs={{0,24},{4,28},{8,16},{12,20},{16,8},{20,12},{24,0},{28,4},{1,25},{... | collective-permute-start | bytes 786440 | tf_op jit(solution)/shard_map/ppermute | solution.py:377
  7.6 12.5 %collective-permute-start.5 = (bf16[128,1024]{1,0:T(8,128)(2,1)S(1)}, bf16[128,1024]{1,0:T(8,128)(2,1)S(1)}, u32[]{:S(2)}, u32[]{:S(2)}) collective-permute-start(bf16[128,1024]{1,0:T(8,128)(2,1)S(1)} %tap_table.1.own), channel_id=1, source_target_pairs={{0,8},{4,12},{8,0},{12,4},{16,24},{20,28},{24,16},{28,20},{1,9},{5... | collective-permute-start | bytes 786440 | tf_op jit(solution)/shard_map/ppermute | solution.py:377
  8.1 12.0 %collective-permute-start.6 = (bf16[128,1024]{1,0:T(8,128)(2,1)S(1)}, bf16[128,1024]{1,0:T(8,128)(2,1)S(1)}, u32[]{:S(2)}, u32[]{:S(2)}) collective-permute-start(bf16[128,1024]{1,0:T(8,128)(2,1)S(1)} %tap_table.1.own), channel_id=1, source_target_pairs={{0,16},{4,20},{8,24},{12,28},{16,0},{20,4},{24,8},{28,12},{1,17},{... | collective-permute-start | bytes 786440 | tf_op jit(solution)/shard_map/ppermute | solution.py:377
  8.7 3.6 %collective-permute-start.2 = (s32[1,1024]{1,0:T(1,128)S(1)}, s32[1,1024]{1,0:T(1,128)S(1)}, u32[]{:S(2)}, u32[]{:S(2)}) collective-permute-start(s32[1,1024]{1,0:T(1,128)S(1)} %copy-done.6), channel_id=1, source_target_pairs={{0,1},{1,0},{2,3},{3,2},{4,5},{5,4},{6,7},{7,6},{8,9},{9,8},{10,11... | collective-permute-start | bytes 12296 | tf_op jit(solution)/shard_map/ppermute | solution.py:380
  9.1 6.4 %collective-permute-start.3 = (s32[1,1024]{1,0:T(1,128)S(1)}, s32[1,1024]{1,0:T(1,128)S(1)}, u32[]{:S(2)}, u32[]{:S(2)}) collective-permute-start(s32[1,1024]{1,0:T(1,128)S(1)} %copy-done.6), channel_id=1, source_target_pairs={{0,2},{1,3},{4,6},{5,7},{8,10},{9,11},{12,14},{13,15},{16,18},{17,... | collective-permute-start | bytes 12296 | tf_op jit(solution)/shard_map/ppermute | solution.py:380
  12.3 7.3 %collective-permute-start.4 = (s32[1,1024]{1,0:T(1,128)S(1)}, s32[1,1024]{1,0:T(1,128)S(1)}, u32[]{:S(2)}, u32[]{:S(2)}) collective-permute-start(s32[1,1024]{1,0:T(1,128)S(1)} %copy-done.6), channel_id=1, source_target_pairs={{0,3},{1,2},{4,7},{5,6},{8,11},{9,10},{12,15},{13,14},{16,19},{17,... | collective-permute-start | bytes 12296 | tf_op jit(solution)/shard_map/ppermute | solution.py:380
  15.5 6.7 %collective-permute-start.10 = (bf16[128,1024]{1,0:T(8,128)(2,1)S(1)}, bf16[128,1024]{1,0:T(8,128)(2,1)S(1)}, u32[]{:S(2)}, u32[]{:S(2)}) collective-permute-start(bf16[128,1024]{1,0:T(8,128)(2,1)S(1)} %tap_table.1.own), channel_id=1, source_target_pairs={{0,4},{4,0},{8,12},{12,8},{16,20},{20,16},{24,28},{28,24},{1,5},{5... | collective-permute-start | bytes 786440 | tf_op jit(solution)/shard_map/ppermute | solution.py:377
  19.6 3.7 %collective-permute-start.13 = (bf16[128,1024]{1,0:T(8,128)(2,1)S(1)}, bf16[128,1024]{1,0:T(8,128)(2,1)S(1)}, u32[]{:S(2)}, u32[]{:S(2)}) collective-permute-start(bf16[128,1024]{1,0:T(8,128)(2,1)S(1)} %collective-permute-done.1.near_2_), channel_id=1, source_target_pairs={{0,4},{4,0},{8,12},{12,8},{16,20},{20,16},{24,28},{28,24},{1,5},{5... | collective-permute-start | bytes 786440 | tf_op jit(solution)/shard_map/ppermute | solution.py:377
  20.1 5.7 %collective-permute-start.11 = (bf16[128,1024]{1,0:T(8,128)(2,1)S(1)}, bf16[128,1024]{1,0:T(8,128)(2,1)S(1)}, u32[]{:S(2)}, u32[]{:S(2)}) collective-permute-start(bf16[128,1024]{1,0:T(8,128)(2,1)S(1)} %collective-permute-done.5.near_0_), channel_id=1, source_target_pairs={{0,4},{4,0},{8,12},{12,8},{16,20},{20,16},{24,28},{28,24},{1,5},{5... | collective-permute-start | bytes 786440 | tf_op jit(solution)/shard_map/ppermute | solution.py:377
  20.1 5.7 %collective-permute-start.12 = (bf16[128,1024]{1,0:T(8,128)(2,1)S(1)}, bf16[128,1024]{1,0:T(8,128)(2,1)S(1)}, u32[]{:S(2)}, u32[]{:S(2)}) collective-permute-start(bf16[128,1024]{1,0:T(8,128)(2,1)S(1)} %collective-permute-done.6.near_1_), channel_id=1, source_target_pairs={{0,4},{4,0},{8,12},{12,8},{16,20},{20,16},{24,28},{28,24},{1,5},{5... | collective-permute-start | bytes 786440 | tf_op jit(solution)/shard_map/ppermute | solution.py:377
  20.7 9.3 %collective-permute-start.7 = (bf16[128,768]{1,0:T(8,128)(2,1)S(1)}, bf16[128,768]{1,0:T(8,128)(2,1)S(1)}, u32[]{:S(2)}, u32[]{:S(2)}) collective-permute-start(bf16[128,768]{1,0:T(8,128)(2,1)S(1)} %get-tuple-element.36.own), channel_id=1, source_target_pairs={{0,8},{4,12},{8,0},{12,4},{16,24},{20,28},{24,16},{28,20},{1,9},{5... | collective-permute-start | bytes 589832 | tf_op jit(solution)/shard_map/ppermute | solution.py:377
  22.2 10.8 %collective-permute-start.8 = (bf16[128,768]{1,0:T(8,128)(2,1)S(1)}, bf16[128,768]{1,0:T(8,128)(2,1)S(1)}, u32[]{:S(2)}, u32[]{:S(2)}) collective-permute-start(bf16[128,768]{1,0:T(8,128)(2,1)S(1)} %get-tuple-element.36.own), channel_id=1, source_target_pairs={{0,16},{4,20},{8,24},{12,28},{16,0},{20,4},{24,8},{28,12},{1,17},{... | collective-permute-start | bytes 589832 | tf_op jit(solution)/shard_map/ppermute | solution.py:377
  23.2 9.7 %collective-permute-start.9 = (bf16[128,768]{1,0:T(8,128)(2,1)S(1)}, bf16[128,768]{1,0:T(8,128)(2,1)S(1)}, u32[]{:S(2)}, u32[]{:S(2)}) collective-permute-start(bf16[128,768]{1,0:T(8,128)(2,1)S(1)} %get-tuple-element.36.own), channel_id=1, source_target_pairs={{0,24},{4,28},{8,16},{12,20},{16,8},{20,12},{24,0},{28,4},{1,25},{... | collective-permute-start | bytes 589832 | tf_op jit(solution)/shard_map/ppermute | solution.py:377
  25.8 7.7 %copy-start.5 = (bf16[128,1024]{1,0:T(8,128)(2,1)S(1)}, bf16[128,1024]{1,0:T(8,128)(2,1)}, u32[]{:S(2)}) copy-start(bf16[128,1024]{1,0:T(8,128)(2,1)} %own) | copy-start | bytes 786436
  25.8 8.8 %collective-permute-start.14 = (bf16[128,768]{1,0:T(8,128)(2,1)S(1)}, bf16[128,768]{1,0:T(8,128)(2,1)S(1)}, u32[]{:S(2)}, u32[]{:S(2)}) collective-permute-start(bf16[128,768]{1,0:T(8,128)(2,1)S(1)} %get-tuple-element.36.own), channel_id=1, source_target_pairs={{0,4},{4,0},{8,12},{12,8},{16,20},{20,16},{24,28},{28,24},{1,5},{5... | collective-permute-start | bytes 589832 | tf_op jit(solution)/shard_map/ppermute | solution.py:377
  33.0 2.5 %collective-permute-start.15 = (bf16[128,768]{1,0:T(8,128)(2,1)S(1)}, bf16[128,768]{1,0:T(8,128)(2,1)S(1)}, u32[]{:S(2)}, u32[]{:S(2)}) collective-permute-start(bf16[128,768]{1,0:T(8,128)(2,1)S(1)} %collective-permute-done.7.near_0_), channel_id=1, source_target_pairs={{0,4},{4,0},{8,12},{12,8},{16,20},{20,16},{24,28},{28,24},{1,5},{5... | collective-permute-start | bytes 589832 | tf_op jit(solution)/shard_map/ppermute | solution.py:377
  33.0 4.0 %collective-permute-start.16 = (bf16[128,768]{1,0:T(8,128)(2,1)S(1)}, bf16[128,768]{1,0:T(8,128)(2,1)S(1)}, u32[]{:S(2)}, u32[]{:S(2)}) collective-permute-start(bf16[128,768]{1,0:T(8,128)(2,1)S(1)} %collective-permute-done.8.near_1_), channel_id=1, source_target_pairs={{0,4},{4,0},{8,12},{12,8},{16,20},{20,16},{24,28},{28,24},{1,5},{5... | collective-permute-start | bytes 589832 | tf_op jit(solution)/shard_map/ppermute | solution.py:377
  33.5 3.5 %collective-permute-start.17 = (bf16[128,768]{1,0:T(8,128)(2,1)S(1)}, bf16[128,768]{1,0:T(8,128)(2,1)S(1)}, u32[]{:S(2)}, u32[]{:S(2)}) collective-permute-start(bf16[128,768]{1,0:T(8,128)(2,1)S(1)} %collective-permute-done.9.near_2_), channel_id=1, source_target_pairs={{0,4},{4,0},{8,12},{12,8},{16,20},{20,16},{24,28},{28,24},{1,5},{5... | collective-permute-start | bytes 589832 | tf_op jit(solution)/shard_map/ppermute | solution.py:377
  33.5 15.2 %collective-permute-start.18 = (bf16[128,1024]{1,0:T(8,128)(2,1)S(1)}, bf16[128,1024]{1,0:T(8,128)(2,1)S(1)}, u32[]{:S(2)}, u32[]{:S(2)}) collective-permute-start(bf16[128,1024]{1,0:T(8,128)(2,1)S(1)} %copy-done.5), channel_id=1, source_target_pairs={{0,8},{4,12},{8,0},{12,4},{16,24},{20,28},{24,16},{28,20},{1,9},{5... | collective-permute-start | bytes 786440 | tf_op jit(solution)/shard_map/ppermute | solution.py:377
  34.6 14.0 %collective-permute-start.19 = (bf16[128,1024]{1,0:T(8,128)(2,1)S(1)}, bf16[128,1024]{1,0:T(8,128)(2,1)S(1)}, u32[]{:S(2)}, u32[]{:S(2)}) collective-permute-start(bf16[128,1024]{1,0:T(8,128)(2,1)S(1)} %copy-done.5), channel_id=1, source_target_pairs={{0,16},{4,20},{8,24},{12,28},{16,0},{20,4},{24,8},{28,12},{1,17},{... | collective-permute-start | bytes 786440 | tf_op jit(solution)/shard_map/ppermute | solution.py:377
  35.5 13.2 %collective-permute-start.20 = (bf16[128,1024]{1,0:T(8,128)(2,1)S(1)}, bf16[128,1024]{1,0:T(8,128)(2,1)S(1)}, u32[]{:S(2)}, u32[]{:S(2)}) collective-permute-start(bf16[128,1024]{1,0:T(8,128)(2,1)S(1)} %copy-done.5), channel_id=1, source_target_pairs={{0,24},{4,28},{8,16},{12,20},{16,8},{20,12},{24,0},{28,4},{1,25},{... | collective-permute-start | bytes 786440 | tf_op jit(solution)/shard_map/ppermute | solution.py:377
  37.0 12.5 %collective-permute-start.22 = (bf16[128,1024]{1,0:T(8,128)(2,1)S(1)}, bf16[128,1024]{1,0:T(8,128)(2,1)S(1)}, u32[]{:S(2)}, u32[]{:S(2)}) collective-permute-start(bf16[128,1024]{1,0:T(8,128)(2,1)S(1)} %copy-done.5), channel_id=1, source_target_pairs={{0,4},{4,0},{8,12},{12,8},{16,20},{20,16},{24,28},{28,24},{1,5},{5... | collective-permute-start | bytes 786440 | tf_op jit(solution)/shard_map/ppermute | solution.py:377
  43.1 8.8 %collective-permute-start.21 = (bf16[256,512]{1,0:T(8,128)(2,1)S(1)}, bf16[256,512]{1,0:T(8,128)(2,1)S(1)}, u32[]{:S(2)}, u32[]{:S(2)}) collective-permute-start(bf16[256,512]{1,0:T(8,128)(2,1)S(1)} %get-tuple-element.52), channel_id=1, source_target_pairs={{0,1},{1,0},{2,3},{3,2},{4,5},{5,4},{6,7},{7,6},{8,9},{9,8},{10,11... | collective-permute-start | bytes 786440 | tf_op jit(solution)/shard_map/ppermute | solution.py:380
  44.3 7.6 %copy-start.4 = (bf16[1,256,1024]{2,1,0:T(8,128)(2,1)S(1)}, bf16[1,256,1024]{2,1,0:T(8,128)(2,1)}, u32[]{:S(2)}) copy-start(bf16[1,256,1024]{2,1,0:T(8,128)(2,1)} %param.15) | copy-start | bytes 1572868
  48.7 3.2 %collective-permute-start.23 = (bf16[128,1024]{1,0:T(8,128)(2,1)S(1)}, bf16[128,1024]{1,0:T(8,128)(2,1)S(1)}, u32[]{:S(2)}, u32[]{:S(2)}) collective-permute-start(bf16[128,1024]{1,0:T(8,128)(2,1)S(1)} %collective-permute-done.18.near_0_), channel_id=1, source_target_pairs={{0,4},{4,0},{8,12},{12,8},{16,20},{20,16},{24,28},{28,24},{1,5},{5... | collective-permute-start | bytes 786440 | tf_op jit(solution)/shard_map/ppermute | solution.py:377
  49.0 3.0 %collective-permute-start.24 = (bf16[128,1024]{1,0:T(8,128)(2,1)S(1)}, bf16[128,1024]{1,0:T(8,128)(2,1)S(1)}, u32[]{:S(2)}, u32[]{:S(2)}) collective-permute-start(bf16[128,1024]{1,0:T(8,128)(2,1)S(1)} %collective-permute-done.19.near_1_), channel_id=1, source_target_pairs={{0,4},{4,0},{8,12},{12,8},{16,20},{20,16},{24,28},{28,24},{1,5},{5... | collective-permute-start | bytes 786440 | tf_op jit(solution)/shard_map/ppermute | solution.py:377
  49.2 2.7 %collective-permute-start.25 = (bf16[128,1024]{1,0:T(8,128)(2,1)S(1)}, bf16[128,1024]{1,0:T(8,128)(2,1)S(1)}, u32[]{:S(2)}, u32[]{:S(2)}) collective-permute-start(bf16[128,1024]{1,0:T(8,128)(2,1)S(1)} %collective-permute-done.20.near_2_), channel_id=1, source_target_pairs={{0,4},{4,0},{8,12},{12,8},{16,20},{20,16},{24,28},{28,24},{1,5},{5... | collective-permute-start | bytes 786440 | tf_op jit(solution)/shard_map/ppermute | solution.py:377

commit v9 on v8

--- a/solution.py
+++ b/solution.py
@@ -157,13 +157,8 @@
         start += width
 
 
-def table_kernel(where_ref, bytes_ref, conv_ref, total_ref, out_ref):
-    core = where_ref[1]
-    taps_in = conv_ref.shape[0]
-    half = total_ref.shape[0]
-    rows = pl.ds(pl.multiple_of(core * half, half), half)
-    mates = bytes_ref[rows, pl.ds(pl.multiple_of((1 - core) * taps_in, taps_in), taps_in)]
-    total = total_ref[...] + jnp.dot(mates, conv_ref[...], preferred_element_type=jnp.float32)
+def table_kernel(bytes_ref, conv_ref, total_ref, out_ref):
+    total = total_ref[...] + jnp.dot(bytes_ref[...], conv_ref[...], preferred_element_type=jnp.float32)
     out_ref[...] = total.astype(jnp.bfloat16)
 
 
@@ -391,10 +386,11 @@
     taps_in = w_conv.shape[0]
     mine = lax.dynamic_slice(byte_table, (core * half, core * taps_in), (half, taps_in))
     total = jnp.dot(mine, w_conv, preferred_element_type=f32)
+    mates = lax.dynamic_slice(byte_table, (core * half, (1 - core) * taps_in), (half, taps_in))
     rope = jnp.asarray(rope_tables(n_ctx, rows))
     (own_t,) = call(
-        table_kernel, "tap_table", 8, 10**8, [SMEM, VMEM, VMEM, VMEM], [((half, features), bf16)]
-    )(where, byte_table, mate_conv, total)
+        table_kernel, "tap_table", 8, 10**8, [VMEM, VMEM, VMEM], [((half, features), bf16)]
+    )(mates, mate_conv, total)
     near_t = to_near(own_t)
 
     ids, late_qkv, unused = lax.optimization_barrier((byte_ids, w_qkv, own_t))

time: 55.3 us -> 54 us (0.976)
  waiting for transfers between devices: 14.2 us -> 13.5 us
  Pallas kernels: 19.9 us -> 19.3 us
    unnamed x16 -> x14, local copies, waits for them, and re-layouts: 1.03 us -> 0.03 us
    dynamic_slice x0 -> x1, local copies, waits for them, and re-layouts: none -> 0.99 us  [head_body(): lax.dynamic_slice(byte_table, (core * half, (1 - core) * taps_in), (half,...]
    ppermute x22, waiting for transfers between devices: 4.55 us -> 3.89 us  [swap(): return lax.ppermute(x, 'fsdp', [(d, d ^ j) for d in range(n_fsdp)])]
  transfers between devices with their start and end apart: 26 -> 26, of which waited for: 7 -> 6; matrix products, arithmetic and copies ran while one was open for 3% -> 5% of each run, Pallas kernels for 31% -> 31%
where the time goes in v9:
time: 54 us; the launch traced here: 53.1 us
  Pallas kernels  19.3 us (36%)
  starting transfers between devices  16.8 us (31%)
  waiting for transfers between devices  13.5 us (25%)
  matrix products  1.5 us (3%)
  local copies, waits for them, and re-layouts  1.02 us (2%)
  between operations  0.91 us (2%)
    ppermute x22, starting transfers between devices, swap(): return lax.ppermute(x, 'fsdp', [(d, d ^ j) for d in range(n_fsdp)])  12.6 us
    ppermute x4, waiting for transfers between devices, along(): return lax.ppermute(x, 'ctx', pairs)  9.6 us
    pallas_call x1, Pallas kernels, head_body(): call(lift_kernel, 'lift', 16, 4 * 10 ** 9, [SMEM, VMEM] + piece_specs + [...  6.13 us
    pallas_call x1, Pallas kernels, head_body(): call(own_kernel, 'own_block', 12, 3 * 10 ** 9, [SMEM, VMEM, VMEM, VMEM],...  4.31 us
    ppermute x4, starting transfers between devices, along(): return lax.ppermute(x, 'ctx', pairs)  4.21 us
    pallas_call x1, Pallas kernels, head_body(): call(latent_kernel, 'latents', 18, 2 * 10 ** 9, [SMEM, VMEM] + piece_spec...  4.02 us
    ppermute x22, waiting for transfers between devices, swap(): return lax.ppermute(x, 'fsdp', [(d, d ^ j) for d in range(n_fsdp)])  3.89 us
    pallas_call x1, Pallas kernels, head_body(): call(out_kernel, 'project_out', 12, 10 ** 9, [SMEM, VMEM, VMEM] + piece_s...  2.44 us
  transfers between devices with their start and end apart: 26, of which 6 were waited for; matrix products, arithmetic and copies ran while one was open for 5% of the time, Pallas kernels for 31%

profile of v9, /device:TPU:24, one launch (start us, length us, event | category | flops | bytes accessed | tf_op | source)
XLA Modules:
  0.0 53.1 jit_solution(2667929479190544973)
XLA Ops:
  0.6 0.0 copy-start.1
  0.7 0.1 collective-permute-start
  0.8 1.0 %dynamic_slice.6.bytes_ref = bf16[128,384]{1,0:T(8,128)(2,1)S(1)} dynamic-slice(bf16[256,768]{1,0:T(8,128)(2,1)} %param.10, s32[]{:T(128)S(6)} %select_n.23, s32[]{:T(128)S(6)} %select_n.24), dynamic_slice_sizes={128,384} | dynamic-slice | bytes 196612 | tf_op jit(solution)/shard_map/dynamic_slice | solution.py:389
  1.8 1.5 %fusion.total_ref = f32[128,1024]{1,0:T(8,128)S(1)} fusion(bf16[384,1024]{1,0:T(8,128)(2,1)} %param.11, bf16[256,768]{1,0:T(8,128)(2,1)} %param.10, s32[]{:T(128)S(6)} %select_n.23, s32[]{:T(128)S(6)} %select_n.25), kind=kOutput, calls=%fused_computation | convolution fusion | flops 100663296 | bytes 1409032 | tf_op jit(solution)/shard_map/dot_general | solution.py:388
  3.3 0.0 collective-permute-done.conv_ref
  3.3 0.3 tap_table.1.own
  3.6 2.5 %collective-permute-start.1 = (bf16[128,1024]{1,0:T(8,128)(2,1)S(1)}, bf16[128,1024]{1,0:T(8,128)(2,1)S(1)}, u32[]{:S(2)}, u32[]{:S(2)}) collective-permute-start(bf16[128,1024]{1,0:T(8,128)(2,1)S(1)} %tap_table.1.own), channel_id=1, source_target_pairs={{0,24},{4,28},{8,16},{12,20},{16,8},{20,12},{24,0},{28,4},{1,25},{... | collective-permute-start | bytes 786440 | tf_op jit(solution)/shard_map/ppermute | solution.py:372
  6.1 0.5 %collective-permute-start.5 = (bf16[128,1024]{1,0:T(8,128)(2,1)S(1)}, bf16[128,1024]{1,0:T(8,128)(2,1)S(1)}, u32[]{:S(2)}, u32[]{:S(2)}) collective-permute-start(bf16[128,1024]{1,0:T(8,128)(2,1)S(1)} %tap_table.1.own), channel_id=1, source_target_pairs={{0,8},{4,12},{8,0},{12,4},{16,24},{20,28},{24,16},{28,20},{1,9},{5... | collective-permute-start | bytes 786440 | tf_op jit(solution)/shard_map/ppermute | solution.py:372
  6.7 0.5 collective-permute-start.6
  7.2 0.5 collective-permute-start.2
  7.7 0.1 pad_add_fusion.where_ref
  7.7 1.3 %collective-permute-start.3 = (s32[1,1024]{1,0:T(1,128)S(1)}, s32[1,1024]{1,0:T(1,128)S(1)}, u32[]{:S(2)}, u32[]{:S(2)}) collective-permute-start(s32[1,1024]{1,0:T(1,128)S(1)} %copy-done.5), channel_id=1, source_target_pairs={{0,2},{1,3},{4,6},{5,7},{8,10},{9,11},{12,14},{13,15},{16,18},{17,... | collective-permute-start | bytes 12296 | tf_op jit(solution)/shard_map/ppermute | solution.py:375
  9.0 1.8 %collective-permute-done.2.ids_refs_1_ = s32[1,1024]{1,0:T(1,128)S(1)} collective-permute-done((s32[1,1024]{1,0:T(1,128)S(1)}, s32[1,1024]{1,0:T(1,128)S(1)}, u32[]{:S(2)}, u32[]{:S(2)}) %collective-permute-start.2) | collective-permute-done | bytes 4128 | tf_op jit(solution)/shard_map/ppermute | solution.py:375
  10.8 1.3 %collective-permute-start.4 = (s32[1,1024]{1,0:T(1,128)S(1)}, s32[1,1024]{1,0:T(1,128)S(1)}, u32[]{:S(2)}, u32[]{:S(2)}) collective-permute-start(s32[1,1024]{1,0:T(1,128)S(1)} %copy-done.5), channel_id=1, source_target_pairs={{0,3},{1,2},{4,7},{5,6},{8,11},{9,10},{12,15},{13,14},{16,19},{17,... | collective-permute-start | bytes 12296 | tf_op jit(solution)/shard_map/ppermute | solution.py:375
  12.1 0.6 %qkv_part.1 = (bf16[128,768]{1,0:T(8,128)(2,1)S(1)}, s32[1,256]{1,0:T(1,128)S(1)}, f32[520,128]{1,0:T(8,128)S(1)}) custom-call(s32[3]{0:T(128)S(1)} %pad_add_fusion.where_ref, bf16[128,1536]{1,0:T(8,128)(2,1)S(1)} %copy-done, s32[1,256]{1,0:T(1,128)S(1)} %copy-done.2, f32[520,128]{1,0:T(8,128)S(1)} %copy-done.1), custom_call_target="tpu_custom_call" | custom-call | flops 100000000 | bytes 4194304 | tf_op jit(solution)/shard_map/qkv_part/pallas_call | solution.py:403
  12.7 1.4 %collective-permute-done.3.ids_refs_2_ = s32[1,1024]{1,0:T(1,128)S(1)} collective-permute-done((s32[1,1024]{1,0:T(1,128)S(1)}, s32[1,1024]{1,0:T(1,128)S(1)}, u32[]{:S(2)}, u32[]{:S(2)}) %collective-permute-start.3) | collective-permute-done | bytes 4128 | tf_op jit(solution)/shard_map/ppermute | solution.py:375
  14.1 0.0 collective-permute-start.10
  14.1 4.0 %collective-permute-done.4.ids_refs_3_ = s32[1,1024]{1,0:T(1,128)S(1)} collective-permute-done((s32[1,1024]{1,0:T(1,128)S(1)}, s32[1,1024]{1,0:T(1,128)S(1)}, u32[]{:S(2)}, u32[]{:S(2)}) %collective-permute-start.4) | collective-permute-done | bytes 4128 | tf_op jit(solution)/shard_map/ppermute | solution.py:375
  18.1 0.0 collective-permute-done.1.near_2_
  18.1 0.0 collective-permute-start.13
  18.1 0.8 %collective-permute-done.5.near_0_ = bf16[128,1024]{1,0:T(8,128)(2,1)S(1)} collective-permute-done((bf16[128,1024]{1,0:T(8,128)(2,1)S(1)}, bf16[128,1024]{1,0:T(8,128)(2,1)S(1)}, u32[]{:S(2)}, u32[]{:S(2)}) %collective-permute-start.5) | collective-permute-done | bytes 262176 | tf_op jit(solution)/shard_map/ppermute | solution.py:372
  18.9 0.0 collective-permute-start.11
  18.9 0.0 collective-permute-done.6.near_1_
  18.9 0.5 collective-permute-start.12
  19.4 1.5 %collective-permute-start.7 = (bf16[128,768]{1,0:T(8,128)(2,1)S(1)}, bf16[128,768]{1,0:T(8,128)(2,1)S(1)}, u32[]{:S(2)}, u32[]{:S(2)}) collective-permute-start(bf16[128,768]{1,0:T(8,128)(2,1)S(1)} %get-tuple-element.36.own), channel_id=1, source_target_pairs={{0,8},{4,12},{8,0},{12,4},{16,24},{20,28},{24,16},{28,20},{1,9},{5... | collective-permute-start | bytes 589832 | tf_op jit(solution)/shard_map/ppermute | solution.py:372
  21.0 0.0 collective-permute-done.10.mate_own
  21.0 0.9 %collective-permute-start.8 = (bf16[128,768]{1,0:T(8,128)(2,1)S(1)}, bf16[128,768]{1,0:T(8,128)(2,1)S(1)}, u32[]{:S(2)}, u32[]{:S(2)}) collective-permute-start(bf16[128,768]{1,0:T(8,128)(2,1)S(1)} %get-tuple-element.36.own), channel_id=1, source_target_pairs={{0,16},{4,20},{8,24},{12,28},{16,0},{20,4},{24,8},{28,12},{1,17},{... | collective-permute-start | bytes 589832 | tf_op jit(solution)/shard_map/ppermute | solution.py:372
  21.9 0.0 collective-permute-done.13.mate_near_2_
  21.9 1.1 %collective-permute-start.9 = (bf16[128,768]{1,0:T(8,128)(2,1)S(1)}, bf16[128,768]{1,0:T(8,128)(2,1)S(1)}, u32[]{:S(2)}, u32[]{:S(2)}) collective-permute-start(bf16[128,768]{1,0:T(8,128)(2,1)S(1)} %get-tuple-element.36.own), channel_id=1, source_target_pairs={{0,24},{4,28},{8,16},{12,20},{16,8},{20,12},{24,0},{28,4},{1,25},{... | collective-permute-start | bytes 589832 | tf_op jit(solution)/shard_map/ppermute | solution.py:372
  23.0 1.6 %one_hot.1.hot_ref = bf16[4,256,1024]{2,1,0:T(8,128)(2,1)S(1)} custom-call(s32[3]{0:T(128)S(1)} %pad_add_fusion.where_ref, s32[1,1024]{1,0:T(1,128)S(1)} %copy-done.5, s32[1,1024]{1,0:T(1,128)S(1)} %collective-permute-done.2.ids_refs_1_, s32[1,1024]{1,0:T(1,128)S(1)} %collective-permute-done.3.ids_refs_2_, s32[1,1024]{1,0:T(1,128)S(1)} %collective-permute-done.4.ids_refs_3_), custom_call_target="tpu_custom_call" | custom-call | flops 1000000000 | bytes 4194304 | tf_op jit(solution)/shard_map/one_hot/pallas_call | solution.py:412
  24.5 0.0 copy-start.4
  24.5 0.0 collective-permute-done.11.mate_near_0_
  24.6 0.1 collective-permute-start.14
  24.6 0.0 collective-permute-done.12.mate_near_1_
  24.6 4.0 %latents.1 = (bf16[4,256,1024]{2,1,0:T(8,128)(2,1)S(1)}, bf16[256,1024]{1,0:T(8,128)(2,1)S(1)}) custom-call(s32[3]{0:T(128)S(1)} %pad_add_fusion.where_ref, bf16[4,256,1024]{2,1,0:T(8,128)(2,1)S(1)} %one_hot.1.hot_ref, bf16[128,1024]{1,0:T(8,128)(2,1)S(1)} %tap_table.1.own, bf16[128,1024]{1,0:T(8,128)(2,1)S(1)} %collective-permute-done.5.near_0_, ...), custom_call_target="tpu_custom_call" | custom-call | flops 2000000000 | bytes 4194304 | tf_op jit(solution)/shard_map/latents/pallas_call | solution.py:417
  28.7 0.0 collective-permute-done.7.near_0_
  28.7 3.0 %collective-permute-done.8.near_1_ = bf16[128,768]{1,0:T(8,128)(2,1)S(1)} collective-permute-done((bf16[128,768]{1,0:T(8,128)(2,1)S(1)}, bf16[128,768]{1,0:T(8,128)(2,1)S(1)}, u32[]{:S(2)}, u32[]{:S(2)}) %collective-permute-start.8) | collective-permute-done | bytes 196640 | tf_op jit(solution)/shard_map/ppermute | solution.py:372
  31.7 0.0 collective-permute-done.9.near_2_
  31.7 0.0 collective-permute-start.15
  31.7 0.5 collective-permute-start.16
  32.2 0.0 collective-permute-start.17
  32.2 1.1 %collective-permute-start.18 = (bf16[128,1024]{1,0:T(8,128)(2,1)S(1)}, bf16[128,1024]{1,0:T(8,128)(2,1)S(1)}, u32[]{:S(2)}, u32[]{:S(2)}) collective-permute-start(bf16[128,1024]{1,0:T(8,128)(2,1)S(1)} %copy-done.4), channel_id=1, source_target_pairs={{0,8},{4,12},{8,0},{12,4},{16,24},{20,28},{24,16},{28,20},{1,9},{5... | collective-permute-start | bytes 786440 | tf_op jit(solution)/shard_map/ppermute | solution.py:372
  33.4 0.0 collective-permute-done.14.mate_own
  33.4 0.8 %collective-permute-start.19 = (bf16[128,1024]{1,0:T(8,128)(2,1)S(1)}, bf16[128,1024]{1,0:T(8,128)(2,1)S(1)}, u32[]{:S(2)}, u32[]{:S(2)}) collective-permute-start(bf16[128,1024]{1,0:T(8,128)(2,1)S(1)} %copy-done.4), channel_id=1, source_target_pairs={{0,16},{4,20},{8,24},{12,28},{16,0},{20,4},{24,8},{28,12},{1,17},{... | collective-permute-start | bytes 786440 | tf_op jit(solution)/shard_map/ppermute | solution.py:372
  34.2 0.0 collective-permute-done.15.mate_near_0_
  34.2 1.6 %collective-permute-start.20 = (bf16[128,1024]{1,0:T(8,128)(2,1)S(1)}, bf16[128,1024]{1,0:T(8,128)(2,1)S(1)}, u32[]{:S(2)}, u32[]{:S(2)}) collective-permute-start(bf16[128,1024]{1,0:T(8,128)(2,1)S(1)} %copy-done.4), channel_id=1, source_target_pairs={{0,24},{4,28},{8,16},{12,20},{16,8},{20,12},{24,0},{28,4},{1,25},{... | collective-permute-start | bytes 786440 | tf_op jit(solution)/shard_map/ppermute | solution.py:372
  35.7 0.0 collective-permute-done.16.mate_near_1_
  35.7 0.0 collective-permute-start.22
  35.7 0.0 collective-permute-done.17.mate_near_2_
  35.8 6.1 %lift.1 = (bf16[256,512]{1,0:T(8,128)(2,1)S(1)}, bf16[8,256,64]{2,1,0:T(8,128)(2,1)S(1)}, bf16[2,1024,64]{2,1,0:T(8,128)(2,1)S(1)}, bf16[2,80,1024]{2,1,0:T(8,128)(2,1)S(1)}) custom-call(s32[3]{0:T(128)S(1)} %pad_add_fusion.where_ref, bf16[4,256,1024]{2,1,0:T(8,128)(2,1)S(1)} %get-tuple-element.42.normed_ref, bf16[128,768]{1,0:T(8,128)(2,1)S(1)} %get-tuple-element.36.own, ...), custom_call_target="tpu_custom_call" | custom-call | flops 4000000000 | bytes 4194304 | tf_op jit(solution)/shard_map/lift/pallas_call | solution.py:428
  41.9 1.2 %collective-permute-start.21 = (bf16[256,512]{1,0:T(8,128)(2,1)S(1)}, bf16[256,512]{1,0:T(8,128)(2,1)S(1)}, u32[]{:S(2)}, u32[]{:S(2)}) collective-permute-start(bf16[256,512]{1,0:T(8,128)(2,1)S(1)} %get-tuple-element.52), channel_id=1, source_target_pairs={{0,1},{1,0},{2,3},{3,2},{4,5},{5,4},{6,7},{7,6},{8,9},{9,8},{10,11... | collective-permute-start | bytes 786440 | tf_op jit(solution)/shard_map/ppermute | solution.py:375
  43.1 4.3 %own_block.1.own_att = bf16[256,512]{1,0:T(8,128)(2,1)S(1)} custom-call(s32[3]{0:T(128)S(1)} %pad_add_fusion.where_ref, bf16[8,256,64]{2,1,0:T(8,128)(2,1)S(1)} %get-tuple-element.47.query_ref, bf16[2,1024,64]{2,1,0:T(8,128)(2,1)S(1)} %get-tuple-element.48.k_ref, bf16[2,80,1024]{2,1,0:T(8,128)(2,1)S(1)} %get-tuple-element.49.v_ref), custom_call_target="tpu_custom_call" | custom-call | flops 3000000000 | bytes 4194304 | tf_op jit(solution)/shard_map/own_block/pallas_call | solution.py:441
  47.4 0.0 collective-permute-done.18.near_0_
  47.4 0.0 collective-permute-done.19.near_1_
  47.4 0.0 collective-permute-done.20.near_2_
  47.4 0.3 collective-permute-start.23
  47.7 0.3 collective-permute-start.24
  48.0 0.2 collective-permute-start.25
  48.2 0.0 collective-permute-done.22.mate_own
  48.2 2.4 %collective-permute-done.21.mate_att = bf16[256,512]{1,0:T(8,128)(2,1)S(1)} collective-permute-done((bf16[256,512]{1,0:T(8,128)(2,1)S(1)}, bf16[256,512]{1,0:T(8,128)(2,1)S(1)}, u32[]{:S(2)}, u32[]{:S(2)}) %collective-permute-start.21) | collective-permute-done | bytes 262176 | tf_op jit(solution)/shard_map/ppermute | solution.py:375
  50.7 0.0 collective-permute-done.23.mate_near_0_
  50.7 0.0 collective-permute-done.24.mate_near_1_
  50.7 0.0 collective-permute-done.25.mate_near_2_
  50.7 2.4 %project_out.1 = (bf16[256,1024]{1,0:T(8,128)(2,1)}, f32[1,256]{1,0:T(1,128)}) custom-call(s32[3]{0:T(128)S(1)} %pad_add_fusion.where_ref, bf16[256,512]{1,0:T(8,128)(2,1)S(1)} %own_block.1.own_att, bf16[256,512]{1,0:T(8,128)(2,1)S(1)} %collective-permute-done.21.mate_att, bf16[128,1024]{1,0:T(8,128)(2,1)S(1)} %copy-done.4, ...), custom_call_target="tpu_custom_call" | custom-call | flops 1000000000 | bytes 4194304 | tf_op jit(solution)/shard_map/project_out/pallas_call | solution.py:445
  (13 shorter events, 0.0 us)
Async XLA Ops:
  0.6 11.5 %copy-start.1 = (f32[520,128]{1,0:T(8,128)S(1)}, f32[520,128]{1,0:T(8,128)}, u32[]{:S(2)}) copy-start(f32[520,128]{1,0:T(8,128)} %constant.45.clone.rope_ref) | copy-start | bytes 798724
  0.6 11.5 %copy-start = (bf16[128,1536]{1,0:T(8,128)(2,1)S(1)}, bf16[128,1536]{1,0:T(8,128)(2,1)}, u32[]{:S(2)}) copy-start(bf16[128,1536]{1,0:T(8,128)(2,1)} %qkv_ref) | copy-start | bytes 1179652
  0.7 6.5 %copy-start.5 = (s32[1,1024]{1,0:T(1,128)S(1)}, s32[1,1024]{1,0:T(1,128)}, u32[]{:S(2)}) copy-start(s32[1,1024]{1,0:T(1,128)} %ids_refs_0_) | copy-start | bytes 12292
  0.7 11.4 %copy-start.2 = (s32[1,256]{1,0:T(1,128)S(1)}, s32[1,256]{1,0:T(1,128)}, u32[]{:S(2)}) copy-start(s32[1,256]{1,0:T(1,128)} %align_ref.1) | copy-start | bytes 3076
  0.7 18.7 %copy-start.6 = (bf16[1024]{0:T(1024)(128)(2,1)S(1)}, bf16[1024]{0:T(1024)(128)(2,1)}, u32[]{:S(2)}) copy-start(bf16[1024]{0:T(1024)(128)(2,1)} %param.14) | copy-start | bytes 6148
  0.7 2.6 %collective-permute-start = (bf16[384,1024]{1,0:T(8,128)(2,1)}, bf16[384,1024]{1,0:T(8,128)(2,1)S(1)}, u32[]{:S(2)}, u32[]{:S(2)}) collective-permute-start(bf16[384,1024]{1,0:T(8,128)(2,1)} %param.11), channel_id=1, source_target_pairs={{0,4},{4,0},{8,12},{12,8},{16,20},{20,16},{24,28},{28,24},{1,5},{5... | collective-permute-start | bytes 2359304 | tf_op jit(solution)/shard_map/ppermute | solution.py:372
  3.6 14.5 %collective-permute-start.1 = (bf16[128,1024]{1,0:T(8,128)(2,1)S(1)}, bf16[128,1024]{1,0:T(8,128)(2,1)S(1)}, u32[]{:S(2)}, u32[]{:S(2)}) collective-permute-start(bf16[128,1024]{1,0:T(8,128)(2,1)S(1)} %tap_table.1.own), channel_id=1, source_target_pairs={{0,24},{4,28},{8,16},{12,20},{16,8},{20,12},{24,0},{28,4},{1,25},{... | collective-permute-start | bytes 786440 | tf_op jit(solution)/shard_map/ppermute | solution.py:372
  6.1 12.7 %collective-permute-start.5 = (bf16[128,1024]{1,0:T(8,128)(2,1)S(1)}, bf16[128,1024]{1,0:T(8,128)(2,1)S(1)}, u32[]{:S(2)}, u32[]{:S(2)}) collective-permute-start(bf16[128,1024]{1,0:T(8,128)(2,1)S(1)} %tap_table.1.own), channel_id=1, source_target_pairs={{0,8},{4,12},{8,0},{12,4},{16,24},{20,28},{24,16},{28,20},{1,9},{5... | collective-permute-start | bytes 786440 | tf_op jit(solution)/shard_map/ppermute | solution.py:372
  6.7 12.2 %collective-permute-start.6 = (bf16[128,1024]{1,0:T(8,128)(2,1)S(1)}, bf16[128,1024]{1,0:T(8,128)(2,1)S(1)}, u32[]{:S(2)}, u32[]{:S(2)}) collective-permute-start(bf16[128,1024]{1,0:T(8,128)(2,1)S(1)} %tap_table.1.own), channel_id=1, source_target_pairs={{0,16},{4,20},{8,24},{12,28},{16,0},{20,4},{24,8},{28,12},{1,17},{... | collective-permute-start | bytes 786440 | tf_op jit(solution)/shard_map/ppermute | solution.py:372
  7.2 3.6 %collective-permute-start.2 = (s32[1,1024]{1,0:T(1,128)S(1)}, s32[1,1024]{1,0:T(1,128)S(1)}, u32[]{:S(2)}, u32[]{:S(2)}) collective-permute-start(s32[1,1024]{1,0:T(1,128)S(1)} %copy-done.5), channel_id=1, source_target_pairs={{0,1},{1,0},{2,3},{3,2},{4,5},{5,4},{6,7},{7,6},{8,9},{9,8},{10,11... | collective-permute-start | bytes 12296 | tf_op jit(solution)/shard_map/ppermute | solution.py:375
  7.7 6.4 %collective-permute-start.3 = (s32[1,1024]{1,0:T(1,128)S(1)}, s32[1,1024]{1,0:T(1,128)S(1)}, u32[]{:S(2)}, u32[]{:S(2)}) collective-permute-start(s32[1,1024]{1,0:T(1,128)S(1)} %copy-done.5), channel_id=1, source_target_pairs={{0,2},{1,3},{4,6},{5,7},{8,10},{9,11},{12,14},{13,15},{16,18},{17,... | collective-permute-start | bytes 12296 | tf_op jit(solution)/shard_map/ppermute | solution.py:375
  10.8 7.3 %collective-permute-start.4 = (s32[1,1024]{1,0:T(1,128)S(1)}, s32[1,1024]{1,0:T(1,128)S(1)}, u32[]{:S(2)}, u32[]{:S(2)}) collective-permute-start(s32[1,1024]{1,0:T(1,128)S(1)} %copy-done.5), channel_id=1, source_target_pairs={{0,3},{1,2},{4,7},{5,6},{8,11},{9,10},{12,15},{13,14},{16,19},{17,... | collective-permute-start | bytes 12296 | tf_op jit(solution)/shard_map/ppermute | solution.py:375
  14.1 6.8 %collective-permute-start.10 = (bf16[128,1024]{1,0:T(8,128)(2,1)S(1)}, bf16[128,1024]{1,0:T(8,128)(2,1)S(1)}, u32[]{:S(2)}, u32[]{:S(2)}) collective-permute-start(bf16[128,1024]{1,0:T(8,128)(2,1)S(1)} %tap_table.1.own), channel_id=1, source_target_pairs={{0,4},{4,0},{8,12},{12,8},{16,20},{20,16},{24,28},{28,24},{1,5},{5... | collective-permute-start | bytes 786440 | tf_op jit(solution)/shard_map/ppermute | solution.py:372
  18.1 3.8 %collective-permute-start.13 = (bf16[128,1024]{1,0:T(8,128)(2,1)S(1)}, bf16[128,1024]{1,0:T(8,128)(2,1)S(1)}, u32[]{:S(2)}, u32[]{:S(2)}) collective-permute-start(bf16[128,1024]{1,0:T(8,128)(2,1)S(1)} %collective-permute-done.1.near_2_), channel_id=1, source_target_pairs={{0,4},{4,0},{8,12},{12,8},{16,20},{20,16},{24,28},{28,24},{1,5},{5... | collective-permute-start | bytes 786440 | tf_op jit(solution)/shard_map/ppermute | solution.py:372
  18.9 5.7 %collective-permute-start.11 = (bf16[128,1024]{1,0:T(8,128)(2,1)S(1)}, bf16[128,1024]{1,0:T(8,128)(2,1)S(1)}, u32[]{:S(2)}, u32[]{:S(2)}) collective-permute-start(bf16[128,1024]{1,0:T(8,128)(2,1)S(1)} %collective-permute-done.5.near_0_), channel_id=1, source_target_pairs={{0,4},{4,0},{8,12},{12,8},{16,20},{20,16},{24,28},{28,24},{1,5},{5... | collective-permute-start | bytes 786440 | tf_op jit(solution)/shard_map/ppermute | solution.py:372
  18.9 5.7 %collective-permute-start.12 = (bf16[128,1024]{1,0:T(8,128)(2,1)S(1)}, bf16[128,1024]{1,0:T(8,128)(2,1)S(1)}, u32[]{:S(2)}, u32[]{:S(2)}) collective-permute-start(bf16[128,1024]{1,0:T(8,128)(2,1)S(1)} %collective-permute-done.6.near_1_), channel_id=1, source_target_pairs={{0,4},{4,0},{8,12},{12,8},{16,20},{20,16},{24,28},{28,24},{1,5},{5... | collective-permute-start | bytes 786440 | tf_op jit(solution)/shard_map/ppermute | solution.py:372
  19.4 9.3 %collective-permute-start.7 = (bf16[128,768]{1,0:T(8,128)(2,1)S(1)}, bf16[128,768]{1,0:T(8,128)(2,1)S(1)}, u32[]{:S(2)}, u32[]{:S(2)}) collective-permute-start(bf16[128,768]{1,0:T(8,128)(2,1)S(1)} %get-tuple-element.36.own), channel_id=1, source_target_pairs={{0,8},{4,12},{8,0},{12,4},{16,24},{20,28},{24,16},{28,20},{1,9},{5... | collective-permute-start | bytes 589832 | tf_op jit(solution)/shard_map/ppermute | solution.py:372
  21.0 10.8 %collective-permute-start.8 = (bf16[128,768]{1,0:T(8,128)(2,1)S(1)}, bf16[128,768]{1,0:T(8,128)(2,1)S(1)}, u32[]{:S(2)}, u32[]{:S(2)}) collective-permute-start(bf16[128,768]{1,0:T(8,128)(2,1)S(1)} %get-tuple-element.36.own), channel_id=1, source_target_pairs={{0,16},{4,20},{8,24},{12,28},{16,0},{20,4},{24,8},{28,12},{1,17},{... | collective-permute-start | bytes 589832 | tf_op jit(solution)/shard_map/ppermute | solution.py:372
  21.9 9.8 %collective-permute-start.9 = (bf16[128,768]{1,0:T(8,128)(2,1)S(1)}, bf16[128,768]{1,0:T(8,128)(2,1)S(1)}, u32[]{:S(2)}, u32[]{:S(2)}) collective-permute-start(bf16[128,768]{1,0:T(8,128)(2,1)S(1)} %get-tuple-element.36.own), channel_id=1, source_target_pairs={{0,24},{4,28},{8,16},{12,20},{16,8},{20,12},{24,0},{28,4},{1,25},{... | collective-permute-start | bytes 589832 | tf_op jit(solution)/shard_map/ppermute | solution.py:372
  24.5 7.7 %copy-start.4 = (bf16[128,1024]{1,0:T(8,128)(2,1)S(1)}, bf16[128,1024]{1,0:T(8,128)(2,1)}, u32[]{:S(2)}) copy-start(bf16[128,1024]{1,0:T(8,128)(2,1)} %own) | copy-start | bytes 786436
  24.6 8.8 %collective-permute-start.14 = (bf16[128,768]{1,0:T(8,128)(2,1)S(1)}, bf16[128,768]{1,0:T(8,128)(2,1)S(1)}, u32[]{:S(2)}, u32[]{:S(2)}) collective-permute-start(bf16[128,768]{1,0:T(8,128)(2,1)S(1)} %get-tuple-element.36.own), channel_id=1, source_target_pairs={{0,4},{4,0},{8,12},{12,8},{16,20},{20,16},{24,28},{28,24},{1,5},{5... | collective-permute-start | bytes 589832 | tf_op jit(solution)/shard_map/ppermute | solution.py:372
  31.7 2.5 %collective-permute-start.15 = (bf16[128,768]{1,0:T(8,128)(2,1)S(1)}, bf16[128,768]{1,0:T(8,128)(2,1)S(1)}, u32[]{:S(2)}, u32[]{:S(2)}) collective-permute-start(bf16[128,768]{1,0:T(8,128)(2,1)S(1)} %collective-permute-done.7.near_0_), channel_id=1, source_target_pairs={{0,4},{4,0},{8,12},{12,8},{16,20},{20,16},{24,28},{28,24},{1,5},{5... | collective-permute-start | bytes 589832 | tf_op jit(solution)/shard_map/ppermute | solution.py:372
  31.7 4.0 %collective-permute-start.16 = (bf16[128,768]{1,0:T(8,128)(2,1)S(1)}, bf16[128,768]{1,0:T(8,128)(2,1)S(1)}, u32[]{:S(2)}, u32[]{:S(2)}) collective-permute-start(bf16[128,768]{1,0:T(8,128)(2,1)S(1)} %collective-permute-done.8.near_1_), channel_id=1, source_target_pairs={{0,4},{4,0},{8,12},{12,8},{16,20},{20,16},{24,28},{28,24},{1,5},{5... | collective-permute-start | bytes 589832 | tf_op jit(solution)/shard_map/ppermute | solution.py:372
  32.2 3.5 %collective-permute-start.17 = (bf16[128,768]{1,0:T(8,128)(2,1)S(1)}, bf16[128,768]{1,0:T(8,128)(2,1)S(1)}, u32[]{:S(2)}, u32[]{:S(2)}) collective-permute-start(bf16[128,768]{1,0:T(8,128)(2,1)S(1)} %collective-permute-done.9.near_2_), channel_id=1, source_target_pairs={{0,4},{4,0},{8,12},{12,8},{16,20},{20,16},{24,28},{28,24},{1,5},{5... | collective-permute-start | bytes 589832 | tf_op jit(solution)/shard_map/ppermute | solution.py:372
  32.2 15.2 %collective-permute-start.18 = (bf16[128,1024]{1,0:T(8,128)(2,1)S(1)}, bf16[128,1024]{1,0:T(8,128)(2,1)S(1)}, u32[]{:S(2)}, u32[]{:S(2)}) collective-permute-start(bf16[128,1024]{1,0:T(8,128)(2,1)S(1)} %copy-done.4), channel_id=1, source_target_pairs={{0,8},{4,12},{8,0},{12,4},{16,24},{20,28},{24,16},{28,20},{1,9},{5... | collective-permute-start | bytes 786440 | tf_op jit(solution)/shard_map/ppermute | solution.py:372
  33.4 14.1 %collective-permute-start.19 = (bf16[128,1024]{1,0:T(8,128)(2,1)S(1)}, bf16[128,1024]{1,0:T(8,128)(2,1)S(1)}, u32[]{:S(2)}, u32[]{:S(2)}) collective-permute-start(bf16[128,1024]{1,0:T(8,128)(2,1)S(1)} %copy-done.4), channel_id=1, source_target_pairs={{0,16},{4,20},{8,24},{12,28},{16,0},{20,4},{24,8},{28,12},{1,17},{... | collective-permute-start | bytes 786440 | tf_op jit(solution)/shard_map/ppermute | solution.py:372
  34.2 13.2 %collective-permute-start.20 = (bf16[128,1024]{1,0:T(8,128)(2,1)S(1)}, bf16[128,1024]{1,0:T(8,128)(2,1)S(1)}, u32[]{:S(2)}, u32[]{:S(2)}) collective-permute-start(bf16[128,1024]{1,0:T(8,128)(2,1)S(1)} %copy-done.4), channel_id=1, source_target_pairs={{0,24},{4,28},{8,16},{12,20},{16,8},{20,12},{24,0},{28,4},{1,25},{... | collective-permute-start | bytes 786440 | tf_op jit(solution)/shard_map/ppermute | solution.py:372
  35.7 12.5 %collective-permute-start.22 = (bf16[128,1024]{1,0:T(8,128)(2,1)S(1)}, bf16[128,1024]{1,0:T(8,128)(2,1)S(1)}, u32[]{:S(2)}, u32[]{:S(2)}) collective-permute-start(bf16[128,1024]{1,0:T(8,128)(2,1)S(1)} %copy-done.4), channel_id=1, source_target_pairs={{0,4},{4,0},{8,12},{12,8},{16,20},{20,16},{24,28},{28,24},{1,5},{5... | collective-permute-start | bytes 786440 | tf_op jit(solution)/shard_map/ppermute | solution.py:372
  41.9 8.8 %collective-permute-start.21 = (bf16[256,512]{1,0:T(8,128)(2,1)S(1)}, bf16[256,512]{1,0:T(8,128)(2,1)S(1)}, u32[]{:S(2)}, u32[]{:S(2)}) collective-permute-start(bf16[256,512]{1,0:T(8,128)(2,1)S(1)} %get-tuple-element.52), channel_id=1, source_target_pairs={{0,1},{1,0},{2,3},{3,2},{4,5},{5,4},{6,7},{7,6},{8,9},{9,8},{10,11... | collective-permute-start | bytes 786440 | tf_op jit(solution)/shard_map/ppermute | solution.py:375
  43.1 7.6 %copy-start.3 = (bf16[1,256,1024]{2,1,0:T(8,128)(2,1)S(1)}, bf16[1,256,1024]{2,1,0:T(8,128)(2,1)}, u32[]{:S(2)}) copy-start(bf16[1,256,1024]{2,1,0:T(8,128)(2,1)} %param.15) | copy-start | bytes 1572868
  47.4 3.2 %collective-permute-start.23 = (bf16[128,1024]{1,0:T(8,128)(2,1)S(1)}, bf16[128,1024]{1,0:T(8,128)(2,1)S(1)}, u32[]{:S(2)}, u32[]{:S(2)}) collective-permute-start(bf16[128,1024]{1,0:T(8,128)(2,1)S(1)} %collective-permute-done.18.near_0_), channel_id=1, source_target_pairs={{0,4},{4,0},{8,12},{12,8},{16,20},{20,16},{24,28},{28,24},{1,5},{5... | collective-permute-start | bytes 786440 | tf_op jit(solution)/shard_map/ppermute | solution.py:372
  47.7 3.0 %collective-permute-start.24 = (bf16[128,1024]{1,0:T(8,128)(2,1)S(1)}, bf16[128,1024]{1,0:T(8,128)(2,1)S(1)}, u32[]{:S(2)}, u32[]{:S(2)}) collective-permute-start(bf16[128,1024]{1,0:T(8,128)(2,1)S(1)} %collective-permute-done.19.near_1_), channel_id=1, source_target_pairs={{0,4},{4,0},{8,12},{12,8},{16,20},{20,16},{24,28},{28,24},{1,5},{5... | collective-permute-start | bytes 786440 | tf_op jit(solution)/shard_map/ppermute | solution.py:372
  48.0 2.7 %collective-permute-start.25 = (bf16[128,1024]{1,0:T(8,128)(2,1)S(1)}, bf16[128,1024]{1,0:T(8,128)(2,1)S(1)}, u32[]{:S(2)}, u32[]{:S(2)}) collective-permute-start(bf16[128,1024]{1,0:T(8,128)(2,1)S(1)} %collective-permute-done.20.near_2_), channel_id=1, source_target_pairs={{0,4},{4,0},{8,12},{12,8},{16,20},{20,16},{24,28},{28,24},{1,5},{5... | collective-permute-start | bytes 786440 | tf_op jit(solution)/shard_map/ppermute | solution.py:372
